TPU v7x, 32 devices: a whole 2x2x4 slice. The times are simulated.
32 devices in a mesh: groups: 2 (over x), dp: 8 (over z, y), ep: 2 (over core).
Axes of the slice: x: 2, y: 2, z: 4, core: 2. Of those that a mesh axis runs over, the one named last changes fastest.
Arguments:
- queries: bfloat16 [2048, 8192], P(('groups', 'dp'), 'ep'), parts along dimension 0, may hold values from -6 to 6
- key_weight: bfloat16 [64, 128, 512], P('ep'), may hold values from -0.25 to 0.25
- value_weight: bfloat16 [64, 512, 128], P('ep'), may hold values from -3 to 3
- prefix_latent: bfloat16 [16384, 512], P(('groups', 'dp')), parts along dimension 0
- fresh_latent: bfloat16 [2048, 512], P(('groups', 'dp')), parts along dimension 0
- span_counts: int32 [16], P(('groups', 'dp')), parts along dimension 0, may hold values from 1 to 2, as said below
- prefix_lengths: int32 [16], P(('groups', 'dp')), parts along dimension 0, may hold values from 0 to 1024, as said below
- routes: int32 [2048, 2], P(('groups', 'dp')), parts along dimension 0, may hold values from 0 to 15, all different within a row; in each aligned block of 128 rows (0 to 127, 128 to 255, ...) at most 16 rows name the same one
Outputs:
- expert_inputs: bfloat16 [32, 8, 16, 8192], P(('groups', 'dp', 'ep')), parts along dimension 0
There are 2 independent parts, one for each index of `groups`. A program takes and returns all parts, laid end to end along the dimension named above; an argument that names none is the same for every part. Nothing has to cross between parts.
Inputs may be any that keep to these rules, and one draw needn't show every extreme that they name: `span_counts`: some prompt has 2 spans. `prefix_lengths`: some prompt has 1024 cached rows. `routes`: among each prompt's 128 slots every expert is named exactly 16 times; a slot names 2 different experts.
All inputs are finite; a program needn't handle non-finite values.
Results may differ from a plain program's by a relative error of at most 0.012.
Values may be sent and summed in bfloat16 or wider, within the bound.
No kernel may reach another device: no remote copies, remote signals or barrier semaphores. Data moves between devices by JAX's collectives and lax.ppermute only.
A program may use at most 64 MiB of HBM per device.

v0:
```python
import jax
import jax.numpy as jnp
from jax import lax
from jax.sharding import PartitionSpec as P

SPAN = 64
KEYBLK = 128
EXP_DEV = 1


def lift(queries, key_weight):
    slots = queries.shape[0]
    split = queries.reshape(slots, key_weight.shape[0], key_weight.shape[1])
    return jnp.einsum("thd,hdc->htc", split, key_weight, preferred_element_type=jnp.float32).astype(
        jnp.bfloat16
    )


def partial_attention(
    lifted, prefix, fresh, fresh_count, prefix_size, offset, stride, value_weight
):
    heads, slots, width = lifted.shape
    scale = 1.0 / jnp.sqrt(jnp.float32(value_weight.shape[2]))
    prefix_blocks = (prefix_size + KEYBLK - 1) // KEYBLK
    fresh_rows = fresh_count * SPAN
    fresh_blocks = (fresh_rows + KEYBLK - 1) // KEYBLK
    limit = prefix_blocks + fresh_blocks
    trips = jnp.maximum(limit - offset + stride - 1, 0) // stride
    query_pos = jnp.arange(slots, dtype=jnp.int32)
    lane = jnp.arange(KEYBLK, dtype=jnp.int32)

    def advance(step_index, carry):
        highest, total, accum = carry
        block_index = offset + step_index * stride
        in_prefix = block_index < prefix_blocks
        prefix_start = jnp.clip(block_index, 0, prefix.shape[0] // KEYBLK - 1) * KEYBLK
        fresh_start = (
            jnp.clip(block_index - prefix_blocks, 0, fresh.shape[0] // KEYBLK - 1) * KEYBLK
        )
        prefix_keys = lax.dynamic_slice_in_dim(prefix, prefix_start, KEYBLK, 0)
        keys = jnp.where(in_prefix, prefix_keys, fresh)
        prefix_ok = jnp.broadcast_to((prefix_start + lane < prefix_size)[None, :], (slots, KEYBLK))
        fresh_pos = fresh_start + lane
        fresh_ok = (fresh_pos[None, :] <= query_pos[:, None]) & (fresh_pos[None, :] < fresh_rows)
        allowed = jnp.where(in_prefix, prefix_ok, fresh_ok)
        scores = jnp.einsum("htc,kc->htk", lifted, keys, preferred_element_type=jnp.float32) * scale
        scores = jnp.where(allowed[None], scores, jnp.float32(-1e30))
        new_high = jnp.maximum(highest, jnp.max(scores, axis=-1))
        weights = jnp.where(allowed[None], jnp.exp(scores - new_high[..., None]), jnp.float32(0.0))
        factor = jnp.exp(highest - new_high)
        total = total * factor + jnp.sum(weights, axis=-1)
        update = jnp.einsum(
            "htk,kc->htc", weights.astype(jnp.bfloat16), keys, preferred_element_type=jnp.float32
        )
        accum = accum * factor[..., None] + update
        return (new_high, total, accum)

    start_state = (
        jnp.full((heads, slots), -1e30, jnp.float32),
        jnp.zeros((heads, slots), jnp.float32),
        jnp.zeros((heads, slots, width), jnp.float32),
    )
    highest, total, accum = lax.fori_loop(0, trips, advance, start_state)
    projected = jnp.einsum(
        "htc,hce->the",
        accum,
        value_weight.astype(jnp.float32),
        precision=lax.Precision.HIGHEST,
        preferred_element_type=jnp.float32,
    )
    return (highest.T, total.T, projected)


def local(
    queries,
    key_weight,
    value_weight,
    prefix_latent,
    fresh_latent,
    span_counts,
    prefix_lengths,
    routes,
):
    slots = queries.shape[0]
    fresh_count = span_counts[0]
    prefix_size = prefix_lengths[0]
    lifted = lift(queries, key_weight)
    highest, total, projected = partial_attention(
        lifted, prefix_latent, fresh_latent, fresh_count, prefix_size, 0, 1, value_weight
    )
    attended = (projected / total[..., None]).reshape(slots, -1).astype(jnp.bfloat16)
    ranks_here = lax.axis_size("dp")
    cores_here = lax.axis_size("ep")
    experts = EXP_DEV * ranks_here * cores_here
    capacity = slots * routes.shape[1] // experts
    valid = jnp.arange(slots, dtype=jnp.int32) < fresh_count * SPAN
    hits = (
        (routes[:, :, None] == jnp.arange(experts, dtype=jnp.int32)[None, None, :])
        & valid[:, None, None]
    ).astype(jnp.int32)
    per_token = jnp.sum(hits, axis=1)
    before = jnp.cumsum(per_token, axis=0) - per_token
    place = jnp.sum(hits * before[:, None, :], axis=-1)
    target = routes * capacity + place
    table = (
        target[:, :, None] == jnp.arange(experts * capacity, dtype=jnp.int32)[None, None, :]
    ) & valid[:, None, None]
    table = jnp.any(table, axis=1).astype(jnp.bfloat16)
    outgoing = jnp.einsum("tp,tf->pf", table, attended, preferred_element_type=jnp.float32).astype(
        jnp.bfloat16
    )
    features = attended.shape[1]
    arrived = lax.all_to_all(
        outgoing.reshape(experts, capacity, features),
        ("dp", "ep"),
        split_axis=0,
        concat_axis=0,
        tiled=True,
    )
    arrived = arrived.reshape(ranks_here, cores_here, EXP_DEV, capacity, features)
    arrived = jnp.transpose(arrived, (2, 0, 3, 1, 4))
    return arrived.reshape(EXP_DEV, ranks_here, capacity, cores_here * features)


def solution(mesh):
    in_specs = (
        P(("groups", "dp"), "ep"),
        P("ep", None, None),
        P("ep", None, None),
        P(("groups", "dp"), None),
        P(("groups", "dp"), None),
        P(("groups", "dp")),
        P(("groups", "dp")),
        P(("groups", "dp"), None),
    )
    out_specs = P(("groups", "dp", "ep"), None, None, None)
    return jax.shard_map(local, mesh=mesh, in_specs=in_specs, out_specs=out_specs, check_vma=False)
```

profile of v0, /device:TPU:0, one launch (start us, length us, event | category | flops | bytes accessed | tf_op | source)
XLA Modules:
  0.0 192.1 jit_solution(14947653135219130508)
XLA Ops:
  1.5 5.4 %convolution_convert_fusion.1 = bf16[32,128,512]{2,1,0:T(8,128)(2,1)} fusion(bf16[32,128,512]{2,1,0:T(8,128)(2,1)} %param.11, bf16[128,4096]{1,0:T(8,128)(2,1)S(1)} %copy-done), kind=kOutput, calls=%fused_computation.31 | convolution fusion | flops 538968064 | bytes 9437184 | tf_op jit(solution)/shard_map/thd,hdc->htc/dot_general | solution.py:14
  6.9 4.3 %broadcast_in_dim.64 = f32[32,128,512]{2,1,0:T(8,128)} broadcast(f32[]{:T(128)} %constant.77.clone.1), dimensions={} | broadcast | bytes 8388612 | tf_op jit(solution)/shard_map/broadcast_in_dim | solution.py:61
  11.2 37.3 %while.17 = (s32[]{:T(128)}, f32[32,128]{1,0:T(8,128)S(1)}, f32[32,128]{1,0:T(8,128)S(1)}, f32[32,128,512]{2,1,0:T(8,128)}, s32[]{:T(128)}, /*index=5*/s32[]{:T(...) while((s32[]{:T(128)}, f32[32,128]{1,0:T(8,128)S(1)}, ...), condition=%wide.region_7.8_spmd.clone.clone, body=%wide.region_4.7_spmd.clone.clone.sunk | while | flops 1084940928 | bytes 95225704 | solution.py:63
  11.2 0.7 fusion.45
  11.9 0.1 fusion.46
  12.1 3.9 %fusion.47 = (f32[32,128]{1,0:T(8,128)S(1)}, f32[128,32,128]{2,0,1:T(8,128)S(1)}) fusion(pred[128,128]{0,1:T(8,128)(4,1)S(1)} %fusion.46, bf16[32,128,512]{2,1,0:T(8,128)(2,1)} %get-tuple-element.313, bf16[128,512]{1,0:T(8,128)(2,1)S(1)} %get-tuple-element.312, bf16[1024,512]{1,0:T(8,128)(2,1)} %get-tuple-element.311, s32[]{:T(128)S(6)} %select_n.121, ...), kind=kOutput, calls=%fused_computation.4.clone.1 | convolution fusion | flops 538505216 | bytes 6586373 | tf_op jit(solution)/shard_map/while/body/htc,kc->htk/dot_general | solution.py:46
  16.0 0.6 fusion.48
  16.6 0.2 copy-done.1
  16.8 3.7 %multiply_add_fusion.6 = f32[32,128,512]{2,1,0:T(8,128)S(1)} fusion(f32[32,128,512]{2,1,0:T(8,128)S(1)} %copy-done.1, f32[32,128]{1,0:T(8,128)S(1)} %get-tuple-element.270, f32[128,32,128]{2,0,1:T(8,128)S(1)} %get-tuple-element.268, f32[32,128]{1,0:T(8,128)S(1)} %max.29, pred[128,128]{0,1:T(8,128)(4,1)S(1)} %fusion.46, ...), kind=kOutput, calls=%fused_computation.1.clone.1 | convolution fusion | flops 543752192 | bytes 19185668 | tf_op jit(solution)/shard_map/while/body/htk,kc->htc/dot_general | solution.py:52
  20.5 3.2 %copy-done.2 = f32[32,128,512]{2,1,0:T(8,128)} copy-done((f32[32,128,512]{2,1,0:T(8,128)}, f32[32,128,512]{2,1,0:T(8,128)S(1)}, u32[]{:S(2)}) %copy-start.2) | copy-done | bytes 8388632 | tf_op jit(solution)/shard_map/while
  23.7 0.7 fusion.45
  24.3 0.1 fusion.46
  24.5 3.9 %fusion.47 = (f32[32,128]{1,0:T(8,128)S(1)}, f32[128,32,128]{2,0,1:T(8,128)S(1)}) fusion(pred[128,128]{0,1:T(8,128)(4,1)S(1)} %fusion.46, bf16[32,128,512]{2,1,0:T(8,128)(2,1)} %get-tuple-element.313, bf16[128,512]{1,0:T(8,128)(2,1)S(1)} %get-tuple-element.312, bf16[1024,512]{1,0:T(8,128)(2,1)} %get-tuple-element.311, s32[]{:T(128)S(6)} %select_n.121, ...), kind=kOutput, calls=%fused_computation.4.clone.1 | convolution fusion | flops 538505216 | bytes 6586373 | tf_op jit(solution)/shard_map/while/body/htc,kc->htk/dot_general | solution.py:46
  28.4 0.6 fusion.48
  29.0 0.2 copy-done.1
  29.2 3.7 %multiply_add_fusion.6 = f32[32,128,512]{2,1,0:T(8,128)S(1)} fusion(f32[32,128,512]{2,1,0:T(8,128)S(1)} %copy-done.1, f32[32,128]{1,0:T(8,128)S(1)} %get-tuple-element.270, f32[128,32,128]{2,0,1:T(8,128)S(1)} %get-tuple-element.268, f32[32,128]{1,0:T(8,128)S(1)} %max.29, pred[128,128]{0,1:T(8,128)(4,1)S(1)} %fusion.46, ...), kind=kOutput, calls=%fused_computation.1.clone.1 | convolution fusion | flops 543752192 | bytes 19185668 | tf_op jit(solution)/shard_map/while/body/htk,kc->htc/dot_general | solution.py:52
  32.9 3.2 %copy-done.2 = f32[32,128,512]{2,1,0:T(8,128)} copy-done((f32[32,128,512]{2,1,0:T(8,128)}, f32[32,128,512]{2,1,0:T(8,128)S(1)}, u32[]{:S(2)}) %copy-start.2) | copy-done | bytes 8388632 | tf_op jit(solution)/shard_map/while
  36.1 0.7 fusion.45
  36.8 0.1 fusion.46
  36.9 3.9 %fusion.47 = (f32[32,128]{1,0:T(8,128)S(1)}, f32[128,32,128]{2,0,1:T(8,128)S(1)}) fusion(pred[128,128]{0,1:T(8,128)(4,1)S(1)} %fusion.46, bf16[32,128,512]{2,1,0:T(8,128)(2,1)} %get-tuple-element.313, bf16[128,512]{1,0:T(8,128)(2,1)S(1)} %get-tuple-element.312, bf16[1024,512]{1,0:T(8,128)(2,1)} %get-tuple-element.311, s32[]{:T(128)S(6)} %select_n.121, ...), kind=kOutput, calls=%fused_computation.4.clone.1 | convolution fusion | flops 538505216 | bytes 6586373 | tf_op jit(solution)/shard_map/while/body/htc,kc->htk/dot_general | solution.py:46
  40.9 0.6 fusion.48
  41.4 0.2 copy-done.1
  41.6 3.7 %multiply_add_fusion.6 = f32[32,128,512]{2,1,0:T(8,128)S(1)} fusion(f32[32,128,512]{2,1,0:T(8,128)S(1)} %copy-done.1, f32[32,128]{1,0:T(8,128)S(1)} %get-tuple-element.270, f32[128,32,128]{2,0,1:T(8,128)S(1)} %get-tuple-element.268, f32[32,128]{1,0:T(8,128)S(1)} %max.29, pred[128,128]{0,1:T(8,128)(4,1)S(1)} %fusion.46, ...), kind=kOutput, calls=%fused_computation.1.clone.1 | convolution fusion | flops 543752192 | bytes 19185668 | tf_op jit(solution)/shard_map/while/body/htk,kc->htc/dot_general | solution.py:52
  45.3 3.2 %copy-done.2 = f32[32,128,512]{2,1,0:T(8,128)} copy-done((f32[32,128,512]{2,1,0:T(8,128)}, f32[32,128,512]{2,1,0:T(8,128)S(1)}, u32[]{:S(2)}) %copy-start.2) | copy-done | bytes 8388632 | tf_op jit(solution)/shard_map/while
  48.6 0.1 copy.16
  48.7 0.2 reduce_window_sum.11
  48.9 0.1 fusion.26
  49.1 9.2 %fusion.22 = bf16[128,32,128]{0,2,1:T(8,128)(2,1)S(1)} fusion(f32[32,128,512]{2,1,0:T(8,128)} %get-tuple-element.106, bf16[32,512,128]{2,1,0:T(8,128)(2,1)} %param.12, f32[128,32]{0,1:T(8,128)S(1)} %bitcast.60), kind=kOutput, calls=%fused_computation.33 | convolution fusion | flops 3222274048 | bytes 13647872 | tf_op jit(solution)/shard_map/htc,hce->the/dot_general | solution.py:64
  58.3 0.7 convolution_convert_fusion
  59.0 128.1 %all_to_all.5 = bf16[16,16,4096]{2,1,0:T(8,128)(2,1)S(1)} all-to-all(bf16[16,16,4096]{2,1,0:T(8,128)(2,1)S(1)} %bitcast.56), channel_id=1, replica_groups=mesh['groups'=2,'dp'=8,'ep'=2] {'dp','ep'}, dimensions={0} | all-to-all | bytes 4194304 | tf_op jit(solution)/shard_map/all_to_all | solution.py:113
  187.1 2.2 %copy.30 = bf16[8,2,1,16,4096]{4,1,3,0,2:T(2,128)(2,1)S(1)} copy(bf16[8,2,1,16,4096]{4,3,1,0,2:T(8,128)(2,1)S(1)} %bitcast.57) | data formatting | bytes 4194304 | tf_op jit(solution)/shard_map/reshape | solution.py:120
  189.3 2.8 %reshape.104 = bf16[1,8,16,8192]{3,2,1,0:T(8,128)(2,1)} reshape(bf16[1,8,16,2,4096]{4,3,2,1,0:T(2,128)(2,1)S(1)} %bitcast.58) | data formatting | bytes 4194304 | tf_op jit(solution)/shard_map/reshape | solution.py:122
  (32 shorter events, 0.2 us)
Async XLA Ops:
  0.0 1.5 copy-start
  6.9 4.3 %copy-start.3 = (bf16[128,512]{1,0:T(8,128)(2,1)S(1)}, bf16[128,512]{1,0:T(8,128)(2,1)}, u32[]{:S(2)}) copy-start(bf16[128,512]{1,0:T(8,128)(2,1)} %param.14) | copy-start | bytes 393220
  11.2 37.3 %copy-start.4 = (s32[128,2]{0,1:T(2,128)S(1)}, s32[128,2]{0,1:T(2,128)}, u32[]{:S(2)}) copy-start(s32[128,2]{0,1:T(2,128)} %param.17) | copy-start | bytes 3076
  12.0 4.7 %copy-start.1 = (f32[32,128,512]{2,1,0:T(8,128)S(1)}, f32[32,128,512]{2,1,0:T(8,128)}, u32[]{:S(2)}) copy-start(f32[32,128,512]{2,1,0:T(8,128)} %get-tuple-element.290) | copy-start | bytes 25165828 | tf_op jit(solution)/shard_map/while
  20.4 3.2 %copy-start.2 = (f32[32,128,512]{2,1,0:T(8,128)}, f32[32,128,512]{2,1,0:T(8,128)S(1)}, u32[]{:S(2)}) copy-start(f32[32,128,512]{2,1,0:T(8,128)S(1)} %multiply_add_fusion.6) | copy-start | bytes 25165828 | tf_op jit(solution)/shard_map/while
  24.5 4.7 %copy-start.1 = (f32[32,128,512]{2,1,0:T(8,128)S(1)}, f32[32,128,512]{2,1,0:T(8,128)}, u32[]{:S(2)}) copy-start(f32[32,128,512]{2,1,0:T(8,128)} %get-tuple-element.290) | copy-start | bytes 25165828 | tf_op jit(solution)/shard_map/while
  32.9 3.2 %copy-start.2 = (f32[32,128,512]{2,1,0:T(8,128)}, f32[32,128,512]{2,1,0:T(8,128)S(1)}, u32[]{:S(2)}) copy-start(f32[32,128,512]{2,1,0:T(8,128)S(1)} %multiply_add_fusion.6) | copy-start | bytes 25165828 | tf_op jit(solution)/shard_map/while
  36.9 4.7 %copy-start.1 = (f32[32,128,512]{2,1,0:T(8,128)S(1)}, f32[32,128,512]{2,1,0:T(8,128)}, u32[]{:S(2)}) copy-start(f32[32,128,512]{2,1,0:T(8,128)} %get-tuple-element.290) | copy-start | bytes 25165828 | tf_op jit(solution)/shard_map/while
  45.3 3.2 %copy-start.2 = (f32[32,128,512]{2,1,0:T(8,128)}, f32[32,128,512]{2,1,0:T(8,128)S(1)}, u32[]{:S(2)}) copy-start(f32[32,128,512]{2,1,0:T(8,128)S(1)} %multiply_add_fusion.6) | copy-start | bytes 25165828 | tf_op jit(solution)/shard_map/while
where the time goes:
time: 193 us; the launch traced here: 192 us
  blocking collectives  128 us (66%)
  matrix products  38.1 us (20%)
  local copies, waits for them, and re-layouts  19.7 us (10%)
  other arithmetic  4.41 us (2%)
    all_to_all x1, blocking collectives, local(): lax.all_to_all(outgoing.reshape(experts, capacity, features), ('dp', 'ep'...  128 us
    dot_general x3, matrix products, advance(): jnp.einsum('htc,kc->htk', lifted, keys, preferred_element_type=jnp.float32)  11.7 us
    dot_general x3, matrix products, advance(): jnp.einsum('htk,kc->htc', weights.astype(jnp.bfloat16), keys, preferred_e...  11.1 us
    while x15, local copies, waits for them, and re-layouts  10.2 us
    dot_general x1, matrix products, partial_attention(): jnp.einsum('htc,hce->the', accum, value_weight.astype(jnp.float32), preci...  9.18 us
    dot_general x1, matrix products, lift(): jnp.einsum('thd,hdc->htc', split, key_weight, preferred_element_type=jnp....  5.41 us
    broadcast_in_dim x1, local copies, waits for them, and re-layouts, partial_attention(): jnp.zeros((heads, slots, width), jnp.float32)  4.29 us

commit v1 on v0

v1 whole, which is shorter than its diff:
```python
import functools
import math

import jax
import jax.numpy as jnp
from jax import lax
from jax.experimental import pallas as pl
from jax.experimental.pallas import tpu as pltpu
from jax.sharding import PartitionSpec as P

SPAN = 64
GROUP = 4
UNROLL = 2
MASKED = -1e30
OPEN = 3e38
NT = (((1,), (1,)), ((), ()))


def dot(left, right):
    return jnp.dot(left, right, preferred_element_type=jnp.float32)


def build_table(count, routes_ref, table_ref, capacity):
    slots = routes_ref.shape[1]
    rows = table_ref.shape[0]
    place = lax.broadcasted_iota(jnp.int32, (rows, slots), 0)
    token = lax.broadcasted_iota(jnp.int32, (rows, slots), 1)
    expert = place // capacity
    hit = ((routes_ref[0:1, :] == expert) | (routes_ref[1:2, :] == expert)) & (
        token < count * SPAN
    )
    hit = jnp.where(hit, jnp.float32(1.0), jnp.float32(0.0))
    first = lax.broadcasted_iota(jnp.int32, (slots, slots), 0)
    second = lax.broadcasted_iota(jnp.int32, (slots, slots), 1)
    earlier = jnp.where(first < second, jnp.float32(1.0), jnp.float32(0.0))
    before = dot(hit.astype(jnp.bfloat16), earlier.astype(jnp.bfloat16))
    wanted = (place - expert * capacity).astype(jnp.float32)
    table_ref[...] = jnp.where(before == wanted, hit, jnp.float32(0.0)).astype(jnp.bfloat16)


def attend_kernel(
    capacity,
    count_ref,
    size_ref,
    routes_ref,
    queries_ref,
    key_weight_ref,
    value_weight_ref,
    prefix_ref,
    fresh_ref,
    out_ref,
    keys_ref,
    cap_ref,
    table_ref,
):
    slots = queries_ref.shape[0]
    past = prefix_ref.shape[0]
    dim = key_weight_ref.shape[1]

    @pl.when(pl.program_id(0) == 0)
    def _():
        count, size = count_ref[0], size_ref[0]
        keys_ref[:past] = prefix_ref[...]
        keys_ref[past:] = fresh_ref[...]
        lane = lax.broadcasted_iota(jnp.int32, (slots, past), 1)
        cap_ref[:, :past] = jnp.where(lane < size, jnp.float32(OPEN), jnp.float32(MASKED))
        row = lax.broadcasted_iota(jnp.int32, (slots, slots), 0)
        col = lax.broadcasted_iota(jnp.int32, (slots, slots), 1)
        cap_ref[:, past:] = jnp.where(
            (col <= row) & (col < count * SPAN), jnp.float32(OPEN), jnp.float32(MASKED)
        )
        build_table(count, routes_ref, table_ref, capacity)

    scale = math.log2(math.e) / math.sqrt(dim)
    keys = keys_ref[...]
    scores = []
    for stack in range(UNROLL):
        lifted = []
        for h in range(stack * GROUP, (stack + 1) * GROUP):
            one = dot(queries_ref[:, h * dim : (h + 1) * dim], key_weight_ref[h])
            lifted.append(one.astype(jnp.bfloat16))
        lifted = jnp.concatenate(lifted, axis=0)
        score = lax.dot_general(lifted, keys, NT, preferred_element_type=jnp.float32)
        scores.append(score)
    for stack in range(UNROLL):
        score = scores[stack].reshape(GROUP, slots, keys.shape[0])
        score = jnp.minimum(score, cap_ref[...][None])
        highest = jnp.max(score, axis=-1, keepdims=True) * scale
        weights = jnp.exp2(score * scale - highest)
        total = jnp.sum(weights, axis=-1, keepdims=True)
        weights = weights.astype(jnp.bfloat16).reshape(GROUP * slots, keys.shape[0])
        mixed = dot(weights, keys).astype(jnp.bfloat16)
        for g in range(GROUP):
            h = stack * GROUP + g
            projected = dot(mixed[g * slots : (g + 1) * slots], value_weight_ref[h])
            attended = (projected / total[g]).astype(jnp.bfloat16)
            out_ref[:, h * dim : (h + 1) * dim] = dot(table_ref[...], attended).astype(
                jnp.bfloat16
            )


def attend(queries, key_weight, value_weight, prefix, fresh, count, size, routes, experts):
    slots = queries.shape[0]
    heads, dim, latent = key_weight.shape
    step = GROUP * UNROLL
    places = slots * routes.shape[1]
    keys = prefix.shape[0] + slots
    whole = lambda shape: pl.BlockSpec(shape, lambda i: (0,) * len(shape))
    smem = pl.BlockSpec(memory_space=pltpu.SMEM)
    return pl.pallas_call(
        functools.partial(attend_kernel, places // experts),
        grid=(heads // step,),
        in_specs=[
            smem,
            smem,
            whole((routes.shape[1], slots)),
            pl.BlockSpec((slots, step * dim), lambda i: (0, i)),
            pl.BlockSpec((step, dim, latent), lambda i: (i, 0, 0)),
            pl.BlockSpec((step, latent, dim), lambda i: (i, 0, 0)),
            whole(prefix.shape),
            whole(fresh.shape),
        ],
        out_specs=pl.BlockSpec((places, step * dim), lambda i: (0, i)),
        out_shape=jax.ShapeDtypeStruct((places, heads * dim), jnp.bfloat16),
        scratch_shapes=[
            pltpu.VMEM((keys, latent), jnp.bfloat16),
            pltpu.VMEM((slots, keys), jnp.float32),
            pltpu.VMEM((places, slots), jnp.bfloat16),
        ],
        compiler_params=pltpu.CompilerParams(vmem_limit_bytes=48 * 1024 * 1024),
    )(count, size, routes.T, queries, key_weight, value_weight, prefix, fresh)


def place_kernel(arrived_ref, out_ref, sem):
    sources, _, features = arrived_ref.shape
    ranks = out_ref.shape[1]
    cores = sources // ranks
    copies = [
        pltpu.make_async_copy(
            arrived_ref.at[s],
            out_ref.at[0, s // cores, :, pl.ds(s % cores * features, features)],
            sem.at[s],
        )
        for s in range(sources)
    ]
    for copy in copies:
        copy.start()
    for copy in copies:
        copy.wait()


def assemble(arrived, ranks, cores):
    sources, capacity, features = arrived.shape
    if capacity % 16:
        arrived = arrived.reshape(ranks, cores, capacity, features).transpose(0, 2, 1, 3)
        return arrived.reshape(1, ranks, capacity, cores * features)
    return pl.pallas_call(
        place_kernel,
        in_specs=[pl.BlockSpec(memory_space=pl.ANY)],
        out_specs=pl.BlockSpec(memory_space=pl.ANY),
        out_shape=jax.ShapeDtypeStruct((1, ranks, capacity, cores * features), arrived.dtype),
        scratch_shapes=[pltpu.SemaphoreType.DMA((sources,))],
    )(arrived)


def local(
    queries,
    key_weight,
    value_weight,
    prefix_latent,
    fresh_latent,
    span_counts,
    prefix_lengths,
    routes,
):
    ranks, cores = lax.axis_size("dp"), lax.axis_size("ep")
    experts = ranks * cores
    outgoing = attend(
        queries,
        key_weight,
        value_weight,
        prefix_latent,
        fresh_latent,
        span_counts,
        prefix_lengths,
        routes,
        experts,
    )
    arrived = lax.all_to_all(
        outgoing.reshape(experts, -1, outgoing.shape[1]),
        ("dp", "ep"),
        split_axis=0,
        concat_axis=0,
        tiled=True,
    )
    return assemble(arrived, ranks, cores)


def solution(mesh):
    in_specs = (
        P(("groups", "dp"), "ep"),
        P("ep", None, None),
        P("ep", None, None),
        P(("groups", "dp"), None),
        P(("groups", "dp"), None),
        P(("groups", "dp")),
        P(("groups", "dp")),
        P(("groups", "dp"), None),
    )
    out_specs = P(("groups", "dp", "ep"), None, None, None)
    return jax.shard_map(local, mesh=mesh, in_specs=in_specs, out_specs=out_specs, check_vma=False)
```

time: 193 us -> 148 us (0.77)
  Pallas kernels: 0 us -> 87.9 us
  blocking collectives: 128 us -> 54.6 us
  matrix products: 38.1 us -> 0 us
  local copies, waits for them, and re-layouts: 19.7 us -> 4.02 us
  other arithmetic: 4.41 us -> 0 us
    pallas_call x0 -> x2, Pallas kernels: none -> 87.9 us  [the longest x1 64.8 us: assemble(): pl.pallas_call(place_kernel, in_specs=[pl.BlockSpec(memory_space=pl.ANY)]...]
    all_to_all x1, blocking collectives: 128 us -> 54.6 us  [local(): lax.all_to_all(outgoing.reshape(experts, -1, outgoing.shape[1]), ('dp', '...]
    dot_general x9 -> x0, matrix products: 38.1 us -> none  [the longest x3 11.7 us: advance(): jnp.einsum('htc,kc->htk', lifted, keys, preferred_element_type=jnp.float32)]
    while x15 -> x0, local copies, waits for them, and re-layouts: 10.2 us -> none
    reshape x2 -> x0, local copies, waits for them, and re-layouts: 5 us -> none  [the longest x1 2.81 us: local(): return arrived.reshape(EXP_DEV, ranks_here, capacity, cores_here * features)]
    broadcast_in_dim x3 -> x0, local copies, waits for them, and re-layouts: 4.3 us -> none  [the longest x1 4.29 us: partial_attention(): jnp.zeros((heads, slots, width), jnp.float32)]
    unnamed x6 -> x8, local copies, waits for them, and re-layouts: 0.01 us -> 4.02 us
    lt x4 -> x0, other arithmetic: 1.96 us -> none  [the longest x3 1.95 us: advance(): prefix_start + lane < prefix_size]
where the time goes in v1:
time: 148 us
  Pallas kernels  87.9 us (59%)
  blocking collectives  54.6 us (37%)
  local copies, waits for them, and re-layouts  4.02 us (3%)
    pallas_call x1, Pallas kernels, assemble(): pl.pallas_call(place_kernel, in_specs=[pl.BlockSpec(memory_space=pl.ANY)]...  64.8 us
    all_to_all x1, blocking collectives, local(): lax.all_to_all(outgoing.reshape(experts, -1, outgoing.shape[1]), ('dp', '...  54.6 us
    pallas_call x1, Pallas kernels, attend(): pl.pallas_call(functools.partial(attend_kernel, places // experts), grid=...  23.1 us
    unnamed x8, local copies, waits for them, and re-layouts  4.02 us

profile of v1, /device:TPU:0, one launch (start us, length us, event | category | flops | bytes accessed | tf_op | source)
XLA Modules:
  0.0 147.8 jit_solution(2560824396369593144)
XLA Ops:
  1.3 0.0 copy-start
  1.3 1.2 copy-done
  2.5 0.0 copy-start.1
  2.5 1.2 copy-done.1
  3.7 0.0 copy-start.2
  3.8 0.9 copy-done.2
  4.7 0.0 copy-start.3
  4.7 0.7 copy-done.3
  5.3 23.1 %shard_map.82 = bf16[256,4096]{1,0:T(8,128)(2,1)S(1)} custom-call(s32[1]{0:T(128)S(6)} %copy.9.count_ref, s32[1]{0:T(128)S(6)} %copy.10.size_ref, s32[2,128]{1,0:T(2,128)S(1)} %bitcast.3, bf16[128,4096]{1,0:T(8,128)(2,1)S(1)} %copy-done, bf16[32,128,512]{2,1,0:T(8,128)(2,1)} %key_weight_ref.1, bf16[32,512,128]{2,1,0:T(8,128)(2,1)} %value_weight_ref.1, ...), custom_call_target="tpu_custom_call" | custom-call | tf_op jit(solution)/shard_map/pallas_call | solution.py:110
  28.5 54.6 %all_to_all.5.arrived_ref = bf16[16,16,4096]{2,1,0:T(8,128)(2,1)} all-to-all(bf16[16,16,4096]{2,1,0:T(8,128)(2,1)S(1)} %bitcast.2), channel_id=1, replica_groups=mesh['groups'=2,'dp'=8,'ep'=2] {'dp','ep'}, dimensions={0} | all-to-all | bytes 4194304 | tf_op jit(solution)/shard_map/all_to_all | solution.py:189
  83.1 64.8 %shard_map.83 = bf16[1,8,16,8192]{3,2,1,0:T(8,128)(2,1)} custom-call(bf16[16,16,4096]{2,1,0:T(8,128)(2,1)} %all_to_all.5.arrived_ref), custom_call_target="tpu_custom_call" | custom-call | tf_op jit(solution)/shard_map/pallas_call | solution.py:157
Async XLA Ops:
  1.3 1.2 copy-start
  2.5 1.2 copy-start.1
  3.7 0.9 copy-start.2
  4.7 0.7 copy-start.3

commit v2 on v1

v2 whole, which is shorter than its diff:
```python
import functools
import math

import jax
import jax.numpy as jnp
from jax import lax
from jax.experimental import pallas as pl
from jax.experimental.pallas import tpu as pltpu
from jax.sharding import PartitionSpec as P

SPAN = 64
GROUP = 4
CHUNKS = 4
DIRECT = 32
MASKED = -1e30
OPEN = 3e38
NT = (((1,), (1,)), ((), ()))


def dot(left, right):
    return jnp.dot(left, right, preferred_element_type=jnp.float32)


def build_table(me, count, routes_ref, table_ref, capacity):
    slots = routes_ref.shape[1]
    rows = table_ref.shape[0]
    place = lax.broadcasted_iota(jnp.int32, (rows, slots), 0)
    token = lax.broadcasted_iota(jnp.int32, (rows, slots), 1)
    block = place // capacity
    expert = block ^ me
    hit = ((routes_ref[0:1, :] == expert) | (routes_ref[1:2, :] == expert)) & (
        token < count * SPAN
    )
    hit = jnp.where(hit, jnp.float32(1.0), jnp.float32(0.0))
    first = lax.broadcasted_iota(jnp.int32, (slots, slots), 0)
    second = lax.broadcasted_iota(jnp.int32, (slots, slots), 1)
    earlier = jnp.where(first < second, jnp.float32(1.0), jnp.float32(0.0))
    before = dot(hit.astype(jnp.bfloat16), earlier.astype(jnp.bfloat16))
    wanted = (place - block * capacity).astype(jnp.float32)
    table_ref[...] = jnp.where(before == wanted, hit, jnp.float32(0.0)).astype(jnp.bfloat16)


def attend_kernel(
    capacity,
    me_ref,
    count_ref,
    size_ref,
    routes_ref,
    queries_ref,
    key_weight_ref,
    value_weight_ref,
    prefix_ref,
    fresh_ref,
    *rest,
):
    *out_refs, keys_ref, cap_ref, table_ref, attended_ref = rest
    slots = queries_ref.shape[0]
    past = prefix_ref.shape[0]
    dim = key_weight_ref.shape[1]
    count, size = count_ref[0], size_ref[0]
    keys_ref[:past] = prefix_ref[...]
    keys_ref[past:] = fresh_ref[...]
    lane = lax.broadcasted_iota(jnp.int32, (slots, past), 1)
    cap_ref[:, :past] = jnp.where(lane < size, jnp.float32(OPEN), jnp.float32(MASKED))
    row = lax.broadcasted_iota(jnp.int32, (slots, slots), 0)
    col = lax.broadcasted_iota(jnp.int32, (slots, slots), 1)
    cap_ref[:, past:] = jnp.where(
        (col <= row) & (col < count * SPAN), jnp.float32(OPEN), jnp.float32(MASKED)
    )
    build_table(me_ref[0], count, routes_ref, table_ref, capacity)

    scale = math.log2(math.e) / math.sqrt(dim)
    keys = keys_ref[...]
    stacks = key_weight_ref.shape[0] // GROUP
    scores = []
    for stack in range(stacks):
        lifted = []
        for h in range(stack * GROUP, (stack + 1) * GROUP):
            one = dot(queries_ref[:, h * dim : (h + 1) * dim], key_weight_ref[h])
            lifted.append(one.astype(jnp.bfloat16))
        lifted = jnp.concatenate(lifted, axis=0)
        score = lax.dot_general(lifted, keys, NT, preferred_element_type=jnp.float32)
        scores.append(score)
    for stack in range(stacks):
        score = scores[stack].reshape(GROUP, slots, keys.shape[0])
        score = jnp.minimum(score, cap_ref[...][None])
        highest = jnp.max(score, axis=-1, keepdims=True) * scale
        weights = jnp.exp2(score * scale - highest)
        total = jnp.sum(weights, axis=-1, keepdims=True)
        weights = weights.astype(jnp.bfloat16).reshape(GROUP * slots, keys.shape[0])
        mixed = dot(weights, keys).astype(jnp.bfloat16)
        for g in range(GROUP):
            h = stack * GROUP + g
            projected = dot(mixed[g * slots : (g + 1) * slots], value_weight_ref[h])
            attended_ref[:, h * dim : (h + 1) * dim] = (projected / total[g]).astype(jnp.bfloat16)
    grouped = dot(table_ref[...], attended_ref[...]).astype(jnp.bfloat16)
    rows = out_refs[0].shape[0]
    for k, out_ref in enumerate(out_refs):
        out_ref[...] = grouped[k * rows : (k + 1) * rows]


def attend(
    chunk, heads, me, queries, key_weight, value_weight, prefix, fresh, count, size, routes, experts, pieces
):
    slots = queries.shape[0]
    _, dim, latent = key_weight.shape
    places = slots * routes.shape[1]
    keys = prefix.shape[0] + slots
    whole = lambda shape: pl.BlockSpec(shape, lambda i: (0,) * len(shape))
    smem = pl.BlockSpec(memory_space=pltpu.SMEM)
    piece = (places // pieces, heads * dim)
    flops = 4 * slots * heads * keys * latent
    return pl.pallas_call(
        functools.partial(attend_kernel, places // experts),
        grid=(1,),
        in_specs=[
            smem,
            smem,
            smem,
            whole((routes.shape[1], slots)),
            pl.BlockSpec((slots, heads * dim), lambda i: (0, chunk)),
            pl.BlockSpec((heads, dim, latent), lambda i: (chunk, 0, 0)),
            pl.BlockSpec((heads, latent, dim), lambda i: (chunk, 0, 0)),
            whole(prefix.shape),
            whole(fresh.shape),
        ],
        out_specs=[whole(piece)] * pieces,
        out_shape=[jax.ShapeDtypeStruct(piece, jnp.bfloat16)] * pieces,
        scratch_shapes=[
            pltpu.VMEM((keys, latent), jnp.bfloat16),
            pltpu.VMEM((slots, keys), jnp.float32),
            pltpu.VMEM((places, slots), jnp.bfloat16),
            pltpu.VMEM((slots, heads * dim), jnp.bfloat16),
        ],
        compiler_params=pltpu.CompilerParams(vmem_limit_bytes=40 * 1024 * 1024),
        cost_estimate=pl.CostEstimate(
            flops=flops, bytes_accessed=4 * heads * dim * latent, transcendentals=heads * slots * keys
        ),
    )(me, count, size, routes.T, queries, key_weight, value_weight, prefix, fresh)


def place_kernel(chunks, cores, me_ref, *rest):
    *piece_refs, out_ref, sem = rest
    sources = len(piece_refs) // chunks
    width = piece_refs[0].shape[1]
    me = me_ref[0]
    copies = []
    for i, piece_ref in enumerate(piece_refs):
        chunk, k = divmod(i, sources)
        source = me ^ k
        start = (source % cores * chunks + chunk) * width
        target = out_ref.at[0, source // cores, :, pl.ds(pl.multiple_of(start, width), width)]
        copies.append(pltpu.make_async_copy(piece_ref, target, sem.at[i]))
    for copy in copies:
        copy.start()
    for copy in copies:
        copy.wait()


def assemble(me, chunks, ranks, cores):
    pieces = [piece for chunk in chunks for piece in chunk]
    capacity, width = pieces[0].shape
    return pl.pallas_call(
        functools.partial(place_kernel, len(chunks), cores),
        in_specs=[pl.BlockSpec(memory_space=pltpu.SMEM)]
        + [pl.BlockSpec(memory_space=pltpu.VMEM)] * len(pieces),
        out_specs=pl.BlockSpec(memory_space=pl.ANY),
        out_shape=jax.ShapeDtypeStruct(
            (1, ranks, capacity, cores * len(chunks) * width), jnp.bfloat16
        ),
        scratch_shapes=[pltpu.SemaphoreType.DMA((len(pieces),))],
    )(me, *pieces)


def exchange_order(experts):
    near, far = list(range(1, experts // 2)), list(range(experts // 2, experts))
    early, late = far[len(far) // 2 :], far[: len(far) // 2]
    mixed = []
    while near or early:
        mixed += early[:1] + near[:1]
        early, near = early[1:], near[1:]
    return mixed + late


def local(
    queries,
    key_weight,
    value_weight,
    prefix_latent,
    fresh_latent,
    span_counts,
    prefix_lengths,
    routes,
):
    ranks, cores = lax.axis_size("dp"), lax.axis_size("ep")
    experts = ranks * cores
    direct = experts <= DIRECT
    index = lax.axis_index("dp") * cores + lax.axis_index("ep")
    me = (index if direct else jnp.int32(0)).astype(jnp.int32).reshape(1)
    heads = key_weight.shape[0] // CHUNKS
    chunks = []
    for chunk in range(CHUNKS):
        outgoing = attend(
            chunk,
            heads,
            me,
            queries,
            key_weight,
            value_weight,
            prefix_latent,
            fresh_latent,
            span_counts,
            prefix_lengths,
            routes,
            experts,
            experts if direct else 1,
        )
        if direct:
            arrived = list(outgoing)
            for k in exchange_order(experts):
                pairs = [(i, i ^ k) for i in range(experts)]
                arrived[k] = lax.ppermute(outgoing[k], ("dp", "ep"), pairs)
        else:
            arrived = lax.all_to_all(
                outgoing[0].reshape(experts, -1, outgoing[0].shape[1]),
                ("dp", "ep"),
                split_axis=0,
                concat_axis=0,
                tiled=True,
            )
        chunks.append(arrived)
    if direct:
        return assemble(me, chunks, ranks, cores)
    arrived = jnp.stack(chunks).reshape(CHUNKS, ranks, cores, -1, chunks[0].shape[2])
    arrived = arrived.transpose(1, 3, 2, 0, 4)
    return arrived.reshape(1, ranks, arrived.shape[1], -1)


def solution(mesh):
    in_specs = (
        P(("groups", "dp"), "ep"),
        P("ep", None, None),
        P("ep", None, None),
        P(("groups", "dp"), None),
        P(("groups", "dp"), None),
        P(("groups", "dp")),
        P(("groups", "dp")),
        P(("groups", "dp"), None),
    )
    out_specs = P(("groups", "dp", "ep"), None, None, None)
    return jax.shard_map(local, mesh=mesh, in_specs=in_specs, out_specs=out_specs, check_vma=False)
```

time: 148 us -> 124 us (0.84)
  starting transfers between devices: 0 us -> 84 us
  Pallas kernels: 87.9 us -> 19.9 us
  blocking collectives: 54.6 us -> 0 us
  local copies, waits for them, and re-layouts: 4.02 us -> 11.4 us
  waiting for transfers between devices: 0 us -> 6.44 us
    ppermute x0 -> x60, starting transfers between devices: none -> 84 us  [local(): arrived[k] = lax.ppermute(outgoing[k], ('dp', 'ep'), pairs)]
    pallas_call x1, Pallas kernels: 64.8 us -> 3.36 us  [assemble(): pl.pallas_call(functools.partial(place_kernel, len(chunks), cores), in_sp...]
    all_to_all x1 -> x0, blocking collectives: 54.6 us -> none  [local(): lax.all_to_all(outgoing.reshape(experts, -1, outgoing.shape[1]), ('dp', '...]
    unnamed x8 -> x140, local copies, waits for them, and re-layouts: 4.02 us -> 11.4 us
    pallas_call x1 -> x4, Pallas kernels: 23.1 us -> 16.6 us  [attend(): pl.pallas_call(functools.partial(attend_kernel, places // experts), grid=...]
    ppermute x0 -> x60, waiting for transfers between devices: none -> 6.44 us  [local(): arrived[k] = lax.ppermute(outgoing[k], ('dp', 'ep'), pairs)]
  transfers between devices with their start and end apart: 0 -> 60, of which waited for: 0 -> 3; matrix products, arithmetic and copies ran while one was open for 0% -> 0% of each run, Pallas kernels for 0% -> 10%
where the time goes in v2:
time: 124 us
  starting transfers between devices  84 us (68%)
  Pallas kernels  19.9 us (16%)
  local copies, waits for them, and re-layouts  11.4 us (9%)
  waiting for transfers between devices  6.44 us (5%)
  between operations  2.19 us (2%)
    ppermute x60, starting transfers between devices, local(): arrived[k] = lax.ppermute(outgoing[k], ('dp', 'ep'), pairs)  84 us
    pallas_call x4, Pallas kernels, attend(): pl.pallas_call(functools.partial(attend_kernel, places // experts), grid=...  16.6 us
    unnamed x140, local copies, waits for them, and re-layouts  11.4 us
    ppermute x60, waiting for transfers between devices, local(): arrived[k] = lax.ppermute(outgoing[k], ('dp', 'ep'), pairs)  6.44 us
    pallas_call x1, Pallas kernels, assemble(): pl.pallas_call(functools.partial(place_kernel, len(chunks), cores), in_sp...  3.36 us
  transfers between devices with their start and end apart: 60, of which 3 were waited for; matrix products, arithmetic and copies ran while one was open for 0% of the time, Pallas kernels for 10%

profile of v2, /device:TPU:0, one launch (start us, length us, event | category | flops | bytes accessed | tf_op | source)
XLA Modules:
  0.0 124.0 jit_solution(11279275150718356291)
XLA Ops:
  1.3 2.2 %copy-done = bf16[32,128,512]{2,1,0:T(8,128)(2,1)S(1)} copy-done((bf16[32,128,512]{2,1,0:T(8,128)(2,1)S(1)}, bf16[32,128,512]{2,1,0:T(8,128)(2,1)}, u32[]{:S(2)}) %copy-start) | copy-done | bytes 4194328
  3.5 2.2 %copy-done.1 = bf16[32,512,128]{2,1,0:T(8,128)(2,1)S(1)} copy-done((bf16[32,512,128]{2,1,0:T(8,128)(2,1)S(1)}, bf16[32,512,128]{2,1,0:T(8,128)(2,1)}, u32[]{:S(2)}) %copy-start.1) | copy-done | bytes 4194328
  9.7 4.1 %shard_map.85 = (bf16[16,1024]{1,0:T(8,128)(2,1)S(1)}, bf16[16,1024]{1,0:T(8,128)(2,1)S(1)}, bf16[16,1024]{1,0:T(8,128)(2,1)S(1)}, bf16[16,1024]{1,0:T(8,128)(2,...) custom-call(s32[1]{0:T(128)} %bitcast.me_ref, ...), custom_call_target="tpu_custom_call" | custom-call | flops 2415919104 | bytes 2097152 | tf_op jit(solution)/shard_map/pallas_call | solution.py:113
  14.9 2.5 %collective-permute-start.46 = (bf16[16,1024]{1,0:T(8,128)(2,1)S(1)}, bf16[16,1024]{1,0:T(8,128)(2,1)S(1)}, u32[]{:S(2)}, u32[]{:S(2)}) collective-permute-start(bf16[16,1024]{1,0:T(8,128)(2,1)S(1)} %get-tuple-element.119), channel_id=1, source_target_pairs={{0,2},{1,3},{2,0},{3,1},{4,6},{5,7},{6,4},{7,5},{8,10},{9,11},{10,... | collective-permute-start | bytes 98312 | tf_op jit(solution)/shard_map/ppermute | solution.py:222
  17.5 1.8 %collective-permute-start.48 = (bf16[16,1024]{1,0:T(8,128)(2,1)S(1)}, bf16[16,1024]{1,0:T(8,128)(2,1)S(1)}, u32[]{:S(2)}, u32[]{:S(2)}) collective-permute-start(bf16[16,1024]{1,0:T(8,128)(2,1)S(1)} %get-tuple-element.121), channel_id=1, source_target_pairs={{0,4},{1,5},{2,6},{3,7},{4,0},{5,1},{6,2},{7,3},{8,12},{9,13},{10,... | collective-permute-start | bytes 98312 | tf_op jit(solution)/shard_map/ppermute | solution.py:222
  19.3 2.6 %collective-permute-start.50 = (bf16[16,1024]{1,0:T(8,128)(2,1)S(1)}, bf16[16,1024]{1,0:T(8,128)(2,1)S(1)}, u32[]{:S(2)}, u32[]{:S(2)}) collective-permute-start(bf16[16,1024]{1,0:T(8,128)(2,1)S(1)} %get-tuple-element.123), channel_id=1, source_target_pairs={{0,6},{1,7},{2,4},{3,5},{4,2},{5,3},{6,0},{7,1},{8,14},{9,15},{10,... | collective-permute-start | bytes 98312 | tf_op jit(solution)/shard_map/ppermute | solution.py:222
  22.1 2.6 %collective-permute-start.52 = (bf16[16,1024]{1,0:T(8,128)(2,1)S(1)}, bf16[16,1024]{1,0:T(8,128)(2,1)S(1)}, u32[]{:S(2)}, u32[]{:S(2)}) collective-permute-start(bf16[16,1024]{1,0:T(8,128)(2,1)S(1)} %get-tuple-element.125), channel_id=1, source_target_pairs={{0,8},{1,9},{2,10},{3,11},{4,12},{5,13},{6,14},{7,15},{8,0},{9,1},... | collective-permute-start | bytes 98312 | tf_op jit(solution)/shard_map/ppermute | solution.py:222
  25.0 3.2 %collective-permute-start.54 = (bf16[16,1024]{1,0:T(8,128)(2,1)S(1)}, bf16[16,1024]{1,0:T(8,128)(2,1)S(1)}, u32[]{:S(2)}, u32[]{:S(2)}) collective-permute-start(bf16[16,1024]{1,0:T(8,128)(2,1)S(1)} %get-tuple-element.127), channel_id=1, source_target_pairs={{0,10},{1,11},{2,8},{3,9},{4,14},{5,15},{6,12},{7,13},{8,2},{9,3},... | collective-permute-start | bytes 98312 | tf_op jit(solution)/shard_map/ppermute | solution.py:222
  28.5 3.5 %collective-permute-start.56 = (bf16[16,1024]{1,0:T(8,128)(2,1)S(1)}, bf16[16,1024]{1,0:T(8,128)(2,1)S(1)}, u32[]{:S(2)}, u32[]{:S(2)}) collective-permute-start(bf16[16,1024]{1,0:T(8,128)(2,1)S(1)} %get-tuple-element.129), channel_id=1, source_target_pairs={{0,12},{1,13},{2,14},{3,15},{4,8},{5,9},{6,10},{7,11},{8,4},{9,5},... | collective-permute-start | bytes 98312 | tf_op jit(solution)/shard_map/ppermute | solution.py:222
  32.1 4.2 %collective-permute-start.58 = (bf16[16,1024]{1,0:T(8,128)(2,1)S(1)}, bf16[16,1024]{1,0:T(8,128)(2,1)S(1)}, u32[]{:S(2)}, u32[]{:S(2)}) collective-permute-start(bf16[16,1024]{1,0:T(8,128)(2,1)S(1)} %get-tuple-element.131), channel_id=1, source_target_pairs={{0,14},{1,15},{2,12},{3,13},{4,10},{5,11},{6,8},{7,9},{8,6},{9,7},... | collective-permute-start | bytes 98312 | tf_op jit(solution)/shard_map/ppermute | solution.py:222
  36.6 4.1 %shard_map.84 = (bf16[16,1024]{1,0:T(8,128)(2,1)S(1)}, bf16[16,1024]{1,0:T(8,128)(2,1)S(1)}, bf16[16,1024]{1,0:T(8,128)(2,1)S(1)}, bf16[16,1024]{1,0:T(8,128)(2,...) custom-call(s32[1]{0:T(128)} %bitcast.me_ref, ...), custom_call_target="tpu_custom_call" | custom-call | flops 2415919104 | bytes 2097152 | tf_op jit(solution)/shard_map/pallas_call | solution.py:113
  43.4 1.9 %collective-permute-start.34 = (bf16[16,1024]{1,0:T(8,128)(2,1)S(1)}, bf16[16,1024]{1,0:T(8,128)(2,1)S(1)}, u32[]{:S(2)}, u32[]{:S(2)}) collective-permute-start(bf16[16,1024]{1,0:T(8,128)(2,1)S(1)} %get-tuple-element.106), channel_id=1, source_target_pairs={{0,5},{1,4},{2,7},{3,6},{4,1},{5,0},{6,3},{7,2},{8,13},{9,12},{10,... | collective-permute-start | bytes 98312 | tf_op jit(solution)/shard_map/ppermute | solution.py:222
  47.8 2.4 %collective-permute-start.37 = (bf16[16,1024]{1,0:T(8,128)(2,1)S(1)}, bf16[16,1024]{1,0:T(8,128)(2,1)S(1)}, u32[]{:S(2)}, u32[]{:S(2)}) collective-permute-start(bf16[16,1024]{1,0:T(8,128)(2,1)S(1)} %get-tuple-element.109), channel_id=1, source_target_pairs={{0,8},{1,9},{2,10},{3,11},{4,12},{5,13},{6,14},{7,15},{8,0},{9,1},... | collective-permute-start | bytes 98312 | tf_op jit(solution)/shard_map/ppermute | solution.py:222
  50.6 3.2 %collective-permute-start.39 = (bf16[16,1024]{1,0:T(8,128)(2,1)S(1)}, bf16[16,1024]{1,0:T(8,128)(2,1)S(1)}, u32[]{:S(2)}, u32[]{:S(2)}) collective-permute-start(bf16[16,1024]{1,0:T(8,128)(2,1)S(1)} %get-tuple-element.111), channel_id=1, source_target_pairs={{0,10},{1,11},{2,8},{3,9},{4,14},{5,15},{6,12},{7,13},{8,2},{9,3},... | collective-permute-start | bytes 98312 | tf_op jit(solution)/shard_map/ppermute | solution.py:222
  54.0 3.3 %collective-permute-start.41 = (bf16[16,1024]{1,0:T(8,128)(2,1)S(1)}, bf16[16,1024]{1,0:T(8,128)(2,1)S(1)}, u32[]{:S(2)}, u32[]{:S(2)}) collective-permute-start(bf16[16,1024]{1,0:T(8,128)(2,1)S(1)} %get-tuple-element.113), channel_id=1, source_target_pairs={{0,12},{1,13},{2,14},{3,15},{4,8},{5,9},{6,10},{7,11},{8,4},{9,5},... | collective-permute-start | bytes 98312 | tf_op jit(solution)/shard_map/ppermute | solution.py:222
  57.7 4.2 %collective-permute-start.43 = (bf16[16,1024]{1,0:T(8,128)(2,1)S(1)}, bf16[16,1024]{1,0:T(8,128)(2,1)S(1)}, u32[]{:S(2)}, u32[]{:S(2)}) collective-permute-start(bf16[16,1024]{1,0:T(8,128)(2,1)S(1)} %get-tuple-element.115), channel_id=1, source_target_pairs={{0,14},{1,15},{2,12},{3,13},{4,10},{5,11},{6,8},{7,9},{8,6},{9,7},... | collective-permute-start | bytes 98312 | tf_op jit(solution)/shard_map/ppermute | solution.py:222
  62.0 4.3 %shard_map.83 = (bf16[16,1024]{1,0:T(8,128)(2,1)S(1)}, bf16[16,1024]{1,0:T(8,128)(2,1)S(1)}, bf16[16,1024]{1,0:T(8,128)(2,1)S(1)}, bf16[16,1024]{1,0:T(8,128)(2,...) custom-call(s32[1]{0:T(128)} %bitcast.me_ref, ...), custom_call_target="tpu_custom_call" | custom-call | flops 2415919104 | bytes 2097152 | tf_op jit(solution)/shard_map/pallas_call | solution.py:113
  69.3 1.9 %collective-permute-start.19 = (bf16[16,1024]{1,0:T(8,128)(2,1)S(1)}, bf16[16,1024]{1,0:T(8,128)(2,1)S(1)}, u32[]{:S(2)}, u32[]{:S(2)}) collective-permute-start(bf16[16,1024]{1,0:T(8,128)(2,1)S(1)} %get-tuple-element.90), channel_id=1, source_target_pairs={{0,5},{1,4},{2,7},{3,6},{4,1},{5,0},{6,3},{7,2},{8,13},{9,12},{10,... | collective-permute-start | bytes 98312 | tf_op jit(solution)/shard_map/ppermute | solution.py:222
  73.6 2.4 %collective-permute-start.22 = (bf16[16,1024]{1,0:T(8,128)(2,1)S(1)}, bf16[16,1024]{1,0:T(8,128)(2,1)S(1)}, u32[]{:S(2)}, u32[]{:S(2)}) collective-permute-start(bf16[16,1024]{1,0:T(8,128)(2,1)S(1)} %get-tuple-element.93), channel_id=1, source_target_pairs={{0,8},{1,9},{2,10},{3,11},{4,12},{5,13},{6,14},{7,15},{8,0},{9,1},... | collective-permute-start | bytes 98312 | tf_op jit(solution)/shard_map/ppermute | solution.py:222
  76.5 3.2 %collective-permute-start.24 = (bf16[16,1024]{1,0:T(8,128)(2,1)S(1)}, bf16[16,1024]{1,0:T(8,128)(2,1)S(1)}, u32[]{:S(2)}, u32[]{:S(2)}) collective-permute-start(bf16[16,1024]{1,0:T(8,128)(2,1)S(1)} %get-tuple-element.95), channel_id=1, source_target_pairs={{0,10},{1,11},{2,8},{3,9},{4,14},{5,15},{6,12},{7,13},{8,2},{9,3},... | collective-permute-start | bytes 98312 | tf_op jit(solution)/shard_map/ppermute | solution.py:222
  79.9 3.3 %collective-permute-start.26 = (bf16[16,1024]{1,0:T(8,128)(2,1)S(1)}, bf16[16,1024]{1,0:T(8,128)(2,1)S(1)}, u32[]{:S(2)}, u32[]{:S(2)}) collective-permute-start(bf16[16,1024]{1,0:T(8,128)(2,1)S(1)} %get-tuple-element.97), channel_id=1, source_target_pairs={{0,12},{1,13},{2,14},{3,15},{4,8},{5,9},{6,10},{7,11},{8,4},{9,5},... | collective-permute-start | bytes 98312 | tf_op jit(solution)/shard_map/ppermute | solution.py:222
  83.6 4.2 %collective-permute-start.28 = (bf16[16,1024]{1,0:T(8,128)(2,1)S(1)}, bf16[16,1024]{1,0:T(8,128)(2,1)S(1)}, u32[]{:S(2)}, u32[]{:S(2)}) collective-permute-start(bf16[16,1024]{1,0:T(8,128)(2,1)S(1)} %get-tuple-element.99), channel_id=1, source_target_pairs={{0,14},{1,15},{2,12},{3,13},{4,10},{5,11},{6,8},{7,9},{8,6},{9,7},... | collective-permute-start | bytes 98312 | tf_op jit(solution)/shard_map/ppermute | solution.py:222
  87.9 4.1 %shard_map.82 = (bf16[16,1024]{1,0:T(8,128)(2,1)S(1)}, bf16[16,1024]{1,0:T(8,128)(2,1)S(1)}, bf16[16,1024]{1,0:T(8,128)(2,1)S(1)}, bf16[16,1024]{1,0:T(8,128)(2,...) custom-call(s32[1]{0:T(128)} %bitcast.me_ref, ...), custom_call_target="tpu_custom_call" | custom-call | flops 2415919104 | bytes 2097152 | tf_op jit(solution)/shard_map/pallas_call | solution.py:113
  93.3 1.5 %collective-permute-start.1 = (bf16[16,1024]{1,0:T(8,128)(2,1)S(1)}, bf16[16,1024]{1,0:T(8,128)(2,1)S(1)}, u32[]{:S(2)}, u32[]{:S(2)}) collective-permute-start(bf16[16,1024]{1,0:T(8,128)(2,1)S(1)} %get-tuple-element.71), channel_id=1, source_target_pairs={{0,2},{1,3},{2,0},{3,1},{4,6},{5,7},{6,4},{7,5},{8,10},{9,11},{10,... | collective-permute-start | bytes 98312 | tf_op jit(solution)/shard_map/ppermute | solution.py:222
  94.9 1.9 %collective-permute-start.4 = (bf16[16,1024]{1,0:T(8,128)(2,1)S(1)}, bf16[16,1024]{1,0:T(8,128)(2,1)S(1)}, u32[]{:S(2)}, u32[]{:S(2)}) collective-permute-start(bf16[16,1024]{1,0:T(8,128)(2,1)S(1)} %get-tuple-element.74), channel_id=1, source_target_pairs={{0,5},{1,4},{2,7},{3,6},{4,1},{5,0},{6,3},{7,2},{8,13},{9,12},{10,... | collective-permute-start | bytes 98312 | tf_op jit(solution)/shard_map/ppermute | solution.py:222
  99.3 2.4 %collective-permute-start.7 = (bf16[16,1024]{1,0:T(8,128)(2,1)S(1)}, bf16[16,1024]{1,0:T(8,128)(2,1)S(1)}, u32[]{:S(2)}, u32[]{:S(2)}) collective-permute-start(bf16[16,1024]{1,0:T(8,128)(2,1)S(1)} %get-tuple-element.77), channel_id=1, source_target_pairs={{0,8},{1,9},{2,10},{3,11},{4,12},{5,13},{6,14},{7,15},{8,0},{9,1},... | collective-permute-start | bytes 98312 | tf_op jit(solution)/shard_map/ppermute | solution.py:222
  102.1 3.2 %collective-permute-start.9 = (bf16[16,1024]{1,0:T(8,128)(2,1)S(1)}, bf16[16,1024]{1,0:T(8,128)(2,1)S(1)}, u32[]{:S(2)}, u32[]{:S(2)}) collective-permute-start(bf16[16,1024]{1,0:T(8,128)(2,1)S(1)} %get-tuple-element.79), channel_id=1, source_target_pairs={{0,10},{1,11},{2,8},{3,9},{4,14},{5,15},{6,12},{7,13},{8,2},{9,3},... | collective-permute-start | bytes 98312 | tf_op jit(solution)/shard_map/ppermute | solution.py:222
  105.5 3.3 %collective-permute-start.11 = (bf16[16,1024]{1,0:T(8,128)(2,1)S(1)}, bf16[16,1024]{1,0:T(8,128)(2,1)S(1)}, u32[]{:S(2)}, u32[]{:S(2)}) collective-permute-start(bf16[16,1024]{1,0:T(8,128)(2,1)S(1)} %get-tuple-element.81), channel_id=1, source_target_pairs={{0,12},{1,13},{2,14},{3,15},{4,8},{5,9},{6,10},{7,11},{8,4},{9,5},... | collective-permute-start | bytes 98312 | tf_op jit(solution)/shard_map/ppermute | solution.py:222
  109.2 4.3 %collective-permute-start.13 = (bf16[16,1024]{1,0:T(8,128)(2,1)S(1)}, bf16[16,1024]{1,0:T(8,128)(2,1)S(1)}, u32[]{:S(2)}, u32[]{:S(2)}) collective-permute-start(bf16[16,1024]{1,0:T(8,128)(2,1)S(1)} %get-tuple-element.83), channel_id=1, source_target_pairs={{0,14},{1,15},{2,12},{3,13},{4,10},{5,11},{6,8},{7,9},{8,6},{9,7},... | collective-permute-start | bytes 98312 | tf_op jit(solution)/shard_map/ppermute | solution.py:222
  114.1 1.9 %collective-permute-done.13.rest_14_ = bf16[16,1024]{1,0:T(8,128)(2,1)S(1)} collective-permute-done((bf16[16,1024]{1,0:T(8,128)(2,1)S(1)}, bf16[16,1024]{1,0:T(8,128)(2,1)S(1)}, u32[]{:S(2)}, u32[]{:S(2)}) %collective-permute-start.13) | collective-permute-done | bytes 32800 | tf_op jit(solution)/shard_map/ppermute | solution.py:222
  115.9 3.9 %collective-permute-done.14.rest_15_ = bf16[16,1024]{1,0:T(8,128)(2,1)S(1)} collective-permute-done((bf16[16,1024]{1,0:T(8,128)(2,1)S(1)}, bf16[16,1024]{1,0:T(8,128)(2,1)S(1)}, u32[]{:S(2)}, u32[]{:S(2)}) %collective-permute-start.14) | collective-permute-done | bytes 32800 | tf_op jit(solution)/shard_map/ppermute | solution.py:222
  120.5 3.4 %shard_map.86 = bf16[1,8,16,8192]{3,2,1,0:T(8,128)(2,1)} custom-call(s32[1]{0:T(128)} %bitcast.me_ref, bf16[16,1024]{1,0:T(8,128)(2,1)} %copy-done.8, bf16[16,1024]{1,0:T(8,128)(2,1)} %copy-done.55, bf16[16,1024]{1,0:T(8,128)(2,1)} %copy-done.56, bf16[16,1024]{1,0:T(8,128)(2,1)} %copy-done.57, bf16[16,1024]{1,0:T(8,128)(2,1)} %copy-done.58, ...), custom_call_target="tpu_custom_call" | custom-call | tf_op jit(solution)/shard_map/pallas_call | solution.py:163
  (233 shorter events, 24.7 us)
Async XLA Ops:
  19.3 8.9 %collective-permute-start.50 = (bf16[16,1024]{1,0:T(8,128)(2,1)S(1)}, bf16[16,1024]{1,0:T(8,128)(2,1)S(1)}, u32[]{:S(2)}, u32[]{:S(2)}) collective-permute-start(bf16[16,1024]{1,0:T(8,128)(2,1)S(1)} %get-tuple-element.123), channel_id=1, source_target_pairs={{0,6},{1,7},{2,4},{3,5},{4,2},{5,3},{6,0},{7,1},{8,14},{9,15},{10,... | collective-permute-start | bytes 98312 | tf_op jit(solution)/shard_map/ppermute | solution.py:222
  22.1 9.9 %collective-permute-start.52 = (bf16[16,1024]{1,0:T(8,128)(2,1)S(1)}, bf16[16,1024]{1,0:T(8,128)(2,1)S(1)}, u32[]{:S(2)}, u32[]{:S(2)}) collective-permute-start(bf16[16,1024]{1,0:T(8,128)(2,1)S(1)} %get-tuple-element.125), channel_id=1, source_target_pairs={{0,8},{1,9},{2,10},{3,11},{4,12},{5,13},{6,14},{7,15},{8,0},{9,1},... | collective-permute-start | bytes 98312 | tf_op jit(solution)/shard_map/ppermute | solution.py:222
  25.0 11.3 %collective-permute-start.54 = (bf16[16,1024]{1,0:T(8,128)(2,1)S(1)}, bf16[16,1024]{1,0:T(8,128)(2,1)S(1)}, u32[]{:S(2)}, u32[]{:S(2)}) collective-permute-start(bf16[16,1024]{1,0:T(8,128)(2,1)S(1)} %get-tuple-element.127), channel_id=1, source_target_pairs={{0,10},{1,11},{2,8},{3,9},{4,14},{5,15},{6,12},{7,13},{8,2},{9,3},... | collective-permute-start | bytes 98312 | tf_op jit(solution)/shard_map/ppermute | solution.py:222
  28.2 13.2 %collective-permute-start.55 = (bf16[16,1024]{1,0:T(8,128)(2,1)S(1)}, bf16[16,1024]{1,0:T(8,128)(2,1)S(1)}, u32[]{:S(2)}, u32[]{:S(2)}) collective-permute-start(bf16[16,1024]{1,0:T(8,128)(2,1)S(1)} %get-tuple-element.128), channel_id=1, source_target_pairs={{0,11},{1,10},{2,9},{3,8},{4,15},{5,14},{6,13},{7,12},{8,3},{9,2},... | collective-permute-start | bytes 98312 | tf_op jit(solution)/shard_map/ppermute | solution.py:222
  28.5 13.3 %collective-permute-start.56 = (bf16[16,1024]{1,0:T(8,128)(2,1)S(1)}, bf16[16,1024]{1,0:T(8,128)(2,1)S(1)}, u32[]{:S(2)}, u32[]{:S(2)}) collective-permute-start(bf16[16,1024]{1,0:T(8,128)(2,1)S(1)} %get-tuple-element.129), channel_id=1, source_target_pairs={{0,12},{1,13},{2,14},{3,15},{4,8},{5,9},{6,10},{7,11},{8,4},{9,5},... | collective-permute-start | bytes 98312 | tf_op jit(solution)/shard_map/ppermute | solution.py:222
  32.0 11.3 %collective-permute-start.57 = (bf16[16,1024]{1,0:T(8,128)(2,1)S(1)}, bf16[16,1024]{1,0:T(8,128)(2,1)S(1)}, u32[]{:S(2)}, u32[]{:S(2)}) collective-permute-start(bf16[16,1024]{1,0:T(8,128)(2,1)S(1)} %get-tuple-element.130), channel_id=1, source_target_pairs={{0,13},{1,12},{2,15},{3,14},{4,9},{5,8},{6,11},{7,10},{8,5},{9,4},... | collective-permute-start | bytes 98312 | tf_op jit(solution)/shard_map/ppermute | solution.py:222
  32.1 11.2 %collective-permute-start.58 = (bf16[16,1024]{1,0:T(8,128)(2,1)S(1)}, bf16[16,1024]{1,0:T(8,128)(2,1)S(1)}, u32[]{:S(2)}, u32[]{:S(2)}) collective-permute-start(bf16[16,1024]{1,0:T(8,128)(2,1)S(1)} %get-tuple-element.131), channel_id=1, source_target_pairs={{0,14},{1,15},{2,12},{3,13},{4,10},{5,11},{6,8},{7,9},{8,6},{9,7},... | collective-permute-start | bytes 98312 | tf_op jit(solution)/shard_map/ppermute | solution.py:222
  45.3 8.5 %collective-permute-start.35 = (bf16[16,1024]{1,0:T(8,128)(2,1)S(1)}, bf16[16,1024]{1,0:T(8,128)(2,1)S(1)}, u32[]{:S(2)}, u32[]{:S(2)}) collective-permute-start(bf16[16,1024]{1,0:T(8,128)(2,1)S(1)} %get-tuple-element.107), channel_id=1, source_target_pairs={{0,6},{1,7},{2,4},{3,5},{4,2},{5,3},{6,0},{7,1},{8,14},{9,15},{10,... | collective-permute-start | bytes 98312 | tf_op jit(solution)/shard_map/ppermute | solution.py:222
  46.6 7.4 %collective-permute-start.36 = (bf16[16,1024]{1,0:T(8,128)(2,1)S(1)}, bf16[16,1024]{1,0:T(8,128)(2,1)S(1)}, u32[]{:S(2)}, u32[]{:S(2)}) collective-permute-start(bf16[16,1024]{1,0:T(8,128)(2,1)S(1)} %get-tuple-element.108), channel_id=1, source_target_pairs={{0,7},{1,6},{2,5},{3,4},{4,3},{5,2},{6,1},{7,0},{8,15},{9,14},{10,... | collective-permute-start | bytes 98312 | tf_op jit(solution)/shard_map/ppermute | solution.py:222
  47.8 9.5 %collective-permute-start.37 = (bf16[16,1024]{1,0:T(8,128)(2,1)S(1)}, bf16[16,1024]{1,0:T(8,128)(2,1)S(1)}, u32[]{:S(2)}, u32[]{:S(2)}) collective-permute-start(bf16[16,1024]{1,0:T(8,128)(2,1)S(1)} %get-tuple-element.109), channel_id=1, source_target_pairs={{0,8},{1,9},{2,10},{3,11},{4,12},{5,13},{6,14},{7,15},{8,0},{9,1},... | collective-permute-start | bytes 98312 | tf_op jit(solution)/shard_map/ppermute | solution.py:222
  50.2 7.5 %collective-permute-start.38 = (bf16[16,1024]{1,0:T(8,128)(2,1)S(1)}, bf16[16,1024]{1,0:T(8,128)(2,1)S(1)}, u32[]{:S(2)}, u32[]{:S(2)}) collective-permute-start(bf16[16,1024]{1,0:T(8,128)(2,1)S(1)} %get-tuple-element.110), channel_id=1, source_target_pairs={{0,9},{1,8},{2,11},{3,10},{4,13},{5,12},{6,15},{7,14},{8,1},{9,0},... | collective-permute-start | bytes 98312 | tf_op jit(solution)/shard_map/ppermute | solution.py:222
  50.6 11.3 %collective-permute-start.39 = (bf16[16,1024]{1,0:T(8,128)(2,1)S(1)}, bf16[16,1024]{1,0:T(8,128)(2,1)S(1)}, u32[]{:S(2)}, u32[]{:S(2)}) collective-permute-start(bf16[16,1024]{1,0:T(8,128)(2,1)S(1)} %get-tuple-element.111), channel_id=1, source_target_pairs={{0,10},{1,11},{2,8},{3,9},{4,14},{5,15},{6,12},{7,13},{8,2},{9,3},... | collective-permute-start | bytes 98312 | tf_op jit(solution)/shard_map/ppermute | solution.py:222
  53.8 13.3 %collective-permute-start.40 = (bf16[16,1024]{1,0:T(8,128)(2,1)S(1)}, bf16[16,1024]{1,0:T(8,128)(2,1)S(1)}, u32[]{:S(2)}, u32[]{:S(2)}) collective-permute-start(bf16[16,1024]{1,0:T(8,128)(2,1)S(1)} %get-tuple-element.112), channel_id=1, source_target_pairs={{0,11},{1,10},{2,9},{3,8},{4,15},{5,14},{6,13},{7,12},{8,3},{9,2},... | collective-permute-start | bytes 98312 | tf_op jit(solution)/shard_map/ppermute | solution.py:222
  54.0 13.6 %collective-permute-start.41 = (bf16[16,1024]{1,0:T(8,128)(2,1)S(1)}, bf16[16,1024]{1,0:T(8,128)(2,1)S(1)}, u32[]{:S(2)}, u32[]{:S(2)}) collective-permute-start(bf16[16,1024]{1,0:T(8,128)(2,1)S(1)} %get-tuple-element.113), channel_id=1, source_target_pairs={{0,12},{1,13},{2,14},{3,15},{4,8},{5,9},{6,10},{7,11},{8,4},{9,5},... | collective-permute-start | bytes 98312 | tf_op jit(solution)/shard_map/ppermute | solution.py:222
  57.3 11.8 %collective-permute-start.42 = (bf16[16,1024]{1,0:T(8,128)(2,1)S(1)}, bf16[16,1024]{1,0:T(8,128)(2,1)S(1)}, u32[]{:S(2)}, u32[]{:S(2)}) collective-permute-start(bf16[16,1024]{1,0:T(8,128)(2,1)S(1)} %get-tuple-element.114), channel_id=1, source_target_pairs={{0,13},{1,12},{2,15},{3,14},{4,9},{5,8},{6,11},{7,10},{8,5},{9,4},... | collective-permute-start | bytes 98312 | tf_op jit(solution)/shard_map/ppermute | solution.py:222
  57.7 11.4 %collective-permute-start.43 = (bf16[16,1024]{1,0:T(8,128)(2,1)S(1)}, bf16[16,1024]{1,0:T(8,128)(2,1)S(1)}, u32[]{:S(2)}, u32[]{:S(2)}) collective-permute-start(bf16[16,1024]{1,0:T(8,128)(2,1)S(1)} %get-tuple-element.115), channel_id=1, source_target_pairs={{0,14},{1,15},{2,12},{3,13},{4,10},{5,11},{6,8},{7,9},{8,6},{9,7},... | collective-permute-start | bytes 98312 | tf_op jit(solution)/shard_map/ppermute | solution.py:222
  71.2 8.5 %collective-permute-start.20 = (bf16[16,1024]{1,0:T(8,128)(2,1)S(1)}, bf16[16,1024]{1,0:T(8,128)(2,1)S(1)}, u32[]{:S(2)}, u32[]{:S(2)}) collective-permute-start(bf16[16,1024]{1,0:T(8,128)(2,1)S(1)} %get-tuple-element.91), channel_id=1, source_target_pairs={{0,6},{1,7},{2,4},{3,5},{4,2},{5,3},{6,0},{7,1},{8,14},{9,15},{10,... | collective-permute-start | bytes 98312 | tf_op jit(solution)/shard_map/ppermute | solution.py:222
  72.4 7.4 %collective-permute-start.21 = (bf16[16,1024]{1,0:T(8,128)(2,1)S(1)}, bf16[16,1024]{1,0:T(8,128)(2,1)S(1)}, u32[]{:S(2)}, u32[]{:S(2)}) collective-permute-start(bf16[16,1024]{1,0:T(8,128)(2,1)S(1)} %get-tuple-element.92), channel_id=1, source_target_pairs={{0,7},{1,6},{2,5},{3,4},{4,3},{5,2},{6,1},{7,0},{8,15},{9,14},{10,... | collective-permute-start | bytes 98312 | tf_op jit(solution)/shard_map/ppermute | solution.py:222
  73.6 9.5 %collective-permute-start.22 = (bf16[16,1024]{1,0:T(8,128)(2,1)S(1)}, bf16[16,1024]{1,0:T(8,128)(2,1)S(1)}, u32[]{:S(2)}, u32[]{:S(2)}) collective-permute-start(bf16[16,1024]{1,0:T(8,128)(2,1)S(1)} %get-tuple-element.93), channel_id=1, source_target_pairs={{0,8},{1,9},{2,10},{3,11},{4,12},{5,13},{6,14},{7,15},{8,0},{9,1},... | collective-permute-start | bytes 98312 | tf_op jit(solution)/shard_map/ppermute | solution.py:222
  76.1 7.5 %collective-permute-start.23 = (bf16[16,1024]{1,0:T(8,128)(2,1)S(1)}, bf16[16,1024]{1,0:T(8,128)(2,1)S(1)}, u32[]{:S(2)}, u32[]{:S(2)}) collective-permute-start(bf16[16,1024]{1,0:T(8,128)(2,1)S(1)} %get-tuple-element.94), channel_id=1, source_target_pairs={{0,9},{1,8},{2,11},{3,10},{4,13},{5,12},{6,15},{7,14},{8,1},{9,0},... | collective-permute-start | bytes 98312 | tf_op jit(solution)/shard_map/ppermute | solution.py:222
  76.5 11.4 %collective-permute-start.24 = (bf16[16,1024]{1,0:T(8,128)(2,1)S(1)}, bf16[16,1024]{1,0:T(8,128)(2,1)S(1)}, u32[]{:S(2)}, u32[]{:S(2)}) collective-permute-start(bf16[16,1024]{1,0:T(8,128)(2,1)S(1)} %get-tuple-element.95), channel_id=1, source_target_pairs={{0,10},{1,11},{2,8},{3,9},{4,14},{5,15},{6,12},{7,13},{8,2},{9,3},... | collective-permute-start | bytes 98312 | tf_op jit(solution)/shard_map/ppermute | solution.py:222
  79.6 13.1 %collective-permute-start.25 = (bf16[16,1024]{1,0:T(8,128)(2,1)S(1)}, bf16[16,1024]{1,0:T(8,128)(2,1)S(1)}, u32[]{:S(2)}, u32[]{:S(2)}) collective-permute-start(bf16[16,1024]{1,0:T(8,128)(2,1)S(1)} %get-tuple-element.96), channel_id=1, source_target_pairs={{0,11},{1,10},{2,9},{3,8},{4,15},{5,14},{6,13},{7,12},{8,3},{9,2},... | collective-permute-start | bytes 98312 | tf_op jit(solution)/shard_map/ppermute | solution.py:222
  79.9 13.4 %collective-permute-start.26 = (bf16[16,1024]{1,0:T(8,128)(2,1)S(1)}, bf16[16,1024]{1,0:T(8,128)(2,1)S(1)}, u32[]{:S(2)}, u32[]{:S(2)}) collective-permute-start(bf16[16,1024]{1,0:T(8,128)(2,1)S(1)} %get-tuple-element.97), channel_id=1, source_target_pairs={{0,12},{1,13},{2,14},{3,15},{4,8},{5,9},{6,10},{7,11},{8,4},{9,5},... | collective-permute-start | bytes 98312 | tf_op jit(solution)/shard_map/ppermute | solution.py:222
  83.2 11.6 %collective-permute-start.27 = (bf16[16,1024]{1,0:T(8,128)(2,1)S(1)}, bf16[16,1024]{1,0:T(8,128)(2,1)S(1)}, u32[]{:S(2)}, u32[]{:S(2)}) collective-permute-start(bf16[16,1024]{1,0:T(8,128)(2,1)S(1)} %get-tuple-element.98), channel_id=1, source_target_pairs={{0,13},{1,12},{2,15},{3,14},{4,9},{5,8},{6,11},{7,10},{8,5},{9,4},... | collective-permute-start | bytes 98312 | tf_op jit(solution)/shard_map/ppermute | solution.py:222
  83.6 11.2 %collective-permute-start.28 = (bf16[16,1024]{1,0:T(8,128)(2,1)S(1)}, bf16[16,1024]{1,0:T(8,128)(2,1)S(1)}, u32[]{:S(2)}, u32[]{:S(2)}) collective-permute-start(bf16[16,1024]{1,0:T(8,128)(2,1)S(1)} %get-tuple-element.99), channel_id=1, source_target_pairs={{0,14},{1,15},{2,12},{3,13},{4,10},{5,11},{6,8},{7,9},{8,6},{9,7},... | collective-permute-start | bytes 98312 | tf_op jit(solution)/shard_map/ppermute | solution.py:222
  96.8 8.5 %collective-permute-start.5 = (bf16[16,1024]{1,0:T(8,128)(2,1)S(1)}, bf16[16,1024]{1,0:T(8,128)(2,1)S(1)}, u32[]{:S(2)}, u32[]{:S(2)}) collective-permute-start(bf16[16,1024]{1,0:T(8,128)(2,1)S(1)} %get-tuple-element.75), channel_id=1, source_target_pairs={{0,6},{1,7},{2,4},{3,5},{4,2},{5,3},{6,0},{7,1},{8,14},{9,15},{10,... | collective-permute-start | bytes 98312 | tf_op jit(solution)/shard_map/ppermute | solution.py:222
  98.1 7.4 %collective-permute-start.6 = (bf16[16,1024]{1,0:T(8,128)(2,1)S(1)}, bf16[16,1024]{1,0:T(8,128)(2,1)S(1)}, u32[]{:S(2)}, u32[]{:S(2)}) collective-permute-start(bf16[16,1024]{1,0:T(8,128)(2,1)S(1)} %get-tuple-element.76), channel_id=1, source_target_pairs={{0,7},{1,6},{2,5},{3,4},{4,3},{5,2},{6,1},{7,0},{8,15},{9,14},{10,... | collective-permute-start | bytes 98312 | tf_op jit(solution)/shard_map/ppermute | solution.py:222
  99.3 9.5 %collective-permute-start.7 = (bf16[16,1024]{1,0:T(8,128)(2,1)S(1)}, bf16[16,1024]{1,0:T(8,128)(2,1)S(1)}, u32[]{:S(2)}, u32[]{:S(2)}) collective-permute-start(bf16[16,1024]{1,0:T(8,128)(2,1)S(1)} %get-tuple-element.77), channel_id=1, source_target_pairs={{0,8},{1,9},{2,10},{3,11},{4,12},{5,13},{6,14},{7,15},{8,0},{9,1},... | collective-permute-start | bytes 98312 | tf_op jit(solution)/shard_map/ppermute | solution.py:222
  101.7 7.5 %collective-permute-start.8 = (bf16[16,1024]{1,0:T(8,128)(2,1)S(1)}, bf16[16,1024]{1,0:T(8,128)(2,1)S(1)}, u32[]{:S(2)}, u32[]{:S(2)}) collective-permute-start(bf16[16,1024]{1,0:T(8,128)(2,1)S(1)} %get-tuple-element.78), channel_id=1, source_target_pairs={{0,9},{1,8},{2,11},{3,10},{4,13},{5,12},{6,15},{7,14},{8,1},{9,0},... | collective-permute-start | bytes 98312 | tf_op jit(solution)/shard_map/ppermute | solution.py:222
  102.1 11.4 %collective-permute-start.9 = (bf16[16,1024]{1,0:T(8,128)(2,1)S(1)}, bf16[16,1024]{1,0:T(8,128)(2,1)S(1)}, u32[]{:S(2)}, u32[]{:S(2)}) collective-permute-start(bf16[16,1024]{1,0:T(8,128)(2,1)S(1)} %get-tuple-element.79), channel_id=1, source_target_pairs={{0,10},{1,11},{2,8},{3,9},{4,14},{5,15},{6,12},{7,13},{8,2},{9,3},... | collective-permute-start | bytes 98312 | tf_op jit(solution)/shard_map/ppermute | solution.py:222
  105.3 8.2 %collective-permute-start.10 = (bf16[16,1024]{1,0:T(8,128)(2,1)S(1)}, bf16[16,1024]{1,0:T(8,128)(2,1)S(1)}, u32[]{:S(2)}, u32[]{:S(2)}) collective-permute-start(bf16[16,1024]{1,0:T(8,128)(2,1)S(1)} %get-tuple-element.80), channel_id=1, source_target_pairs={{0,11},{1,10},{2,9},{3,8},{4,15},{5,14},{6,13},{7,12},{8,3},{9,2},... | collective-permute-start | bytes 98312 | tf_op jit(solution)/shard_map/ppermute | solution.py:222
  105.5 8.0 %collective-permute-start.11 = (bf16[16,1024]{1,0:T(8,128)(2,1)S(1)}, bf16[16,1024]{1,0:T(8,128)(2,1)S(1)}, u32[]{:S(2)}, u32[]{:S(2)}) collective-permute-start(bf16[16,1024]{1,0:T(8,128)(2,1)S(1)} %get-tuple-element.81), channel_id=1, source_target_pairs={{0,12},{1,13},{2,14},{3,15},{4,8},{5,9},{6,10},{7,11},{8,4},{9,5},... | collective-permute-start | bytes 98312 | tf_op jit(solution)/shard_map/ppermute | solution.py:222
  (98 other events, 1136.4 us)

commit v3 on v2

v3 whole, which is shorter than its diff:
```python
import functools
import math

import jax
import jax.numpy as jnp
from jax import lax
from jax.experimental import pallas as pl
from jax.experimental.pallas import tpu as pltpu
from jax.sharding import PartitionSpec as P

SPAN = 64
GROUP = 4
CHUNKS = (1, 1, 1, 1)
DIRECT = 16
MASKED = -1e30
OPEN = 3e38
NT = (((1,), (1,)), ((), ()))


def dot(left, right):
    return jnp.dot(left, right, preferred_element_type=jnp.float32)


def build_table(me, count, routes_ref, table_ref, capacity):
    slots = routes_ref.shape[1]
    rows = table_ref.shape[0]
    place = lax.broadcasted_iota(jnp.int32, (rows, slots), 0)
    token = lax.broadcasted_iota(jnp.int32, (rows, slots), 1)
    block = place // capacity
    expert = block ^ me
    hit = ((routes_ref[0:1, :] == expert) | (routes_ref[1:2, :] == expert)) & (
        token < count * SPAN
    )
    hit = jnp.where(hit, jnp.float32(1.0), jnp.float32(0.0))
    first = lax.broadcasted_iota(jnp.int32, (slots, slots), 0)
    second = lax.broadcasted_iota(jnp.int32, (slots, slots), 1)
    earlier = jnp.where(first < second, jnp.float32(1.0), jnp.float32(0.0))
    before = dot(hit.astype(jnp.bfloat16), earlier.astype(jnp.bfloat16))
    wanted = (place - block * capacity).astype(jnp.float32)
    table_ref[...] = jnp.where(before == wanted, hit, jnp.float32(0.0)).astype(jnp.bfloat16)


def attend_kernel(
    capacity,
    first,
    me_ref,
    count_ref,
    size_ref,
    routes_ref,
    queries_hbm,
    key_weight_hbm,
    value_weight_hbm,
    prefix_hbm,
    fresh_hbm,
    *rest,
):
    *out_refs, queries_ref, key_weight_ref, value_weight_ref, keys_ref = rest[:-4]
    cap_ref, table_ref, attended_ref, sem = rest[-4:]
    slots = queries_ref.shape[0]
    past = prefix_hbm.shape[0]
    heads, dim, _ = key_weight_ref.shape
    here = pl.ds(first, heads)
    copies = [
        pltpu.make_async_copy(
            queries_hbm.at[:, pl.ds(first * dim, heads * dim)], queries_ref, sem.at[0]
        ),
        pltpu.make_async_copy(key_weight_hbm.at[here], key_weight_ref, sem.at[1]),
        pltpu.make_async_copy(prefix_hbm, keys_ref.at[pl.ds(0, past)], sem.at[2]),
        pltpu.make_async_copy(fresh_hbm, keys_ref.at[pl.ds(past, slots)], sem.at[3]),
        pltpu.make_async_copy(value_weight_hbm.at[here], value_weight_ref, sem.at[4]),
    ]
    for copy in copies:
        copy.start()
    count, size = count_ref[0], size_ref[0]
    lane = lax.broadcasted_iota(jnp.int32, (slots, past), 1)
    cap_ref[:, :past] = jnp.where(lane < size, jnp.float32(OPEN), jnp.float32(MASKED))
    row = lax.broadcasted_iota(jnp.int32, (slots, slots), 0)
    col = lax.broadcasted_iota(jnp.int32, (slots, slots), 1)
    cap_ref[:, past:] = jnp.where(
        (col <= row) & (col < count * SPAN), jnp.float32(OPEN), jnp.float32(MASKED)
    )
    build_table(me_ref[0], count, routes_ref, table_ref, capacity)
    for copy in copies:
        copy.wait()

    scale = math.log2(math.e) / math.sqrt(dim)
    keys = keys_ref[...]
    stacks = heads // GROUP
    scores = []
    for stack in range(stacks):
        lifted = []
        for h in range(stack * GROUP, (stack + 1) * GROUP):
            one = dot(queries_ref[:, h * dim : (h + 1) * dim], key_weight_ref[h])
            lifted.append(one.astype(jnp.bfloat16))
        lifted = jnp.concatenate(lifted, axis=0)
        score = lax.dot_general(lifted, keys, NT, preferred_element_type=jnp.float32)
        scores.append(score)
    for stack in range(stacks):
        score = scores[stack].reshape(GROUP, slots, keys.shape[0])
        score = jnp.minimum(score, cap_ref[...][None])
        highest = jnp.max(score, axis=-1, keepdims=True) * scale
        weights = jnp.exp2(score * scale - highest)
        total = jnp.sum(weights, axis=-1, keepdims=True)
        weights = weights.astype(jnp.bfloat16).reshape(GROUP * slots, keys.shape[0])
        mixed = dot(weights, keys).astype(jnp.bfloat16)
        for g in range(GROUP):
            h = stack * GROUP + g
            projected = dot(mixed[g * slots : (g + 1) * slots], value_weight_ref[h])
            attended_ref[:, h * dim : (h + 1) * dim] = (projected / total[g]).astype(jnp.bfloat16)
    grouped = dot(table_ref[...], attended_ref[...]).astype(jnp.bfloat16)
    rows = out_refs[0].shape[0]
    for k, out_ref in enumerate(out_refs):
        out_ref[...] = grouped[k * rows : (k + 1) * rows]


def attend(
    first, heads, me, queries, key_weight, value_weight, prefix, fresh, count, size, routes, experts, pieces
):
    slots = queries.shape[0]
    _, dim, latent = key_weight.shape
    places = slots * routes.shape[1]
    keys = prefix.shape[0] + slots
    smem = pl.BlockSpec(memory_space=pltpu.SMEM)
    vmem = pl.BlockSpec(memory_space=pltpu.VMEM)
    hbm = pl.BlockSpec(memory_space=pltpu.HBM)
    piece = (places // pieces, heads * dim)
    return pl.pallas_call(
        functools.partial(attend_kernel, places // experts, first),
        in_specs=[smem, smem, smem, vmem, hbm, hbm, hbm, hbm, hbm],
        out_specs=[vmem] * pieces,
        out_shape=[jax.ShapeDtypeStruct(piece, jnp.bfloat16)] * pieces,
        scratch_shapes=[
            pltpu.VMEM((slots, heads * dim), jnp.bfloat16),
            pltpu.VMEM((heads, dim, latent), jnp.bfloat16),
            pltpu.VMEM((heads, latent, dim), jnp.bfloat16),
            pltpu.VMEM((keys, latent), jnp.bfloat16),
            pltpu.VMEM((slots, keys), jnp.float32),
            pltpu.VMEM((places, slots), jnp.bfloat16),
            pltpu.VMEM((slots, heads * dim), jnp.bfloat16),
            pltpu.SemaphoreType.DMA((5,)),
        ],
        compiler_params=pltpu.CompilerParams(vmem_limit_bytes=54 * 1024 * 1024),
        cost_estimate=pl.CostEstimate(
            flops=4 * slots * heads * keys * latent,
            bytes_accessed=4 * heads * dim * latent,
            transcendentals=heads * slots * keys,
        ),
    )(me, count, size, routes.T, queries, key_weight, value_weight, prefix, fresh)


def run_copies(copies):
    for copy in copies:
        copy.start()
    for copy in copies:
        copy.wait()


def pass_on_kernel(cores, *refs):
    *piece_refs, out_ref, sem = refs
    capacity = piece_refs[0].shape[0] // cores
    run_copies(
        [
            pltpu.make_async_copy(
                piece_ref.at[pl.ds(capacity, capacity)],
                out_ref.at[pl.ds(j * capacity, capacity)],
                sem.at[j],
            )
            for j, piece_ref in enumerate(piece_refs)
        ]
    )


def pass_on(pieces, cores):
    rows, width = pieces[0].shape
    return pl.pallas_call(
        functools.partial(pass_on_kernel, cores),
        in_specs=[pl.BlockSpec(memory_space=pl.ANY)] * len(pieces),
        out_specs=pl.BlockSpec(memory_space=pltpu.VMEM),
        out_shape=jax.ShapeDtypeStruct((len(pieces) * rows // cores, width), jnp.bfloat16),
        scratch_shapes=[pltpu.SemaphoreType.DMA((len(pieces),))],
    )(*pieces)


def place_kernel(plan, cores, me_ref, *rest):
    *refs, out_ref, whole_ref, sem = rest
    _, capacity, features = whole_ref.shape
    features //= cores
    me = me_ref[0]
    copies = []
    for i, (ref, (first, start, source)) in enumerate(plan):
        ref = refs[ref]
        width = ref.shape[1]
        who = me ^ source
        left = pl.multiple_of(who % cores * features + first, math.gcd(features, first))
        copies.append(
            pltpu.make_async_copy(
                ref.at[pl.ds(start, capacity)],
                whole_ref.at[who // cores, :, pl.ds(left, width)],
                sem.at[i],
            )
        )
    run_copies(copies)
    run_copies([pltpu.make_async_copy(whole_ref, out_ref.at[0], sem.at[0])])


def assemble(me, arrays, plan, shape, cores):
    return pl.pallas_call(
        functools.partial(place_kernel, plan, cores),
        in_specs=[pl.BlockSpec(memory_space=pltpu.SMEM)]
        + [pl.BlockSpec(memory_space=pl.ANY)] * len(arrays),
        out_specs=pl.BlockSpec(memory_space=pl.ANY),
        out_shape=jax.ShapeDtypeStruct(shape, jnp.bfloat16),
        scratch_shapes=[
            pltpu.VMEM(shape[1:], jnp.bfloat16),
            pltpu.SemaphoreType.DMA((len(plan),)),
        ],
    )(me, *arrays)


def exchange_order(ranks):
    near, far = list(range(1, ranks // 2)), list(range(ranks // 2, ranks))
    mixed = []
    while len(far) > 2 or near:
        mixed += near[:1] + (far[:1] if len(far) > 2 else [])
        near, far = near[1:], (far[1:] if len(far) > 2 else far)
    return mixed + far


def local(
    queries,
    key_weight,
    value_weight,
    prefix_latent,
    fresh_latent,
    span_counts,
    prefix_lengths,
    routes,
):
    ranks, cores = lax.axis_size("dp"), lax.axis_size("ep")
    experts = ranks * cores
    slots = queries.shape[0]
    heads, dim, _ = key_weight.shape
    capacity = slots * routes.shape[1] // experts
    direct = ranks <= DIRECT and capacity % 16 == 0
    index = lax.axis_index("dp") * cores + lax.axis_index("ep")
    me = (index if direct else jnp.int32(0)).astype(jnp.int32).reshape(1)
    shares = [heads * share // sum(CHUNKS) for share in CHUNKS]
    chunks, plan = [], []
    first = 0
    for share in shares:
        outgoing = attend(
            first,
            share,
            me,
            queries,
            key_weight,
            value_weight,
            prefix_latent,
            fresh_latent,
            span_counts,
            prefix_lengths,
            routes,
            experts,
            ranks if direct else 1,
        )
        if direct:
            order = exchange_order(ranks)
            pieces = [outgoing[0]]
            for j in order:
                pairs = [(i, i ^ j) for i in range(ranks)]
                pieces.append(lax.ppermute(outgoing[j], "dp", pairs))
            swapped = lax.ppermute(
                pass_on(pieces, cores), "ep", [(i, i ^ 1) for i in range(cores)]
            )
            for at, j in enumerate([0] + order):
                plan.append((len(chunks) + at, (first * dim, 0, j * cores)))
                plan.append((len(chunks) + ranks, (first * dim, at * capacity, j * cores + 1)))
            chunks += pieces + [swapped]
        else:
            arrived = lax.all_to_all(
                outgoing[0].reshape(experts, capacity, share * dim),
                ("dp", "ep"),
                split_axis=0,
                concat_axis=0,
                tiled=True,
            )
            chunks.append(arrived.reshape(ranks, cores, capacity, share * dim))
        first += share
    if direct:
        return assemble(me, chunks, plan, (1, ranks, capacity, cores * heads * dim), cores)
    arrived = jnp.concatenate(chunks, axis=3).transpose(0, 2, 1, 3)
    return arrived.reshape(1, ranks, capacity, cores * heads * dim)


def solution(mesh):
    in_specs = (
        P(("groups", "dp"), "ep"),
        P("ep", None, None),
        P("ep", None, None),
        P(("groups", "dp"), None),
        P(("groups", "dp"), None),
        P(("groups", "dp")),
        P(("groups", "dp")),
        P(("groups", "dp"), None),
    )
    out_specs = P(("groups", "dp", "ep"), None, None, None)
    return jax.shard_map(local, mesh=mesh, in_specs=in_specs, out_specs=out_specs, check_vma=False)
```

time: 124 us -> 94.8 us (0.76)
  starting transfers between devices: 84 us -> 45.5 us
  Pallas kernels: 19.9 us -> 40.2 us
  local copies, waits for them, and re-layouts: 11.4 us -> 1.4 us
  waiting for transfers between devices: 6.44 us -> 4.98 us
    ppermute x60 -> x32, starting transfers between devices: 84 us -> 45.5 us  [the longest x28 44.8 us: local(): pieces.append(lax.ppermute(outgoing[j], 'dp', pairs))]
    pallas_call x5 -> x9, Pallas kernels: 19.9 us -> 40.2 us  [the longest x4 30.3 us: attend(): pl.pallas_call(functools.partial(attend_kernel, places // experts, first)...]
    unnamed x140 -> x76, local copies, waits for them, and re-layouts: 11.4 us -> 1.4 us
    ppermute x60 -> x32, waiting for transfers between devices: 6.44 us -> 4.98 us  [the longest x28 3.3 us: local(): pieces.append(lax.ppermute(outgoing[j], 'dp', pairs))]
  transfers between devices with their start and end apart: 60 -> 32, of which waited for: 3 -> 4; matrix products, arithmetic and copies ran while one was open for 0% -> 0% of each run, Pallas kernels for 10% -> 31%
where the time goes in v3:
time: 94.8 us; the launch traced here: 94.1 us
  starting transfers between devices  45.5 us (48%)
  Pallas kernels  40.2 us (42%)
  waiting for transfers between devices  4.98 us (5%)
  between operations  1.97 us (2%)
  local copies, waits for them, and re-layouts  1.4 us (1%)
    ppermute x28, starting transfers between devices, local(): pieces.append(lax.ppermute(outgoing[j], 'dp', pairs))  44.8 us
    pallas_call x4, Pallas kernels, attend(): pl.pallas_call(functools.partial(attend_kernel, places // experts, first)...  30.3 us
    pallas_call x4, Pallas kernels, pass_on(): pl.pallas_call(functools.partial(pass_on_kernel, cores), in_specs=[pl.Blo...  6.56 us
    pallas_call x1, Pallas kernels, assemble(): pl.pallas_call(functools.partial(place_kernel, plan, cores), in_specs=[pl...  3.38 us
    ppermute x28, waiting for transfers between devices, local(): pieces.append(lax.ppermute(outgoing[j], 'dp', pairs))  3.3 us
  transfers between devices with their start and end apart: 32, of which 4 were waited for; matrix products, arithmetic and copies ran while one was open for 0% of the time, Pallas kernels for 31%

profile of v3, /device:TPU:0, one launch (start us, length us, event | category | flops | bytes accessed | tf_op | source)
XLA Modules:
  0.0 94.1 jit_solution(3451047151609484090)
XLA Ops:
  1.3 7.6 %shard_map.88 = (bf16[32,1024]{1,0:T(8,128)(2,1)}, bf16[32,1024]{1,0:T(8,128)(2,1)}, bf16[32,1024]{1,0:T(8,128)(2,1)}, bf16[32,1024]{1,0:T(8,128)(2,1)}, bf16[32...) custom-call(s32[1]{0:T(128)} %bitcast.me_ref, ...), custom_call_target="tpu_custom_call" | custom-call | flops 2415919104 | bytes 2097152 | tf_op jit(solution)/shard_map/pallas_call | solution.py:127
  8.9 3.0 %collective-permute-start.24 = (bf16[32,1024]{1,0:T(8,128)(2,1)}, bf16[32,1024]{1,0:T(8,128)(2,1)S(1)}, u32[]{:S(2)}, u32[]{:S(2)}) collective-permute-start(bf16[32,1024]{1,0:T(8,128)(2,1)} %get-tuple-element.62), channel_id=1, source_target_pairs={{0,2},{2,0},{4,6},{6,4},{8,10},{10,8},{12,14},{14,12},{1,3},{3,1},... | collective-permute-start | bytes 196616 | tf_op jit(solution)/shard_map/ppermute | solution.py:271
  11.9 2.6 %collective-permute-start.25 = (bf16[32,1024]{1,0:T(8,128)(2,1)}, bf16[32,1024]{1,0:T(8,128)(2,1)S(1)}, u32[]{:S(2)}, u32[]{:S(2)}) collective-permute-start(bf16[32,1024]{1,0:T(8,128)(2,1)} %get-tuple-element.63), channel_id=1, source_target_pairs={{0,8},{2,10},{4,12},{6,14},{8,0},{10,2},{12,4},{14,6},{1,9},{3,11}... | collective-permute-start | bytes 196616 | tf_op jit(solution)/shard_map/ppermute | solution.py:271
  14.5 1.6 %collective-permute-start.26 = (bf16[32,1024]{1,0:T(8,128)(2,1)}, bf16[32,1024]{1,0:T(8,128)(2,1)S(1)}, u32[]{:S(2)}, u32[]{:S(2)}) collective-permute-start(bf16[32,1024]{1,0:T(8,128)(2,1)} %get-tuple-element.64), channel_id=1, source_target_pairs={{0,4},{2,6},{4,0},{6,2},{8,12},{10,14},{12,8},{14,10},{1,5},{3,7},... | collective-permute-start | bytes 196616 | tf_op jit(solution)/shard_map/ppermute | solution.py:271
  16.4 1.4 %collective-permute-start.28 = (bf16[32,1024]{1,0:T(8,128)(2,1)}, bf16[32,1024]{1,0:T(8,128)(2,1)S(1)}, u32[]{:S(2)}, u32[]{:S(2)}) collective-permute-start(bf16[32,1024]{1,0:T(8,128)(2,1)} %get-tuple-element.66), channel_id=1, source_target_pairs={{0,6},{2,4},{4,2},{6,0},{8,14},{10,12},{12,10},{14,8},{1,7},{3,5},... | collective-permute-start | bytes 196616 | tf_op jit(solution)/shard_map/ppermute | solution.py:271
  17.8 7.6 %shard_map.86 = (bf16[32,1024]{1,0:T(8,128)(2,1)}, bf16[32,1024]{1,0:T(8,128)(2,1)}, bf16[32,1024]{1,0:T(8,128)(2,1)}, bf16[32,1024]{1,0:T(8,128)(2,1)}, bf16[32...) custom-call(s32[1]{0:T(128)} %bitcast.me_ref, ...), custom_call_target="tpu_custom_call" | custom-call | flops 2415919104 | bytes 2097152 | tf_op jit(solution)/shard_map/pallas_call | solution.py:127
  25.4 3.7 %collective-permute-start.29 = (bf16[32,1024]{1,0:T(8,128)(2,1)S(1)}, bf16[32,1024]{1,0:T(8,128)(2,1)S(1)}, u32[]{:S(2)}, u32[]{:S(2)}) collective-permute-start(bf16[32,1024]{1,0:T(8,128)(2,1)S(1)} %copy-done.37), channel_id=1, source_target_pairs={{0,12},{2,14},{4,8},{6,10},{8,4},{10,6},{12,0},{14,2},{1,13},{3,15... | collective-permute-start | bytes 196616 | tf_op jit(solution)/shard_map/ppermute | solution.py:271
  29.1 1.7 %collective-permute-start.16 = (bf16[32,1024]{1,0:T(8,128)(2,1)}, bf16[32,1024]{1,0:T(8,128)(2,1)S(1)}, u32[]{:S(2)}, u32[]{:S(2)}) collective-permute-start(bf16[32,1024]{1,0:T(8,128)(2,1)} %get-tuple-element.54), channel_id=1, source_target_pairs={{0,2},{2,0},{4,6},{6,4},{8,10},{10,8},{12,14},{14,12},{1,3},{3,1},... | collective-permute-start | bytes 196616 | tf_op jit(solution)/shard_map/ppermute | solution.py:271
  30.8 0.8 collective-permute-start.17
  31.6 3.4 %collective-permute-start.18 = (bf16[32,1024]{1,0:T(8,128)(2,1)}, bf16[32,1024]{1,0:T(8,128)(2,1)S(1)}, u32[]{:S(2)}, u32[]{:S(2)}) collective-permute-start(bf16[32,1024]{1,0:T(8,128)(2,1)} %get-tuple-element.56), channel_id=1, source_target_pairs={{0,4},{2,6},{4,0},{6,2},{8,12},{10,14},{12,8},{14,10},{1,5},{3,7},... | collective-permute-start | bytes 196616 | tf_op jit(solution)/shard_map/ppermute | solution.py:271
  35.0 1.2 %collective-permute-done.30.refs_7_.rest_34_ = bf16[32,1024]{1,0:T(8,128)(2,1)S(1)} collective-permute-done((bf16[32,1024]{1,0:T(8,128)(2,1)S(1)}, bf16[32,1024]{1,0:T(8,128)(2,1)S(1)}, u32[]{:S(2)}, u32[]{:S(2)}) %collective-permute-start.30) | collective-permute-done | bytes 65568 | tf_op jit(solution)/shard_map/ppermute | solution.py:271
  36.2 0.6 collective-permute-start.20
  36.8 3.5 %collective-permute-start.21 = (bf16[32,1024]{1,0:T(8,128)(2,1)}, bf16[32,1024]{1,0:T(8,128)(2,1)S(1)}, u32[]{:S(2)}, u32[]{:S(2)}) collective-permute-start(bf16[32,1024]{1,0:T(8,128)(2,1)} %get-tuple-element.59), channel_id=1, source_target_pairs={{0,12},{2,14},{4,8},{6,10},{8,4},{10,6},{12,0},{14,2},{1,13},{3,15... | collective-permute-start | bytes 196616 | tf_op jit(solution)/shard_map/ppermute | solution.py:271
  40.3 7.6 %shard_map.84 = (bf16[32,1024]{1,0:T(8,128)(2,1)}, bf16[32,1024]{1,0:T(8,128)(2,1)}, bf16[32,1024]{1,0:T(8,128)(2,1)}, bf16[32,1024]{1,0:T(8,128)(2,1)}, bf16[32...) custom-call(s32[1]{0:T(128)} %bitcast.me_ref, ...), custom_call_target="tpu_custom_call" | custom-call | flops 2415919104 | bytes 2097152 | tf_op jit(solution)/shard_map/pallas_call | solution.py:127
  48.3 1.5 %collective-permute-start.8 = (bf16[32,1024]{1,0:T(8,128)(2,1)}, bf16[32,1024]{1,0:T(8,128)(2,1)S(1)}, u32[]{:S(2)}, u32[]{:S(2)}) collective-permute-start(bf16[32,1024]{1,0:T(8,128)(2,1)} %get-tuple-element.46), channel_id=1, source_target_pairs={{0,2},{2,0},{4,6},{6,4},{8,10},{10,8},{12,14},{14,12},{1,3},{3,1},... | collective-permute-start | bytes 196616 | tf_op jit(solution)/shard_map/ppermute | solution.py:271
  50.2 3.7 %collective-permute-start.10 = (bf16[32,1024]{1,0:T(8,128)(2,1)}, bf16[32,1024]{1,0:T(8,128)(2,1)S(1)}, u32[]{:S(2)}, u32[]{:S(2)}) collective-permute-start(bf16[32,1024]{1,0:T(8,128)(2,1)} %get-tuple-element.48), channel_id=1, source_target_pairs={{0,4},{2,6},{4,0},{6,2},{8,12},{10,14},{12,8},{14,10},{1,5},{3,7},... | collective-permute-start | bytes 196616 | tf_op jit(solution)/shard_map/ppermute | solution.py:271
  54.0 7.6 %shard_map.82 = (bf16[32,1024]{1,0:T(8,128)(2,1)}, bf16[32,1024]{1,0:T(8,128)(2,1)}, bf16[32,1024]{1,0:T(8,128)(2,1)}, bf16[32,1024]{1,0:T(8,128)(2,1)}, bf16[32...) custom-call(s32[1]{0:T(128)} %bitcast.me_ref, ...), custom_call_target="tpu_custom_call" | custom-call | flops 2415919104 | bytes 2097152 | tf_op jit(solution)/shard_map/pallas_call | solution.py:127
  61.7 1.8 %collective-permute-start.12 = (bf16[32,1024]{1,0:T(8,128)(2,1)S(1)}, bf16[32,1024]{1,0:T(8,128)(2,1)S(1)}, u32[]{:S(2)}, u32[]{:S(2)}) collective-permute-start(bf16[32,1024]{1,0:T(8,128)(2,1)S(1)} %copy-done.35), channel_id=1, source_target_pairs={{0,6},{2,4},{4,2},{6,0},{8,14},{10,12},{12,10},{14,8},{1,7},{3,5},... | collective-permute-start | bytes 196616 | tf_op jit(solution)/shard_map/ppermute | solution.py:271
  63.5 3.6 %collective-permute-start.13 = (bf16[32,1024]{1,0:T(8,128)(2,1)S(1)}, bf16[32,1024]{1,0:T(8,128)(2,1)S(1)}, u32[]{:S(2)}, u32[]{:S(2)}) collective-permute-start(bf16[32,1024]{1,0:T(8,128)(2,1)S(1)} %copy-done.34), channel_id=1, source_target_pairs={{0,12},{2,14},{4,8},{6,10},{8,4},{10,6},{12,0},{14,2},{1,13},{3,15... | collective-permute-start | bytes 196616 | tf_op jit(solution)/shard_map/ppermute | solution.py:271
  67.4 1.6 %collective-permute-start = (bf16[32,1024]{1,0:T(8,128)(2,1)}, bf16[32,1024]{1,0:T(8,128)(2,1)S(1)}, u32[]{:S(2)}, u32[]{:S(2)}) collective-permute-start(bf16[32,1024]{1,0:T(8,128)(2,1)} %get-tuple-element.38), channel_id=1, source_target_pairs={{0,2},{2,0},{4,6},{6,4},{8,10},{10,8},{12,14},{14,12},{1,3},{3,1},... | collective-permute-start | bytes 196616 | tf_op jit(solution)/shard_map/ppermute | solution.py:271
  69.2 3.8 %collective-permute-start.2 = (bf16[32,1024]{1,0:T(8,128)(2,1)}, bf16[32,1024]{1,0:T(8,128)(2,1)S(1)}, u32[]{:S(2)}, u32[]{:S(2)}) collective-permute-start(bf16[32,1024]{1,0:T(8,128)(2,1)} %get-tuple-element.40), channel_id=1, source_target_pairs={{0,4},{2,6},{4,0},{6,2},{8,12},{10,14},{12,8},{14,10},{1,5},{3,7},... | collective-permute-start | bytes 196616 | tf_op jit(solution)/shard_map/ppermute | solution.py:271
  73.0 1.1 %collective-permute-done.14.refs_7_.rest_16_ = bf16[32,1024]{1,0:T(8,128)(2,1)S(1)} collective-permute-done((bf16[32,1024]{1,0:T(8,128)(2,1)S(1)}, bf16[32,1024]{1,0:T(8,128)(2,1)S(1)}, u32[]{:S(2)}, u32[]{:S(2)}) %collective-permute-start.14) | collective-permute-done | bytes 65568 | tf_op jit(solution)/shard_map/ppermute | solution.py:271
  74.1 1.2 %collective-permute-start.4 = (bf16[32,1024]{1,0:T(8,128)(2,1)}, bf16[32,1024]{1,0:T(8,128)(2,1)S(1)}, u32[]{:S(2)}, u32[]{:S(2)}) collective-permute-start(bf16[32,1024]{1,0:T(8,128)(2,1)} %get-tuple-element.42), channel_id=1, source_target_pairs={{0,6},{2,4},{4,2},{6,0},{8,14},{10,12},{12,10},{14,8},{1,7},{3,5},... | collective-permute-start | bytes 196616 | tf_op jit(solution)/shard_map/ppermute | solution.py:271
  75.3 3.3 %collective-permute-start.5 = (bf16[32,1024]{1,0:T(8,128)(2,1)}, bf16[32,1024]{1,0:T(8,128)(2,1)S(1)}, u32[]{:S(2)}, u32[]{:S(2)}) collective-permute-start(bf16[32,1024]{1,0:T(8,128)(2,1)} %get-tuple-element.43), channel_id=1, source_target_pairs={{0,12},{2,14},{4,8},{6,10},{8,4},{10,6},{12,0},{14,2},{1,13},{3,15... | collective-permute-start | bytes 196616 | tf_op jit(solution)/shard_map/ppermute | solution.py:271
  79.0 1.6 %shard_map.89 = bf16[128,1024]{1,0:T(8,128)(2,1)} custom-call(bf16[32,1024]{1,0:T(8,128)(2,1)} %get-tuple-element.61.refs_0_.rest_27_, bf16[32,1024]{1,0:T(8,128)(2,1)} %copy-done, bf16[32,1024]{1,0:T(8,128)(2,1)} %copy-done.1, bf16[32,1024]{1,0:T(8,128)(2,1)} %copy-done.2, bf16[32,1024]{1,0:T(8,128)(2,1)} %copy-done.3, bf16[32,1024]{1,0:T(8,128)(2,1)} %copy-done.4, ...), custom_call_target="tpu_custom_call" | custom-call | tf_op jit(solution)/shard_map/pallas_call | solution.py:175
  80.7 1.6 %shard_map.87 = bf16[128,1024]{1,0:T(8,128)(2,1)} custom-call(bf16[32,1024]{1,0:T(8,128)(2,1)} %get-tuple-element.53.refs_0_.rest_18_, bf16[32,1024]{1,0:T(8,128)(2,1)} %copy-done.7, bf16[32,1024]{1,0:T(8,128)(2,1)} %copy-done.8, bf16[32,1024]{1,0:T(8,128)(2,1)} %copy-done.9, bf16[32,1024]{1,0:T(8,128)(2,1)} %copy-done.10, bf16[32,1024]{1,0:T(8,128)(2,1)} %copy-done.11, ...), custom_call_target="tpu_custom_call" | custom-call | tf_op jit(solution)/shard_map/pallas_call | solution.py:175
  82.4 1.6 %shard_map.85 = bf16[128,1024]{1,0:T(8,128)(2,1)} custom-call(bf16[32,1024]{1,0:T(8,128)(2,1)} %get-tuple-element.45.refs_0_.rest_9_, bf16[32,1024]{1,0:T(8,128)(2,1)} %copy-done.14, bf16[32,1024]{1,0:T(8,128)(2,1)} %copy-done.15, bf16[32,1024]{1,0:T(8,128)(2,1)} %copy-done.16, bf16[32,1024]{1,0:T(8,128)(2,1)} %copy-done.17, bf16[32,1024]{1,0:T(8,128)(2,1)} %copy-done.18, ...), custom_call_target="tpu_custom_call" | custom-call | tf_op jit(solution)/shard_map/pallas_call | solution.py:175
  84.8 1.0 %collective-permute-done.6.refs_7_.rest_7_ = bf16[32,1024]{1,0:T(8,128)(2,1)S(1)} collective-permute-done((bf16[32,1024]{1,0:T(8,128)(2,1)}, bf16[32,1024]{1,0:T(8,128)(2,1)S(1)}, u32[]{:S(2)}, u32[]{:S(2)}) %collective-permute-start.6) | collective-permute-done | bytes 65568 | tf_op jit(solution)/shard_map/ppermute | solution.py:271
  86.4 1.6 %shard_map.83 = bf16[128,1024]{1,0:T(8,128)(2,1)} custom-call(bf16[32,1024]{1,0:T(8,128)(2,1)} %get-tuple-element.37.refs_0_.rest_0_, bf16[32,1024]{1,0:T(8,128)(2,1)} %copy-done.21, bf16[32,1024]{1,0:T(8,128)(2,1)} %copy-done.22, bf16[32,1024]{1,0:T(8,128)(2,1)} %copy-done.23, bf16[32,1024]{1,0:T(8,128)(2,1)} %copy-done.24, bf16[32,1024]{1,0:T(8,128)(2,1)} %copy-done.25, ...), custom_call_target="tpu_custom_call" | custom-call | tf_op jit(solution)/shard_map/pallas_call | solution.py:175
  88.2 1.7 %collective-permute-done.7.rest_8_ = bf16[128,1024]{1,0:T(8,128)(2,1)S(1)} collective-permute-done((bf16[128,1024]{1,0:T(8,128)(2,1)}, bf16[128,1024]{1,0:T(8,128)(2,1)S(1)}, u32[]{:S(2)}, u32[]{:S(2)}) %collective-permute-start.7) | collective-permute-done | bytes 262176 | tf_op jit(solution)/shard_map/ppermute | solution.py:272
  89.9 0.7 copy-done.31
  90.5 3.4 %shard_map.90 = bf16[1,8,16,8192]{3,2,1,0:T(8,128)(2,1)} custom-call(s32[1]{0:T(128)} %bitcast.me_ref, bf16[32,1024]{1,0:T(8,128)(2,1)} %get-tuple-element.37.refs_0_.rest_0_, bf16[32,1024]{1,0:T(8,128)(2,1)} %copy-done.21, bf16[32,1024]{1,0:T(8,128)(2,1)} %copy-done.22, bf16[32,1024]{1,0:T(8,128)(2,1)} %copy-done.23, bf16[32,1024]{1,0:T(8,128)(2,1)} %copy-done.24, ...), custom_call_target="tpu_custom_call" | custom-call | tf_op jit(solution)/shard_map/pallas_call | solution.py:207
  (117 shorter events, 3.6 us)
Async XLA Ops:
  8.9 16.5 %collective-permute-start.24 = (bf16[32,1024]{1,0:T(8,128)(2,1)}, bf16[32,1024]{1,0:T(8,128)(2,1)S(1)}, u32[]{:S(2)}, u32[]{:S(2)}) collective-permute-start(bf16[32,1024]{1,0:T(8,128)(2,1)} %get-tuple-element.62), channel_id=1, source_target_pairs={{0,2},{2,0},{4,6},{6,4},{8,10},{10,8},{12,14},{14,12},{1,3},{3,1},... | collective-permute-start | bytes 196616 | tf_op jit(solution)/shard_map/ppermute | solution.py:271
  11.9 17.1 %collective-permute-start.25 = (bf16[32,1024]{1,0:T(8,128)(2,1)}, bf16[32,1024]{1,0:T(8,128)(2,1)S(1)}, u32[]{:S(2)}, u32[]{:S(2)}) collective-permute-start(bf16[32,1024]{1,0:T(8,128)(2,1)} %get-tuple-element.63), channel_id=1, source_target_pairs={{0,8},{2,10},{4,12},{6,14},{8,0},{10,2},{12,4},{14,6},{1,9},{3,11}... | collective-permute-start | bytes 196616 | tf_op jit(solution)/shard_map/ppermute | solution.py:271
  14.5 14.6 %collective-permute-start.26 = (bf16[32,1024]{1,0:T(8,128)(2,1)}, bf16[32,1024]{1,0:T(8,128)(2,1)S(1)}, u32[]{:S(2)}, u32[]{:S(2)}) collective-permute-start(bf16[32,1024]{1,0:T(8,128)(2,1)} %get-tuple-element.64), channel_id=1, source_target_pairs={{0,4},{2,6},{4,0},{6,2},{8,12},{10,14},{12,8},{14,10},{1,5},{3,7},... | collective-permute-start | bytes 196616 | tf_op jit(solution)/shard_map/ppermute | solution.py:271
  16.1 14.7 %collective-permute-start.27 = (bf16[32,1024]{1,0:T(8,128)(2,1)}, bf16[32,1024]{1,0:T(8,128)(2,1)S(1)}, u32[]{:S(2)}, u32[]{:S(2)}) collective-permute-start(bf16[32,1024]{1,0:T(8,128)(2,1)} %get-tuple-element.65), channel_id=1, source_target_pairs={{0,10},{2,8},{4,14},{6,12},{8,2},{10,0},{12,6},{14,4},{1,11},{3,9}... | collective-permute-start | bytes 196616 | tf_op jit(solution)/shard_map/ppermute | solution.py:271
  16.4 15.2 %collective-permute-start.28 = (bf16[32,1024]{1,0:T(8,128)(2,1)}, bf16[32,1024]{1,0:T(8,128)(2,1)S(1)}, u32[]{:S(2)}, u32[]{:S(2)}) collective-permute-start(bf16[32,1024]{1,0:T(8,128)(2,1)} %get-tuple-element.66), channel_id=1, source_target_pairs={{0,6},{2,4},{4,2},{6,0},{8,14},{10,12},{12,10},{14,8},{1,7},{3,5},... | collective-permute-start | bytes 196616 | tf_op jit(solution)/shard_map/ppermute | solution.py:271
  25.4 9.6 %collective-permute-start.29 = (bf16[32,1024]{1,0:T(8,128)(2,1)S(1)}, bf16[32,1024]{1,0:T(8,128)(2,1)S(1)}, u32[]{:S(2)}, u32[]{:S(2)}) collective-permute-start(bf16[32,1024]{1,0:T(8,128)(2,1)S(1)} %copy-done.37), channel_id=1, source_target_pairs={{0,12},{2,14},{4,8},{6,10},{8,4},{10,6},{12,0},{14,2},{1,13},{3,15... | collective-permute-start | bytes 196616 | tf_op jit(solution)/shard_map/ppermute | solution.py:271
  29.0 7.1 %collective-permute-start.30 = (bf16[32,1024]{1,0:T(8,128)(2,1)S(1)}, bf16[32,1024]{1,0:T(8,128)(2,1)S(1)}, u32[]{:S(2)}, u32[]{:S(2)}) collective-permute-start(bf16[32,1024]{1,0:T(8,128)(2,1)S(1)} %copy-done.36), channel_id=1, source_target_pairs={{0,14},{2,12},{4,10},{6,8},{8,6},{10,4},{12,2},{14,0},{1,15},{3,13... | collective-permute-start | bytes 196616 | tf_op jit(solution)/shard_map/ppermute | solution.py:271
  29.1 7.6 %collective-permute-start.16 = (bf16[32,1024]{1,0:T(8,128)(2,1)}, bf16[32,1024]{1,0:T(8,128)(2,1)S(1)}, u32[]{:S(2)}, u32[]{:S(2)}) collective-permute-start(bf16[32,1024]{1,0:T(8,128)(2,1)} %get-tuple-element.54), channel_id=1, source_target_pairs={{0,2},{2,0},{4,6},{6,4},{8,10},{10,8},{12,14},{14,12},{1,3},{3,1},... | collective-permute-start | bytes 196616 | tf_op jit(solution)/shard_map/ppermute | solution.py:271
  30.8 17.1 %collective-permute-start.17 = (bf16[32,1024]{1,0:T(8,128)(2,1)}, bf16[32,1024]{1,0:T(8,128)(2,1)S(1)}, u32[]{:S(2)}, u32[]{:S(2)}) collective-permute-start(bf16[32,1024]{1,0:T(8,128)(2,1)} %get-tuple-element.55), channel_id=1, source_target_pairs={{0,8},{2,10},{4,12},{6,14},{8,0},{10,2},{12,4},{14,6},{1,9},{3,11}... | collective-permute-start | bytes 196616 | tf_op jit(solution)/shard_map/ppermute | solution.py:271
  31.6 16.7 %collective-permute-start.18 = (bf16[32,1024]{1,0:T(8,128)(2,1)}, bf16[32,1024]{1,0:T(8,128)(2,1)S(1)}, u32[]{:S(2)}, u32[]{:S(2)}) collective-permute-start(bf16[32,1024]{1,0:T(8,128)(2,1)} %get-tuple-element.56), channel_id=1, source_target_pairs={{0,4},{2,6},{4,0},{6,2},{8,12},{10,14},{12,8},{14,10},{1,5},{3,7},... | collective-permute-start | bytes 196616 | tf_op jit(solution)/shard_map/ppermute | solution.py:271
  35.0 14.8 %collective-permute-start.19 = (bf16[32,1024]{1,0:T(8,128)(2,1)}, bf16[32,1024]{1,0:T(8,128)(2,1)S(1)}, u32[]{:S(2)}, u32[]{:S(2)}) collective-permute-start(bf16[32,1024]{1,0:T(8,128)(2,1)} %get-tuple-element.57), channel_id=1, source_target_pairs={{0,10},{2,8},{4,14},{6,12},{8,2},{10,0},{12,6},{14,4},{1,11},{3,9}... | collective-permute-start | bytes 196616 | tf_op jit(solution)/shard_map/ppermute | solution.py:271
  36.2 14.0 %collective-permute-start.20 = (bf16[32,1024]{1,0:T(8,128)(2,1)}, bf16[32,1024]{1,0:T(8,128)(2,1)S(1)}, u32[]{:S(2)}, u32[]{:S(2)}) collective-permute-start(bf16[32,1024]{1,0:T(8,128)(2,1)} %get-tuple-element.58), channel_id=1, source_target_pairs={{0,6},{2,4},{4,2},{6,0},{8,14},{10,12},{12,10},{14,8},{1,7},{3,5},... | collective-permute-start | bytes 196616 | tf_op jit(solution)/shard_map/ppermute | solution.py:271
  36.8 17.1 %collective-permute-start.21 = (bf16[32,1024]{1,0:T(8,128)(2,1)}, bf16[32,1024]{1,0:T(8,128)(2,1)S(1)}, u32[]{:S(2)}, u32[]{:S(2)}) collective-permute-start(bf16[32,1024]{1,0:T(8,128)(2,1)} %get-tuple-element.59), channel_id=1, source_target_pairs={{0,12},{2,14},{4,8},{6,10},{8,4},{10,6},{12,0},{14,2},{1,13},{3,15... | collective-permute-start | bytes 196616 | tf_op jit(solution)/shard_map/ppermute | solution.py:271
  48.0 13.7 %collective-permute-start.22 = (bf16[32,1024]{1,0:T(8,128)(2,1)S(1)}, bf16[32,1024]{1,0:T(8,128)(2,1)S(1)}, u32[]{:S(2)}, u32[]{:S(2)}) collective-permute-start(bf16[32,1024]{1,0:T(8,128)(2,1)S(1)} %copy-done.32), channel_id=1, source_target_pairs={{0,14},{2,12},{4,10},{6,8},{8,6},{10,4},{12,2},{14,0},{1,15},{3,13... | collective-permute-start | bytes 196616 | tf_op jit(solution)/shard_map/ppermute | solution.py:271
  48.3 15.2 %collective-permute-start.8 = (bf16[32,1024]{1,0:T(8,128)(2,1)}, bf16[32,1024]{1,0:T(8,128)(2,1)S(1)}, u32[]{:S(2)}, u32[]{:S(2)}) collective-permute-start(bf16[32,1024]{1,0:T(8,128)(2,1)} %get-tuple-element.46), channel_id=1, source_target_pairs={{0,2},{2,0},{4,6},{6,4},{8,10},{10,8},{12,14},{14,12},{1,3},{3,1},... | collective-permute-start | bytes 196616 | tf_op jit(solution)/shard_map/ppermute | solution.py:271
  49.8 17.2 %collective-permute-start.9 = (bf16[32,1024]{1,0:T(8,128)(2,1)}, bf16[32,1024]{1,0:T(8,128)(2,1)S(1)}, u32[]{:S(2)}, u32[]{:S(2)}) collective-permute-start(bf16[32,1024]{1,0:T(8,128)(2,1)} %get-tuple-element.47), channel_id=1, source_target_pairs={{0,8},{2,10},{4,12},{6,14},{8,0},{10,2},{12,4},{14,6},{1,9},{3,11}... | collective-permute-start | bytes 196616 | tf_op jit(solution)/shard_map/ppermute | solution.py:271
  50.2 17.2 %collective-permute-start.10 = (bf16[32,1024]{1,0:T(8,128)(2,1)}, bf16[32,1024]{1,0:T(8,128)(2,1)S(1)}, u32[]{:S(2)}, u32[]{:S(2)}) collective-permute-start(bf16[32,1024]{1,0:T(8,128)(2,1)} %get-tuple-element.48), channel_id=1, source_target_pairs={{0,4},{2,6},{4,0},{6,2},{8,12},{10,14},{12,8},{14,10},{1,5},{3,7},... | collective-permute-start | bytes 196616 | tf_op jit(solution)/shard_map/ppermute | solution.py:271
  53.9 15.0 %collective-permute-start.11 = (bf16[32,1024]{1,0:T(8,128)(2,1)}, bf16[32,1024]{1,0:T(8,128)(2,1)S(1)}, u32[]{:S(2)}, u32[]{:S(2)}) collective-permute-start(bf16[32,1024]{1,0:T(8,128)(2,1)} %get-tuple-element.49), channel_id=1, source_target_pairs={{0,10},{2,8},{4,14},{6,12},{8,2},{10,0},{12,6},{14,4},{1,11},{3,9}... | collective-permute-start | bytes 196616 | tf_op jit(solution)/shard_map/ppermute | solution.py:271
  61.7 7.5 %collective-permute-start.12 = (bf16[32,1024]{1,0:T(8,128)(2,1)S(1)}, bf16[32,1024]{1,0:T(8,128)(2,1)S(1)}, u32[]{:S(2)}, u32[]{:S(2)}) collective-permute-start(bf16[32,1024]{1,0:T(8,128)(2,1)S(1)} %copy-done.35), channel_id=1, source_target_pairs={{0,6},{2,4},{4,2},{6,0},{8,14},{10,12},{12,10},{14,8},{1,7},{3,5},... | collective-permute-start | bytes 196616 | tf_op jit(solution)/shard_map/ppermute | solution.py:271
  63.5 9.5 %collective-permute-start.13 = (bf16[32,1024]{1,0:T(8,128)(2,1)S(1)}, bf16[32,1024]{1,0:T(8,128)(2,1)S(1)}, u32[]{:S(2)}, u32[]{:S(2)}) collective-permute-start(bf16[32,1024]{1,0:T(8,128)(2,1)S(1)} %copy-done.34), channel_id=1, source_target_pairs={{0,12},{2,14},{4,8},{6,10},{8,4},{10,6},{12,0},{14,2},{1,13},{3,15... | collective-permute-start | bytes 196616 | tf_op jit(solution)/shard_map/ppermute | solution.py:271
  67.1 7.0 %collective-permute-start.14 = (bf16[32,1024]{1,0:T(8,128)(2,1)S(1)}, bf16[32,1024]{1,0:T(8,128)(2,1)S(1)}, u32[]{:S(2)}, u32[]{:S(2)}) collective-permute-start(bf16[32,1024]{1,0:T(8,128)(2,1)S(1)} %copy-done.33), channel_id=1, source_target_pairs={{0,14},{2,12},{4,10},{6,8},{8,6},{10,4},{12,2},{14,0},{1,15},{3,13... | collective-permute-start | bytes 196616 | tf_op jit(solution)/shard_map/ppermute | solution.py:271
  67.4 7.9 %collective-permute-start = (bf16[32,1024]{1,0:T(8,128)(2,1)}, bf16[32,1024]{1,0:T(8,128)(2,1)S(1)}, u32[]{:S(2)}, u32[]{:S(2)}) collective-permute-start(bf16[32,1024]{1,0:T(8,128)(2,1)} %get-tuple-element.38), channel_id=1, source_target_pairs={{0,2},{2,0},{4,6},{6,4},{8,10},{10,8},{12,14},{14,12},{1,3},{3,1},... | collective-permute-start | bytes 196616 | tf_op jit(solution)/shard_map/ppermute | solution.py:271
  68.9 9.7 %collective-permute-start.1 = (bf16[32,1024]{1,0:T(8,128)(2,1)}, bf16[32,1024]{1,0:T(8,128)(2,1)S(1)}, u32[]{:S(2)}, u32[]{:S(2)}) collective-permute-start(bf16[32,1024]{1,0:T(8,128)(2,1)} %get-tuple-element.39), channel_id=1, source_target_pairs={{0,8},{2,10},{4,12},{6,14},{8,0},{10,2},{12,4},{14,6},{1,9},{3,11}... | collective-permute-start | bytes 196616 | tf_op jit(solution)/shard_map/ppermute | solution.py:271
  69.2 14.9 %collective-permute-start.2 = (bf16[32,1024]{1,0:T(8,128)(2,1)}, bf16[32,1024]{1,0:T(8,128)(2,1)S(1)}, u32[]{:S(2)}, u32[]{:S(2)}) collective-permute-start(bf16[32,1024]{1,0:T(8,128)(2,1)} %get-tuple-element.40), channel_id=1, source_target_pairs={{0,4},{2,6},{4,0},{6,2},{8,12},{10,14},{12,8},{14,10},{1,5},{3,7},... | collective-permute-start | bytes 196616 | tf_op jit(solution)/shard_map/ppermute | solution.py:271
  73.0 11.1 %collective-permute-start.3 = (bf16[32,1024]{1,0:T(8,128)(2,1)}, bf16[32,1024]{1,0:T(8,128)(2,1)S(1)}, u32[]{:S(2)}, u32[]{:S(2)}) collective-permute-start(bf16[32,1024]{1,0:T(8,128)(2,1)} %get-tuple-element.41), channel_id=1, source_target_pairs={{0,10},{2,8},{4,14},{6,12},{8,2},{10,0},{12,6},{14,4},{1,11},{3,9}... | collective-permute-start | bytes 196616 | tf_op jit(solution)/shard_map/ppermute | solution.py:271
  74.1 10.5 %collective-permute-start.4 = (bf16[32,1024]{1,0:T(8,128)(2,1)}, bf16[32,1024]{1,0:T(8,128)(2,1)S(1)}, u32[]{:S(2)}, u32[]{:S(2)}) collective-permute-start(bf16[32,1024]{1,0:T(8,128)(2,1)} %get-tuple-element.42), channel_id=1, source_target_pairs={{0,6},{2,4},{4,2},{6,0},{8,14},{10,12},{12,10},{14,8},{1,7},{3,5},... | collective-permute-start | bytes 196616 | tf_op jit(solution)/shard_map/ppermute | solution.py:271
  75.3 9.5 %collective-permute-start.5 = (bf16[32,1024]{1,0:T(8,128)(2,1)}, bf16[32,1024]{1,0:T(8,128)(2,1)S(1)}, u32[]{:S(2)}, u32[]{:S(2)}) collective-permute-start(bf16[32,1024]{1,0:T(8,128)(2,1)} %get-tuple-element.43), channel_id=1, source_target_pairs={{0,12},{2,14},{4,8},{6,10},{8,4},{10,6},{12,0},{14,2},{1,13},{3,15... | collective-permute-start | bytes 196616 | tf_op jit(solution)/shard_map/ppermute | solution.py:271
  78.6 7.2 %collective-permute-start.6 = (bf16[32,1024]{1,0:T(8,128)(2,1)}, bf16[32,1024]{1,0:T(8,128)(2,1)S(1)}, u32[]{:S(2)}, u32[]{:S(2)}) collective-permute-start(bf16[32,1024]{1,0:T(8,128)(2,1)} %get-tuple-element.44), channel_id=1, source_target_pairs={{0,14},{2,12},{4,10},{6,8},{8,6},{10,4},{12,2},{14,0},{1,15},{3,13... | collective-permute-start | bytes 196616 | tf_op jit(solution)/shard_map/ppermute | solution.py:271
  84.1 4.0 %collective-permute-start.31 = (bf16[128,1024]{1,0:T(8,128)(2,1)}, bf16[128,1024]{1,0:T(8,128)(2,1)S(1)}, u32[]{:S(2)}, u32[]{:S(2)}) collective-permute-start(bf16[128,1024]{1,0:T(8,128)(2,1)} %shard_map.89), channel_id=1, source_target_pairs={{0,1},{1,0},{2,3},{3,2},{4,5},{5,4},{6,7},{7,6},{8,9},{9,8},{10,11... | collective-permute-start | bytes 786440 | tf_op jit(solution)/shard_map/ppermute | solution.py:272
  84.2 4.0 %collective-permute-start.23 = (bf16[128,1024]{1,0:T(8,128)(2,1)}, bf16[128,1024]{1,0:T(8,128)(2,1)S(1)}, u32[]{:S(2)}, u32[]{:S(2)}) collective-permute-start(bf16[128,1024]{1,0:T(8,128)(2,1)} %shard_map.87), channel_id=1, source_target_pairs={{0,1},{1,0},{2,3},{3,2},{4,5},{5,4},{6,7},{7,6},{8,9},{9,8},{10,11... | collective-permute-start | bytes 786440 | tf_op jit(solution)/shard_map/ppermute | solution.py:272
  84.7 3.5 %collective-permute-start.15 = (bf16[128,1024]{1,0:T(8,128)(2,1)}, bf16[128,1024]{1,0:T(8,128)(2,1)S(1)}, u32[]{:S(2)}, u32[]{:S(2)}) collective-permute-start(bf16[128,1024]{1,0:T(8,128)(2,1)} %shard_map.85), channel_id=1, source_target_pairs={{0,1},{1,0},{2,3},{3,2},{4,5},{5,4},{6,7},{7,6},{8,9},{9,8},{10,11... | collective-permute-start | bytes 786440 | tf_op jit(solution)/shard_map/ppermute | solution.py:272
  88.0 1.8 %collective-permute-start.7 = (bf16[128,1024]{1,0:T(8,128)(2,1)}, bf16[128,1024]{1,0:T(8,128)(2,1)S(1)}, u32[]{:S(2)}, u32[]{:S(2)}) collective-permute-start(bf16[128,1024]{1,0:T(8,128)(2,1)} %shard_map.83), channel_id=1, source_target_pairs={{0,1},{1,0},{2,3},{3,2},{4,5},{5,4},{6,7},{7,6},{8,9},{9,8},{10,11... | collective-permute-start | bytes 786440 | tf_op jit(solution)/shard_map/ppermute | solution.py:272
  (38 other events, 392.8 us)

commit v4 on v3

--- a/solution.py
+++ b/solution.py
@@ -10,8 +10,9 @@
 
 SPAN = 64
 GROUP = 4
-CHUNKS = (1, 1, 1, 1)
+CHUNKS = (1, 1)
 DIRECT = 16
+VMEM = 58 * 1024 * 1024
 MASKED = -1e30
 OPEN = 3e38
 NT = (((1,), (1,)), ((), ()))
@@ -71,6 +72,7 @@
     ]
     for copy in copies:
         copy.start()
+    for_queries, for_keys, for_values = copies[:2], copies[2:4], copies[4:]
     count, size = count_ref[0], size_ref[0]
     lane = lax.broadcasted_iota(jnp.int32, (slots, past), 1)
     cap_ref[:, :past] = jnp.where(lane < size, jnp.float32(OPEN), jnp.float32(MASKED))
@@ -80,21 +82,24 @@
         (col <= row) & (col < count * SPAN), jnp.float32(OPEN), jnp.float32(MASKED)
     )
     build_table(me_ref[0], count, routes_ref, table_ref, capacity)
-    for copy in copies:
+
+    scale = math.log2(math.e) / math.sqrt(dim)
+    stacks = heads // GROUP
+    for copy in for_queries:
         copy.wait()
-
-    scale = math.log2(math.e) / math.sqrt(dim)
+    lifted = []
+    for h in range(heads):
+        one = dot(queries_ref[:, h * dim : (h + 1) * dim], key_weight_ref[h])
+        lifted.append(one.astype(jnp.bfloat16))
+    for copy in for_keys:
+        copy.wait()
     keys = keys_ref[...]
-    stacks = heads // GROUP
     scores = []
     for stack in range(stacks):
-        lifted = []
-        for h in range(stack * GROUP, (stack + 1) * GROUP):
-            one = dot(queries_ref[:, h * dim : (h + 1) * dim], key_weight_ref[h])
-            lifted.append(one.astype(jnp.bfloat16))
-        lifted = jnp.concatenate(lifted, axis=0)
-        score = lax.dot_general(lifted, keys, NT, preferred_element_type=jnp.float32)
-        scores.append(score)
+        rows = jnp.concatenate(lifted[stack * GROUP : (stack + 1) * GROUP], axis=0)
+        scores.append(lax.dot_general(rows, keys, NT, preferred_element_type=jnp.float32))
+    for copy in for_values:
+        copy.wait()
     for stack in range(stacks):
         score = scores[stack].reshape(GROUP, slots, keys.shape[0])
         score = jnp.minimum(score, cap_ref[...][None])
@@ -139,7 +144,7 @@
             pltpu.VMEM((slots, heads * dim), jnp.bfloat16),
             pltpu.SemaphoreType.DMA((5,)),
         ],
-        compiler_params=pltpu.CompilerParams(vmem_limit_bytes=54 * 1024 * 1024),
+        compiler_params=pltpu.CompilerParams(vmem_limit_bytes=VMEM),
         cost_estimate=pl.CostEstimate(
             flops=4 * slots * heads * keys * latent,
             bytes_accessed=4 * heads * dim * latent,
@@ -155,30 +160,42 @@
         copy.wait()
 
 
-def pass_on_kernel(cores, *refs):
+def exchange(piece, axis, size, bits):
+    pairs = [[i, i ^ bits] for i in range(size) if i < i ^ bits]
+    return lax.all_gather(piece, axis, axis_index_groups=pairs)
+
+
+def partner(ref, me, bits):
+    return ref.at[((me ^ bits) > me).astype(jnp.int32)] if bits else ref
+
+
+def pass_on_kernel(cores, order, me_ref, *refs):
     *piece_refs, out_ref, sem = refs
     capacity = piece_refs[0].shape[0] // cores
-    run_copies(
-        [
+    copies = []
+    for i, (piece_ref, j) in enumerate(zip(piece_refs, order)):
+        piece_ref = partner(piece_ref, me_ref[0], j * cores)
+        copies.append(
             pltpu.make_async_copy(
                 piece_ref.at[pl.ds(capacity, capacity)],
-                out_ref.at[pl.ds(j * capacity, capacity)],
-                sem.at[j],
+                out_ref.at[pl.ds(i * capacity, capacity)],
+                sem.at[i],
             )
-            for j, piece_ref in enumerate(piece_refs)
-        ]
-    )
-
-
-def pass_on(pieces, cores):
+        )
+    run_copies(copies)
+
+
+def pass_on(me, pieces, order, cores):
     rows, width = pieces[0].shape
     return pl.pallas_call(
-        functools.partial(pass_on_kernel, cores),
-        in_specs=[pl.BlockSpec(memory_space=pl.ANY)] * len(pieces),
+        functools.partial(pass_on_kernel, cores, order),
+        in_specs=[pl.BlockSpec(memory_space=pltpu.SMEM)]
+        + [pl.BlockSpec(memory_space=pl.ANY)] * len(pieces),
         out_specs=pl.BlockSpec(memory_space=pltpu.VMEM),
         out_shape=jax.ShapeDtypeStruct((len(pieces) * rows // cores, width), jnp.bfloat16),
         scratch_shapes=[pltpu.SemaphoreType.DMA((len(pieces),))],
-    )(*pieces)
+        compiler_params=pltpu.CompilerParams(vmem_limit_bytes=VMEM),
+    )(me, *pieces)
 
 
 def place_kernel(plan, cores, me_ref, *rest):
@@ -187,9 +204,9 @@
     features //= cores
     me = me_ref[0]
     copies = []
-    for i, (ref, (first, start, source)) in enumerate(plan):
-        ref = refs[ref]
-        width = ref.shape[1]
+    for i, (ref, (first, start, source, bits)) in enumerate(plan):
+        ref = partner(refs[ref], me, bits)
+        width = ref.shape[-1]
         who = me ^ source
         left = pl.multiple_of(who % cores * features + first, math.gcd(features, first))
         copies.append(
@@ -214,6 +231,7 @@
             pltpu.VMEM(shape[1:], jnp.bfloat16),
             pltpu.SemaphoreType.DMA((len(plan),)),
         ],
+        compiler_params=pltpu.CompilerParams(vmem_limit_bytes=VMEM),
     )(me, *arrays)
 
 
@@ -267,14 +285,11 @@
             order = exchange_order(ranks)
             pieces = [outgoing[0]]
             for j in order:
-                pairs = [(i, i ^ j) for i in range(ranks)]
-                pieces.append(lax.ppermute(outgoing[j], "dp", pairs))
-            swapped = lax.ppermute(
-                pass_on(pieces, cores), "ep", [(i, i ^ 1) for i in range(cores)]
-            )
+                pieces.append(exchange(outgoing[j], "dp", ranks, j))
+            swapped = exchange(pass_on(me, pieces, [0] + order, cores), "ep", cores, 1)
             for at, j in enumerate([0] + order):
-                plan.append((len(chunks) + at, (first * dim, 0, j * cores)))
-                plan.append((len(chunks) + ranks, (first * dim, at * capacity, j * cores + 1)))
+                plan.append((len(chunks) + at, (first * dim, 0, j * cores, j * cores)))
+                plan.append((len(chunks) + ranks, (first * dim, at * capacity, j * cores + 1, 1)))
             chunks += pieces + [swapped]
         else:
             arrived = lax.all_to_all(

time: 94.8 us -> 172 us (1.81)
  blocking collectives: 0 us -> 116 us
  starting transfers between devices: 45.5 us -> 0.22 us
  between operations: 1.97 us -> 14.8 us
  Pallas kernels: 40.2 us -> 32 us
  waiting for transfers between devices: 4.98 us -> 8.27 us
    all_gather x0 -> x14, blocking collectives: none -> 116 us  [exchange(): return lax.all_gather(piece, axis, axis_index_groups=pairs)]
    ppermute x32 -> x0, starting transfers between devices: 45.5 us -> none  [the longest x28 44.8 us: local(): pieces.append(lax.ppermute(outgoing[j], 'dp', pairs))]
    all_gather x0 -> x2, waiting for transfers between devices: none -> 8.24 us  [exchange(): return lax.all_gather(piece, axis, axis_index_groups=pairs)]
    pallas_call x4 -> x2, Pallas kernels: 30.3 us -> 25 us  [attend(): pl.pallas_call(functools.partial(attend_kernel, places // experts, first)...]
    ppermute x32 -> x0, waiting for transfers between devices: 4.98 us -> none  [the longest x28 3.3 us: local(): pieces.append(lax.ppermute(outgoing[j], 'dp', pairs))]
    pallas_call x4 -> x2, Pallas kernels: 6.56 us -> 3.85 us  [pass_on(): pl.pallas_call(functools.partial(pass_on_kernel, cores, order), in_specs=...]
  transfers between devices with their start and end apart: 32 -> 2, of which waited for: 4 -> 1; matrix products, arithmetic and copies ran while one was open for 0% -> 0% of each run, Pallas kernels for 31% -> 8%
where the time goes in v4:
time: 172 us
  blocking collectives  116 us (67%)
  Pallas kernels  32 us (19%)
  between operations  14.8 us (9%)
  waiting for transfers between devices  8.27 us (5%)
    all_gather x14, blocking collectives, exchange(): return lax.all_gather(piece, axis, axis_index_groups=pairs)  116 us
    pallas_call x2, Pallas kernels, attend(): pl.pallas_call(functools.partial(attend_kernel, places // experts, first)...  25 us
    all_gather x2, waiting for transfers between devices, exchange(): return lax.all_gather(piece, axis, axis_index_groups=pairs)  8.24 us
    pallas_call x2, Pallas kernels, pass_on(): pl.pallas_call(functools.partial(pass_on_kernel, cores, order), in_specs=...  3.85 us
  transfers between devices with their start and end apart: 2, of which 1 were waited for; matrix products, arithmetic and copies ran while one was open for 0% of the time, Pallas kernels for 8%

profile of v4, /device:TPU:0, one launch (start us, length us, event | category | flops | bytes accessed | tf_op | source)
XLA Modules:
  0.0 171.5 jit_solution(4145789095546019438)
XLA Ops:
  6.5 0.0 all-gather.21.cloned.1.call-start
  7.8 12.5 %shard_map.84 = (bf16[32,2048]{1,0:T(8,128)(2,1)}, bf16[32,2048]{1,0:T(8,128)(2,1)}, bf16[32,2048]{1,0:T(8,128)(2,1)}, bf16[32,2048]{1,0:T(8,128)(2,1)}, bf16[32...) custom-call(s32[1]{0:T(128)} %bitcast.me_ref, ...), custom_call_target="tpu_custom_call" | custom-call | flops 4831838208 | bytes 4194304 | tf_op jit(solution)/shard_map/pallas_call | solution.py:132
  20.3 9.0 %all-gather.8 = bf16[64,2048]{1,0:T(8,128)(2,1)} all-gather(bf16[32,2048]{1,0:T(8,128)(2,1)} %get-tuple-element.30), channel_id=10, replica_groups={{0,2},{4,6},{8,10},{12,14},{1,3},{5,7},{9,11},{13,15},{16,18},{20,22},{..., dimensions={0}, use_global_device_ids=true | all-gather | bytes 393216 | tf_op jit(solution)/shard_map/all_gather | solution.py:165
  29.3 10.8 %all-gather.9 = bf16[64,2048]{1,0:T(8,128)(2,1)} all-gather(bf16[32,2048]{1,0:T(8,128)(2,1)} %get-tuple-element.31), channel_id=11, replica_groups={{0,8},{2,10},{4,12},{6,14},{1,9},{3,11},{5,13},{7,15},{16,24},{18,26},{..., dimensions={0}, use_global_device_ids=true | all-gather | bytes 393216 | tf_op jit(solution)/shard_map/all_gather | solution.py:165
  40.2 5.9 %all-gather.10 = bf16[64,2048]{1,0:T(8,128)(2,1)} all-gather(bf16[32,2048]{1,0:T(8,128)(2,1)} %get-tuple-element.32), channel_id=12, replica_groups={{0,4},{2,6},{8,12},{10,14},{1,5},{3,7},{9,13},{11,15},{16,20},{18,22},{..., dimensions={0}, use_global_device_ids=true | all-gather | bytes 393216 | tf_op jit(solution)/shard_map/all_gather | solution.py:165
  46.1 10.2 %all-gather.11 = bf16[64,2048]{1,0:T(8,128)(2,1)} all-gather(bf16[32,2048]{1,0:T(8,128)(2,1)} %get-tuple-element.33), channel_id=13, replica_groups={{0,10},{2,8},{4,14},{6,12},{1,11},{3,9},{5,15},{7,13},{16,26},{18,24},{..., dimensions={0}, use_global_device_ids=true | all-gather | bytes 393216 | tf_op jit(solution)/shard_map/all_gather | solution.py:165
  56.3 6.8 %all-gather.12 = bf16[64,2048]{1,0:T(8,128)(2,1)} all-gather(bf16[32,2048]{1,0:T(8,128)(2,1)} %get-tuple-element.34), channel_id=14, replica_groups={{0,6},{2,4},{8,14},{10,12},{1,7},{3,5},{9,15},{11,13},{16,22},{18,20},{..., dimensions={0}, use_global_device_ids=true | all-gather | bytes 393216 | tf_op jit(solution)/shard_map/all_gather | solution.py:165
  63.1 7.9 %all-gather.13 = bf16[64,2048]{1,0:T(8,128)(2,1)} all-gather(bf16[32,2048]{1,0:T(8,128)(2,1)} %get-tuple-element.35), channel_id=15, replica_groups={{0,12},{2,14},{4,8},{6,10},{1,13},{3,15},{5,9},{7,11},{16,28},{18,30},{..., dimensions={0}, use_global_device_ids=true | all-gather | bytes 393216 | tf_op jit(solution)/shard_map/all_gather | solution.py:165
  71.0 8.7 %all-gather.14 = bf16[64,2048]{1,0:T(8,128)(2,1)} all-gather(bf16[32,2048]{1,0:T(8,128)(2,1)} %get-tuple-element.36), channel_id=16, replica_groups={{0,14},{2,12},{4,10},{6,8},{1,15},{3,13},{5,11},{7,9},{16,30},{18,28},{..., dimensions={0}, use_global_device_ids=true | all-gather | bytes 393216 | tf_op jit(solution)/shard_map/all_gather | solution.py:165
  79.7 1.9 %shard_map.85 = bf16[128,2048]{1,0:T(8,128)(2,1)} custom-call(s32[1]{0:T(128)} %bitcast.me_ref, bf16[32,2048]{1,0:T(8,128)(2,1)} %get-tuple-element.29.refs_0_.rest_9_, bf16[2,32,2048]{2,1,0:T(8,128)(2,1)} %bitcast.18, bf16[2,32,2048]{2,1,0:T(8,128)(2,1)} %bitcast.20, bf16[2,32,2048]{2,1,0:T(8,128)(2,1)} %bitcast.22, bf16[2,32,2048]{2,1,0:T(8,128)(2,1)} %bitcast.24, ...), custom_call_target="tpu_custom_call" | custom-call | tf_op jit(solution)/shard_map/pallas_call | solution.py:190
  81.6 0.0 all-gather.21.cloned.1.call-update
  81.7 0.2 all-gather.19.cloned.1.call-start
  81.9 12.5 %shard_map.82 = (bf16[32,2048]{1,0:T(8,128)(2,1)}, bf16[32,2048]{1,0:T(8,128)(2,1)}, bf16[32,2048]{1,0:T(8,128)(2,1)}, bf16[32,2048]{1,0:T(8,128)(2,1)}, bf16[32...) custom-call(s32[1]{0:T(128)} %bitcast.me_ref, ...), custom_call_target="tpu_custom_call" | custom-call | flops 4831838208 | bytes 4194304 | tf_op jit(solution)/shard_map/pallas_call | solution.py:132
  94.4 7.1 %all-gather = bf16[64,2048]{1,0:T(8,128)(2,1)} all-gather(bf16[32,2048]{1,0:T(8,128)(2,1)} %get-tuple-element.22), channel_id=2, replica_groups={{0,2},{4,6},{8,10},{12,14},{1,3},{5,7},{9,11},{13,15},{16,18},{20,22},{..., dimensions={0}, use_global_device_ids=true | all-gather | bytes 393216 | tf_op jit(solution)/shard_map/all_gather | solution.py:165
  101.4 8.6 %all-gather.1 = bf16[64,2048]{1,0:T(8,128)(2,1)} all-gather(bf16[32,2048]{1,0:T(8,128)(2,1)} %get-tuple-element.23), channel_id=3, replica_groups={{0,8},{2,10},{4,12},{6,14},{1,9},{3,11},{5,13},{7,15},{16,24},{18,26},{..., dimensions={0}, use_global_device_ids=true | all-gather | bytes 393216 | tf_op jit(solution)/shard_map/all_gather | solution.py:165
  110.1 7.1 %all-gather.2 = bf16[64,2048]{1,0:T(8,128)(2,1)} all-gather(bf16[32,2048]{1,0:T(8,128)(2,1)} %get-tuple-element.24), channel_id=4, replica_groups={{0,4},{2,6},{8,12},{10,14},{1,5},{3,7},{9,13},{11,15},{16,20},{18,22},{..., dimensions={0}, use_global_device_ids=true | all-gather | bytes 393216 | tf_op jit(solution)/shard_map/all_gather | solution.py:165
  117.2 8.2 %all-gather.3 = bf16[64,2048]{1,0:T(8,128)(2,1)} all-gather(bf16[32,2048]{1,0:T(8,128)(2,1)} %get-tuple-element.25), channel_id=5, replica_groups={{0,10},{2,8},{4,14},{6,12},{1,11},{3,9},{5,15},{7,13},{16,26},{18,24},{..., dimensions={0}, use_global_device_ids=true | all-gather | bytes 393216 | tf_op jit(solution)/shard_map/all_gather | solution.py:165
  125.4 9.3 %all-gather.4 = bf16[64,2048]{1,0:T(8,128)(2,1)} all-gather(bf16[32,2048]{1,0:T(8,128)(2,1)} %get-tuple-element.26), channel_id=6, replica_groups={{0,6},{2,4},{8,14},{10,12},{1,7},{3,5},{9,15},{11,13},{16,22},{18,20},{..., dimensions={0}, use_global_device_ids=true | all-gather | bytes 393216 | tf_op jit(solution)/shard_map/all_gather | solution.py:165
  134.7 7.9 %all-gather.5 = bf16[64,2048]{1,0:T(8,128)(2,1)} all-gather(bf16[32,2048]{1,0:T(8,128)(2,1)} %get-tuple-element.27), channel_id=7, replica_groups={{0,12},{2,14},{4,8},{6,10},{1,13},{3,15},{5,9},{7,11},{16,28},{18,30},{..., dimensions={0}, use_global_device_ids=true | all-gather | bytes 393216 | tf_op jit(solution)/shard_map/all_gather | solution.py:165
  142.6 8.7 %all-gather.6 = bf16[64,2048]{1,0:T(8,128)(2,1)} all-gather(bf16[32,2048]{1,0:T(8,128)(2,1)} %get-tuple-element.28), channel_id=8, replica_groups={{0,14},{2,12},{4,10},{6,8},{1,15},{3,13},{5,11},{7,9},{16,30},{18,28},{..., dimensions={0}, use_global_device_ids=true | all-gather | bytes 393216 | tf_op jit(solution)/shard_map/all_gather | solution.py:165
  151.3 1.9 %shard_map.83 = bf16[128,2048]{1,0:T(8,128)(2,1)} custom-call(s32[1]{0:T(128)} %bitcast.me_ref, bf16[32,2048]{1,0:T(8,128)(2,1)} %get-tuple-element.21.refs_0_.rest_0_, bf16[2,32,2048]{2,1,0:T(8,128)(2,1)} %bitcast.32, bf16[2,32,2048]{2,1,0:T(8,128)(2,1)} %bitcast.34, bf16[2,32,2048]{2,1,0:T(8,128)(2,1)} %bitcast.36, bf16[2,32,2048]{2,1,0:T(8,128)(2,1)} %bitcast.38, ...), custom_call_target="tpu_custom_call" | custom-call | tf_op jit(solution)/shard_map/pallas_call | solution.py:190
  153.2 0.0 all-gather.19.cloned.1.call-update
  153.3 0.0 all-gather.21.cloned.1.call-done
  153.3 8.2 %all-gather.19.cloned.1.call-done = bf16[256,2048]{1,0:T(8,128)(2,1)} async-done(((bf16[128,2048]{1,0:T(8,128)(2,1)}), bf16[256,2048]{1,0:T(8,128)(2,1)}) %all-gather.19.cloned.1.call-update) | async-done | bytes 1048592 | tf_op jit(solution)/shard_map/all_gather | solution.py:165
  161.5 3.2 %shard_map.86 = bf16[1,8,16,8192]{3,2,1,0:T(8,128)(2,1)} custom-call(s32[1]{0:T(128)} %bitcast.me_ref, bf16[32,2048]{1,0:T(8,128)(2,1)} %get-tuple-element.21.refs_0_.rest_0_, bf16[2,32,2048]{2,1,0:T(8,128)(2,1)} %bitcast.33, bf16[2,32,2048]{2,1,0:T(8,128)(2,1)} %bitcast.35, bf16[2,32,2048]{2,1,0:T(8,128)(2,1)} %bitcast.37, bf16[2,32,2048]{2,1,0:T(8,128)(2,1)} %bitcast.39, ...), custom_call_target="tpu_custom_call" | custom-call | tf_op jit(solution)/shard_map/pallas_call | solution.py:224
Async XLA Ops:
  6.5 146.8 %all-gather.21.cloned.1.call-start = ((), (), s32[]{:S(2)}) async-start(), calls=%async_computation.1 | async-start | bytes 1572864 | tf_op jit(solution)/shard_map/all_gather | solution.py:165
  81.7 79.8 %all-gather.19.cloned.1.call-start = ((), (), s32[]{:S(2)}) async-start(), calls=%async_computation | async-start | bytes 1572864 | tf_op jit(solution)/shard_map/all_gather | solution.py:165
Sparse Core Ops, SparseCore 0:
  81.8 8.3 all-gather.20
  153.4 8.0 all-gather.18

commit v5 on v3

--- a/solution.py
+++ b/solution.py
@@ -10,8 +10,10 @@
 
 SPAN = 64
 GROUP = 4
-CHUNKS = (1, 1, 1, 1)
+CHUNKS = (1, 1)
 DIRECT = 16
+KEY_PARTS = 2
+VMEM = 58 * 1024 * 1024
 MASKED = -1e30
 OPEN = 3e38
 NT = (((1,), (1,)), ((), ()))
@@ -60,17 +62,37 @@
     past = prefix_hbm.shape[0]
     heads, dim, _ = key_weight_ref.shape
     here = pl.ds(first, heads)
-    copies = [
+    stacks = heads // GROUP
+    part = past // KEY_PARTS
+
+    def copy_stack(source, target, stack, index):
+        here, there = pl.ds(stack * GROUP, GROUP), pl.ds(first + stack * GROUP, GROUP)
+        return pltpu.make_async_copy(source.at[there], target.at[here], sem.at[index])
+
+    for_queries, for_values = [], []
+    for s in range(stacks):
+        here, there = pl.ds(s * GROUP * dim, GROUP * dim), pl.ds((first + s * GROUP) * dim, GROUP * dim)
+        for_queries += [
+            pltpu.make_async_copy(queries_hbm.at[:, there], queries_ref.at[:, here], sem.at[3 * s]),
+            copy_stack(key_weight_hbm, key_weight_ref, s, 3 * s + 1),
+        ]
+        for_values.append(copy_stack(value_weight_hbm, value_weight_ref, s, 3 * s + 2))
+    for_keys = [
         pltpu.make_async_copy(
-            queries_hbm.at[:, pl.ds(first * dim, heads * dim)], queries_ref, sem.at[0]
-        ),
-        pltpu.make_async_copy(key_weight_hbm.at[here], key_weight_ref, sem.at[1]),
-        pltpu.make_async_copy(prefix_hbm, keys_ref.at[pl.ds(0, past)], sem.at[2]),
-        pltpu.make_async_copy(fresh_hbm, keys_ref.at[pl.ds(past, slots)], sem.at[3]),
-        pltpu.make_async_copy(value_weight_hbm.at[here], value_weight_ref, sem.at[4]),
+            prefix_hbm.at[pl.ds(i * part, part)],
+            keys_ref.at[pl.ds(i * part, part)],
+            sem.at[3 * stacks + i],
+        )
+        for i in range(KEY_PARTS)
     ]
-    for copy in copies:
+    for_keys.append(
+        pltpu.make_async_copy(
+            fresh_hbm, keys_ref.at[pl.ds(past, slots)], sem.at[3 * stacks + KEY_PARTS]
+        )
+    )
+    for copy in for_queries[:2] + for_keys + for_queries[2:] + for_values:
         copy.start()
+
     count, size = count_ref[0], size_ref[0]
     lane = lax.broadcasted_iota(jnp.int32, (slots, past), 1)
     cap_ref[:, :past] = jnp.where(lane < size, jnp.float32(OPEN), jnp.float32(MASKED))
@@ -80,26 +102,25 @@
         (col <= row) & (col < count * SPAN), jnp.float32(OPEN), jnp.float32(MASKED)
     )
     build_table(me_ref[0], count, routes_ref, table_ref, capacity)
-    for copy in copies:
-        copy.wait()
 
     scale = math.log2(math.e) / math.sqrt(dim)
-    keys = keys_ref[...]
-    stacks = heads // GROUP
-    scores = []
-    for stack in range(stacks):
+
+    def score(stack):
+        for copy in for_queries[2 * stack : 2 * stack + 2] + (for_keys if stack == 0 else []):
+            copy.wait()
         lifted = []
         for h in range(stack * GROUP, (stack + 1) * GROUP):
             one = dot(queries_ref[:, h * dim : (h + 1) * dim], key_weight_ref[h])
             lifted.append(one.astype(jnp.bfloat16))
         lifted = jnp.concatenate(lifted, axis=0)
-        score = lax.dot_general(lifted, keys, NT, preferred_element_type=jnp.float32)
-        scores.append(score)
-    for stack in range(stacks):
-        score = scores[stack].reshape(GROUP, slots, keys.shape[0])
-        score = jnp.minimum(score, cap_ref[...][None])
-        highest = jnp.max(score, axis=-1, keepdims=True) * scale
-        weights = jnp.exp2(score * scale - highest)
+        return lax.dot_general(lifted, keys_ref[...], NT, preferred_element_type=jnp.float32)
+
+    def finish(stack, scores):
+        keys = keys_ref[...]
+        scores = scores.reshape(GROUP, slots, keys.shape[0])
+        scores = jnp.minimum(scores, cap_ref[...][None])
+        highest = jnp.max(scores, axis=-1, keepdims=True) * scale
+        weights = jnp.exp2(scores * scale - highest)
         total = jnp.sum(weights, axis=-1, keepdims=True)
         weights = weights.astype(jnp.bfloat16).reshape(GROUP * slots, keys.shape[0])
         mixed = dot(weights, keys).astype(jnp.bfloat16)
@@ -107,6 +128,13 @@
             h = stack * GROUP + g
             projected = dot(mixed[g * slots : (g + 1) * slots], value_weight_ref[h])
             attended_ref[:, h * dim : (h + 1) * dim] = (projected / total[g]).astype(jnp.bfloat16)
+
+    before = score(0)
+    for stack in range(1, stacks + 1):
+        for_values[stack - 1].wait()
+        after = score(stack) if stack < stacks else None
+        finish(stack - 1, before)
+        before = after
     grouped = dot(table_ref[...], attended_ref[...]).astype(jnp.bfloat16)
     rows = out_refs[0].shape[0]
     for k, out_ref in enumerate(out_refs):
@@ -137,9 +165,9 @@
             pltpu.VMEM((slots, keys), jnp.float32),
             pltpu.VMEM((places, slots), jnp.bfloat16),
             pltpu.VMEM((slots, heads * dim), jnp.bfloat16),
-            pltpu.SemaphoreType.DMA((5,)),
+            pltpu.SemaphoreType.DMA((3 * heads // GROUP + KEY_PARTS + 1,)),
         ],
-        compiler_params=pltpu.CompilerParams(vmem_limit_bytes=54 * 1024 * 1024),
+        compiler_params=pltpu.CompilerParams(vmem_limit_bytes=VMEM),
         cost_estimate=pl.CostEstimate(
             flops=4 * slots * heads * keys * latent,
             bytes_accessed=4 * heads * dim * latent,
@@ -178,6 +206,7 @@
         out_specs=pl.BlockSpec(memory_space=pltpu.VMEM),
         out_shape=jax.ShapeDtypeStruct((len(pieces) * rows // cores, width), jnp.bfloat16),
         scratch_shapes=[pltpu.SemaphoreType.DMA((len(pieces),))],
+        compiler_params=pltpu.CompilerParams(vmem_limit_bytes=VMEM),
     )(*pieces)
 
 
@@ -214,16 +243,15 @@
             pltpu.VMEM(shape[1:], jnp.bfloat16),
             pltpu.SemaphoreType.DMA((len(plan),)),
         ],
+        compiler_params=pltpu.CompilerParams(vmem_limit_bytes=VMEM),
     )(me, *arrays)
 
 
 def exchange_order(ranks):
     near, far = list(range(1, ranks // 2)), list(range(ranks // 2, ranks))
-    mixed = []
-    while len(far) > 2 or near:
-        mixed += near[:1] + (far[:1] if len(far) > 2 else [])
-        near, far = near[1:], (far[1:] if len(far) > 2 else far)
-    return mixed + far
+    far = far[::2] + far[1::2]
+    half = len(far) // 2
+    return far[:half] + near[:1] + far[half:] + near[1:]
 
 
 def local(

time: 94.8 us -> 76.1 us (0.80)
  starting transfers between devices: 45.5 us -> 28.9 us
  Pallas kernels: 40.2 us -> 32.6 us
  waiting for transfers between devices: 4.98 us -> 11.1 us
    ppermute x28 -> x14, starting transfers between devices: 44.8 us -> 28.7 us  [local(): pieces.append(lax.ppermute(outgoing[j], 'dp', pairs))]
    ppermute x28 -> x14, waiting for transfers between devices: 3.3 us -> 9 us  [local(): pieces.append(lax.ppermute(outgoing[j], 'dp', pairs))]
    pallas_call x4 -> x2, Pallas kernels: 30.3 us -> 25.6 us  [attend(): pl.pallas_call(functools.partial(attend_kernel, places // experts, first)...]
    pallas_call x4 -> x2, Pallas kernels: 6.56 us -> 3.84 us  [pass_on(): pl.pallas_call(functools.partial(pass_on_kernel, cores), in_specs=[pl.Blo...]
    ppermute x4 -> x2, waiting for transfers between devices: 1.68 us -> 2.09 us  [local(): lax.ppermute(pass_on(pieces, cores), 'ep', [(i, i ^ 1) for i in range(cor...]
  transfers between devices with their start and end apart: 32 -> 16, of which waited for: 4 -> 4; matrix products, arithmetic and copies ran while one was open for 0% -> 0% of each run, Pallas kernels for 31% -> 22%
where the time goes in v5:
time: 76.1 us; the launch traced here: 75.7 us
  Pallas kernels  32.6 us (43%)
  starting transfers between devices  28.9 us (38%)
  waiting for transfers between devices  11.1 us (15%)
  between operations  1.68 us (2%)
  local copies, waits for them, and re-layouts  1.45 us (2%)
    ppermute x14, starting transfers between devices, local(): pieces.append(lax.ppermute(outgoing[j], 'dp', pairs))  28.7 us
    pallas_call x2, Pallas kernels, attend(): pl.pallas_call(functools.partial(attend_kernel, places // experts, first)...  25.6 us
    ppermute x14, waiting for transfers between devices, local(): pieces.append(lax.ppermute(outgoing[j], 'dp', pairs))  9 us
    pallas_call x2, Pallas kernels, pass_on(): pl.pallas_call(functools.partial(pass_on_kernel, cores), in_specs=[pl.Blo...  3.84 us
    pallas_call x1, Pallas kernels, assemble(): pl.pallas_call(functools.partial(place_kernel, plan, cores), in_specs=[pl...  3.16 us
    ppermute x2, waiting for transfers between devices, local(): lax.ppermute(pass_on(pieces, cores), 'ep', [(i, i ^ 1) for i in range(cor...  2.09 us
  transfers between devices with their start and end apart: 16, of which 4 were waited for; matrix products, arithmetic and copies ran while one was open for 0% of the time, Pallas kernels for 22%

profile of v5, /device:TPU:0, one launch (start us, length us, event | category | flops | bytes accessed | tf_op | source)
XLA Modules:
  0.0 75.7 jit_solution(2375557969963577026)
XLA Ops:
  1.3 12.7 %shard_map.84 = (bf16[32,2048]{1,0:T(8,128)(2,1)}, bf16[32,2048]{1,0:T(8,128)(2,1)}, bf16[32,2048]{1,0:T(8,128)(2,1)}, bf16[32,2048]{1,0:T(8,128)(2,1)}, bf16[32...) custom-call(s32[1]{0:T(128)} %bitcast.me_ref, ...), custom_call_target="tpu_custom_call" | custom-call | flops 4831838208 | bytes 4194304 | tf_op jit(solution)/shard_map/pallas_call | solution.py:155
  14.0 4.1 %collective-permute-start.8 = (bf16[32,2048]{1,0:T(8,128)(2,1)}, bf16[32,2048]{1,0:T(8,128)(2,1)S(1)}, u32[]{:S(2)}, u32[]{:S(2)}) collective-permute-start(bf16[32,2048]{1,0:T(8,128)(2,1)} %get-tuple-element.30), channel_id=1, source_target_pairs={{0,8},{2,10},{4,12},{6,14},{8,0},{10,2},{12,4},{14,6},{1,9},{3,11}... | collective-permute-start | bytes 393224 | tf_op jit(solution)/shard_map/ppermute | solution.py:299
  18.1 1.4 %collective-permute-start.9 = (bf16[32,2048]{1,0:T(8,128)(2,1)}, bf16[32,2048]{1,0:T(8,128)(2,1)S(1)}, u32[]{:S(2)}, u32[]{:S(2)}) collective-permute-start(bf16[32,2048]{1,0:T(8,128)(2,1)} %get-tuple-element.31), channel_id=1, source_target_pairs={{0,12},{2,14},{4,8},{6,10},{8,4},{10,6},{12,0},{14,2},{1,13},{3,15... | collective-permute-start | bytes 393224 | tf_op jit(solution)/shard_map/ppermute | solution.py:299
  19.5 1.5 %collective-permute-start.10 = (bf16[32,2048]{1,0:T(8,128)(2,1)}, bf16[32,2048]{1,0:T(8,128)(2,1)S(1)}, u32[]{:S(2)}, u32[]{:S(2)}) collective-permute-start(bf16[32,2048]{1,0:T(8,128)(2,1)} %get-tuple-element.32), channel_id=1, source_target_pairs={{0,2},{2,0},{4,6},{6,4},{8,10},{10,8},{12,14},{14,12},{1,3},{3,1},... | collective-permute-start | bytes 393224 | tf_op jit(solution)/shard_map/ppermute | solution.py:299
  21.0 1.6 %collective-permute-start.11 = (bf16[32,2048]{1,0:T(8,128)(2,1)}, bf16[32,2048]{1,0:T(8,128)(2,1)S(1)}, u32[]{:S(2)}, u32[]{:S(2)}) collective-permute-start(bf16[32,2048]{1,0:T(8,128)(2,1)} %get-tuple-element.33), channel_id=1, source_target_pairs={{0,10},{2,8},{4,14},{6,12},{8,2},{10,0},{12,6},{14,4},{1,11},{3,9}... | collective-permute-start | bytes 393224 | tf_op jit(solution)/shard_map/ppermute | solution.py:299
  22.6 1.8 %collective-permute-start.12 = (bf16[32,2048]{1,0:T(8,128)(2,1)}, bf16[32,2048]{1,0:T(8,128)(2,1)S(1)}, u32[]{:S(2)}, u32[]{:S(2)}) collective-permute-start(bf16[32,2048]{1,0:T(8,128)(2,1)} %get-tuple-element.34), channel_id=1, source_target_pairs={{0,14},{2,12},{4,10},{6,8},{8,6},{10,4},{12,2},{14,0},{1,15},{3,13... | collective-permute-start | bytes 393224 | tf_op jit(solution)/shard_map/ppermute | solution.py:299
  24.5 12.9 %shard_map.82 = (bf16[32,2048]{1,0:T(8,128)(2,1)}, bf16[32,2048]{1,0:T(8,128)(2,1)}, bf16[32,2048]{1,0:T(8,128)(2,1)}, bf16[32,2048]{1,0:T(8,128)(2,1)}, bf16[32...) custom-call(s32[1]{0:T(128)} %bitcast.me_ref, ...), custom_call_target="tpu_custom_call" | custom-call | flops 4831838208 | bytes 4194304 | tf_op jit(solution)/shard_map/pallas_call | solution.py:155
  37.4 0.0 collective-permute-done.8.refs_1_.rest_10_
  37.4 1.0 %collective-permute-start.13 = (bf16[32,2048]{1,0:T(8,128)(2,1)S(1)}, bf16[32,2048]{1,0:T(8,128)(2,1)S(1)}, u32[]{:S(2)}, u32[]{:S(2)}) collective-permute-start(bf16[32,2048]{1,0:T(8,128)(2,1)S(1)} %copy-done.17), channel_id=1, source_target_pairs={{0,4},{2,6},{4,0},{6,2},{8,12},{10,14},{12,8},{14,10},{1,5},{3,7},... | collective-permute-start | bytes 393224 | tf_op jit(solution)/shard_map/ppermute | solution.py:299
  38.4 1.1 %collective-permute-start.14 = (bf16[32,2048]{1,0:T(8,128)(2,1)S(1)}, bf16[32,2048]{1,0:T(8,128)(2,1)S(1)}, u32[]{:S(2)}, u32[]{:S(2)}) collective-permute-start(bf16[32,2048]{1,0:T(8,128)(2,1)S(1)} %copy-done.16), channel_id=1, source_target_pairs={{0,6},{2,4},{4,2},{6,0},{8,14},{10,12},{12,10},{14,8},{1,7},{3,5},... | collective-permute-start | bytes 393224 | tf_op jit(solution)/shard_map/ppermute | solution.py:299
  39.5 1.9 %collective-permute-start = (bf16[32,2048]{1,0:T(8,128)(2,1)}, bf16[32,2048]{1,0:T(8,128)(2,1)S(1)}, u32[]{:S(2)}, u32[]{:S(2)}) collective-permute-start(bf16[32,2048]{1,0:T(8,128)(2,1)} %get-tuple-element.22), channel_id=1, source_target_pairs={{0,8},{2,10},{4,12},{6,14},{8,0},{10,2},{12,4},{14,6},{1,9},{3,11}... | collective-permute-start | bytes 393224 | tf_op jit(solution)/shard_map/ppermute | solution.py:299
  41.5 1.8 %collective-permute-start.1 = (bf16[32,2048]{1,0:T(8,128)(2,1)}, bf16[32,2048]{1,0:T(8,128)(2,1)S(1)}, u32[]{:S(2)}, u32[]{:S(2)}) collective-permute-start(bf16[32,2048]{1,0:T(8,128)(2,1)} %get-tuple-element.23), channel_id=1, source_target_pairs={{0,12},{2,14},{4,8},{6,10},{8,4},{10,6},{12,0},{14,2},{1,13},{3,15... | collective-permute-start | bytes 393224 | tf_op jit(solution)/shard_map/ppermute | solution.py:299
  43.3 0.0 collective-permute-done.12.refs_5_.rest_14_
  43.3 1.0 %collective-permute-start.2 = (bf16[32,2048]{1,0:T(8,128)(2,1)}, bf16[32,2048]{1,0:T(8,128)(2,1)S(1)}, u32[]{:S(2)}, u32[]{:S(2)}) collective-permute-start(bf16[32,2048]{1,0:T(8,128)(2,1)} %get-tuple-element.24), channel_id=1, source_target_pairs={{0,2},{2,0},{4,6},{6,4},{8,10},{10,8},{12,14},{14,12},{1,3},{3,1},... | collective-permute-start | bytes 393224 | tf_op jit(solution)/shard_map/ppermute | solution.py:299
  44.4 0.6 collective-permute-done.13.refs_6_.rest_15_
  45.0 3.4 %collective-permute-start.3 = (bf16[32,2048]{1,0:T(8,128)(2,1)}, bf16[32,2048]{1,0:T(8,128)(2,1)S(1)}, u32[]{:S(2)}, u32[]{:S(2)}) collective-permute-start(bf16[32,2048]{1,0:T(8,128)(2,1)} %get-tuple-element.25), channel_id=1, source_target_pairs={{0,10},{2,8},{4,14},{6,12},{8,2},{10,0},{12,6},{14,4},{1,11},{3,9}... | collective-permute-start | bytes 393224 | tf_op jit(solution)/shard_map/ppermute | solution.py:299
  48.4 3.6 %collective-permute-start.4 = (bf16[32,2048]{1,0:T(8,128)(2,1)}, bf16[32,2048]{1,0:T(8,128)(2,1)S(1)}, u32[]{:S(2)}, u32[]{:S(2)}) collective-permute-start(bf16[32,2048]{1,0:T(8,128)(2,1)} %get-tuple-element.26), channel_id=1, source_target_pairs={{0,14},{2,12},{4,10},{6,8},{8,6},{10,4},{12,2},{14,0},{1,15},{3,13... | collective-permute-start | bytes 393224 | tf_op jit(solution)/shard_map/ppermute | solution.py:299
  51.9 5.7 %collective-permute-done.refs_1_.rest_1_ = bf16[32,2048]{1,0:T(8,128)(2,1)S(1)} collective-permute-done((bf16[32,2048]{1,0:T(8,128)(2,1)}, bf16[32,2048]{1,0:T(8,128)(2,1)S(1)}, u32[]{:S(2)}, u32[]{:S(2)}) %collective-permute-start) | collective-permute-done | bytes 131104 | tf_op jit(solution)/shard_map/ppermute | solution.py:299
  57.7 4.4 %collective-permute-start.6 = (bf16[32,2048]{1,0:T(8,128)(2,1)}, bf16[32,2048]{1,0:T(8,128)(2,1)S(1)}, u32[]{:S(2)}, u32[]{:S(2)}) collective-permute-start(bf16[32,2048]{1,0:T(8,128)(2,1)} %get-tuple-element.28), channel_id=1, source_target_pairs={{0,6},{2,4},{4,2},{6,0},{8,14},{10,12},{12,10},{14,8},{1,7},{3,5},... | collective-permute-start | bytes 393224 | tf_op jit(solution)/shard_map/ppermute | solution.py:299
  62.2 1.9 %shard_map.85 = bf16[128,2048]{1,0:T(8,128)(2,1)} custom-call(bf16[32,2048]{1,0:T(8,128)(2,1)} %get-tuple-element.29.refs_0_.rest_9_, bf16[32,2048]{1,0:T(8,128)(2,1)} %copy-done, bf16[32,2048]{1,0:T(8,128)(2,1)} %copy-done.1, bf16[32,2048]{1,0:T(8,128)(2,1)} %copy-done.2, bf16[32,2048]{1,0:T(8,128)(2,1)} %copy-done.3, bf16[32,2048]{1,0:T(8,128)(2,1)} %copy-done.4, ...), custom_call_target="tpu_custom_call" | custom-call | tf_op jit(solution)/shard_map/pallas_call | solution.py:203
  64.1 0.0 collective-permute-done.2.refs_3_.rest_3_
  64.1 0.1 collective-permute-start.15
  64.2 0.0 collective-permute-done.4.refs_5_.rest_5_
  64.2 0.0 collective-permute-done.5.refs_6_.rest_6_
  64.3 2.6 %collective-permute-done.6.refs_7_.rest_7_ = bf16[32,2048]{1,0:T(8,128)(2,1)S(1)} collective-permute-done((bf16[32,2048]{1,0:T(8,128)(2,1)}, bf16[32,2048]{1,0:T(8,128)(2,1)S(1)}, u32[]{:S(2)}, u32[]{:S(2)}) %collective-permute-start.6) | collective-permute-done | bytes 131104 | tf_op jit(solution)/shard_map/ppermute | solution.py:299
  66.9 0.6 copy-done.13
  67.5 1.9 %shard_map.83 = bf16[128,2048]{1,0:T(8,128)(2,1)} custom-call(bf16[32,2048]{1,0:T(8,128)(2,1)} %get-tuple-element.21.refs_0_.rest_0_, bf16[32,2048]{1,0:T(8,128)(2,1)} %copy-done.7, bf16[32,2048]{1,0:T(8,128)(2,1)} %copy-done.8, bf16[32,2048]{1,0:T(8,128)(2,1)} %copy-done.9, bf16[32,2048]{1,0:T(8,128)(2,1)} %copy-done.10, bf16[32,2048]{1,0:T(8,128)(2,1)} %copy-done.11, ...), custom_call_target="tpu_custom_call" | custom-call | tf_op jit(solution)/shard_map/pallas_call | solution.py:203
  69.4 0.1 collective-permute-start.7
  69.5 0.0 collective-permute-done.15.rest_17_
  69.5 2.1 %collective-permute-done.7.rest_8_ = bf16[128,2048]{1,0:T(8,128)(2,1)S(1)} collective-permute-done((bf16[128,2048]{1,0:T(8,128)(2,1)}, bf16[128,2048]{1,0:T(8,128)(2,1)S(1)}, u32[]{:S(2)}, u32[]{:S(2)}) %collective-permute-start.7) | collective-permute-done | bytes 524320 | tf_op jit(solution)/shard_map/ppermute | solution.py:300
  71.6 0.8 %copy-done.15 = bf16[128,2048]{1,0:T(8,128)(2,1)} copy-done((bf16[128,2048]{1,0:T(8,128)(2,1)}, bf16[128,2048]{1,0:T(8,128)(2,1)S(1)}, u32[]{:S(2)}) %copy-start.15) | copy-done | bytes 524312
  72.4 3.2 %shard_map.86 = bf16[1,8,16,8192]{3,2,1,0:T(8,128)(2,1)} custom-call(s32[1]{0:T(128)} %bitcast.me_ref, bf16[32,2048]{1,0:T(8,128)(2,1)} %get-tuple-element.21.refs_0_.rest_0_, bf16[32,2048]{1,0:T(8,128)(2,1)} %copy-done.7, bf16[32,2048]{1,0:T(8,128)(2,1)} %copy-done.8, bf16[32,2048]{1,0:T(8,128)(2,1)} %copy-done.9, bf16[32,2048]{1,0:T(8,128)(2,1)} %copy-done.10, ...), custom_call_target="tpu_custom_call" | custom-call | tf_op jit(solution)/shard_map/pallas_call | solution.py:236
  (41 shorter events, 0.1 us)
Async XLA Ops:
  14.0 23.4 %collective-permute-start.8 = (bf16[32,2048]{1,0:T(8,128)(2,1)}, bf16[32,2048]{1,0:T(8,128)(2,1)S(1)}, u32[]{:S(2)}, u32[]{:S(2)}) collective-permute-start(bf16[32,2048]{1,0:T(8,128)(2,1)} %get-tuple-element.30), channel_id=1, source_target_pairs={{0,8},{2,10},{4,12},{6,14},{8,0},{10,2},{12,4},{14,6},{1,9},{3,11}... | collective-permute-start | bytes 393224 | tf_op jit(solution)/shard_map/ppermute | solution.py:299
  18.1 20.3 %collective-permute-start.9 = (bf16[32,2048]{1,0:T(8,128)(2,1)}, bf16[32,2048]{1,0:T(8,128)(2,1)S(1)}, u32[]{:S(2)}, u32[]{:S(2)}) collective-permute-start(bf16[32,2048]{1,0:T(8,128)(2,1)} %get-tuple-element.31), channel_id=1, source_target_pairs={{0,12},{2,14},{4,8},{6,10},{8,4},{10,6},{12,0},{14,2},{1,13},{3,15... | collective-permute-start | bytes 393224 | tf_op jit(solution)/shard_map/ppermute | solution.py:299
  19.5 20.1 %collective-permute-start.10 = (bf16[32,2048]{1,0:T(8,128)(2,1)}, bf16[32,2048]{1,0:T(8,128)(2,1)S(1)}, u32[]{:S(2)}, u32[]{:S(2)}) collective-permute-start(bf16[32,2048]{1,0:T(8,128)(2,1)} %get-tuple-element.32), channel_id=1, source_target_pairs={{0,2},{2,0},{4,6},{6,4},{8,10},{10,8},{12,14},{14,12},{1,3},{3,1},... | collective-permute-start | bytes 393224 | tf_op jit(solution)/shard_map/ppermute | solution.py:299
  21.0 20.5 %collective-permute-start.11 = (bf16[32,2048]{1,0:T(8,128)(2,1)}, bf16[32,2048]{1,0:T(8,128)(2,1)S(1)}, u32[]{:S(2)}, u32[]{:S(2)}) collective-permute-start(bf16[32,2048]{1,0:T(8,128)(2,1)} %get-tuple-element.33), channel_id=1, source_target_pairs={{0,10},{2,8},{4,14},{6,12},{8,2},{10,0},{12,6},{14,4},{1,11},{3,9}... | collective-permute-start | bytes 393224 | tf_op jit(solution)/shard_map/ppermute | solution.py:299
  22.6 14.8 %copy-start.17 = (bf16[32,2048]{1,0:T(8,128)(2,1)S(1)}, bf16[32,2048]{1,0:T(8,128)(2,1)}, u32[]{:S(2)}) copy-start(bf16[32,2048]{1,0:T(8,128)(2,1)} %get-tuple-element.35) | copy-start | bytes 393220
  22.6 15.8 %copy-start.16 = (bf16[32,2048]{1,0:T(8,128)(2,1)S(1)}, bf16[32,2048]{1,0:T(8,128)(2,1)}, u32[]{:S(2)}) copy-start(bf16[32,2048]{1,0:T(8,128)(2,1)} %get-tuple-element.36) | copy-start | bytes 393220
  22.6 20.7 %collective-permute-start.12 = (bf16[32,2048]{1,0:T(8,128)(2,1)}, bf16[32,2048]{1,0:T(8,128)(2,1)S(1)}, u32[]{:S(2)}, u32[]{:S(2)}) collective-permute-start(bf16[32,2048]{1,0:T(8,128)(2,1)} %get-tuple-element.34), channel_id=1, source_target_pairs={{0,14},{2,12},{4,10},{6,8},{8,6},{10,4},{12,2},{14,0},{1,15},{3,13... | collective-permute-start | bytes 393224 | tf_op jit(solution)/shard_map/ppermute | solution.py:299
  37.4 24.7 %copy-start = (bf16[32,2048]{1,0:T(8,128)(2,1)}, bf16[32,2048]{1,0:T(8,128)(2,1)S(1)}, u32[]{:S(2)}) copy-start(bf16[32,2048]{1,0:T(8,128)(2,1)S(1)} %collective-permute-done.8.refs_1_.rest_10_) | copy-start | bytes 393220
  37.4 7.5 %collective-permute-start.13 = (bf16[32,2048]{1,0:T(8,128)(2,1)S(1)}, bf16[32,2048]{1,0:T(8,128)(2,1)S(1)}, u32[]{:S(2)}, u32[]{:S(2)}) collective-permute-start(bf16[32,2048]{1,0:T(8,128)(2,1)S(1)} %copy-done.17), channel_id=1, source_target_pairs={{0,4},{2,6},{4,0},{6,2},{8,12},{10,14},{12,8},{14,10},{1,5},{3,7},... | collective-permute-start | bytes 393224 | tf_op jit(solution)/shard_map/ppermute | solution.py:299
  38.4 23.7 %copy-start.1 = (bf16[32,2048]{1,0:T(8,128)(2,1)}, bf16[32,2048]{1,0:T(8,128)(2,1)S(1)}, u32[]{:S(2)}) copy-start(bf16[32,2048]{1,0:T(8,128)(2,1)S(1)} %collective-permute-done.9.refs_2_.rest_11_) | copy-start | bytes 393220
  38.4 9.9 %collective-permute-start.14 = (bf16[32,2048]{1,0:T(8,128)(2,1)S(1)}, bf16[32,2048]{1,0:T(8,128)(2,1)S(1)}, u32[]{:S(2)}, u32[]{:S(2)}) collective-permute-start(bf16[32,2048]{1,0:T(8,128)(2,1)S(1)} %copy-done.16), channel_id=1, source_target_pairs={{0,6},{2,4},{4,2},{6,0},{8,14},{10,12},{12,10},{14,8},{1,7},{3,5},... | collective-permute-start | bytes 393224 | tf_op jit(solution)/shard_map/ppermute | solution.py:299
  39.5 22.6 %copy-start.2 = (bf16[32,2048]{1,0:T(8,128)(2,1)}, bf16[32,2048]{1,0:T(8,128)(2,1)S(1)}, u32[]{:S(2)}) copy-start(bf16[32,2048]{1,0:T(8,128)(2,1)S(1)} %collective-permute-done.10.refs_3_.rest_12_) | copy-start | bytes 393220
  39.5 18.1 %collective-permute-start = (bf16[32,2048]{1,0:T(8,128)(2,1)}, bf16[32,2048]{1,0:T(8,128)(2,1)S(1)}, u32[]{:S(2)}, u32[]{:S(2)}) collective-permute-start(bf16[32,2048]{1,0:T(8,128)(2,1)} %get-tuple-element.22), channel_id=1, source_target_pairs={{0,8},{2,10},{4,12},{6,14},{8,0},{10,2},{12,4},{14,6},{1,9},{3,11}... | collective-permute-start | bytes 393224 | tf_op jit(solution)/shard_map/ppermute | solution.py:299
  41.5 20.7 %copy-start.3 = (bf16[32,2048]{1,0:T(8,128)(2,1)}, bf16[32,2048]{1,0:T(8,128)(2,1)S(1)}, u32[]{:S(2)}) copy-start(bf16[32,2048]{1,0:T(8,128)(2,1)S(1)} %collective-permute-done.11.refs_4_.rest_13_) | copy-start | bytes 393220
  41.5 16.2 %collective-permute-start.1 = (bf16[32,2048]{1,0:T(8,128)(2,1)}, bf16[32,2048]{1,0:T(8,128)(2,1)S(1)}, u32[]{:S(2)}, u32[]{:S(2)}) collective-permute-start(bf16[32,2048]{1,0:T(8,128)(2,1)} %get-tuple-element.23), channel_id=1, source_target_pairs={{0,12},{2,14},{4,8},{6,10},{8,4},{10,6},{12,0},{14,2},{1,13},{3,15... | collective-permute-start | bytes 393224 | tf_op jit(solution)/shard_map/ppermute | solution.py:299
  43.3 18.8 %copy-start.4 = (bf16[32,2048]{1,0:T(8,128)(2,1)}, bf16[32,2048]{1,0:T(8,128)(2,1)S(1)}, u32[]{:S(2)}) copy-start(bf16[32,2048]{1,0:T(8,128)(2,1)S(1)} %collective-permute-done.12.refs_5_.rest_14_) | copy-start | bytes 393220
  43.3 20.8 %collective-permute-start.2 = (bf16[32,2048]{1,0:T(8,128)(2,1)}, bf16[32,2048]{1,0:T(8,128)(2,1)S(1)}, u32[]{:S(2)}, u32[]{:S(2)}) collective-permute-start(bf16[32,2048]{1,0:T(8,128)(2,1)} %get-tuple-element.24), channel_id=1, source_target_pairs={{0,2},{2,0},{4,6},{6,4},{8,10},{10,8},{12,14},{14,12},{1,3},{3,1},... | collective-permute-start | bytes 393224 | tf_op jit(solution)/shard_map/ppermute | solution.py:299
  45.0 17.2 %copy-start.5 = (bf16[32,2048]{1,0:T(8,128)(2,1)}, bf16[32,2048]{1,0:T(8,128)(2,1)S(1)}, u32[]{:S(2)}) copy-start(bf16[32,2048]{1,0:T(8,128)(2,1)S(1)} %collective-permute-done.13.refs_6_.rest_15_) | copy-start | bytes 393220
  45.0 19.2 %collective-permute-start.3 = (bf16[32,2048]{1,0:T(8,128)(2,1)}, bf16[32,2048]{1,0:T(8,128)(2,1)S(1)}, u32[]{:S(2)}, u32[]{:S(2)}) collective-permute-start(bf16[32,2048]{1,0:T(8,128)(2,1)} %get-tuple-element.25), channel_id=1, source_target_pairs={{0,10},{2,8},{4,14},{6,12},{8,2},{10,0},{12,6},{14,4},{1,11},{3,9}... | collective-permute-start | bytes 393224 | tf_op jit(solution)/shard_map/ppermute | solution.py:299
  48.3 13.8 %copy-start.6 = (bf16[32,2048]{1,0:T(8,128)(2,1)}, bf16[32,2048]{1,0:T(8,128)(2,1)S(1)}, u32[]{:S(2)}) copy-start(bf16[32,2048]{1,0:T(8,128)(2,1)S(1)} %collective-permute-done.14.refs_7_.rest_16_) | copy-start | bytes 393220
  48.4 15.9 %collective-permute-start.4 = (bf16[32,2048]{1,0:T(8,128)(2,1)}, bf16[32,2048]{1,0:T(8,128)(2,1)S(1)}, u32[]{:S(2)}, u32[]{:S(2)}) collective-permute-start(bf16[32,2048]{1,0:T(8,128)(2,1)} %get-tuple-element.26), channel_id=1, source_target_pairs={{0,14},{2,12},{4,10},{6,8},{8,6},{10,4},{12,2},{14,0},{1,15},{3,13... | collective-permute-start | bytes 393224 | tf_op jit(solution)/shard_map/ppermute | solution.py:299
  57.7 9.2 %copy-start.7 = (bf16[32,2048]{1,0:T(8,128)(2,1)}, bf16[32,2048]{1,0:T(8,128)(2,1)S(1)}, u32[]{:S(2)}) copy-start(bf16[32,2048]{1,0:T(8,128)(2,1)S(1)} %collective-permute-done.refs_1_.rest_1_) | copy-start | bytes 393220
  57.7 6.6 %collective-permute-start.5 = (bf16[32,2048]{1,0:T(8,128)(2,1)}, bf16[32,2048]{1,0:T(8,128)(2,1)S(1)}, u32[]{:S(2)}, u32[]{:S(2)}) collective-permute-start(bf16[32,2048]{1,0:T(8,128)(2,1)} %get-tuple-element.27), channel_id=1, source_target_pairs={{0,4},{2,6},{4,0},{6,2},{8,12},{10,14},{12,8},{14,10},{1,5},{3,7},... | collective-permute-start | bytes 393224 | tf_op jit(solution)/shard_map/ppermute | solution.py:299
  57.7 9.2 %copy-start.8 = (bf16[32,2048]{1,0:T(8,128)(2,1)}, bf16[32,2048]{1,0:T(8,128)(2,1)S(1)}, u32[]{:S(2)}) copy-start(bf16[32,2048]{1,0:T(8,128)(2,1)S(1)} %collective-permute-done.1.refs_2_.rest_2_) | copy-start | bytes 393220
  57.7 9.2 %collective-permute-start.6 = (bf16[32,2048]{1,0:T(8,128)(2,1)}, bf16[32,2048]{1,0:T(8,128)(2,1)S(1)}, u32[]{:S(2)}, u32[]{:S(2)}) collective-permute-start(bf16[32,2048]{1,0:T(8,128)(2,1)} %get-tuple-element.28), channel_id=1, source_target_pairs={{0,6},{2,4},{4,2},{6,0},{8,14},{10,12},{12,10},{14,8},{1,7},{3,5},... | collective-permute-start | bytes 393224 | tf_op jit(solution)/shard_map/ppermute | solution.py:299
  64.1 2.8 %copy-start.9 = (bf16[32,2048]{1,0:T(8,128)(2,1)}, bf16[32,2048]{1,0:T(8,128)(2,1)S(1)}, u32[]{:S(2)}) copy-start(bf16[32,2048]{1,0:T(8,128)(2,1)S(1)} %collective-permute-done.2.refs_3_.rest_3_) | copy-start | bytes 393220
  64.1 5.4 %collective-permute-start.15 = (bf16[128,2048]{1,0:T(8,128)(2,1)}, bf16[128,2048]{1,0:T(8,128)(2,1)S(1)}, u32[]{:S(2)}, u32[]{:S(2)}) collective-permute-start(bf16[128,2048]{1,0:T(8,128)(2,1)} %shard_map.85), channel_id=1, source_target_pairs={{0,1},{1,0},{2,3},{3,2},{4,5},{5,4},{6,7},{7,6},{8,9},{9,8},{10,11... | collective-permute-start | bytes 1572872 | tf_op jit(solution)/shard_map/ppermute | solution.py:300
  64.2 2.7 %copy-start.10 = (bf16[32,2048]{1,0:T(8,128)(2,1)}, bf16[32,2048]{1,0:T(8,128)(2,1)S(1)}, u32[]{:S(2)}) copy-start(bf16[32,2048]{1,0:T(8,128)(2,1)S(1)} %collective-permute-done.3.refs_4_.rest_4_) | copy-start | bytes 393220
  64.2 2.7 %copy-start.11 = (bf16[32,2048]{1,0:T(8,128)(2,1)}, bf16[32,2048]{1,0:T(8,128)(2,1)S(1)}, u32[]{:S(2)}) copy-start(bf16[32,2048]{1,0:T(8,128)(2,1)S(1)} %collective-permute-done.4.refs_5_.rest_5_) | copy-start | bytes 393220
  64.3 2.6 %copy-start.12 = (bf16[32,2048]{1,0:T(8,128)(2,1)}, bf16[32,2048]{1,0:T(8,128)(2,1)S(1)}, u32[]{:S(2)}) copy-start(bf16[32,2048]{1,0:T(8,128)(2,1)S(1)} %collective-permute-done.5.refs_6_.rest_6_) | copy-start | bytes 393220
  69.4 2.2 %collective-permute-start.7 = (bf16[128,2048]{1,0:T(8,128)(2,1)}, bf16[128,2048]{1,0:T(8,128)(2,1)S(1)}, u32[]{:S(2)}, u32[]{:S(2)}) collective-permute-start(bf16[128,2048]{1,0:T(8,128)(2,1)} %shard_map.83), channel_id=1, source_target_pairs={{0,1},{1,0},{2,3},{3,2},{4,5},{5,4},{6,7},{7,6},{8,9},{9,8},{10,11... | collective-permute-start | bytes 1572872 | tf_op jit(solution)/shard_map/ppermute | solution.py:300
  69.5 2.1 %copy-start.14 = (bf16[128,2048]{1,0:T(8,128)(2,1)}, bf16[128,2048]{1,0:T(8,128)(2,1)S(1)}, u32[]{:S(2)}) copy-start(bf16[128,2048]{1,0:T(8,128)(2,1)S(1)} %collective-permute-done.15.rest_17_) | copy-start | bytes 1572868
  (2 other events, 1.4 us)

commit v6 on v5

--- a/solution.py
+++ b/solution.py
@@ -9,7 +9,8 @@
 from jax.sharding import PartitionSpec as P
 
 SPAN = 64
-GROUP = 4
+GROUPS = (2, 4)
+UNROLL = 2
 CHUNKS = (1, 1)
 DIRECT = 16
 KEY_PARTS = 2
@@ -44,6 +45,7 @@
 
 def attend_kernel(
     capacity,
+    group,
     first,
     me_ref,
     count_ref,
@@ -62,36 +64,41 @@
     past = prefix_hbm.shape[0]
     heads, dim, _ = key_weight_ref.shape
     here = pl.ds(first, heads)
-    stacks = heads // GROUP
+    step = group * UNROLL
+    steps = heads // step
     part = past // KEY_PARTS
 
-    def copy_stack(source, target, stack, index):
-        here, there = pl.ds(stack * GROUP, GROUP), pl.ds(first + stack * GROUP, GROUP)
-        return pltpu.make_async_copy(source.at[there], target.at[here], sem.at[index])
-
-    for_queries, for_values = [], []
-    for s in range(stacks):
-        here, there = pl.ds(s * GROUP * dim, GROUP * dim), pl.ds((first + s * GROUP) * dim, GROUP * dim)
-        for_queries += [
-            pltpu.make_async_copy(queries_hbm.at[:, there], queries_ref.at[:, here], sem.at[3 * s]),
-            copy_stack(key_weight_hbm, key_weight_ref, s, 3 * s + 1),
+    def copy_step(i):
+        def of(source, target, index):
+            here, there = pl.ds(i * step, step), pl.ds(first + i * step, step)
+            return pltpu.make_async_copy(source.at[there], target.at[here], sem.at[3 * i + index])
+
+        here, there = pl.ds(i * step * dim, step * dim), pl.ds((first + i * step) * dim, step * dim)
+        return [
+            pltpu.make_async_copy(queries_hbm.at[:, there], queries_ref.at[:, here], sem.at[3 * i]),
+            of(key_weight_hbm, key_weight_ref, 1),
+            of(value_weight_hbm, value_weight_ref, 2),
         ]
-        for_values.append(copy_stack(value_weight_hbm, value_weight_ref, s, 3 * s + 2))
+
     for_keys = [
         pltpu.make_async_copy(
             prefix_hbm.at[pl.ds(i * part, part)],
             keys_ref.at[pl.ds(i * part, part)],
-            sem.at[3 * stacks + i],
+            sem.at[3 * steps + i],
         )
         for i in range(KEY_PARTS)
     ]
     for_keys.append(
         pltpu.make_async_copy(
-            fresh_hbm, keys_ref.at[pl.ds(past, slots)], sem.at[3 * stacks + KEY_PARTS]
+            fresh_hbm, keys_ref.at[pl.ds(past, slots)], sem.at[3 * steps + KEY_PARTS]
         )
     )
-    for copy in for_queries[:2] + for_keys + for_queries[2:] + for_values:
+    opening = copy_step(0)
+    for copy in opening[:2] + for_keys + opening[2:]:
         copy.start()
+    for i in range(1, steps):
+        for copy in copy_step(i):
+            copy.start()
 
     count, size = count_ref[0], size_ref[0]
     lane = lax.broadcasted_iota(jnp.int32, (slots, past), 1)
@@ -104,37 +111,39 @@
     build_table(me_ref[0], count, routes_ref, table_ref, capacity)
 
     scale = math.log2(math.e) / math.sqrt(dim)
-
-    def score(stack):
-        for copy in for_queries[2 * stack : 2 * stack + 2] + (for_keys if stack == 0 else []):
+    for copy in for_keys:
+        copy.wait()
+
+    def body(i, carry):
+        for copy in copy_step(i):
             copy.wait()
-        lifted = []
-        for h in range(stack * GROUP, (stack + 1) * GROUP):
-            one = dot(queries_ref[:, h * dim : (h + 1) * dim], key_weight_ref[h])
-            lifted.append(one.astype(jnp.bfloat16))
-        lifted = jnp.concatenate(lifted, axis=0)
-        return lax.dot_general(lifted, keys_ref[...], NT, preferred_element_type=jnp.float32)
-
-    def finish(stack, scores):
         keys = keys_ref[...]
-        scores = scores.reshape(GROUP, slots, keys.shape[0])
-        scores = jnp.minimum(scores, cap_ref[...][None])
-        highest = jnp.max(scores, axis=-1, keepdims=True) * scale
-        weights = jnp.exp2(scores * scale - highest)
-        total = jnp.sum(weights, axis=-1, keepdims=True)
-        weights = weights.astype(jnp.bfloat16).reshape(GROUP * slots, keys.shape[0])
-        mixed = dot(weights, keys).astype(jnp.bfloat16)
-        for g in range(GROUP):
-            h = stack * GROUP + g
-            projected = dot(mixed[g * slots : (g + 1) * slots], value_weight_ref[h])
-            attended_ref[:, h * dim : (h + 1) * dim] = (projected / total[g]).astype(jnp.bfloat16)
-
-    before = score(0)
-    for stack in range(1, stacks + 1):
-        for_values[stack - 1].wait()
-        after = score(stack) if stack < stacks else None
-        finish(stack - 1, before)
-        before = after
+        scores = []
+        for stack in range(UNROLL):
+            lifted = []
+            for g in range(group):
+                h = i * step + stack * group + g
+                query = queries_ref[:, pl.ds(pl.multiple_of(h * dim, dim), dim)]
+                lifted.append(dot(query, key_weight_ref[h]).astype(jnp.bfloat16))
+            lifted = jnp.concatenate(lifted, axis=0)
+            scores.append(lax.dot_general(lifted, keys, NT, preferred_element_type=jnp.float32))
+        for stack in range(UNROLL):
+            score = scores[stack].reshape(group, slots, keys.shape[0])
+            score = jnp.minimum(score, cap_ref[...][None])
+            highest = jnp.max(score, axis=-1, keepdims=True) * scale
+            weights = jnp.exp2(score * scale - highest)
+            total = jnp.sum(weights, axis=-1, keepdims=True)
+            weights = weights.astype(jnp.bfloat16).reshape(group * slots, keys.shape[0])
+            mixed = dot(weights, keys).astype(jnp.bfloat16)
+            for g in range(group):
+                h = i * step + stack * group + g
+                projected = dot(mixed[g * slots : (g + 1) * slots], value_weight_ref[h])
+                attended_ref[:, pl.ds(pl.multiple_of(h * dim, dim), dim)] = (
+                    projected / total[g]
+                ).astype(jnp.bfloat16)
+        return carry
+
+    lax.fori_loop(0, steps, body, 0)
     grouped = dot(table_ref[...], attended_ref[...]).astype(jnp.bfloat16)
     rows = out_refs[0].shape[0]
     for k, out_ref in enumerate(out_refs):
@@ -142,7 +151,20 @@
 
 
 def attend(
-    first, heads, me, queries, key_weight, value_weight, prefix, fresh, count, size, routes, experts, pieces
+    group,
+    first,
+    heads,
+    me,
+    queries,
+    key_weight,
+    value_weight,
+    prefix,
+    fresh,
+    count,
+    size,
+    routes,
+    experts,
+    pieces,
 ):
     slots = queries.shape[0]
     _, dim, latent = key_weight.shape
@@ -153,7 +175,7 @@
     hbm = pl.BlockSpec(memory_space=pltpu.HBM)
     piece = (places // pieces, heads * dim)
     return pl.pallas_call(
-        functools.partial(attend_kernel, places // experts, first),
+        functools.partial(attend_kernel, places // experts, group, first),
         in_specs=[smem, smem, smem, vmem, hbm, hbm, hbm, hbm, hbm],
         out_specs=[vmem] * pieces,
         out_shape=[jax.ShapeDtypeStruct(piece, jnp.bfloat16)] * pieces,
@@ -165,7 +187,7 @@
             pltpu.VMEM((slots, keys), jnp.float32),
             pltpu.VMEM((places, slots), jnp.bfloat16),
             pltpu.VMEM((slots, heads * dim), jnp.bfloat16),
-            pltpu.SemaphoreType.DMA((3 * heads // GROUP + KEY_PARTS + 1,)),
+            pltpu.SemaphoreType.DMA((3 * heads // (group * UNROLL) + KEY_PARTS + 1,)),
         ],
         compiler_params=pltpu.CompilerParams(vmem_limit_bytes=VMEM),
         cost_estimate=pl.CostEstimate(
@@ -275,8 +297,9 @@
     shares = [heads * share // sum(CHUNKS) for share in CHUNKS]
     chunks, plan = [], []
     first = 0
-    for share in shares:
+    for group, share in zip(GROUPS, shares):
         outgoing = attend(
+            group,
             first,
             share,
             me,

time: 76.1 us -> 75.5 us (level)
  Pallas kernels: 32.6 us -> 31.7 us
    pallas_call x2, Pallas kernels: 25.6 us -> 24.7 us  [attend(): pl.pallas_call(functools.partial(attend_kernel, places // experts, group,...]
where the time goes in v6:
time: 75.5 us; the launch traced here: 75.1 us
  Pallas kernels  31.7 us (42%)
  starting transfers between devices  29.1 us (39%)
  waiting for transfers between devices  11.3 us (15%)
  between operations  1.54 us (2%)
  local copies, waits for them, and re-layouts  1.45 us (2%)
    ppermute x14, starting transfers between devices, local(): pieces.append(lax.ppermute(outgoing[j], 'dp', pairs))  28.9 us
    pallas_call x2, Pallas kernels, attend(): pl.pallas_call(functools.partial(attend_kernel, places // experts, group,...  24.7 us
    ppermute x14, waiting for transfers between devices, local(): pieces.append(lax.ppermute(outgoing[j], 'dp', pairs))  9.19 us
    pallas_call x2, Pallas kernels, pass_on(): pl.pallas_call(functools.partial(pass_on_kernel, cores), in_specs=[pl.Blo...  3.84 us
    pallas_call x1, Pallas kernels, assemble(): pl.pallas_call(functools.partial(place_kernel, plan, cores), in_specs=[pl...  3.16 us
    ppermute x2, waiting for transfers between devices, local(): lax.ppermute(pass_on(pieces, cores), 'ep', [(i, i ^ 1) for i in range(cor...  2.09 us
  transfers between devices with their start and end apart: 16, of which 4 were waited for; matrix products, arithmetic and copies ran while one was open for 0% of the time, Pallas kernels for 22%

profile of v6, /device:TPU:0, one launch (start us, length us, event | category | flops | bytes accessed | tf_op | source)
XLA Modules:
  0.0 75.1 jit_solution(12032341487616635627)
XLA Ops:
  1.3 12.0 %shard_map.84 = (bf16[32,2048]{1,0:T(8,128)(2,1)}, bf16[32,2048]{1,0:T(8,128)(2,1)}, bf16[32,2048]{1,0:T(8,128)(2,1)}, bf16[32,2048]{1,0:T(8,128)(2,1)}, bf16[32...) custom-call(s32[1]{0:T(128)} %bitcast.me_ref, ...), custom_call_target="tpu_custom_call" | custom-call | flops 4831838208 | bytes 4194304 | tf_op jit(solution)/shard_map/pallas_call | solution.py:177
  13.3 4.1 %collective-permute-start.8 = (bf16[32,2048]{1,0:T(8,128)(2,1)}, bf16[32,2048]{1,0:T(8,128)(2,1)S(1)}, u32[]{:S(2)}, u32[]{:S(2)}) collective-permute-start(bf16[32,2048]{1,0:T(8,128)(2,1)} %get-tuple-element.30), channel_id=1, source_target_pairs={{0,8},{2,10},{4,12},{6,14},{8,0},{10,2},{12,4},{14,6},{1,9},{3,11}... | collective-permute-start | bytes 393224 | tf_op jit(solution)/shard_map/ppermute | solution.py:322
  17.4 1.4 %collective-permute-start.9 = (bf16[32,2048]{1,0:T(8,128)(2,1)}, bf16[32,2048]{1,0:T(8,128)(2,1)S(1)}, u32[]{:S(2)}, u32[]{:S(2)}) collective-permute-start(bf16[32,2048]{1,0:T(8,128)(2,1)} %get-tuple-element.31), channel_id=1, source_target_pairs={{0,12},{2,14},{4,8},{6,10},{8,4},{10,6},{12,0},{14,2},{1,13},{3,15... | collective-permute-start | bytes 393224 | tf_op jit(solution)/shard_map/ppermute | solution.py:322
  18.8 1.5 %collective-permute-start.10 = (bf16[32,2048]{1,0:T(8,128)(2,1)}, bf16[32,2048]{1,0:T(8,128)(2,1)S(1)}, u32[]{:S(2)}, u32[]{:S(2)}) collective-permute-start(bf16[32,2048]{1,0:T(8,128)(2,1)} %get-tuple-element.32), channel_id=1, source_target_pairs={{0,2},{2,0},{4,6},{6,4},{8,10},{10,8},{12,14},{14,12},{1,3},{3,1},... | collective-permute-start | bytes 393224 | tf_op jit(solution)/shard_map/ppermute | solution.py:322
  20.3 1.6 %collective-permute-start.11 = (bf16[32,2048]{1,0:T(8,128)(2,1)}, bf16[32,2048]{1,0:T(8,128)(2,1)S(1)}, u32[]{:S(2)}, u32[]{:S(2)}) collective-permute-start(bf16[32,2048]{1,0:T(8,128)(2,1)} %get-tuple-element.33), channel_id=1, source_target_pairs={{0,10},{2,8},{4,14},{6,12},{8,2},{10,0},{12,6},{14,4},{1,11},{3,9}... | collective-permute-start | bytes 393224 | tf_op jit(solution)/shard_map/ppermute | solution.py:322
  21.9 1.9 %collective-permute-start.12 = (bf16[32,2048]{1,0:T(8,128)(2,1)}, bf16[32,2048]{1,0:T(8,128)(2,1)S(1)}, u32[]{:S(2)}, u32[]{:S(2)}) collective-permute-start(bf16[32,2048]{1,0:T(8,128)(2,1)} %get-tuple-element.34), channel_id=1, source_target_pairs={{0,14},{2,12},{4,10},{6,8},{8,6},{10,4},{12,2},{14,0},{1,15},{3,13... | collective-permute-start | bytes 393224 | tf_op jit(solution)/shard_map/ppermute | solution.py:322
  23.8 12.7 %shard_map.82 = (bf16[32,2048]{1,0:T(8,128)(2,1)}, bf16[32,2048]{1,0:T(8,128)(2,1)}, bf16[32,2048]{1,0:T(8,128)(2,1)}, bf16[32,2048]{1,0:T(8,128)(2,1)}, bf16[32...) custom-call(s32[1]{0:T(128)} %bitcast.me_ref, ...), custom_call_target="tpu_custom_call" | custom-call | flops 4831838208 | bytes 4194304 | tf_op jit(solution)/shard_map/pallas_call | solution.py:177
  36.5 0.0 collective-permute-done.8.refs_1_.rest_10_
  36.6 1.0 %collective-permute-start.13 = (bf16[32,2048]{1,0:T(8,128)(2,1)S(1)}, bf16[32,2048]{1,0:T(8,128)(2,1)S(1)}, u32[]{:S(2)}, u32[]{:S(2)}) collective-permute-start(bf16[32,2048]{1,0:T(8,128)(2,1)S(1)} %copy-done.17), channel_id=1, source_target_pairs={{0,4},{2,6},{4,0},{6,2},{8,12},{10,14},{12,8},{14,10},{1,5},{3,7},... | collective-permute-start | bytes 393224 | tf_op jit(solution)/shard_map/ppermute | solution.py:322
  37.5 0.0 collective-permute-done.9.refs_2_.rest_11_
  37.5 1.2 %collective-permute-start.14 = (bf16[32,2048]{1,0:T(8,128)(2,1)S(1)}, bf16[32,2048]{1,0:T(8,128)(2,1)S(1)}, u32[]{:S(2)}, u32[]{:S(2)}) collective-permute-start(bf16[32,2048]{1,0:T(8,128)(2,1)S(1)} %copy-done.16), channel_id=1, source_target_pairs={{0,6},{2,4},{4,2},{6,0},{8,14},{10,12},{12,10},{14,8},{1,7},{3,5},... | collective-permute-start | bytes 393224 | tf_op jit(solution)/shard_map/ppermute | solution.py:322
  38.7 1.9 %collective-permute-start = (bf16[32,2048]{1,0:T(8,128)(2,1)}, bf16[32,2048]{1,0:T(8,128)(2,1)S(1)}, u32[]{:S(2)}, u32[]{:S(2)}) collective-permute-start(bf16[32,2048]{1,0:T(8,128)(2,1)} %get-tuple-element.22), channel_id=1, source_target_pairs={{0,8},{2,10},{4,12},{6,14},{8,0},{10,2},{12,4},{14,6},{1,9},{3,11}... | collective-permute-start | bytes 393224 | tf_op jit(solution)/shard_map/ppermute | solution.py:322
  40.6 2.0 %collective-permute-start.1 = (bf16[32,2048]{1,0:T(8,128)(2,1)}, bf16[32,2048]{1,0:T(8,128)(2,1)S(1)}, u32[]{:S(2)}, u32[]{:S(2)}) collective-permute-start(bf16[32,2048]{1,0:T(8,128)(2,1)} %get-tuple-element.23), channel_id=1, source_target_pairs={{0,12},{2,14},{4,8},{6,10},{8,4},{10,6},{12,0},{14,2},{1,13},{3,15... | collective-permute-start | bytes 393224 | tf_op jit(solution)/shard_map/ppermute | solution.py:322
  42.6 0.8 %collective-permute-start.2 = (bf16[32,2048]{1,0:T(8,128)(2,1)}, bf16[32,2048]{1,0:T(8,128)(2,1)S(1)}, u32[]{:S(2)}, u32[]{:S(2)}) collective-permute-start(bf16[32,2048]{1,0:T(8,128)(2,1)} %get-tuple-element.24), channel_id=1, source_target_pairs={{0,2},{2,0},{4,6},{6,4},{8,10},{10,8},{12,14},{14,12},{1,3},{3,1},... | collective-permute-start | bytes 393224 | tf_op jit(solution)/shard_map/ppermute | solution.py:322
  43.5 0.8 %collective-permute-done.13.refs_6_.rest_15_ = bf16[32,2048]{1,0:T(8,128)(2,1)S(1)} collective-permute-done((bf16[32,2048]{1,0:T(8,128)(2,1)S(1)}, bf16[32,2048]{1,0:T(8,128)(2,1)S(1)}, u32[]{:S(2)}, u32[]{:S(2)}) %collective-permute-start.13) | collective-permute-done | bytes 131104 | tf_op jit(solution)/shard_map/ppermute | solution.py:322
  44.2 3.6 %collective-permute-start.3 = (bf16[32,2048]{1,0:T(8,128)(2,1)}, bf16[32,2048]{1,0:T(8,128)(2,1)S(1)}, u32[]{:S(2)}, u32[]{:S(2)}) collective-permute-start(bf16[32,2048]{1,0:T(8,128)(2,1)} %get-tuple-element.25), channel_id=1, source_target_pairs={{0,10},{2,8},{4,14},{6,12},{8,2},{10,0},{12,6},{14,4},{1,11},{3,9}... | collective-permute-start | bytes 393224 | tf_op jit(solution)/shard_map/ppermute | solution.py:322
  47.9 0.0 collective-permute-done.14.refs_7_.rest_16_
  47.9 3.3 %collective-permute-start.4 = (bf16[32,2048]{1,0:T(8,128)(2,1)}, bf16[32,2048]{1,0:T(8,128)(2,1)S(1)}, u32[]{:S(2)}, u32[]{:S(2)}) collective-permute-start(bf16[32,2048]{1,0:T(8,128)(2,1)} %get-tuple-element.26), channel_id=1, source_target_pairs={{0,14},{2,12},{4,10},{6,8},{8,6},{10,4},{12,2},{14,0},{1,15},{3,13... | collective-permute-start | bytes 393224 | tf_op jit(solution)/shard_map/ppermute | solution.py:322
  51.1 5.7 %collective-permute-done.refs_1_.rest_1_ = bf16[32,2048]{1,0:T(8,128)(2,1)S(1)} collective-permute-done((bf16[32,2048]{1,0:T(8,128)(2,1)}, bf16[32,2048]{1,0:T(8,128)(2,1)S(1)}, u32[]{:S(2)}, u32[]{:S(2)}) %collective-permute-start) | collective-permute-done | bytes 131104 | tf_op jit(solution)/shard_map/ppermute | solution.py:322
  56.8 0.0 collective-permute-start.5
  56.8 0.0 collective-permute-done.1.refs_2_.rest_2_
  56.8 4.7 %collective-permute-start.6 = (bf16[32,2048]{1,0:T(8,128)(2,1)}, bf16[32,2048]{1,0:T(8,128)(2,1)S(1)}, u32[]{:S(2)}, u32[]{:S(2)}) collective-permute-start(bf16[32,2048]{1,0:T(8,128)(2,1)} %get-tuple-element.28), channel_id=1, source_target_pairs={{0,6},{2,4},{4,2},{6,0},{8,14},{10,12},{12,10},{14,8},{1,7},{3,5},... | collective-permute-start | bytes 393224 | tf_op jit(solution)/shard_map/ppermute | solution.py:322
  61.6 1.9 %shard_map.85 = bf16[128,2048]{1,0:T(8,128)(2,1)} custom-call(bf16[32,2048]{1,0:T(8,128)(2,1)} %get-tuple-element.29.refs_0_.rest_9_, bf16[32,2048]{1,0:T(8,128)(2,1)} %copy-done, bf16[32,2048]{1,0:T(8,128)(2,1)} %copy-done.1, bf16[32,2048]{1,0:T(8,128)(2,1)} %copy-done.2, bf16[32,2048]{1,0:T(8,128)(2,1)} %copy-done.3, bf16[32,2048]{1,0:T(8,128)(2,1)} %copy-done.4, ...), custom_call_target="tpu_custom_call" | custom-call | tf_op jit(solution)/shard_map/pallas_call | solution.py:225
  63.5 0.0 collective-permute-done.2.refs_3_.rest_3_
  63.5 0.1 collective-permute-start.15
  63.7 2.7 %collective-permute-done.6.refs_7_.rest_7_ = bf16[32,2048]{1,0:T(8,128)(2,1)S(1)} collective-permute-done((bf16[32,2048]{1,0:T(8,128)(2,1)}, bf16[32,2048]{1,0:T(8,128)(2,1)S(1)}, u32[]{:S(2)}, u32[]{:S(2)}) %collective-permute-start.6) | collective-permute-done | bytes 131104 | tf_op jit(solution)/shard_map/ppermute | solution.py:322
  66.4 0.6 copy-done.13
  67.0 1.9 %shard_map.83 = bf16[128,2048]{1,0:T(8,128)(2,1)} custom-call(bf16[32,2048]{1,0:T(8,128)(2,1)} %get-tuple-element.21.refs_0_.rest_0_, bf16[32,2048]{1,0:T(8,128)(2,1)} %copy-done.7, bf16[32,2048]{1,0:T(8,128)(2,1)} %copy-done.8, bf16[32,2048]{1,0:T(8,128)(2,1)} %copy-done.9, bf16[32,2048]{1,0:T(8,128)(2,1)} %copy-done.10, bf16[32,2048]{1,0:T(8,128)(2,1)} %copy-done.11, ...), custom_call_target="tpu_custom_call" | custom-call | tf_op jit(solution)/shard_map/pallas_call | solution.py:225
  69.0 0.1 collective-permute-start.7
  69.1 2.1 %collective-permute-done.7.rest_8_ = bf16[128,2048]{1,0:T(8,128)(2,1)S(1)} collective-permute-done((bf16[128,2048]{1,0:T(8,128)(2,1)}, bf16[128,2048]{1,0:T(8,128)(2,1)S(1)}, u32[]{:S(2)}, u32[]{:S(2)}) %collective-permute-start.7) | collective-permute-done | bytes 524320 | tf_op jit(solution)/shard_map/ppermute | solution.py:323
  71.2 0.8 %copy-done.15 = bf16[128,2048]{1,0:T(8,128)(2,1)} copy-done((bf16[128,2048]{1,0:T(8,128)(2,1)}, bf16[128,2048]{1,0:T(8,128)(2,1)S(1)}, u32[]{:S(2)}) %copy-start.15) | copy-done | bytes 524312
  71.9 3.2 %shard_map.86 = bf16[1,8,16,8192]{3,2,1,0:T(8,128)(2,1)} custom-call(s32[1]{0:T(128)} %bitcast.me_ref, bf16[32,2048]{1,0:T(8,128)(2,1)} %get-tuple-element.21.refs_0_.rest_0_, bf16[32,2048]{1,0:T(8,128)(2,1)} %copy-done.7, bf16[32,2048]{1,0:T(8,128)(2,1)} %copy-done.8, bf16[32,2048]{1,0:T(8,128)(2,1)} %copy-done.9, bf16[32,2048]{1,0:T(8,128)(2,1)} %copy-done.10, ...), custom_call_target="tpu_custom_call" | custom-call | tf_op jit(solution)/shard_map/pallas_call | solution.py:258
  (41 shorter events, 0.1 us)
Async XLA Ops:
  13.3 23.2 %collective-permute-start.8 = (bf16[32,2048]{1,0:T(8,128)(2,1)}, bf16[32,2048]{1,0:T(8,128)(2,1)S(1)}, u32[]{:S(2)}, u32[]{:S(2)}) collective-permute-start(bf16[32,2048]{1,0:T(8,128)(2,1)} %get-tuple-element.30), channel_id=1, source_target_pairs={{0,8},{2,10},{4,12},{6,14},{8,0},{10,2},{12,4},{14,6},{1,9},{3,11}... | collective-permute-start | bytes 393224 | tf_op jit(solution)/shard_map/ppermute | solution.py:322
  17.4 20.1 %collective-permute-start.9 = (bf16[32,2048]{1,0:T(8,128)(2,1)}, bf16[32,2048]{1,0:T(8,128)(2,1)S(1)}, u32[]{:S(2)}, u32[]{:S(2)}) collective-permute-start(bf16[32,2048]{1,0:T(8,128)(2,1)} %get-tuple-element.31), channel_id=1, source_target_pairs={{0,12},{2,14},{4,8},{6,10},{8,4},{10,6},{12,0},{14,2},{1,13},{3,15... | collective-permute-start | bytes 393224 | tf_op jit(solution)/shard_map/ppermute | solution.py:322
  18.8 19.9 %collective-permute-start.10 = (bf16[32,2048]{1,0:T(8,128)(2,1)}, bf16[32,2048]{1,0:T(8,128)(2,1)S(1)}, u32[]{:S(2)}, u32[]{:S(2)}) collective-permute-start(bf16[32,2048]{1,0:T(8,128)(2,1)} %get-tuple-element.32), channel_id=1, source_target_pairs={{0,2},{2,0},{4,6},{6,4},{8,10},{10,8},{12,14},{14,12},{1,3},{3,1},... | collective-permute-start | bytes 393224 | tf_op jit(solution)/shard_map/ppermute | solution.py:322
  20.3 20.3 %collective-permute-start.11 = (bf16[32,2048]{1,0:T(8,128)(2,1)}, bf16[32,2048]{1,0:T(8,128)(2,1)S(1)}, u32[]{:S(2)}, u32[]{:S(2)}) collective-permute-start(bf16[32,2048]{1,0:T(8,128)(2,1)} %get-tuple-element.33), channel_id=1, source_target_pairs={{0,10},{2,8},{4,14},{6,12},{8,2},{10,0},{12,6},{14,4},{1,11},{3,9}... | collective-permute-start | bytes 393224 | tf_op jit(solution)/shard_map/ppermute | solution.py:322
  21.9 14.6 %copy-start.17 = (bf16[32,2048]{1,0:T(8,128)(2,1)S(1)}, bf16[32,2048]{1,0:T(8,128)(2,1)}, u32[]{:S(2)}) copy-start(bf16[32,2048]{1,0:T(8,128)(2,1)} %get-tuple-element.35) | copy-start | bytes 393220
  21.9 15.6 %copy-start.16 = (bf16[32,2048]{1,0:T(8,128)(2,1)S(1)}, bf16[32,2048]{1,0:T(8,128)(2,1)}, u32[]{:S(2)}) copy-start(bf16[32,2048]{1,0:T(8,128)(2,1)} %get-tuple-element.36) | copy-start | bytes 393220
  21.9 20.7 %collective-permute-start.12 = (bf16[32,2048]{1,0:T(8,128)(2,1)}, bf16[32,2048]{1,0:T(8,128)(2,1)S(1)}, u32[]{:S(2)}, u32[]{:S(2)}) collective-permute-start(bf16[32,2048]{1,0:T(8,128)(2,1)} %get-tuple-element.34), channel_id=1, source_target_pairs={{0,14},{2,12},{4,10},{6,8},{8,6},{10,4},{12,2},{14,0},{1,15},{3,13... | collective-permute-start | bytes 393224 | tf_op jit(solution)/shard_map/ppermute | solution.py:322
  36.5 25.0 %copy-start = (bf16[32,2048]{1,0:T(8,128)(2,1)}, bf16[32,2048]{1,0:T(8,128)(2,1)S(1)}, u32[]{:S(2)}) copy-start(bf16[32,2048]{1,0:T(8,128)(2,1)S(1)} %collective-permute-done.8.refs_1_.rest_10_) | copy-start | bytes 393220
  36.6 7.7 %collective-permute-start.13 = (bf16[32,2048]{1,0:T(8,128)(2,1)S(1)}, bf16[32,2048]{1,0:T(8,128)(2,1)S(1)}, u32[]{:S(2)}, u32[]{:S(2)}) collective-permute-start(bf16[32,2048]{1,0:T(8,128)(2,1)S(1)} %copy-done.17), channel_id=1, source_target_pairs={{0,4},{2,6},{4,0},{6,2},{8,12},{10,14},{12,8},{14,10},{1,5},{3,7},... | collective-permute-start | bytes 393224 | tf_op jit(solution)/shard_map/ppermute | solution.py:322
  37.5 24.0 %copy-start.1 = (bf16[32,2048]{1,0:T(8,128)(2,1)}, bf16[32,2048]{1,0:T(8,128)(2,1)S(1)}, u32[]{:S(2)}) copy-start(bf16[32,2048]{1,0:T(8,128)(2,1)S(1)} %collective-permute-done.9.refs_2_.rest_11_) | copy-start | bytes 393220
  37.5 10.3 %collective-permute-start.14 = (bf16[32,2048]{1,0:T(8,128)(2,1)S(1)}, bf16[32,2048]{1,0:T(8,128)(2,1)S(1)}, u32[]{:S(2)}, u32[]{:S(2)}) collective-permute-start(bf16[32,2048]{1,0:T(8,128)(2,1)S(1)} %copy-done.16), channel_id=1, source_target_pairs={{0,6},{2,4},{4,2},{6,0},{8,14},{10,12},{12,10},{14,8},{1,7},{3,5},... | collective-permute-start | bytes 393224 | tf_op jit(solution)/shard_map/ppermute | solution.py:322
  38.7 22.9 %copy-start.2 = (bf16[32,2048]{1,0:T(8,128)(2,1)}, bf16[32,2048]{1,0:T(8,128)(2,1)S(1)}, u32[]{:S(2)}) copy-start(bf16[32,2048]{1,0:T(8,128)(2,1)S(1)} %collective-permute-done.10.refs_3_.rest_12_) | copy-start | bytes 393220
  38.7 18.1 %collective-permute-start = (bf16[32,2048]{1,0:T(8,128)(2,1)}, bf16[32,2048]{1,0:T(8,128)(2,1)S(1)}, u32[]{:S(2)}, u32[]{:S(2)}) collective-permute-start(bf16[32,2048]{1,0:T(8,128)(2,1)} %get-tuple-element.22), channel_id=1, source_target_pairs={{0,8},{2,10},{4,12},{6,14},{8,0},{10,2},{12,4},{14,6},{1,9},{3,11}... | collective-permute-start | bytes 393224 | tf_op jit(solution)/shard_map/ppermute | solution.py:322
  40.6 21.0 %copy-start.3 = (bf16[32,2048]{1,0:T(8,128)(2,1)}, bf16[32,2048]{1,0:T(8,128)(2,1)S(1)}, u32[]{:S(2)}) copy-start(bf16[32,2048]{1,0:T(8,128)(2,1)S(1)} %collective-permute-done.11.refs_4_.rest_13_) | copy-start | bytes 393220
  40.6 16.3 %collective-permute-start.1 = (bf16[32,2048]{1,0:T(8,128)(2,1)}, bf16[32,2048]{1,0:T(8,128)(2,1)S(1)}, u32[]{:S(2)}, u32[]{:S(2)}) collective-permute-start(bf16[32,2048]{1,0:T(8,128)(2,1)} %get-tuple-element.23), channel_id=1, source_target_pairs={{0,12},{2,14},{4,8},{6,10},{8,4},{10,6},{12,0},{14,2},{1,13},{3,15... | collective-permute-start | bytes 393224 | tf_op jit(solution)/shard_map/ppermute | solution.py:322
  42.6 18.9 %copy-start.4 = (bf16[32,2048]{1,0:T(8,128)(2,1)}, bf16[32,2048]{1,0:T(8,128)(2,1)S(1)}, u32[]{:S(2)}) copy-start(bf16[32,2048]{1,0:T(8,128)(2,1)S(1)} %collective-permute-done.12.refs_5_.rest_14_) | copy-start | bytes 393220
  42.6 20.9 %collective-permute-start.2 = (bf16[32,2048]{1,0:T(8,128)(2,1)}, bf16[32,2048]{1,0:T(8,128)(2,1)S(1)}, u32[]{:S(2)}, u32[]{:S(2)}) collective-permute-start(bf16[32,2048]{1,0:T(8,128)(2,1)} %get-tuple-element.24), channel_id=1, source_target_pairs={{0,2},{2,0},{4,6},{6,4},{8,10},{10,8},{12,14},{14,12},{1,3},{3,1},... | collective-permute-start | bytes 393224 | tf_op jit(solution)/shard_map/ppermute | solution.py:322
  44.2 17.4 %copy-start.5 = (bf16[32,2048]{1,0:T(8,128)(2,1)}, bf16[32,2048]{1,0:T(8,128)(2,1)S(1)}, u32[]{:S(2)}) copy-start(bf16[32,2048]{1,0:T(8,128)(2,1)S(1)} %collective-permute-done.13.refs_6_.rest_15_) | copy-start | bytes 393220
  44.2 19.4 %collective-permute-start.3 = (bf16[32,2048]{1,0:T(8,128)(2,1)}, bf16[32,2048]{1,0:T(8,128)(2,1)S(1)}, u32[]{:S(2)}, u32[]{:S(2)}) collective-permute-start(bf16[32,2048]{1,0:T(8,128)(2,1)} %get-tuple-element.25), channel_id=1, source_target_pairs={{0,10},{2,8},{4,14},{6,12},{8,2},{10,0},{12,6},{14,4},{1,11},{3,9}... | collective-permute-start | bytes 393224 | tf_op jit(solution)/shard_map/ppermute | solution.py:322
  47.9 13.7 %copy-start.6 = (bf16[32,2048]{1,0:T(8,128)(2,1)}, bf16[32,2048]{1,0:T(8,128)(2,1)S(1)}, u32[]{:S(2)}) copy-start(bf16[32,2048]{1,0:T(8,128)(2,1)S(1)} %collective-permute-done.14.refs_7_.rest_16_) | copy-start | bytes 393220
  47.9 15.8 %collective-permute-start.4 = (bf16[32,2048]{1,0:T(8,128)(2,1)}, bf16[32,2048]{1,0:T(8,128)(2,1)S(1)}, u32[]{:S(2)}, u32[]{:S(2)}) collective-permute-start(bf16[32,2048]{1,0:T(8,128)(2,1)} %get-tuple-element.26), channel_id=1, source_target_pairs={{0,14},{2,12},{4,10},{6,8},{8,6},{10,4},{12,2},{14,0},{1,15},{3,13... | collective-permute-start | bytes 393224 | tf_op jit(solution)/shard_map/ppermute | solution.py:322
  56.8 9.6 %copy-start.7 = (bf16[32,2048]{1,0:T(8,128)(2,1)}, bf16[32,2048]{1,0:T(8,128)(2,1)S(1)}, u32[]{:S(2)}) copy-start(bf16[32,2048]{1,0:T(8,128)(2,1)S(1)} %collective-permute-done.refs_1_.rest_1_) | copy-start | bytes 393220
  56.8 6.8 %collective-permute-start.5 = (bf16[32,2048]{1,0:T(8,128)(2,1)}, bf16[32,2048]{1,0:T(8,128)(2,1)S(1)}, u32[]{:S(2)}, u32[]{:S(2)}) collective-permute-start(bf16[32,2048]{1,0:T(8,128)(2,1)} %get-tuple-element.27), channel_id=1, source_target_pairs={{0,4},{2,6},{4,0},{6,2},{8,12},{10,14},{12,8},{14,10},{1,5},{3,7},... | collective-permute-start | bytes 393224 | tf_op jit(solution)/shard_map/ppermute | solution.py:322
  56.8 9.6 %copy-start.8 = (bf16[32,2048]{1,0:T(8,128)(2,1)}, bf16[32,2048]{1,0:T(8,128)(2,1)S(1)}, u32[]{:S(2)}) copy-start(bf16[32,2048]{1,0:T(8,128)(2,1)S(1)} %collective-permute-done.1.refs_2_.rest_2_) | copy-start | bytes 393220
  56.8 9.5 %collective-permute-start.6 = (bf16[32,2048]{1,0:T(8,128)(2,1)}, bf16[32,2048]{1,0:T(8,128)(2,1)S(1)}, u32[]{:S(2)}, u32[]{:S(2)}) collective-permute-start(bf16[32,2048]{1,0:T(8,128)(2,1)} %get-tuple-element.28), channel_id=1, source_target_pairs={{0,6},{2,4},{4,2},{6,0},{8,14},{10,12},{12,10},{14,8},{1,7},{3,5},... | collective-permute-start | bytes 393224 | tf_op jit(solution)/shard_map/ppermute | solution.py:322
  63.5 2.9 %copy-start.9 = (bf16[32,2048]{1,0:T(8,128)(2,1)}, bf16[32,2048]{1,0:T(8,128)(2,1)S(1)}, u32[]{:S(2)}) copy-start(bf16[32,2048]{1,0:T(8,128)(2,1)S(1)} %collective-permute-done.2.refs_3_.rest_3_) | copy-start | bytes 393220
  63.5 5.5 %collective-permute-start.15 = (bf16[128,2048]{1,0:T(8,128)(2,1)}, bf16[128,2048]{1,0:T(8,128)(2,1)S(1)}, u32[]{:S(2)}, u32[]{:S(2)}) collective-permute-start(bf16[128,2048]{1,0:T(8,128)(2,1)} %shard_map.85), channel_id=1, source_target_pairs={{0,1},{1,0},{2,3},{3,2},{4,5},{5,4},{6,7},{7,6},{8,9},{9,8},{10,11... | collective-permute-start | bytes 1572872 | tf_op jit(solution)/shard_map/ppermute | solution.py:323
  63.6 2.8 %copy-start.10 = (bf16[32,2048]{1,0:T(8,128)(2,1)}, bf16[32,2048]{1,0:T(8,128)(2,1)S(1)}, u32[]{:S(2)}) copy-start(bf16[32,2048]{1,0:T(8,128)(2,1)S(1)} %collective-permute-done.3.refs_4_.rest_4_) | copy-start | bytes 393220
  63.7 2.8 %copy-start.11 = (bf16[32,2048]{1,0:T(8,128)(2,1)}, bf16[32,2048]{1,0:T(8,128)(2,1)S(1)}, u32[]{:S(2)}) copy-start(bf16[32,2048]{1,0:T(8,128)(2,1)S(1)} %collective-permute-done.4.refs_5_.rest_5_) | copy-start | bytes 393220
  63.7 2.7 %copy-start.12 = (bf16[32,2048]{1,0:T(8,128)(2,1)}, bf16[32,2048]{1,0:T(8,128)(2,1)S(1)}, u32[]{:S(2)}) copy-start(bf16[32,2048]{1,0:T(8,128)(2,1)S(1)} %collective-permute-done.5.refs_6_.rest_6_) | copy-start | bytes 393220
  69.0 2.2 %collective-permute-start.7 = (bf16[128,2048]{1,0:T(8,128)(2,1)}, bf16[128,2048]{1,0:T(8,128)(2,1)S(1)}, u32[]{:S(2)}, u32[]{:S(2)}) collective-permute-start(bf16[128,2048]{1,0:T(8,128)(2,1)} %shard_map.83), channel_id=1, source_target_pairs={{0,1},{1,0},{2,3},{3,2},{4,5},{5,4},{6,7},{7,6},{8,9},{9,8},{10,11... | collective-permute-start | bytes 1572872 | tf_op jit(solution)/shard_map/ppermute | solution.py:323
  69.0 2.1 %copy-start.14 = (bf16[128,2048]{1,0:T(8,128)(2,1)}, bf16[128,2048]{1,0:T(8,128)(2,1)S(1)}, u32[]{:S(2)}) copy-start(bf16[128,2048]{1,0:T(8,128)(2,1)S(1)} %collective-permute-done.15.rest_17_) | copy-start | bytes 1572868
  (2 other events, 1.4 us)

commit v7 on v6

--- a/solution.py
+++ b/solution.py
@@ -9,12 +9,12 @@
 from jax.sharding import PartitionSpec as P
 
 SPAN = 64
-GROUPS = (2, 4)
-UNROLL = 2
+STACKS = ((2, 2), (1, 4))
 CHUNKS = (1, 1)
 DIRECT = 16
 KEY_PARTS = 2
 VMEM = 58 * 1024 * 1024
+SHORT = pl.CostEstimate(flops=0, bytes_accessed=0, transcendentals=0)
 MASKED = -1e30
 OPEN = 3e38
 NT = (((1,), (1,)), ((), ()))
@@ -46,6 +46,7 @@
 def attend_kernel(
     capacity,
     group,
+    unroll,
     first,
     me_ref,
     count_ref,
@@ -64,7 +65,7 @@
     past = prefix_hbm.shape[0]
     heads, dim, _ = key_weight_ref.shape
     here = pl.ds(first, heads)
-    step = group * UNROLL
+    step = group * unroll
     steps = heads // step
     part = past // KEY_PARTS
 
@@ -96,9 +97,6 @@
     opening = copy_step(0)
     for copy in opening[:2] + for_keys + opening[2:]:
         copy.start()
-    for i in range(1, steps):
-        for copy in copy_step(i):
-            copy.start()
 
     count, size = count_ref[0], size_ref[0]
     lane = lax.broadcasted_iota(jnp.int32, (slots, past), 1)
@@ -111,15 +109,22 @@
     build_table(me_ref[0], count, routes_ref, table_ref, capacity)
 
     scale = math.log2(math.e) / math.sqrt(dim)
-    for copy in for_keys:
+    for copy in opening[:2] + for_keys:
         copy.wait()
+    for i in range(1, steps):
+        for copy in copy_step(i):
+            copy.start()
+    opening[2].wait()
 
     def body(i, carry):
-        for copy in copy_step(i):
-            copy.wait()
+        @pl.when(i > 0)
+        def _():
+            for copy in copy_step(i):
+                copy.wait()
+
         keys = keys_ref[...]
         scores = []
-        for stack in range(UNROLL):
+        for stack in range(unroll):
             lifted = []
             for g in range(group):
                 h = i * step + stack * group + g
@@ -127,7 +132,7 @@
                 lifted.append(dot(query, key_weight_ref[h]).astype(jnp.bfloat16))
             lifted = jnp.concatenate(lifted, axis=0)
             scores.append(lax.dot_general(lifted, keys, NT, preferred_element_type=jnp.float32))
-        for stack in range(UNROLL):
+        for stack in range(unroll):
             score = scores[stack].reshape(group, slots, keys.shape[0])
             score = jnp.minimum(score, cap_ref[...][None])
             highest = jnp.max(score, axis=-1, keepdims=True) * scale
@@ -145,13 +150,15 @@
 
     lax.fori_loop(0, steps, body, 0)
     grouped = dot(table_ref[...], attended_ref[...]).astype(jnp.bfloat16)
-    rows = out_refs[0].shape[0]
-    for k, out_ref in enumerate(out_refs):
-        out_ref[...] = grouped[k * rows : (k + 1) * rows]
+    row = 0
+    for out_ref in out_refs:
+        out_ref[...] = grouped[row : row + out_ref.shape[0]]
+        row += out_ref.shape[0]
 
 
 def attend(
     group,
+    unroll,
     first,
     heads,
     me,
@@ -164,7 +171,7 @@
     size,
     routes,
     experts,
-    pieces,
+    parts,
 ):
     slots = queries.shape[0]
     _, dim, latent = key_weight.shape
@@ -173,12 +180,12 @@
     smem = pl.BlockSpec(memory_space=pltpu.SMEM)
     vmem = pl.BlockSpec(memory_space=pltpu.VMEM)
     hbm = pl.BlockSpec(memory_space=pltpu.HBM)
-    piece = (places // pieces, heads * dim)
+    pieces = [(rows, heads * dim) for rows in parts]
     return pl.pallas_call(
-        functools.partial(attend_kernel, places // experts, group, first),
-        in_specs=[smem, smem, smem, vmem, hbm, hbm, hbm, hbm, hbm],
-        out_specs=[vmem] * pieces,
-        out_shape=[jax.ShapeDtypeStruct(piece, jnp.bfloat16)] * pieces,
+        functools.partial(attend_kernel, places // experts, group, unroll, first),
+        in_specs=[smem, smem, smem, vmem] + [hbm] * 5,
+        out_specs=[vmem] * len(pieces),
+        out_shape=[jax.ShapeDtypeStruct(piece, jnp.bfloat16) for piece in pieces],
         scratch_shapes=[
             pltpu.VMEM((slots, heads * dim), jnp.bfloat16),
             pltpu.VMEM((heads, dim, latent), jnp.bfloat16),
@@ -187,14 +194,10 @@
             pltpu.VMEM((slots, keys), jnp.float32),
             pltpu.VMEM((places, slots), jnp.bfloat16),
             pltpu.VMEM((slots, heads * dim), jnp.bfloat16),
-            pltpu.SemaphoreType.DMA((3 * heads // (group * UNROLL) + KEY_PARTS + 1,)),
+            pltpu.SemaphoreType.DMA((3 * heads // (group * unroll) + KEY_PARTS + 1,)),
         ],
         compiler_params=pltpu.CompilerParams(vmem_limit_bytes=VMEM),
-        cost_estimate=pl.CostEstimate(
-            flops=4 * slots * heads * keys * latent,
-            bytes_accessed=4 * heads * dim * latent,
-            transcendentals=heads * slots * keys,
-        ),
+        cost_estimate=SHORT,
     )(me, count, size, routes.T, queries, key_weight, value_weight, prefix, fresh)
 
 
@@ -208,65 +211,61 @@
 def pass_on_kernel(cores, *refs):
     *piece_refs, out_ref, sem = refs
     capacity = piece_refs[0].shape[0] // cores
-    run_copies(
-        [
-            pltpu.make_async_copy(
-                piece_ref.at[pl.ds(capacity, capacity)],
-                out_ref.at[pl.ds(j * capacity, capacity)],
-                sem.at[j],
-            )
-            for j, piece_ref in enumerate(piece_refs)
-        ]
-    )
+    copies = []
+    for i, piece_ref in enumerate(piece_refs):
+        target = out_ref.at[pl.ds(i * capacity, capacity)]
+        copies.append(
+            pltpu.make_async_copy(piece_ref.at[pl.ds(capacity, capacity)], target, sem.at[i])
+        )
+    run_copies(copies)
 
 
 def pass_on(pieces, cores):
     rows, width = pieces[0].shape
     return pl.pallas_call(
         functools.partial(pass_on_kernel, cores),
-        in_specs=[pl.BlockSpec(memory_space=pl.ANY)] * len(pieces),
-        out_specs=pl.BlockSpec(memory_space=pltpu.VMEM),
+        in_specs=[pl.BlockSpec(memory_space=pltpu.VMEM)] * len(pieces),
+        out_specs=pl.BlockSpec(memory_space=pl.ANY),
         out_shape=jax.ShapeDtypeStruct((len(pieces) * rows // cores, width), jnp.bfloat16),
         scratch_shapes=[pltpu.SemaphoreType.DMA((len(pieces),))],
         compiler_params=pltpu.CompilerParams(vmem_limit_bytes=VMEM),
+        cost_estimate=SHORT,
     )(*pieces)
 
 
-def place_kernel(plan, cores, me_ref, *rest):
-    *refs, out_ref, whole_ref, sem = rest
-    _, capacity, features = whole_ref.shape
+def place_kernel(first, order, cores, me_ref, *refs):
+    *piece_refs, swapped_ref = refs[: len(order) + 1]
+    out_ref, sem = refs[-2:]
+    me = me_ref[0]
+    _, _, capacity, features = out_ref.shape
     features //= cores
-    me = me_ref[0]
+    width = swapped_ref.shape[1]
     copies = []
-    for i, (ref, (first, start, source)) in enumerate(plan):
-        ref = refs[ref]
-        width = ref.shape[1]
-        who = me ^ source
-        left = pl.multiple_of(who % cores * features + first, math.gcd(features, first))
-        copies.append(
-            pltpu.make_async_copy(
-                ref.at[pl.ds(start, capacity)],
-                whole_ref.at[who // cores, :, pl.ds(left, width)],
-                sem.at[i],
-            )
-        )
+    for i, (j, piece_ref) in enumerate(zip(order, piece_refs)):
+        rows = swapped_ref.at[pl.ds(i * capacity, capacity)]
+        for core, ref in enumerate((piece_ref.at[pl.ds(0, capacity)], rows)):
+            who = me ^ (j * cores + core)
+            left = pl.multiple_of(who % cores * features + first, math.gcd(features, first))
+            target = out_ref.at[0, who // cores, :, pl.ds(left, width)]
+            copies.append(pltpu.make_async_copy(ref, target, sem.at[len(copies)]))
     run_copies(copies)
-    run_copies([pltpu.make_async_copy(whole_ref, out_ref.at[0], sem.at[0])])
-
-
-def assemble(me, arrays, plan, shape, cores):
+
+
+def place(me, pieces, swapped, first, order, cores, shape, placed):
+    anywhere = pl.BlockSpec(memory_space=pl.ANY)
+    operands = [me, *pieces, swapped] + placed
     return pl.pallas_call(
-        functools.partial(place_kernel, plan, cores),
+        functools.partial(place_kernel, first, order, cores),
         in_specs=[pl.BlockSpec(memory_space=pltpu.SMEM)]
-        + [pl.BlockSpec(memory_space=pl.ANY)] * len(arrays),
-        out_specs=pl.BlockSpec(memory_space=pl.ANY),
+        + [pl.BlockSpec(memory_space=pltpu.VMEM)] * (len(pieces) + 1)
+        + [anywhere] * len(placed),
+        out_specs=anywhere,
         out_shape=jax.ShapeDtypeStruct(shape, jnp.bfloat16),
-        scratch_shapes=[
-            pltpu.VMEM(shape[1:], jnp.bfloat16),
-            pltpu.SemaphoreType.DMA((len(plan),)),
-        ],
+        scratch_shapes=[pltpu.SemaphoreType.DMA((2 * len(pieces),))],
+        input_output_aliases={len(operands) - 1: 0} if placed else {},
         compiler_params=pltpu.CompilerParams(vmem_limit_bytes=VMEM),
-    )(me, *arrays)
+        cost_estimate=SHORT,
+    )(*operands)
 
 
 def exchange_order(ranks):
@@ -295,12 +294,12 @@
     index = lax.axis_index("dp") * cores + lax.axis_index("ep")
     me = (index if direct else jnp.int32(0)).astype(jnp.int32).reshape(1)
     shares = [heads * share // sum(CHUNKS) for share in CHUNKS]
-    chunks, plan = [], []
-    first = 0
-    for group, share in zip(GROUPS, shares):
+    sent, start = [], 0
+    for (group, unroll), share in zip(STACKS, shares):
         outgoing = attend(
             group,
-            first,
+            unroll,
+            start,
             share,
             me,
             queries,
@@ -312,35 +311,35 @@
             prefix_lengths,
             routes,
             experts,
-            ranks if direct else 1,
+            [cores * capacity] * ranks if direct else [experts * capacity],
         )
-        if direct:
-            order = exchange_order(ranks)
-            pieces = [outgoing[0]]
-            for j in order:
-                pairs = [(i, i ^ j) for i in range(ranks)]
-                pieces.append(lax.ppermute(outgoing[j], "dp", pairs))
-            swapped = lax.ppermute(
-                pass_on(pieces, cores), "ep", [(i, i ^ 1) for i in range(cores)]
-            )
-            for at, j in enumerate([0] + order):
-                plan.append((len(chunks) + at, (first * dim, 0, j * cores)))
-                plan.append((len(chunks) + ranks, (first * dim, at * capacity, j * cores + 1)))
-            chunks += pieces + [swapped]
-        else:
+        sent.append(outgoing)
+        start += share
+    if not direct:
+        arrays = []
+        for (outgoing,) in sent:
             arrived = lax.all_to_all(
-                outgoing[0].reshape(experts, capacity, share * dim),
+                outgoing.reshape(experts, capacity, -1),
                 ("dp", "ep"),
                 split_axis=0,
                 concat_axis=0,
                 tiled=True,
             )
-            chunks.append(arrived.reshape(ranks, cores, capacity, share * dim))
-        first += share
-    if direct:
-        return assemble(me, chunks, plan, (1, ranks, capacity, cores * heads * dim), cores)
-    arrived = jnp.concatenate(chunks, axis=3).transpose(0, 2, 1, 3)
-    return arrived.reshape(1, ranks, capacity, cores * heads * dim)
+            arrays.append(arrived.reshape(ranks, cores, capacity, -1))
+        arrived = jnp.concatenate(arrays, axis=3).transpose(0, 2, 1, 3)
+        return arrived.reshape(1, ranks, capacity, cores * heads * dim)
+    order = exchange_order(ranks)
+    shape = (1, ranks, capacity, cores * heads * dim)
+    placed, start = [], 0
+    for outgoing, share in zip(sent, shares):
+        pieces = [outgoing[0]]
+        for j in order:
+            pairs = [(i, i ^ j) for i in range(ranks)]
+            pieces.append(lax.ppermute(outgoing[j], "dp", pairs))
+        swapped = lax.ppermute(pass_on(pieces, cores), "ep", [(i, i ^ 1) for i in range(cores)])
+        placed = [place(me, pieces, swapped, start * dim, [0] + order, cores, shape, placed)]
+        start += share
+    return placed[0]
 
 
 def solution(mesh):

time: 75.5 us -> 80 us (1.060)
  Pallas kernels: 31.7 us -> 38.7 us
  waiting for transfers between devices: 11.3 us -> 6.2 us
  starting transfers between devices: 29.1 us -> 30.9 us
    pallas_call x2, Pallas kernels: 24.7 us -> 29.3 us  [attend(): pl.pallas_call(functools.partial(attend_kernel, places // experts, group,...]
    ppermute x14, waiting for transfers between devices: 9.19 us -> 6.2 us  [local(): pieces.append(lax.ppermute(outgoing[j], 'dp', pairs))]
    ppermute x2, waiting for transfers between devices: 2.09 us -> 0.01 us  [local(): lax.ppermute(pass_on(pieces, cores), 'ep', [(i, i ^ 1) for i in range(cor...]
    pallas_call x1 -> x2, Pallas kernels: 3.16 us -> 5.1 us  [place(): pl.pallas_call(functools.partial(place_kernel, first, order, cores), in_s...]
    ppermute x14, starting transfers between devices: 28.9 us -> 30.8 us  [local(): pieces.append(lax.ppermute(outgoing[j], 'dp', pairs))]
  transfers between devices with their start and end apart: 16 -> 16, of which waited for: 4 -> 3; matrix products, arithmetic and copies ran while one was open for 0% -> 0% of each run, Pallas kernels for 22% -> 29%
where the time goes in v7:
time: 80 us; the launch traced here: 79.6 us
  Pallas kernels  38.7 us (48%)
  starting transfers between devices  30.9 us (39%)
  waiting for transfers between devices  6.2 us (8%)
  local copies, waits for them, and re-layouts  2.24 us (3%)
  between operations  1.56 us (2%)
    ppermute x14, starting transfers between devices, local(): pieces.append(lax.ppermute(outgoing[j], 'dp', pairs))  30.8 us
    pallas_call x2, Pallas kernels, attend(): pl.pallas_call(functools.partial(attend_kernel, places // experts, group,...  29.3 us
    ppermute x14, waiting for transfers between devices, local(): pieces.append(lax.ppermute(outgoing[j], 'dp', pairs))  6.2 us
    pallas_call x2, Pallas kernels, place(): pl.pallas_call(functools.partial(place_kernel, first, order, cores), in_s...  5.1 us
    pallas_call x2, Pallas kernels, pass_on(): pl.pallas_call(functools.partial(pass_on_kernel, cores), in_specs=[pl.Blo...  4.27 us
    unnamed x36, local copies, waits for them, and re-layouts  2.24 us
  transfers between devices with their start and end apart: 16, of which 3 were waited for; matrix products, arithmetic and copies ran while one was open for 0% of the time, Pallas kernels for 29%

profile of v7, /device:TPU:0, one launch (start us, length us, event | category | flops | bytes accessed | tf_op | source)
XLA Modules:
  0.0 79.6 jit_solution(12782214823511795196)
XLA Ops:
  1.3 12.8 %shard_map.84 = (bf16[32,2048]{1,0:T(8,128)(2,1)}, bf16[32,2048]{1,0:T(8,128)(2,1)}, bf16[32,2048]{1,0:T(8,128)(2,1)}, bf16[32,2048]{1,0:T(8,128)(2,1)}, bf16[32...) custom-call(s32[1]{0:T(128)} %bitcast.me_ref, ...), custom_call_target="tpu_custom_call" | custom-call | tf_op jit(solution)/shard_map/pallas_call | solution.py:184
  14.1 4.1 %collective-permute-start.8 = (bf16[32,2048]{1,0:T(8,128)(2,1)}, bf16[32,2048]{1,0:T(8,128)(2,1)S(1)}, u32[]{:S(2)}, u32[]{:S(2)}) collective-permute-start(bf16[32,2048]{1,0:T(8,128)(2,1)} %get-tuple-element.30), channel_id=1, source_target_pairs={{0,8},{2,10},{4,12},{6,14},{8,0},{10,2},{12,4},{14,6},{1,9},{3,11}... | collective-permute-start | bytes 393224 | tf_op jit(solution)/shard_map/ppermute | solution.py:338
  18.2 1.3 %collective-permute-start.9 = (bf16[32,2048]{1,0:T(8,128)(2,1)}, bf16[32,2048]{1,0:T(8,128)(2,1)S(1)}, u32[]{:S(2)}, u32[]{:S(2)}) collective-permute-start(bf16[32,2048]{1,0:T(8,128)(2,1)} %get-tuple-element.31), channel_id=1, source_target_pairs={{0,12},{2,14},{4,8},{6,10},{8,4},{10,6},{12,0},{14,2},{1,13},{3,15... | collective-permute-start | bytes 393224 | tf_op jit(solution)/shard_map/ppermute | solution.py:338
  19.5 1.5 %collective-permute-start.10 = (bf16[32,2048]{1,0:T(8,128)(2,1)}, bf16[32,2048]{1,0:T(8,128)(2,1)S(1)}, u32[]{:S(2)}, u32[]{:S(2)}) collective-permute-start(bf16[32,2048]{1,0:T(8,128)(2,1)} %get-tuple-element.32), channel_id=1, source_target_pairs={{0,2},{2,0},{4,6},{6,4},{8,10},{10,8},{12,14},{14,12},{1,3},{3,1},... | collective-permute-start | bytes 393224 | tf_op jit(solution)/shard_map/ppermute | solution.py:338
  21.0 1.6 %collective-permute-start.11 = (bf16[32,2048]{1,0:T(8,128)(2,1)}, bf16[32,2048]{1,0:T(8,128)(2,1)S(1)}, u32[]{:S(2)}, u32[]{:S(2)}) collective-permute-start(bf16[32,2048]{1,0:T(8,128)(2,1)} %get-tuple-element.33), channel_id=1, source_target_pairs={{0,10},{2,8},{4,14},{6,12},{8,2},{10,0},{12,6},{14,4},{1,11},{3,9}... | collective-permute-start | bytes 393224 | tf_op jit(solution)/shard_map/ppermute | solution.py:338
  22.7 1.9 %collective-permute-start.12 = (bf16[32,2048]{1,0:T(8,128)(2,1)}, bf16[32,2048]{1,0:T(8,128)(2,1)S(1)}, u32[]{:S(2)}, u32[]{:S(2)}) collective-permute-start(bf16[32,2048]{1,0:T(8,128)(2,1)} %get-tuple-element.34), channel_id=1, source_target_pairs={{0,14},{2,12},{4,10},{6,8},{8,6},{10,4},{12,2},{14,0},{1,15},{3,13... | collective-permute-start | bytes 393224 | tf_op jit(solution)/shard_map/ppermute | solution.py:338
  24.5 16.5 %shard_map.82 = (bf16[32,2048]{1,0:T(8,128)(2,1)}, bf16[32,2048]{1,0:T(8,128)(2,1)}, bf16[32,2048]{1,0:T(8,128)(2,1)}, bf16[32,2048]{1,0:T(8,128)(2,1)}, bf16[32...) custom-call(s32[1]{0:T(128)} %bitcast.me_ref, ...), custom_call_target="tpu_custom_call" | custom-call | tf_op jit(solution)/shard_map/pallas_call | solution.py:184
  41.1 1.0 %collective-permute-start.13 = (bf16[32,2048]{1,0:T(8,128)(2,1)S(1)}, bf16[32,2048]{1,0:T(8,128)(2,1)S(1)}, u32[]{:S(2)}, u32[]{:S(2)}) collective-permute-start(bf16[32,2048]{1,0:T(8,128)(2,1)S(1)} %copy-done.17), channel_id=1, source_target_pairs={{0,4},{2,6},{4,0},{6,2},{8,12},{10,14},{12,8},{14,10},{1,5},{3,7},... | collective-permute-start | bytes 393224 | tf_op jit(solution)/shard_map/ppermute | solution.py:338
  42.1 1.1 %collective-permute-start.14 = (bf16[32,2048]{1,0:T(8,128)(2,1)S(1)}, bf16[32,2048]{1,0:T(8,128)(2,1)S(1)}, u32[]{:S(2)}, u32[]{:S(2)}) collective-permute-start(bf16[32,2048]{1,0:T(8,128)(2,1)S(1)} %copy-done.16), channel_id=1, source_target_pairs={{0,6},{2,4},{4,2},{6,0},{8,14},{10,12},{12,10},{14,8},{1,7},{3,5},... | collective-permute-start | bytes 393224 | tf_op jit(solution)/shard_map/ppermute | solution.py:338
  43.2 1.9 %collective-permute-start = (bf16[32,2048]{1,0:T(8,128)(2,1)}, bf16[32,2048]{1,0:T(8,128)(2,1)S(1)}, u32[]{:S(2)}, u32[]{:S(2)}) collective-permute-start(bf16[32,2048]{1,0:T(8,128)(2,1)} %get-tuple-element.22), channel_id=1, source_target_pairs={{0,8},{2,10},{4,12},{6,14},{8,0},{10,2},{12,4},{14,6},{1,9},{3,11}... | collective-permute-start | bytes 393224 | tf_op jit(solution)/shard_map/ppermute | solution.py:338
  45.1 0.0 collective-permute-done.11.refs_4_
  45.1 1.3 %collective-permute-start.1 = (bf16[32,2048]{1,0:T(8,128)(2,1)}, bf16[32,2048]{1,0:T(8,128)(2,1)S(1)}, u32[]{:S(2)}, u32[]{:S(2)}) collective-permute-start(bf16[32,2048]{1,0:T(8,128)(2,1)} %get-tuple-element.23), channel_id=1, source_target_pairs={{0,12},{2,14},{4,8},{6,10},{8,4},{10,6},{12,0},{14,2},{1,13},{3,15... | collective-permute-start | bytes 393224 | tf_op jit(solution)/shard_map/ppermute | solution.py:338
  46.5 0.0 collective-permute-done.12.refs_5_
  46.5 1.5 %collective-permute-start.2 = (bf16[32,2048]{1,0:T(8,128)(2,1)}, bf16[32,2048]{1,0:T(8,128)(2,1)S(1)}, u32[]{:S(2)}, u32[]{:S(2)}) collective-permute-start(bf16[32,2048]{1,0:T(8,128)(2,1)} %get-tuple-element.24), channel_id=1, source_target_pairs={{0,2},{2,0},{4,6},{6,4},{8,10},{10,8},{12,14},{14,12},{1,3},{3,1},... | collective-permute-start | bytes 393224 | tf_op jit(solution)/shard_map/ppermute | solution.py:338
  48.0 0.1 collective-permute-done.13.refs_6_
  48.2 1.5 %collective-permute-start.3 = (bf16[32,2048]{1,0:T(8,128)(2,1)}, bf16[32,2048]{1,0:T(8,128)(2,1)S(1)}, u32[]{:S(2)}, u32[]{:S(2)}) collective-permute-start(bf16[32,2048]{1,0:T(8,128)(2,1)} %get-tuple-element.25), channel_id=1, source_target_pairs={{0,10},{2,8},{4,14},{6,12},{8,2},{10,0},{12,6},{14,4},{1,11},{3,9}... | collective-permute-start | bytes 393224 | tf_op jit(solution)/shard_map/ppermute | solution.py:338
  49.7 0.0 collective-permute-done.14.refs_7_
  49.7 5.4 %collective-permute-start.4 = (bf16[32,2048]{1,0:T(8,128)(2,1)}, bf16[32,2048]{1,0:T(8,128)(2,1)S(1)}, u32[]{:S(2)}, u32[]{:S(2)}) collective-permute-start(bf16[32,2048]{1,0:T(8,128)(2,1)} %get-tuple-element.26), channel_id=1, source_target_pairs={{0,14},{2,12},{4,10},{6,8},{8,6},{10,4},{12,2},{14,0},{1,15},{3,13... | collective-permute-start | bytes 393224 | tf_op jit(solution)/shard_map/ppermute | solution.py:338
  55.1 4.5 %collective-permute-done.refs_1_ = bf16[32,2048]{1,0:T(8,128)(2,1)S(1)} collective-permute-done((bf16[32,2048]{1,0:T(8,128)(2,1)}, bf16[32,2048]{1,0:T(8,128)(2,1)S(1)}, u32[]{:S(2)}, u32[]{:S(2)}) %collective-permute-start) | collective-permute-done | bytes 131104 | tf_op jit(solution)/shard_map/ppermute | solution.py:338
  59.6 0.0 collective-permute-start.5
  59.6 0.0 collective-permute-done.1.refs_2_
  59.6 6.5 %collective-permute-start.6 = (bf16[32,2048]{1,0:T(8,128)(2,1)}, bf16[32,2048]{1,0:T(8,128)(2,1)S(1)}, u32[]{:S(2)}, u32[]{:S(2)}) collective-permute-start(bf16[32,2048]{1,0:T(8,128)(2,1)} %get-tuple-element.28), channel_id=1, source_target_pairs={{0,6},{2,4},{4,2},{6,0},{8,14},{10,12},{12,10},{14,8},{1,7},{3,5},... | collective-permute-start | bytes 393224 | tf_op jit(solution)/shard_map/ppermute | solution.py:338
  66.2 2.1 %shard_map.85 = bf16[128,2048]{1,0:T(8,128)(2,1)} custom-call(bf16[32,2048]{1,0:T(8,128)(2,1)} %get-tuple-element.29.refs_0_, bf16[32,2048]{1,0:T(8,128)(2,1)} %copy-done.1, bf16[32,2048]{1,0:T(8,128)(2,1)} %copy-done.2, bf16[32,2048]{1,0:T(8,128)(2,1)} %copy-done.3, bf16[32,2048]{1,0:T(8,128)(2,1)} %copy-done.4, bf16[32,2048]{1,0:T(8,128)(2,1)} %copy-done.5, ...), custom_call_target="tpu_custom_call" | custom-call | tf_op jit(solution)/shard_map/pallas_call | solution.py:225
  68.3 0.1 collective-permute-start.15
  68.5 1.5 %collective-permute-done.6.refs_7_ = bf16[32,2048]{1,0:T(8,128)(2,1)S(1)} collective-permute-done((bf16[32,2048]{1,0:T(8,128)(2,1)}, bf16[32,2048]{1,0:T(8,128)(2,1)S(1)}, u32[]{:S(2)}, u32[]{:S(2)}) %collective-permute-start.6) | collective-permute-done | bytes 131104 | tf_op jit(solution)/shard_map/ppermute | solution.py:338
  70.1 0.6 copy-done.14
  70.7 2.1 %shard_map.83 = bf16[128,2048]{1,0:T(8,128)(2,1)} custom-call(bf16[32,2048]{1,0:T(8,128)(2,1)} %get-tuple-element.21.refs_0_, bf16[32,2048]{1,0:T(8,128)(2,1)} %copy-done.7, bf16[32,2048]{1,0:T(8,128)(2,1)} %copy-done.9, bf16[32,2048]{1,0:T(8,128)(2,1)} %copy-done.10, bf16[32,2048]{1,0:T(8,128)(2,1)} %copy-done.11, bf16[32,2048]{1,0:T(8,128)(2,1)} %copy-done.12, ...), custom_call_target="tpu_custom_call" | custom-call | tf_op jit(solution)/shard_map/pallas_call | solution.py:225
  72.8 0.1 collective-permute-start.7
  72.9 0.8 %copy-done.15 = bf16[128,2048]{1,0:T(8,128)(2,1)} copy-done((bf16[128,2048]{1,0:T(8,128)(2,1)}, bf16[128,2048]{1,0:T(8,128)(2,1)S(1)}, u32[]{:S(2)}) %copy-start.15) | copy-done | bytes 524312
  73.7 2.5 %shard_map.86.refs_9_ = bf16[1,8,16,8192]{3,2,1,0:T(8,128)(2,1)} custom-call(s32[1]{0:T(128)} %bitcast.me_ref, bf16[32,2048]{1,0:T(8,128)(2,1)} %get-tuple-element.29.refs_0_, bf16[32,2048]{1,0:T(8,128)(2,1)} %copy-done.1, bf16[32,2048]{1,0:T(8,128)(2,1)} %copy-done.2, bf16[32,2048]{1,0:T(8,128)(2,1)} %copy-done.3, bf16[32,2048]{1,0:T(8,128)(2,1)} %copy-done.4, ...), custom_call_target="tpu_custom_call" | custom-call | tf_op jit(solution)/shard_map/pallas_call | solution.py:257
  76.3 0.8 copy-done
  77.1 2.5 %shard_map.87 = bf16[1,8,16,8192]{3,2,1,0:T(8,128)(2,1)} custom-call(s32[1]{0:T(128)} %bitcast.me_ref, bf16[32,2048]{1,0:T(8,128)(2,1)} %get-tuple-element.21.refs_0_, bf16[32,2048]{1,0:T(8,128)(2,1)} %copy-done.7, bf16[32,2048]{1,0:T(8,128)(2,1)} %copy-done.9, bf16[32,2048]{1,0:T(8,128)(2,1)} %copy-done.10, ...), custom_call_target="tpu_custom_call", output_to_operand_aliasing={{}: (10, {})} | custom-call | tf_op jit(solution)/shard_map/pallas_call | solution.py:257
  (42 shorter events, 0.1 us)
Async XLA Ops:
  14.1 27.0 %collective-permute-start.8 = (bf16[32,2048]{1,0:T(8,128)(2,1)}, bf16[32,2048]{1,0:T(8,128)(2,1)S(1)}, u32[]{:S(2)}, u32[]{:S(2)}) collective-permute-start(bf16[32,2048]{1,0:T(8,128)(2,1)} %get-tuple-element.30), channel_id=1, source_target_pairs={{0,8},{2,10},{4,12},{6,14},{8,0},{10,2},{12,4},{14,6},{1,9},{3,11}... | collective-permute-start | bytes 393224 | tf_op jit(solution)/shard_map/ppermute | solution.py:338
  18.2 23.9 %collective-permute-start.9 = (bf16[32,2048]{1,0:T(8,128)(2,1)}, bf16[32,2048]{1,0:T(8,128)(2,1)S(1)}, u32[]{:S(2)}, u32[]{:S(2)}) collective-permute-start(bf16[32,2048]{1,0:T(8,128)(2,1)} %get-tuple-element.31), channel_id=1, source_target_pairs={{0,12},{2,14},{4,8},{6,10},{8,4},{10,6},{12,0},{14,2},{1,13},{3,15... | collective-permute-start | bytes 393224 | tf_op jit(solution)/shard_map/ppermute | solution.py:338
  19.5 23.7 %collective-permute-start.10 = (bf16[32,2048]{1,0:T(8,128)(2,1)}, bf16[32,2048]{1,0:T(8,128)(2,1)S(1)}, u32[]{:S(2)}, u32[]{:S(2)}) collective-permute-start(bf16[32,2048]{1,0:T(8,128)(2,1)} %get-tuple-element.32), channel_id=1, source_target_pairs={{0,2},{2,0},{4,6},{6,4},{8,10},{10,8},{12,14},{14,12},{1,3},{3,1},... | collective-permute-start | bytes 393224 | tf_op jit(solution)/shard_map/ppermute | solution.py:338
  21.0 24.1 %collective-permute-start.11 = (bf16[32,2048]{1,0:T(8,128)(2,1)}, bf16[32,2048]{1,0:T(8,128)(2,1)S(1)}, u32[]{:S(2)}, u32[]{:S(2)}) collective-permute-start(bf16[32,2048]{1,0:T(8,128)(2,1)} %get-tuple-element.33), channel_id=1, source_target_pairs={{0,10},{2,8},{4,14},{6,12},{8,2},{10,0},{12,6},{14,4},{1,11},{3,9}... | collective-permute-start | bytes 393224 | tf_op jit(solution)/shard_map/ppermute | solution.py:338
  22.7 18.4 %copy-start.17 = (bf16[32,2048]{1,0:T(8,128)(2,1)S(1)}, bf16[32,2048]{1,0:T(8,128)(2,1)}, u32[]{:S(2)}) copy-start(bf16[32,2048]{1,0:T(8,128)(2,1)} %get-tuple-element.35) | copy-start | bytes 393220
  22.7 19.4 %copy-start.16 = (bf16[32,2048]{1,0:T(8,128)(2,1)S(1)}, bf16[32,2048]{1,0:T(8,128)(2,1)}, u32[]{:S(2)}) copy-start(bf16[32,2048]{1,0:T(8,128)(2,1)} %get-tuple-element.36) | copy-start | bytes 393220
  22.7 23.8 %collective-permute-start.12 = (bf16[32,2048]{1,0:T(8,128)(2,1)}, bf16[32,2048]{1,0:T(8,128)(2,1)S(1)}, u32[]{:S(2)}, u32[]{:S(2)}) collective-permute-start(bf16[32,2048]{1,0:T(8,128)(2,1)} %get-tuple-element.34), channel_id=1, source_target_pairs={{0,14},{2,12},{4,10},{6,8},{8,6},{10,4},{12,2},{14,0},{1,15},{3,13... | collective-permute-start | bytes 393224 | tf_op jit(solution)/shard_map/ppermute | solution.py:338
  41.1 25.1 %copy-start.1 = (bf16[32,2048]{1,0:T(8,128)(2,1)}, bf16[32,2048]{1,0:T(8,128)(2,1)S(1)}, u32[]{:S(2)}) copy-start(bf16[32,2048]{1,0:T(8,128)(2,1)S(1)} %collective-permute-done.8.refs_1_) | copy-start | bytes 393220
  41.1 7.0 %collective-permute-start.13 = (bf16[32,2048]{1,0:T(8,128)(2,1)S(1)}, bf16[32,2048]{1,0:T(8,128)(2,1)S(1)}, u32[]{:S(2)}, u32[]{:S(2)}) collective-permute-start(bf16[32,2048]{1,0:T(8,128)(2,1)S(1)} %copy-done.17), channel_id=1, source_target_pairs={{0,4},{2,6},{4,0},{6,2},{8,12},{10,14},{12,8},{14,10},{1,5},{3,7},... | collective-permute-start | bytes 393224 | tf_op jit(solution)/shard_map/ppermute | solution.py:338
  42.1 24.1 %copy-start.2 = (bf16[32,2048]{1,0:T(8,128)(2,1)}, bf16[32,2048]{1,0:T(8,128)(2,1)S(1)}, u32[]{:S(2)}) copy-start(bf16[32,2048]{1,0:T(8,128)(2,1)S(1)} %collective-permute-done.9.refs_2_) | copy-start | bytes 393220
  42.1 7.6 %collective-permute-start.14 = (bf16[32,2048]{1,0:T(8,128)(2,1)S(1)}, bf16[32,2048]{1,0:T(8,128)(2,1)S(1)}, u32[]{:S(2)}, u32[]{:S(2)}) collective-permute-start(bf16[32,2048]{1,0:T(8,128)(2,1)S(1)} %copy-done.16), channel_id=1, source_target_pairs={{0,6},{2,4},{4,2},{6,0},{8,14},{10,12},{12,10},{14,8},{1,7},{3,5},... | collective-permute-start | bytes 393224 | tf_op jit(solution)/shard_map/ppermute | solution.py:338
  43.2 22.9 %copy-start.3 = (bf16[32,2048]{1,0:T(8,128)(2,1)}, bf16[32,2048]{1,0:T(8,128)(2,1)S(1)}, u32[]{:S(2)}) copy-start(bf16[32,2048]{1,0:T(8,128)(2,1)S(1)} %collective-permute-done.10.refs_3_) | copy-start | bytes 393220
  43.2 16.4 %collective-permute-start = (bf16[32,2048]{1,0:T(8,128)(2,1)}, bf16[32,2048]{1,0:T(8,128)(2,1)S(1)}, u32[]{:S(2)}, u32[]{:S(2)}) collective-permute-start(bf16[32,2048]{1,0:T(8,128)(2,1)} %get-tuple-element.22), channel_id=1, source_target_pairs={{0,8},{2,10},{4,12},{6,14},{8,0},{10,2},{12,4},{14,6},{1,9},{3,11}... | collective-permute-start | bytes 393224 | tf_op jit(solution)/shard_map/ppermute | solution.py:338
  45.1 21.0 %copy-start.4 = (bf16[32,2048]{1,0:T(8,128)(2,1)}, bf16[32,2048]{1,0:T(8,128)(2,1)S(1)}, u32[]{:S(2)}) copy-start(bf16[32,2048]{1,0:T(8,128)(2,1)S(1)} %collective-permute-done.11.refs_4_) | copy-start | bytes 393220
  45.1 14.5 %collective-permute-start.1 = (bf16[32,2048]{1,0:T(8,128)(2,1)}, bf16[32,2048]{1,0:T(8,128)(2,1)S(1)}, u32[]{:S(2)}, u32[]{:S(2)}) collective-permute-start(bf16[32,2048]{1,0:T(8,128)(2,1)} %get-tuple-element.23), channel_id=1, source_target_pairs={{0,12},{2,14},{4,8},{6,10},{8,4},{10,6},{12,0},{14,2},{1,13},{3,15... | collective-permute-start | bytes 393224 | tf_op jit(solution)/shard_map/ppermute | solution.py:338
  46.5 19.7 %copy-start.5 = (bf16[32,2048]{1,0:T(8,128)(2,1)}, bf16[32,2048]{1,0:T(8,128)(2,1)S(1)}, u32[]{:S(2)}) copy-start(bf16[32,2048]{1,0:T(8,128)(2,1)S(1)} %collective-permute-done.12.refs_5_) | copy-start | bytes 393220
  46.5 21.8 %collective-permute-start.2 = (bf16[32,2048]{1,0:T(8,128)(2,1)}, bf16[32,2048]{1,0:T(8,128)(2,1)S(1)}, u32[]{:S(2)}, u32[]{:S(2)}) collective-permute-start(bf16[32,2048]{1,0:T(8,128)(2,1)} %get-tuple-element.24), channel_id=1, source_target_pairs={{0,2},{2,0},{4,6},{6,4},{8,10},{10,8},{12,14},{14,12},{1,3},{3,1},... | collective-permute-start | bytes 393224 | tf_op jit(solution)/shard_map/ppermute | solution.py:338
  48.2 18.0 %copy-start.6 = (bf16[32,2048]{1,0:T(8,128)(2,1)}, bf16[32,2048]{1,0:T(8,128)(2,1)S(1)}, u32[]{:S(2)}) copy-start(bf16[32,2048]{1,0:T(8,128)(2,1)S(1)} %collective-permute-done.13.refs_6_) | copy-start | bytes 393220
  48.2 20.3 %collective-permute-start.3 = (bf16[32,2048]{1,0:T(8,128)(2,1)}, bf16[32,2048]{1,0:T(8,128)(2,1)S(1)}, u32[]{:S(2)}, u32[]{:S(2)}) collective-permute-start(bf16[32,2048]{1,0:T(8,128)(2,1)} %get-tuple-element.25), channel_id=1, source_target_pairs={{0,10},{2,8},{4,14},{6,12},{8,2},{10,0},{12,6},{14,4},{1,11},{3,9}... | collective-permute-start | bytes 393224 | tf_op jit(solution)/shard_map/ppermute | solution.py:338
  49.7 16.5 %copy-start.8 = (bf16[32,2048]{1,0:T(8,128)(2,1)}, bf16[32,2048]{1,0:T(8,128)(2,1)S(1)}, u32[]{:S(2)}) copy-start(bf16[32,2048]{1,0:T(8,128)(2,1)S(1)} %collective-permute-done.14.refs_7_) | copy-start | bytes 393220
  49.7 18.8 %collective-permute-start.4 = (bf16[32,2048]{1,0:T(8,128)(2,1)}, bf16[32,2048]{1,0:T(8,128)(2,1)S(1)}, u32[]{:S(2)}, u32[]{:S(2)}) collective-permute-start(bf16[32,2048]{1,0:T(8,128)(2,1)} %get-tuple-element.26), channel_id=1, source_target_pairs={{0,14},{2,12},{4,10},{6,8},{8,6},{10,4},{12,2},{14,0},{1,15},{3,13... | collective-permute-start | bytes 393224 | tf_op jit(solution)/shard_map/ppermute | solution.py:338
  59.6 10.4 %copy-start.7 = (bf16[32,2048]{1,0:T(8,128)(2,1)}, bf16[32,2048]{1,0:T(8,128)(2,1)S(1)}, u32[]{:S(2)}) copy-start(bf16[32,2048]{1,0:T(8,128)(2,1)S(1)} %collective-permute-done.refs_1_) | copy-start | bytes 393220
  59.6 8.9 %collective-permute-start.5 = (bf16[32,2048]{1,0:T(8,128)(2,1)}, bf16[32,2048]{1,0:T(8,128)(2,1)S(1)}, u32[]{:S(2)}, u32[]{:S(2)}) collective-permute-start(bf16[32,2048]{1,0:T(8,128)(2,1)} %get-tuple-element.27), channel_id=1, source_target_pairs={{0,4},{2,6},{4,0},{6,2},{8,12},{10,14},{12,8},{14,10},{1,5},{3,7},... | collective-permute-start | bytes 393224 | tf_op jit(solution)/shard_map/ppermute | solution.py:338
  59.6 10.4 %copy-start.9 = (bf16[32,2048]{1,0:T(8,128)(2,1)}, bf16[32,2048]{1,0:T(8,128)(2,1)S(1)}, u32[]{:S(2)}) copy-start(bf16[32,2048]{1,0:T(8,128)(2,1)S(1)} %collective-permute-done.1.refs_2_) | copy-start | bytes 393220
  59.6 10.4 %collective-permute-start.6 = (bf16[32,2048]{1,0:T(8,128)(2,1)}, bf16[32,2048]{1,0:T(8,128)(2,1)S(1)}, u32[]{:S(2)}, u32[]{:S(2)}) collective-permute-start(bf16[32,2048]{1,0:T(8,128)(2,1)} %get-tuple-element.28), channel_id=1, source_target_pairs={{0,6},{2,4},{4,2},{6,0},{8,14},{10,12},{12,10},{14,8},{1,7},{3,5},... | collective-permute-start | bytes 393224 | tf_op jit(solution)/shard_map/ppermute | solution.py:338
  68.3 1.7 %copy-start.10 = (bf16[32,2048]{1,0:T(8,128)(2,1)}, bf16[32,2048]{1,0:T(8,128)(2,1)S(1)}, u32[]{:S(2)}) copy-start(bf16[32,2048]{1,0:T(8,128)(2,1)S(1)} %collective-permute-done.2.refs_3_) | copy-start | bytes 393220
  68.3 4.6 %collective-permute-start.15 = (bf16[128,2048]{1,0:T(8,128)(2,1)}, bf16[128,2048]{1,0:T(8,128)(2,1)S(1)}, u32[]{:S(2)}, u32[]{:S(2)}) collective-permute-start(bf16[128,2048]{1,0:T(8,128)(2,1)} %shard_map.85), channel_id=1, source_target_pairs={{0,1},{1,0},{2,3},{3,2},{4,5},{5,4},{6,7},{7,6},{8,9},{9,8},{10,11... | collective-permute-start | bytes 1572872 | tf_op jit(solution)/shard_map/ppermute | solution.py:339
  68.4 1.6 %copy-start.11 = (bf16[32,2048]{1,0:T(8,128)(2,1)}, bf16[32,2048]{1,0:T(8,128)(2,1)S(1)}, u32[]{:S(2)}) copy-start(bf16[32,2048]{1,0:T(8,128)(2,1)S(1)} %collective-permute-done.3.refs_4_) | copy-start | bytes 393220
  68.5 1.6 %copy-start.12 = (bf16[32,2048]{1,0:T(8,128)(2,1)}, bf16[32,2048]{1,0:T(8,128)(2,1)S(1)}, u32[]{:S(2)}) copy-start(bf16[32,2048]{1,0:T(8,128)(2,1)S(1)} %collective-permute-done.4.refs_5_) | copy-start | bytes 393220
  68.5 1.6 %copy-start.13 = (bf16[32,2048]{1,0:T(8,128)(2,1)}, bf16[32,2048]{1,0:T(8,128)(2,1)S(1)}, u32[]{:S(2)}) copy-start(bf16[32,2048]{1,0:T(8,128)(2,1)S(1)} %collective-permute-done.5.refs_6_) | copy-start | bytes 393220
  72.8 3.5 %collective-permute-start.7 = (bf16[128,2048]{1,0:T(8,128)(2,1)}, bf16[128,2048]{1,0:T(8,128)(2,1)S(1)}, u32[]{:S(2)}, u32[]{:S(2)}) collective-permute-start(bf16[128,2048]{1,0:T(8,128)(2,1)} %shard_map.83), channel_id=1, source_target_pairs={{0,1},{1,0},{2,3},{3,2},{4,5},{5,4},{6,7},{7,6},{8,9},{9,8},{10,11... | collective-permute-start | bytes 1572872 | tf_op jit(solution)/shard_map/ppermute | solution.py:339
  72.9 0.8 %copy-start.15 = (bf16[128,2048]{1,0:T(8,128)(2,1)}, bf16[128,2048]{1,0:T(8,128)(2,1)S(1)}, u32[]{:S(2)}) copy-start(bf16[128,2048]{1,0:T(8,128)(2,1)S(1)} %collective-permute-done.15.refs_8_) | copy-start | bytes 1572868
  (2 other events, 1.4 us)

commit v8 on v2

v8 whole, which is shorter than its diff:
```python
import functools
import math

import jax
import jax.numpy as jnp
from jax import lax
from jax.experimental import pallas as pl
from jax.experimental.pallas import tpu as pltpu
from jax.sharding import PartitionSpec as P

SPAN = 64
STACKS = (4, 4)
UNROLL = 2
CHUNKS = (3, 5)
DIRECT = 16
VMEM = 60 * 1024 * 1024
RESIDENT = 40 * 1024 * 1024
SHORT = pl.CostEstimate(flops=0, bytes_accessed=0, transcendentals=0)
MASKED = -1e30
OPEN = 3e38
NT = (((1,), (1,)), ((), ()))


def dot(left, right):
    return jnp.dot(left, right, preferred_element_type=jnp.float32)


def build_table(me, count, routes_ref, table_ref, capacity):
    slots = routes_ref.shape[1]
    rows = table_ref.shape[0]
    place = lax.broadcasted_iota(jnp.int32, (rows, slots), 0)
    token = lax.broadcasted_iota(jnp.int32, (rows, slots), 1)
    block = place // capacity
    side = rows // capacity // 2
    expert = jnp.where(block < side, me // side * side + block, block ^ me)
    hit = ((routes_ref[0:1, :] == expert) | (routes_ref[1:2, :] == expert)) & (
        token < count * SPAN
    )
    hit = jnp.where(hit, jnp.float32(1.0), jnp.float32(0.0))
    first = lax.broadcasted_iota(jnp.int32, (slots, slots), 0)
    second = lax.broadcasted_iota(jnp.int32, (slots, slots), 1)
    earlier = jnp.where(first < second, jnp.float32(1.0), jnp.float32(0.0))
    before = dot(hit.astype(jnp.bfloat16), earlier.astype(jnp.bfloat16))
    wanted = (place - block * capacity).astype(jnp.float32)
    table_ref[...] = jnp.where(before == wanted, hit, jnp.float32(0.0)).astype(jnp.bfloat16)


def attend_kernel(
    capacity,
    stack,
    first,
    heads,
    earlier,
    after,
    resident,
    me_ref,
    count_ref,
    size_ref,
    routes_ref,
    queries_ref,
    key_weight_ref,
    value_weight_ref,
    prefix_ref,
    fresh_ref,
    *rest,
):
    earlier_refs, rest = rest[:earlier], rest[earlier + after :]
    *out_refs, queries_own, key_weight_own, value_weight_own, keys_ref = rest[:-4]
    cap_ref, table_ref, attended_ref, sem = rest[-4:]
    slots = queries_ref.shape[0]
    past = prefix_ref.shape[0]
    dim = key_weight_ref.shape[1]
    steps = heads // stack

    copies = []

    def start_copy(source, target):
        copies.append(pltpu.make_async_copy(source, target, sem.at[len(copies)]))
        copies[-1].start()

    if not resident:
        here = pl.ds(first, heads)
        start_copy(queries_ref.at[:, pl.ds(first * dim, heads * dim)], queries_own)
        start_copy(key_weight_ref.at[here], key_weight_own)
        start_copy(prefix_ref, keys_ref.at[pl.ds(0, past)])
        start_copy(fresh_ref, keys_ref.at[pl.ds(past, slots)])
        start_copy(value_weight_ref.at[here], value_weight_own)
        queries_ref, key_weight_ref, value_weight_ref = queries_own, key_weight_own, value_weight_own
        first = 0
    own = len(copies)
    for piece_ref in earlier_refs:
        start_copy(piece_ref, out_refs[0].at[:, pl.ds(0, piece_ref.shape[1])])
    if resident:
        keys_ref[:past] = prefix_ref[...]
        keys_ref[past:] = fresh_ref[...]

    count, size = count_ref[0], size_ref[0]
    lane = lax.broadcasted_iota(jnp.int32, (slots, past), 1)
    cap_ref[:, :past] = jnp.where(lane < size, jnp.float32(OPEN), jnp.float32(MASKED))
    row = lax.broadcasted_iota(jnp.int32, (slots, slots), 0)
    col = lax.broadcasted_iota(jnp.int32, (slots, slots), 1)
    cap_ref[:, past:] = jnp.where(
        (col <= row) & (col < count * SPAN), jnp.float32(OPEN), jnp.float32(MASKED)
    )
    build_table(me_ref[0], count, routes_ref, table_ref, capacity)
    for copy in copies[:own]:
        copy.wait()

    scale = math.log2(math.e) / math.sqrt(dim)

    def columns(h):
        return pl.ds(pl.multiple_of(h * dim, dim), dim)

    def body(i, carry):
        keys = keys_ref[...]
        lifted = []
        for g in range(stack):
            h = first + i * stack + g
            one = dot(queries_ref[:, columns(h)], key_weight_ref[h])
            lifted.append(one.astype(jnp.bfloat16))
        lifted = jnp.concatenate(lifted, axis=0)
        score = lax.dot_general(lifted, keys, NT, preferred_element_type=jnp.float32)
        score = score.reshape(stack, slots, keys.shape[0])
        score = jnp.minimum(score, cap_ref[...][None])
        highest = jnp.max(score, axis=-1, keepdims=True) * scale
        weights = jnp.exp2(score * scale - highest)
        total = jnp.sum(weights, axis=-1, keepdims=True)
        weights = weights.astype(jnp.bfloat16).reshape(stack * slots, keys.shape[0])
        mixed = dot(weights, keys).astype(jnp.bfloat16)
        for g in range(stack):
            h = i * stack + g
            projected = dot(mixed[g * slots : (g + 1) * slots], value_weight_ref[first + h])
            attended_ref[:, columns(h)] = (projected / total[g]).astype(jnp.bfloat16)
        return carry

    lax.fori_loop(0, steps, body, 0, unroll=min(steps, UNROLL))
    grouped = dot(table_ref[...], attended_ref[...]).astype(jnp.bfloat16)
    row = 0
    for out_ref in out_refs:
        rows, width = out_ref.shape
        out_ref[:, width - heads * dim :] = grouped[row : row + rows]
        row += rows
    for copy in copies[own:]:
        copy.wait()


def attend(
    stack, first, heads, me, queries, key_weight, value_weight, prefix, fresh, count, size, routes, experts, parts, earlier, after
):
    slots = queries.shape[0]
    _, dim, latent = key_weight.shape
    places = slots * routes.shape[1]
    keys = prefix.shape[0] + slots
    resident = first > 0
    smem = pl.BlockSpec(memory_space=pltpu.SMEM)
    vmem = pl.BlockSpec(memory_space=pltpu.VMEM)
    hbm = pl.BlockSpec(memory_space=pltpu.HBM)
    pieces = [(rows, heads * dim) for rows in parts]
    if earlier:
        pieces[0] = (parts[0], heads * dim + earlier[0].shape[1])
    own = 0 if resident else heads
    return pl.pallas_call(
        functools.partial(
            attend_kernel,
            places // experts,
            stack,
            first,
            heads,
            len(earlier),
            len(after),
            resident,
        ),
        in_specs=[smem, smem, smem, vmem] + [vmem if resident else hbm] * 5 + [hbm] * len(earlier + after),
        out_specs=[vmem] * len(pieces),
        out_shape=[jax.ShapeDtypeStruct(piece, jnp.bfloat16) for piece in pieces],
        scratch_shapes=[
            pltpu.VMEM((slots, max(own, 1) * dim), jnp.bfloat16),
            pltpu.VMEM((max(own, 1), dim, latent), jnp.bfloat16),
            pltpu.VMEM((max(own, 1), latent, dim), jnp.bfloat16),
            pltpu.VMEM((keys, latent), jnp.bfloat16),
            pltpu.VMEM((slots, keys), jnp.float32),
            pltpu.VMEM((places, slots), jnp.bfloat16),
            pltpu.VMEM((slots, heads * dim), jnp.bfloat16),
            pltpu.SemaphoreType.DMA((5 + len(earlier),)),
        ],
        compiler_params=pltpu.CompilerParams(vmem_limit_bytes=RESIDENT if resident else VMEM),
        cost_estimate=SHORT,
    )(me, count, size, routes.T, queries, key_weight, value_weight, prefix, fresh, *earlier, *after)


def run_copies(copies):
    for copy in copies:
        copy.start()
    for copy in copies:
        copy.wait()


def pass_on_kernel(count, cores, *refs):
    piece_refs, out_ref = refs[-1 - count : -1], refs[-1]
    capacity = piece_refs[0].shape[0] // cores
    for i, piece_ref in enumerate(piece_refs):
        out_ref[i * capacity : (i + 1) * capacity] = piece_ref[capacity:]


def pass_on(pieces, after, cores):
    rows, width = pieces[0].shape
    vmem = pl.BlockSpec(memory_space=pltpu.VMEM)
    return pl.pallas_call(
        functools.partial(pass_on_kernel, len(pieces), cores),
        in_specs=[pl.BlockSpec(memory_space=pl.ANY)] * len(after) + [vmem] * len(pieces),
        out_specs=vmem,
        out_shape=jax.ShapeDtypeStruct((len(pieces) * rows // cores, width), jnp.bfloat16),
        compiler_params=pltpu.CompilerParams(vmem_limit_bytes=RESIDENT),
        cost_estimate=SHORT,
    )(*after, *pieces)


def place_kernel(plan, cores, me_ref, *refs):
    out_ref, mark_ref, sem = refs[-3:]
    mark_ref[...] = jnp.zeros_like(mark_ref)
    me = me_ref[0]
    _, _, capacity, features = out_ref.shape
    features //= cores
    copies = []
    for ref, row, start, width, bits, side in plan:
        who = me // side * side + bits if side else me ^ bits
        left = pl.multiple_of(who % cores * features + start, math.gcd(features, start))
        target = out_ref.at[0, who // cores, :, pl.ds(left, width)]
        source = refs[ref].at[pl.ds(row, capacity)]
        copies.append(pltpu.make_async_copy(source, target, sem.at[len(copies)]))
    run_copies(copies)


def place(me, arrays, plan, cores, shape, placed):
    anywhere = pl.BlockSpec(memory_space=pl.ANY)
    operands = [me, *arrays] + placed
    return pl.pallas_call(
        functools.partial(place_kernel, plan, cores),
        in_specs=[pl.BlockSpec(memory_space=pltpu.SMEM)]
        + [pl.BlockSpec(memory_space=pltpu.VMEM)] * len(arrays)
        + [anywhere] * len(placed),
        out_specs=[anywhere, pl.BlockSpec(memory_space=pltpu.VMEM)],
        out_shape=[
            jax.ShapeDtypeStruct(shape, jnp.bfloat16),
            jax.ShapeDtypeStruct((8, 128), jnp.float32),
        ],
        scratch_shapes=[pltpu.SemaphoreType.DMA((len(plan),))],
        input_output_aliases={len(operands) - 1: 0} if placed else {},
        compiler_params=pltpu.CompilerParams(vmem_limit_bytes=RESIDENT),
        cost_estimate=SHORT,
    )(*operands)


def local(
    queries,
    key_weight,
    value_weight,
    prefix_latent,
    fresh_latent,
    span_counts,
    prefix_lengths,
    routes,
):
    ranks, cores = lax.axis_size("dp"), lax.axis_size("ep")
    experts = ranks * cores
    slots = queries.shape[0]
    heads, dim, _ = key_weight.shape
    capacity = slots * routes.shape[1] // experts
    direct = ranks <= DIRECT and capacity % 16 == 0
    index = lax.axis_index("dp") * cores + lax.axis_index("ep")
    me = (index if direct else jnp.int32(0)).astype(jnp.int32).reshape(1)
    shares = [heads * share // sum(CHUNKS) for share in CHUNKS]
    far = list(range(ranks // 2, ranks, 2)) + list(range(ranks // 2 + 1, ranks, 2))
    side = experts // 2
    starts = [0]
    for share in shares:
        starts.append(starts[-1] + share)

    def run(chunk, earlier, after):
        return attend(
            STACKS[chunk],
            starts[chunk],
            shares[chunk],
            me,
            queries,
            key_weight,
            value_weight,
            prefix_latent,
            fresh_latent,
            span_counts,
            prefix_lengths,
            routes,
            experts,
            [side * capacity] + [cores * capacity] * len(far) if direct else [experts * capacity],
            earlier,
            after,
        )

    if not direct:
        arrays = []
        for chunk in range(len(shares)):
            arrived = lax.all_to_all(
                run(chunk, [], [])[0].reshape(experts, capacity, -1),
                ("dp", "ep"),
                split_axis=0,
                concat_axis=0,
                tiled=True,
            )
            arrays.append(arrived.reshape(ranks, cores, capacity, -1))
        arrived = jnp.concatenate(arrays, axis=3).transpose(0, 2, 1, 3)
        return arrived.reshape(1, ranks, capacity, cores * heads * dim)

    def to_chip(piece, j):
        return lax.ppermute(piece, "dp", [(i, i ^ j) for i in range(ranks)])

    def to_core(piece):
        return lax.ppermute(piece, "ep", [(i, i ^ 1) for i in range(cores)])

    def far_pieces(outgoing):
        return [to_chip(outgoing[1 + j - ranks // 2], j) for j in far]

    first = run(0, [], [])
    first_far = far_pieces(first)
    last = run(1, first[:1], first[1:2])
    last_far = far_pieces(last)
    near = lax.all_to_all(
        last[0].reshape(side, capacity, -1),
        ("dp", "ep"),
        split_axis=0,
        concat_axis=0,
        axis_index_groups=[list(range(i, i + side)) for i in range(0, experts, side)],
        tiled=True,
    ).reshape(side * capacity, -1)
    first_message = pass_on(first_far, last[1:2], cores)
    first_swapped = to_core(first_message)

    def plan_of(at, start, width):
        plan = []
        for i, j in enumerate(far):
            plan.append((at + i, 0, start, width, j * cores, 0))
            plan.append((at + len(far), i * capacity, start, width, j * cores + 1, 0))
        return plan

    shape = (1, ranks, capacity, cores * heads * dim)
    middle = shares[0] * dim
    plan = plan_of(0, 0, middle)
    plan += [(len(far) + 1, i * capacity, 0, heads * dim, i, side) for i in range(side)]
    placed, mark = place(me, first_far + [first_swapped, near], plan, cores, shape, [])
    last_swapped = to_core(pass_on(last_far, [mark], cores))
    plan = plan_of(0, middle, shares[1] * dim)
    return place(me, last_far + [last_swapped], plan, cores, shape, [placed])[0]


def solution(mesh):
    in_specs = (
        P(("groups", "dp"), "ep"),
        P("ep", None, None),
        P("ep", None, None),
        P(("groups", "dp"), None),
        P(("groups", "dp"), None),
        P(("groups", "dp")),
        P(("groups", "dp")),
        P(("groups", "dp"), None),
    )
    out_specs = P(("groups", "dp", "ep"), None, None, None)
    return jax.shard_map(local, mesh=mesh, in_specs=in_specs, out_specs=out_specs, check_vma=False)
```

time: 124 us -> 97.9 us (0.79)
  starting transfers between devices: 84 us -> 20.2 us
  waiting for transfers between devices: 6.44 us -> 42.6 us
  Pallas kernels: 19.9 us -> 26.9 us
  local copies, waits for them, and re-layouts: 11.4 us -> 6.29 us
    ppermute x60 -> x10, starting transfers between devices: 84 us -> 14.9 us  [the longest x8 14.7 us: to_chip(): return lax.ppermute(piece, 'dp', [(i, i ^ j) for i in range(ranks)])]
    ppermute x60 -> x10, waiting for transfers between devices: 6.44 us -> 42.6 us  [the longest x8 41 us: to_chip(): return lax.ppermute(piece, 'dp', [(i, i ^ j) for i in range(ranks)])]
    pallas_call x5 -> x6, Pallas kernels: 19.9 us -> 26.9 us  [the longest x2 24.2 us: attend(): pl.pallas_call(functools.partial(attend_kernel, places // experts, stack,...]
    all_to_all x0 -> x1, starting transfers between devices: none -> 5.27 us  [local(): lax.all_to_all(last[0].reshape(side, capacity, -1), ('dp', 'ep'), split_a...]
    unnamed x140 -> x24, local copies, waits for them, and re-layouts: 11.4 us -> 6.29 us
  transfers between devices with their start and end apart: 60 -> 11, of which waited for: 3 -> 6; matrix products, arithmetic and copies ran while one was open for 0% -> 0% of each run, Pallas kernels for 10% -> 1%
where the time goes in v8:
time: 97.9 us; the launch traced here: 97.6 us
  waiting for transfers between devices  42.6 us (44%)
  Pallas kernels  26.9 us (27%)
  starting transfers between devices  20.2 us (21%)
  local copies, waits for them, and re-layouts  6.29 us (6%)
  between operations  1.6 us (2%)
    ppermute x8, waiting for transfers between devices, to_chip(): return lax.ppermute(piece, 'dp', [(i, i ^ j) for i in range(ranks)])  41 us
    pallas_call x2, Pallas kernels, attend(): pl.pallas_call(functools.partial(attend_kernel, places // experts, stack,...  24.2 us
    ppermute x8, starting transfers between devices, to_chip(): return lax.ppermute(piece, 'dp', [(i, i ^ j) for i in range(ranks)])  14.7 us
    unnamed x24, local copies, waits for them, and re-layouts  6.29 us
    all_to_all x1, starting transfers between devices, local(): lax.all_to_all(last[0].reshape(side, capacity, -1), ('dp', 'ep'), split_a...  5.27 us
    pallas_call x2, Pallas kernels, place(): pl.pallas_call(functools.partial(place_kernel, plan, cores), in_specs=[pl...  2.7 us
  transfers between devices with their start and end apart: 11, of which 6 were waited for; matrix products, arithmetic and copies ran while one was open for 0% of the time, Pallas kernels for 1%

profile of v8, /device:TPU:0, one launch (start us, length us, event | category | flops | bytes accessed | tf_op | source)
XLA Modules:
  0.0 97.6 jit_solution(1098976492513631109)
XLA Ops:
  1.3 10.7 %shard_map.82 = (bf16[128,1536]{1,0:T(8,128)(2,1)}, bf16[32,1536]{1,0:T(8,128)(2,1)}, bf16[32,1536]{1,0:T(8,128)(2,1)}, bf16[32,1536]{1,0:T(8,128)(2,1)}, bf16[32,1536]{1,0:T(8,128)(2,1)}) custom-call(s32[1]{0:T(128)} %bitcast.me_ref, s32[1]{0:T(128)S(6)} %copy.11.count_ref, s32[1]{0:T(128)S(6)} %copy.12.size_ref, s32[2,128]{1,0:T(2,128)} %bitcast.5, ...), custom_call_target="tpu_custom_call" | custom-call | tf_op jit(solution)/shard_map/pallas_call | solution.py:162
  12.1 0.0 copy-start
  12.1 2.2 %copy-done = bf16[32,128,512]{2,1,0:T(8,128)(2,1)S(1)} copy-done((bf16[32,128,512]{2,1,0:T(8,128)(2,1)S(1)}, bf16[32,128,512]{2,1,0:T(8,128)(2,1)}, u32[]{:S(2)}) %copy-start) | copy-done | bytes 4194328
  14.3 2.2 %copy-done.1 = bf16[32,512,128]{2,1,0:T(8,128)(2,1)S(1)} copy-done((bf16[32,512,128]{2,1,0:T(8,128)(2,1)S(1)}, bf16[32,512,128]{2,1,0:T(8,128)(2,1)}, u32[]{:S(2)}) %copy-start.1) | copy-done | bytes 4194328
  16.5 1.0 %copy-done.5 = bf16[128,1536]{1,0:T(8,128)(2,1)S(1)} copy-done((bf16[128,1536]{1,0:T(8,128)(2,1)S(1)}, bf16[128,1536]{1,0:T(8,128)(2,1)}, u32[]{:S(2)}) %copy-start.5) | copy-done | bytes 393240
  17.5 0.9 copy-done.6
  18.4 13.5 %shard_map.83 = (bf16[128,4096]{1,0:T(8,128)(2,1)}, bf16[32,2560]{1,0:T(8,128)(2,1)S(1)}, bf16[32,2560]{1,0:T(8,128)(2,1)S(1)}, bf16[32,2560]{1,0:T(8,128)(2,1)S(1)}, bf16[32,2560]{1,0:T(8,128)(2,1)S(1)}) custom-call(s32[1]{0:T(128)} %bitcast.me_ref, s32[1]{0:T(128)S(6)} %copy.11.count_ref, s32[1]{0:T(128)S(6)} %copy.12.size_ref, s32[2,128]{1,0:T(2,128)S(1)} %bitcast.6, ...), custom_call_target="tpu_custom_call" | custom-call | tf_op jit(solution)/shard_map/pallas_call | solution.py:162
  31.8 5.3 %all-to-all-start = ((bf16[8,16,4096]{2,1,0:T(8,128)(2,1)}), bf16[8,16,4096]{2,1,0:T(8,128)(2,1)S(1)}, u32[]{:S(2)}, u32[]{:S(2)}) async-start(bf16[8,16,4096]{2,1,0:T(8,128)(2,1)} %bitcast.2), calls=%async_computation | async-start | bytes 2097152 | tf_op jit(solution)/shard_map/all_to_all | solution.py:326
  37.1 0.0 copy-done.11
  37.1 4.0 %collective-permute-start.5 = (bf16[32,1536]{1,0:T(8,128)(2,1)S(1)}, bf16[32,1536]{1,0:T(8,128)(2,1)S(1)}, u32[]{:S(2)}, u32[]{:S(2)}) collective-permute-start(bf16[32,1536]{1,0:T(8,128)(2,1)S(1)} %copy-done.11), channel_id=1, source_target_pairs={{0,12},{2,14},{4,8},{6,10},{8,4},{10,6},{12,0},{14,2},{1,13},{3,15... | collective-permute-start | bytes 294920 | tf_op jit(solution)/shard_map/ppermute | solution.py:314
  41.2 0.3 collective-permute-start.6
  41.5 2.1 %collective-permute-start.7 = (bf16[32,1536]{1,0:T(8,128)(2,1)S(1)}, bf16[32,1536]{1,0:T(8,128)(2,1)S(1)}, u32[]{:S(2)}, u32[]{:S(2)}) collective-permute-start(bf16[32,1536]{1,0:T(8,128)(2,1)S(1)} %copy-done.9), channel_id=1, source_target_pairs={{0,14},{2,12},{4,10},{6,8},{8,6},{10,4},{12,2},{14,0},{1,15},{3,13... | collective-permute-start | bytes 294920 | tf_op jit(solution)/shard_map/ppermute | solution.py:314
  43.6 1.5 %collective-permute-start.4 = (bf16[32,1536]{1,0:T(8,128)(2,1)S(1)}, bf16[32,1536]{1,0:T(8,128)(2,1)S(1)}, u32[]{:S(2)}, u32[]{:S(2)}) collective-permute-start(bf16[32,1536]{1,0:T(8,128)(2,1)S(1)} %copy-done.7), channel_id=1, source_target_pairs={{0,8},{2,10},{4,12},{6,14},{8,0},{10,2},{12,4},{14,6},{1,9},{3,11}... | collective-permute-start | bytes 294920 | tf_op jit(solution)/shard_map/ppermute | solution.py:314
  45.1 12.0 %collective-permute-done.5.refs_2_.refs_1_ = bf16[32,1536]{1,0:T(8,128)(2,1)S(1)} collective-permute-done((bf16[32,1536]{1,0:T(8,128)(2,1)S(1)}, bf16[32,1536]{1,0:T(8,128)(2,1)S(1)}, u32[]{:S(2)}, u32[]{:S(2)}) %collective-permute-start.5) | collective-permute-done | bytes 98336 | tf_op jit(solution)/shard_map/ppermute | solution.py:314
  57.1 0.0 collective-permute-done.6.refs_3_.refs_2_
  57.1 5.0 %collective-permute-done.7.refs_4_.refs_3_ = bf16[32,1536]{1,0:T(8,128)(2,1)S(1)} collective-permute-done((bf16[32,1536]{1,0:T(8,128)(2,1)S(1)}, bf16[32,1536]{1,0:T(8,128)(2,1)S(1)}, u32[]{:S(2)}, u32[]{:S(2)}) %collective-permute-start.7) | collective-permute-done | bytes 98336 | tf_op jit(solution)/shard_map/ppermute | solution.py:314
  62.1 0.0 collective-permute-done.4.refs_1_.refs_0_
  62.2 0.1 collective-permute-start.8
  62.2 0.4 collective-permute-start.1
  62.6 3.4 %collective-permute-start.2 = (bf16[32,2560]{1,0:T(8,128)(2,1)S(1)}, bf16[32,2560]{1,0:T(8,128)(2,1)S(1)}, u32[]{:S(2)}, u32[]{:S(2)}) collective-permute-start(bf16[32,2560]{1,0:T(8,128)(2,1)S(1)} %get-tuple-element.22), channel_id=1, source_target_pairs={{0,10},{2,8},{4,14},{6,12},{8,2},{10,0},{12,6},{14,4},{1,11},{3,9}... | collective-permute-start | bytes 491528 | tf_op jit(solution)/shard_map/ppermute | solution.py:314
  66.0 1.1 %collective-permute-start.3 = (bf16[32,2560]{1,0:T(8,128)(2,1)S(1)}, bf16[32,2560]{1,0:T(8,128)(2,1)S(1)}, u32[]{:S(2)}, u32[]{:S(2)}) collective-permute-start(bf16[32,2560]{1,0:T(8,128)(2,1)S(1)} %get-tuple-element.23), channel_id=1, source_target_pairs={{0,14},{2,12},{4,10},{6,8},{8,6},{10,4},{12,2},{14,0},{1,15},{3,13... | collective-permute-start | bytes 491528 | tf_op jit(solution)/shard_map/ppermute | solution.py:314
  67.0 2.0 %collective-permute-start = (bf16[32,2560]{1,0:T(8,128)(2,1)S(1)}, bf16[32,2560]{1,0:T(8,128)(2,1)S(1)}, u32[]{:S(2)}, u32[]{:S(2)}) collective-permute-start(bf16[32,2560]{1,0:T(8,128)(2,1)S(1)} %get-tuple-element.20.refs_0_), channel_id=1, source_target_pairs={{0,8},{2,10},{4,12},{6,14},{8,0},{10,2},{12,4},{14,6},{1,9},{3,11}... | collective-permute-start | bytes 491528 | tf_op jit(solution)/shard_map/ppermute | solution.py:314
  69.0 0.0 collective-permute-done.8.refs_4_
  69.1 0.0 all-to-all-done
  69.1 1.2 %shard_map.85 = (bf16[1,8,16,8192]{3,2,1,0:T(8,128)(2,1)}, f32[8,128]{1,0:T(8,128)S(1)}) custom-call(s32[1]{0:T(128)} %bitcast.me_ref, bf16[32,1536]{1,0:T(8,128)(2,1)S(1)} %collective-permute-done.4.refs_1_.refs_0_, bf16[32,1536]{1,0:T(8,128)(2,1)S(1)} %collective-permute-done.5.refs_2_.refs_1_, ...), custom_call_target="tpu_custom_call" | custom-call | tf_op jit(solution)/shard_map/pallas_call | solution.py:237
  70.3 0.9 collective-permute-done.1.refs_2_.refs_1_
  71.2 17.2 %collective-permute-done.2.refs_3_.refs_2_ = bf16[32,2560]{1,0:T(8,128)(2,1)S(1)} collective-permute-done((bf16[32,2560]{1,0:T(8,128)(2,1)S(1)}, bf16[32,2560]{1,0:T(8,128)(2,1)S(1)}, u32[]{:S(2)}, u32[]{:S(2)}) %collective-permute-start.2) | collective-permute-done | bytes 163872 | tf_op jit(solution)/shard_map/ppermute | solution.py:314
  88.4 0.0 collective-permute-done.3.refs_4_.refs_3_
  88.4 5.9 %collective-permute-done.refs_1_.refs_0_ = bf16[32,2560]{1,0:T(8,128)(2,1)S(1)} collective-permute-done((bf16[32,2560]{1,0:T(8,128)(2,1)S(1)}, bf16[32,2560]{1,0:T(8,128)(2,1)S(1)}, u32[]{:S(2)}, u32[]{:S(2)}) %collective-permute-start) | collective-permute-done | bytes 163872 | tf_op jit(solution)/shard_map/ppermute | solution.py:314
  94.3 0.1 collective-permute-start.9
  94.3 1.6 %collective-permute-done.9.refs_4_ = bf16[64,2560]{1,0:T(8,128)(2,1)S(1)} collective-permute-done((bf16[64,2560]{1,0:T(8,128)(2,1)S(1)}, bf16[64,2560]{1,0:T(8,128)(2,1)S(1)}, u32[]{:S(2)}, u32[]{:S(2)}) %collective-permute-start.9) | collective-permute-done | bytes 327712 | tf_op jit(solution)/shard_map/ppermute | solution.py:317
  96.0 1.5 %shard_map.87 = (bf16[1,8,16,8192]{3,2,1,0:T(8,128)(2,1)}, f32[8,128]{1,0:T(8,128)}) custom-call(s32[1]{0:T(128)} %bitcast.me_ref, bf16[32,2560]{1,0:T(8,128)(2,1)S(1)} %collective-permute-done.refs_1_.refs_0_, bf16[32,2560]{1,0:T(8,128)(2,1)S(1)} %collective-permute-done.1.refs_2_.refs_1_, ...), custom_call_target="tpu_custom_call", output_to_operand_aliasing={{0}: (6, {})} | custom-call | tf_op jit(solution)/shard_map/pallas_call | solution.py:237
  (20 shorter events, 0.1 us)
Async XLA Ops:
  1.3 10.7 %copy-start.2 = (bf16[128,4096]{1,0:T(8,128)(2,1)S(1)}, bf16[128,4096]{1,0:T(8,128)(2,1)}, u32[]{:S(2)}) copy-start(bf16[128,4096]{1,0:T(8,128)(2,1)} %queries_ref.3) | copy-start | bytes 3145732
  1.3 10.7 %copy-start.3 = (bf16[1024,512]{1,0:T(8,128)(2,1)S(1)}, bf16[1024,512]{1,0:T(8,128)(2,1)}, u32[]{:S(2)}) copy-start(bf16[1024,512]{1,0:T(8,128)(2,1)} %prefix_ref.3) | copy-start | bytes 3145732
  1.3 10.7 %copy-start.4 = (bf16[128,512]{1,0:T(8,128)(2,1)S(1)}, bf16[128,512]{1,0:T(8,128)(2,1)}, u32[]{:S(2)}) copy-start(bf16[128,512]{1,0:T(8,128)(2,1)} %fresh_ref.3) | copy-start | bytes 393220
  1.3 10.7 %copy-start.8 = (s32[128,2]{0,1:T(2,128)S(1)}, s32[128,2]{0,1:T(2,128)}, u32[]{:S(2)}) copy-start(s32[128,2]{0,1:T(2,128)} %param.15) | copy-start | bytes 3076
  12.1 2.2 %copy-start = (bf16[32,128,512]{2,1,0:T(8,128)(2,1)S(1)}, bf16[32,128,512]{2,1,0:T(8,128)(2,1)}, u32[]{:S(2)}) copy-start(bf16[32,128,512]{2,1,0:T(8,128)(2,1)} %key_weight_ref.3) | copy-start | bytes 12582916
  14.3 2.2 %copy-start.1 = (bf16[32,512,128]{2,1,0:T(8,128)(2,1)S(1)}, bf16[32,512,128]{2,1,0:T(8,128)(2,1)}, u32[]{:S(2)}) copy-start(bf16[32,512,128]{2,1,0:T(8,128)(2,1)} %value_weight_ref.3) | copy-start | bytes 12582916
  16.5 1.0 %copy-start.5 = (bf16[128,1536]{1,0:T(8,128)(2,1)S(1)}, bf16[128,1536]{1,0:T(8,128)(2,1)}, u32[]{:S(2)}) copy-start(bf16[128,1536]{1,0:T(8,128)(2,1)} %get-tuple-element.18.rest_0_) | copy-start | bytes 1179652
  17.5 0.9 copy-start.6
  18.3 18.8 %copy-start.11 = (bf16[32,1536]{1,0:T(8,128)(2,1)S(1)}, bf16[32,1536]{1,0:T(8,128)(2,1)}, u32[]{:S(2)}) copy-start(bf16[32,1536]{1,0:T(8,128)(2,1)} %get-tuple-element.24) | copy-start | bytes 294916
  18.4 22.8 %copy-start.10 = (bf16[32,1536]{1,0:T(8,128)(2,1)S(1)}, bf16[32,1536]{1,0:T(8,128)(2,1)}, u32[]{:S(2)}) copy-start(bf16[32,1536]{1,0:T(8,128)(2,1)} %get-tuple-element.25) | copy-start | bytes 294916
  18.4 23.1 %copy-start.9 = (bf16[32,1536]{1,0:T(8,128)(2,1)S(1)}, bf16[32,1536]{1,0:T(8,128)(2,1)}, u32[]{:S(2)}) copy-start(bf16[32,1536]{1,0:T(8,128)(2,1)} %get-tuple-element.26) | copy-start | bytes 294916
  18.4 25.2 %copy-start.7 = (bf16[32,1536]{1,0:T(8,128)(2,1)S(1)}, bf16[32,1536]{1,0:T(8,128)(2,1)}, u32[]{:S(2)}) copy-start(bf16[32,1536]{1,0:T(8,128)(2,1)} %get-tuple-element.19.rest_1_) | copy-start | bytes 294916
  31.8 37.2 %all-to-all-start = ((bf16[8,16,4096]{2,1,0:T(8,128)(2,1)}), bf16[8,16,4096]{2,1,0:T(8,128)(2,1)S(1)}, u32[]{:S(2)}, u32[]{:S(2)}) async-start(bf16[8,16,4096]{2,1,0:T(8,128)(2,1)} %bitcast.2), calls=%async_computation | async-start | bytes 2097152 | tf_op jit(solution)/shard_map/all_to_all | solution.py:326
  37.1 20.0 %collective-permute-start.5 = (bf16[32,1536]{1,0:T(8,128)(2,1)S(1)}, bf16[32,1536]{1,0:T(8,128)(2,1)S(1)}, u32[]{:S(2)}, u32[]{:S(2)}) collective-permute-start(bf16[32,1536]{1,0:T(8,128)(2,1)S(1)} %copy-done.11), channel_id=1, source_target_pairs={{0,12},{2,14},{4,8},{6,10},{8,4},{10,6},{12,0},{14,2},{1,13},{3,15... | collective-permute-start | bytes 294920 | tf_op jit(solution)/shard_map/ppermute | solution.py:314
  41.2 15.9 %collective-permute-start.6 = (bf16[32,1536]{1,0:T(8,128)(2,1)S(1)}, bf16[32,1536]{1,0:T(8,128)(2,1)S(1)}, u32[]{:S(2)}, u32[]{:S(2)}) collective-permute-start(bf16[32,1536]{1,0:T(8,128)(2,1)S(1)} %copy-done.10), channel_id=1, source_target_pairs={{0,10},{2,8},{4,14},{6,12},{8,2},{10,0},{12,6},{14,4},{1,11},{3,9}... | collective-permute-start | bytes 294920 | tf_op jit(solution)/shard_map/ppermute | solution.py:314
  41.5 20.6 %collective-permute-start.7 = (bf16[32,1536]{1,0:T(8,128)(2,1)S(1)}, bf16[32,1536]{1,0:T(8,128)(2,1)S(1)}, u32[]{:S(2)}, u32[]{:S(2)}) collective-permute-start(bf16[32,1536]{1,0:T(8,128)(2,1)S(1)} %copy-done.9), channel_id=1, source_target_pairs={{0,14},{2,12},{4,10},{6,8},{8,6},{10,4},{12,2},{14,0},{1,15},{3,13... | collective-permute-start | bytes 294920 | tf_op jit(solution)/shard_map/ppermute | solution.py:314
  43.6 18.5 %collective-permute-start.4 = (bf16[32,1536]{1,0:T(8,128)(2,1)S(1)}, bf16[32,1536]{1,0:T(8,128)(2,1)S(1)}, u32[]{:S(2)}, u32[]{:S(2)}) collective-permute-start(bf16[32,1536]{1,0:T(8,128)(2,1)S(1)} %copy-done.7), channel_id=1, source_target_pairs={{0,8},{2,10},{4,12},{6,14},{8,0},{10,2},{12,4},{14,6},{1,9},{3,11}... | collective-permute-start | bytes 294920 | tf_op jit(solution)/shard_map/ppermute | solution.py:314
  62.2 6.9 %collective-permute-start.8 = (bf16[64,1536]{1,0:T(8,128)(2,1)S(1)}, bf16[64,1536]{1,0:T(8,128)(2,1)S(1)}, u32[]{:S(2)}, u32[]{:S(2)}) collective-permute-start(bf16[64,1536]{1,0:T(8,128)(2,1)S(1)} %shard_map.84), channel_id=1, source_target_pairs={{0,1},{1,0},{2,3},{3,2},{4,5},{5,4},{6,7},{7,6},{8,9},{9,8},{10,11... | collective-permute-start | bytes 589832 | tf_op jit(solution)/shard_map/ppermute | solution.py:317
  62.2 9.0 %collective-permute-start.1 = (bf16[32,2560]{1,0:T(8,128)(2,1)S(1)}, bf16[32,2560]{1,0:T(8,128)(2,1)S(1)}, u32[]{:S(2)}, u32[]{:S(2)}) collective-permute-start(bf16[32,2560]{1,0:T(8,128)(2,1)S(1)} %get-tuple-element.21), channel_id=1, source_target_pairs={{0,12},{2,14},{4,8},{6,10},{8,4},{10,6},{12,0},{14,2},{1,13},{3,15... | collective-permute-start | bytes 491528 | tf_op jit(solution)/shard_map/ppermute | solution.py:314
  62.6 25.8 %collective-permute-start.2 = (bf16[32,2560]{1,0:T(8,128)(2,1)S(1)}, bf16[32,2560]{1,0:T(8,128)(2,1)S(1)}, u32[]{:S(2)}, u32[]{:S(2)}) collective-permute-start(bf16[32,2560]{1,0:T(8,128)(2,1)S(1)} %get-tuple-element.22), channel_id=1, source_target_pairs={{0,10},{2,8},{4,14},{6,12},{8,2},{10,0},{12,6},{14,4},{1,11},{3,9}... | collective-permute-start | bytes 491528 | tf_op jit(solution)/shard_map/ppermute | solution.py:314
  66.0 22.4 %collective-permute-start.3 = (bf16[32,2560]{1,0:T(8,128)(2,1)S(1)}, bf16[32,2560]{1,0:T(8,128)(2,1)S(1)}, u32[]{:S(2)}, u32[]{:S(2)}) collective-permute-start(bf16[32,2560]{1,0:T(8,128)(2,1)S(1)} %get-tuple-element.23), channel_id=1, source_target_pairs={{0,14},{2,12},{4,10},{6,8},{8,6},{10,4},{12,2},{14,0},{1,15},{3,13... | collective-permute-start | bytes 491528 | tf_op jit(solution)/shard_map/ppermute | solution.py:314
  67.0 27.2 %collective-permute-start = (bf16[32,2560]{1,0:T(8,128)(2,1)S(1)}, bf16[32,2560]{1,0:T(8,128)(2,1)S(1)}, u32[]{:S(2)}, u32[]{:S(2)}) collective-permute-start(bf16[32,2560]{1,0:T(8,128)(2,1)S(1)} %get-tuple-element.20.refs_0_), channel_id=1, source_target_pairs={{0,8},{2,10},{4,12},{6,14},{8,0},{10,2},{12,4},{14,6},{1,9},{3,11}... | collective-permute-start | bytes 491528 | tf_op jit(solution)/shard_map/ppermute | solution.py:314
  94.3 1.7 %collective-permute-start.9 = (bf16[64,2560]{1,0:T(8,128)(2,1)S(1)}, bf16[64,2560]{1,0:T(8,128)(2,1)S(1)}, u32[]{:S(2)}, u32[]{:S(2)}) collective-permute-start(bf16[64,2560]{1,0:T(8,128)(2,1)S(1)} %shard_map.86), channel_id=1, source_target_pairs={{0,1},{1,0},{2,3},{3,2},{4,5},{5,4},{6,7},{7,6},{8,9},{9,8},{10,11... | collective-permute-start | bytes 983048 | tf_op jit(solution)/shard_map/ppermute | solution.py:317

commit v9 on v1

v9 whole, which is shorter than its diff:
```python
import functools
import math

import jax
import jax.numpy as jnp
from jax import lax
from jax.experimental import pallas as pl
from jax.experimental.pallas import tpu as pltpu
from jax.sharding import PartitionSpec as P

SPAN = 64
STACK = 4
CHUNKS = (2, 3, 3)
VMEM = 60 * 1024 * 1024
SHORT = pl.CostEstimate(flops=0, bytes_accessed=0, transcendentals=0)
MASKED = -1e30
OPEN = 3e38
NT = (((1,), (1,)), ((), ()))


def dot(left, right):
    return jnp.dot(left, right, preferred_element_type=jnp.float32)


def build_table(count, routes_ref, table_ref, capacity):
    slots = routes_ref.shape[1]
    rows = table_ref.shape[0]
    place = lax.broadcasted_iota(jnp.int32, (rows, slots), 0)
    token = lax.broadcasted_iota(jnp.int32, (rows, slots), 1)
    expert = place // capacity
    hit = ((routes_ref[0:1, :] == expert) | (routes_ref[1:2, :] == expert)) & (
        token < count * SPAN
    )
    hit = jnp.where(hit, jnp.float32(1.0), jnp.float32(0.0))
    first = lax.broadcasted_iota(jnp.int32, (slots, slots), 0)
    second = lax.broadcasted_iota(jnp.int32, (slots, slots), 1)
    earlier = jnp.where(first < second, jnp.float32(1.0), jnp.float32(0.0))
    before = dot(hit.astype(jnp.bfloat16), earlier.astype(jnp.bfloat16))
    wanted = (place - expert * capacity).astype(jnp.float32)
    table_ref[...] = jnp.where(before == wanted, hit, jnp.float32(0.0)).astype(jnp.bfloat16)


def attend_kernel(
    capacity,
    first,
    count_ref,
    size_ref,
    routes_ref,
    queries_hbm,
    key_weight_hbm,
    value_weight_hbm,
    prefix_hbm,
    fresh_hbm,
    *rest,
):
    out_ref, mark_ref, queries_ref, key_weight_ref, value_weight_ref, keys_ref = rest[-10:-4]
    cap_ref, table_ref, attended_ref, sem = rest[-4:]
    slots = queries_ref.shape[0]
    past = prefix_hbm.shape[0]
    heads, dim, _ = key_weight_ref.shape
    here = pl.ds(first, heads)
    copies = [
        pltpu.make_async_copy(
            queries_hbm.at[:, pl.ds(first * dim, heads * dim)], queries_ref, sem.at[0]
        ),
        pltpu.make_async_copy(key_weight_hbm.at[here], key_weight_ref, sem.at[1]),
        pltpu.make_async_copy(prefix_hbm, keys_ref.at[pl.ds(0, past)], sem.at[2]),
        pltpu.make_async_copy(fresh_hbm, keys_ref.at[pl.ds(past, slots)], sem.at[3]),
        pltpu.make_async_copy(value_weight_hbm.at[here], value_weight_ref, sem.at[4]),
    ]
    for copy in copies:
        copy.start()
    mark_ref[...] = jnp.zeros_like(mark_ref)
    count, size = count_ref[0], size_ref[0]
    lane = lax.broadcasted_iota(jnp.int32, (slots, past), 1)
    cap_ref[:, :past] = jnp.where(lane < size, jnp.float32(OPEN), jnp.float32(MASKED))
    row = lax.broadcasted_iota(jnp.int32, (slots, slots), 0)
    col = lax.broadcasted_iota(jnp.int32, (slots, slots), 1)
    cap_ref[:, past:] = jnp.where(
        (col <= row) & (col < count * SPAN), jnp.float32(OPEN), jnp.float32(MASKED)
    )
    build_table(count, routes_ref, table_ref, capacity)
    for copy in copies:
        copy.wait()

    scale = math.log2(math.e) / math.sqrt(dim)
    keys = keys_ref[...]
    stacks = heads // STACK
    scores = []
    for stack in range(stacks):
        lifted = []
        for h in range(stack * STACK, (stack + 1) * STACK):
            one = dot(queries_ref[:, h * dim : (h + 1) * dim], key_weight_ref[h])
            lifted.append(one.astype(jnp.bfloat16))
        lifted = jnp.concatenate(lifted, axis=0)
        scores.append(lax.dot_general(lifted, keys, NT, preferred_element_type=jnp.float32))
    for stack in range(stacks):
        score = scores[stack].reshape(STACK, slots, keys.shape[0])
        score = jnp.minimum(score, cap_ref[...][None])
        highest = jnp.max(score, axis=-1, keepdims=True) * scale
        weights = jnp.exp2(score * scale - highest)
        total = jnp.sum(weights, axis=-1, keepdims=True)
        weights = weights.astype(jnp.bfloat16).reshape(STACK * slots, keys.shape[0])
        mixed = dot(weights, keys).astype(jnp.bfloat16)
        for g in range(STACK):
            h = stack * STACK + g
            projected = dot(mixed[g * slots : (g + 1) * slots], value_weight_ref[h])
            attended_ref[:, h * dim : (h + 1) * dim] = (projected / total[g]).astype(jnp.bfloat16)
    out_ref[...] = dot(table_ref[...], attended_ref[...]).astype(jnp.bfloat16)


def attend(first, heads, operands, experts, after):
    count, size, routes, queries, key_weight, value_weight, prefix, fresh = operands
    slots = queries.shape[0]
    _, dim, latent = key_weight.shape
    places = slots * routes.shape[0]
    keys = prefix.shape[0] + slots
    smem = pl.BlockSpec(memory_space=pltpu.SMEM)
    vmem = pl.BlockSpec(memory_space=pltpu.VMEM)
    hbm = pl.BlockSpec(memory_space=pltpu.HBM)
    return pl.pallas_call(
        functools.partial(attend_kernel, places // experts, first),
        in_specs=[smem, smem, vmem] + [hbm] * 5 + [vmem] * len(after),
        out_specs=[vmem, vmem],
        out_shape=[
            jax.ShapeDtypeStruct((places, heads * dim), jnp.bfloat16),
            jax.ShapeDtypeStruct((8, 128), jnp.float32),
        ],
        scratch_shapes=[
            pltpu.VMEM((slots, heads * dim), jnp.bfloat16),
            pltpu.VMEM((heads, dim, latent), jnp.bfloat16),
            pltpu.VMEM((heads, latent, dim), jnp.bfloat16),
            pltpu.VMEM((keys, latent), jnp.bfloat16),
            pltpu.VMEM((slots, keys), jnp.float32),
            pltpu.VMEM((places, slots), jnp.bfloat16),
            pltpu.VMEM((slots, heads * dim), jnp.bfloat16),
            pltpu.SemaphoreType.DMA((5,)),
        ],
        compiler_params=pltpu.CompilerParams(vmem_limit_bytes=VMEM),
    )(*operands, *after)


def place_kernel(starts, cores, *refs):
    out_ref, sem = refs[-2:]
    _, ranks, capacity, features = out_ref.shape
    features //= cores
    copies = []
    for ref, start in zip(refs, starts):
        width = ref.shape[1]
        for source in range(ranks * cores):
            left = source % cores * features + start
            target = out_ref.at[0, source // cores, :, pl.ds(left, width)]
            rows = ref.at[pl.ds(source * capacity, capacity)]
            copies.append(pltpu.make_async_copy(rows, target, sem.at[len(copies)]))
    for copy in copies:
        copy.start()
    for copy in copies:
        copy.wait()


def place(chunks, starts, cores, shape, placed):
    anywhere = pl.BlockSpec(memory_space=pl.ANY)
    return pl.pallas_call(
        functools.partial(place_kernel, starts, cores),
        in_specs=[pl.BlockSpec(memory_space=pltpu.VMEM)] * len(chunks) + [anywhere] * len(placed),
        out_specs=anywhere,
        out_shape=jax.ShapeDtypeStruct(shape, jnp.bfloat16),
        scratch_shapes=[pltpu.SemaphoreType.DMA((len(chunks) * shape[1] * cores,))],
        input_output_aliases={len(chunks): 0} if placed else {},
        compiler_params=pltpu.CompilerParams(vmem_limit_bytes=VMEM),
        cost_estimate=SHORT,
    )(*chunks, *placed)


def local(
    queries,
    key_weight,
    value_weight,
    prefix_latent,
    fresh_latent,
    span_counts,
    prefix_lengths,
    routes,
):
    ranks, cores = lax.axis_size("dp"), lax.axis_size("ep")
    experts = ranks * cores
    heads, dim, _ = key_weight.shape
    capacity = queries.shape[0] * routes.shape[1] // experts
    operands = (
        span_counts,
        prefix_lengths,
        routes.T,
        queries,
        key_weight,
        value_weight,
        prefix_latent,
        fresh_latent,
    )
    chunks, starts, after = [], [], []
    first = 0
    for share in CHUNKS:
        size = heads * share // sum(CHUNKS)
        outgoing, mark = attend(first, size, operands, experts, after)
        arrived = lax.all_to_all(
            outgoing.reshape(experts, capacity, size * dim),
            ("dp", "ep"),
            split_axis=0,
            concat_axis=0,
            tiled=True,
        )
        chunks.append(arrived.reshape(experts * capacity, size * dim))
        starts.append(first * dim)
        after = [mark]
        first += size
    shape = (1, ranks, capacity, cores * heads * dim)
    if capacity % 16:
        arrived = jnp.concatenate(chunks, axis=1).reshape(ranks, cores, capacity, heads * dim)
        return arrived.transpose(0, 2, 1, 3).reshape(shape)
    placed = place(chunks[:-1], starts[:-1], cores, shape, [])
    return place(chunks[-1:], starts[-1:], cores, shape, [placed])


def solution(mesh):
    in_specs = (
        P(("groups", "dp"), "ep"),
        P("ep", None, None),
        P("ep", None, None),
        P(("groups", "dp"), None),
        P(("groups", "dp"), None),
        P(("groups", "dp")),
        P(("groups", "dp")),
        P(("groups", "dp"), None),
    )
    out_specs = P(("groups", "dp", "ep"), None, None, None)
    return jax.shard_map(local, mesh=mesh, in_specs=in_specs, out_specs=out_specs, check_vma=False)
```

time: 148 us -> 81.7 us (0.55)
  Pallas kernels: 87.9 us -> 32.4 us
  blocking collectives: 54.6 us -> 0 us
  waiting for transfers between devices: 0 us -> 29.2 us
  starting transfers between devices: 0 us -> 17 us
  local copies, waits for them, and re-layouts: 4.02 us -> 0.9 us
    pallas_call x2 -> x5, Pallas kernels: 87.9 us -> 32.4 us  [the longest x3 27.7 us: attend(): pl.pallas_call(functools.partial(attend_kernel, places // experts, first)...]
    all_to_all x1 -> x0, blocking collectives: 54.6 us -> none  [local(): lax.all_to_all(outgoing.reshape(experts, -1, outgoing.shape[1]), ('dp', '...]
    all_to_all x0 -> x3, waiting for transfers between devices: none -> 29.2 us  [local(): lax.all_to_all(outgoing.reshape(experts, capacity, size * dim), ('dp', 'e...]
    all_to_all x0 -> x3, starting transfers between devices: none -> 17 us  [local(): lax.all_to_all(outgoing.reshape(experts, capacity, size * dim), ('dp', 'e...]
    unnamed x8 -> x6, local copies, waits for them, and re-layouts: 4.02 us -> 0.9 us
  transfers between devices with their start and end apart: 0 -> 3, of which waited for: 0 -> 3; matrix products, arithmetic and copies ran while one was open for 0% -> 0% of each run, Pallas kernels for 0% -> 28%
where the time goes in v9:
time: 81.7 us; the launch traced here: 81 us
  Pallas kernels  32.4 us (40%)
  waiting for transfers between devices  29.2 us (36%)
  starting transfers between devices  17 us (21%)
  between operations  1.53 us (2%)
  local copies, waits for them, and re-layouts  0.9 us (1%)
    all_to_all x3, waiting for transfers between devices, local(): lax.all_to_all(outgoing.reshape(experts, capacity, size * dim), ('dp', 'e...  29.2 us
    pallas_call x3, Pallas kernels, attend(): pl.pallas_call(functools.partial(attend_kernel, places // experts, first)...  27.7 us
    all_to_all x3, starting transfers between devices, local(): lax.all_to_all(outgoing.reshape(experts, capacity, size * dim), ('dp', 'e...  17 us
    pallas_call x2, Pallas kernels, place(): pl.pallas_call(functools.partial(place_kernel, starts, cores), in_specs=[...  4.74 us
  transfers between devices with their start and end apart: 3, of which 3 were waited for; matrix products, arithmetic and copies ran while one was open for 0% of the time, Pallas kernels for 28%

profile of v9, /device:TPU:0, one launch (start us, length us, event | category | flops | bytes accessed | tf_op | source)
XLA Modules:
  0.0 81.0 jit_solution(5876392693711899056)
XLA Ops:
  1.3 7.7 %shard_map.82 = (bf16[256,1024]{1,0:T(8,128)(2,1)}, f32[8,128]{1,0:T(8,128)}) custom-call(s32[1]{0:T(128)S(6)} %copy.11.count_ref, s32[1]{0:T(128)S(6)} %copy.12.size_ref, s32[2,128]{1,0:T(2,128)} %bitcast.13, bf16[128,4096]{1,0:T(8,128)(2,1)} %queries_hbm.5, bf16[32,128,512]{2,1,0:T(8,128)(2,1)} %key_weight_hbm.5, bf16[32,512,128]{2,1,0:T(8,128)(2,1)} %value_weight_hbm.5, ...), custom_call_target="tpu_custom_call" | custom-call | tf_op jit(solution)/shard_map/pallas_call | solution.py:121
  9.0 7.4 %all-to-all-start.1 = ((bf16[16,16,1024]{2,1,0:T(8,128)(2,1)}), bf16[16,16,1024]{2,1,0:T(8,128)(2,1)S(1)}, u32[]{:S(2)}, u32[]{:S(2)}) async-start(bf16[16,16,1024]{2,1,0:T(8,128)(2,1)} %bitcast.12), calls=%async_computation.1 | async-start | bytes 1048576 | tf_op jit(solution)/shard_map/all_to_all | solution.py:204
  16.4 10.0 %shard_map.83 = (bf16[256,1536]{1,0:T(8,128)(2,1)}, f32[8,128]{1,0:T(8,128)}) custom-call(s32[1]{0:T(128)S(6)} %copy.11.count_ref, s32[1]{0:T(128)S(6)} %copy.12.size_ref, s32[2,128]{1,0:T(2,128)} %bitcast.14, bf16[128,4096]{1,0:T(8,128)(2,1)} %queries_hbm.5, bf16[32,128,512]{2,1,0:T(8,128)(2,1)} %key_weight_hbm.5, bf16[32,512,128]{2,1,0:T(8,128)(2,1)} %value_weight_hbm.5, ...), custom_call_target="tpu_custom_call" | custom-call | tf_op jit(solution)/shard_map/pallas_call | solution.py:121
  26.4 4.5 %all-to-all-done.1 = bf16[16,16,1024]{2,1,0:T(8,128)(2,1)S(1)} async-done(((bf16[16,16,1024]{2,1,0:T(8,128)(2,1)}), bf16[16,16,1024]{2,1,0:T(8,128)(2,1)S(1)}, u32[]{:S(2)}, u32[]{:S(2)}) %all-to-all-start.1) | async-done | bytes 524320 | tf_op jit(solution)/shard_map/all_to_all | solution.py:204
  30.8 0.0 copy-start.2
  30.8 4.1 %all-to-all-start.2 = ((bf16[16,16,1536]{2,1,0:T(8,128)(2,1)}), bf16[16,16,1536]{2,1,0:T(8,128)(2,1)S(1)}, u32[]{:S(2)}, u32[]{:S(2)}) async-start(bf16[16,16,1536]{2,1,0:T(8,128)(2,1)} %bitcast.10), calls=%async_computation.2 | async-start | bytes 1572864 | tf_op jit(solution)/shard_map/all_to_all | solution.py:204
  34.9 10.0 %shard_map.84 = (bf16[256,1536]{1,0:T(8,128)(2,1)}, f32[8,128]{1,0:T(8,128)}) custom-call(s32[1]{0:T(128)S(6)} %copy.11.count_ref, s32[1]{0:T(128)S(6)} %copy.12.size_ref, s32[2,128]{1,0:T(2,128)} %bitcast.15, bf16[128,4096]{1,0:T(8,128)(2,1)} %queries_hbm.5, bf16[32,128,512]{2,1,0:T(8,128)(2,1)} %key_weight_hbm.5, bf16[32,512,128]{2,1,0:T(8,128)(2,1)} %value_weight_hbm.5, ...), custom_call_target="tpu_custom_call" | custom-call | tf_op jit(solution)/shard_map/pallas_call | solution.py:121
  45.0 0.0 copy-done.2
  45.0 8.7 %all-to-all-done.2 = bf16[16,16,1536]{2,1,0:T(8,128)(2,1)S(1)} async-done(((bf16[16,16,1536]{2,1,0:T(8,128)(2,1)}), bf16[16,16,1536]{2,1,0:T(8,128)(2,1)S(1)}, u32[]{:S(2)}, u32[]{:S(2)}) %all-to-all-start.2) | async-done | bytes 786464 | tf_op jit(solution)/shard_map/all_to_all | solution.py:204
  53.6 0.0 copy-start.1
  53.6 5.5 %all-to-all-start = ((bf16[16,16,1536]{2,1,0:T(8,128)(2,1)}), bf16[16,16,1536]{2,1,0:T(8,128)(2,1)S(1)}, u32[]{:S(2)}, u32[]{:S(2)}) async-start(bf16[16,16,1536]{2,1,0:T(8,128)(2,1)} %bitcast.11), calls=%async_computation | async-start | bytes 1572864 | tf_op jit(solution)/shard_map/all_to_all | solution.py:204
  59.1 0.0 copy-done.1
  59.1 2.6 %shard_map.85.refs_1_ = bf16[1,8,16,8192]{3,2,1,0:T(8,128)(2,1)} custom-call(bf16[256,1024]{1,0:T(8,128)(2,1)} %bitcast.9, bf16[256,1536]{1,0:T(8,128)(2,1)} %bitcast.8), custom_call_target="tpu_custom_call" | custom-call | tf_op jit(solution)/shard_map/pallas_call | solution.py:163
  61.7 16.1 %all-to-all-done = bf16[16,16,1536]{2,1,0:T(8,128)(2,1)S(1)} async-done(((bf16[16,16,1536]{2,1,0:T(8,128)(2,1)}), bf16[16,16,1536]{2,1,0:T(8,128)(2,1)S(1)}, u32[]{:S(2)}, u32[]{:S(2)}) %all-to-all-start) | async-done | bytes 786464 | tf_op jit(solution)/shard_map/all_to_all | solution.py:204
  77.8 0.0 copy-start
  77.8 0.9 %copy-done = bf16[16,16,1536]{2,1,0:T(8,128)(2,1)} copy-done((bf16[16,16,1536]{2,1,0:T(8,128)(2,1)}, bf16[16,16,1536]{2,1,0:T(8,128)(2,1)S(1)}, u32[]{:S(2)}) %copy-start) | copy-done | bytes 786456
  78.7 2.1 %shard_map.86 = bf16[1,8,16,8192]{3,2,1,0:T(8,128)(2,1)} custom-call(bf16[256,1536]{1,0:T(8,128)(2,1)} %bitcast.7, bf16[1,8,16,8192]{3,2,1,0:T(8,128)(2,1)} %shard_map.85.refs_1_), custom_call_target="tpu_custom_call", output_to_operand_aliasing={{}: (1, {})} | custom-call | tf_op jit(solution)/shard_map/pallas_call | solution.py:163
Async XLA Ops:
  9.0 21.9 %all-to-all-start.1 = ((bf16[16,16,1024]{2,1,0:T(8,128)(2,1)}), bf16[16,16,1024]{2,1,0:T(8,128)(2,1)S(1)}, u32[]{:S(2)}, u32[]{:S(2)}) async-start(bf16[16,16,1024]{2,1,0:T(8,128)(2,1)} %bitcast.12), calls=%async_computation.1 | async-start | bytes 1048576 | tf_op jit(solution)/shard_map/all_to_all | solution.py:204
  30.8 14.1 %copy-start.2 = (bf16[16,16,1024]{2,1,0:T(8,128)(2,1)}, bf16[16,16,1024]{2,1,0:T(8,128)(2,1)S(1)}, u32[]{:S(2)}) copy-start(bf16[16,16,1024]{2,1,0:T(8,128)(2,1)S(1)} %all-to-all-done.1) | copy-start | bytes 1572868
  30.8 22.8 %all-to-all-start.2 = ((bf16[16,16,1536]{2,1,0:T(8,128)(2,1)}), bf16[16,16,1536]{2,1,0:T(8,128)(2,1)S(1)}, u32[]{:S(2)}, u32[]{:S(2)}) async-start(bf16[16,16,1536]{2,1,0:T(8,128)(2,1)} %bitcast.10), calls=%async_computation.2 | async-start | bytes 1572864 | tf_op jit(solution)/shard_map/all_to_all | solution.py:204
  53.6 5.5 %copy-start.1 = (bf16[16,16,1536]{2,1,0:T(8,128)(2,1)}, bf16[16,16,1536]{2,1,0:T(8,128)(2,1)S(1)}, u32[]{:S(2)}) copy-start(bf16[16,16,1536]{2,1,0:T(8,128)(2,1)S(1)} %all-to-all-done.2) | copy-start | bytes 2359300
  53.6 24.2 %all-to-all-start = ((bf16[16,16,1536]{2,1,0:T(8,128)(2,1)}), bf16[16,16,1536]{2,1,0:T(8,128)(2,1)S(1)}, u32[]{:S(2)}, u32[]{:S(2)}) async-start(bf16[16,16,1536]{2,1,0:T(8,128)(2,1)} %bitcast.11), calls=%async_computation | async-start | bytes 1572864 | tf_op jit(solution)/shard_map/all_to_all | solution.py:204
  77.8 0.9 %copy-start = (bf16[16,16,1536]{2,1,0:T(8,128)(2,1)}, bf16[16,16,1536]{2,1,0:T(8,128)(2,1)S(1)}, u32[]{:S(2)}) copy-start(bf16[16,16,1536]{2,1,0:T(8,128)(2,1)S(1)} %all-to-all-done) | copy-start | bytes 2359300

commit v10 on v6

--- a/solution.py
+++ b/solution.py
@@ -9,12 +9,14 @@
 from jax.sharding import PartitionSpec as P
 
 SPAN = 64
-GROUPS = (2, 4)
+GROUPS = (2, 2)
 UNROLL = 2
 CHUNKS = (1, 1)
 DIRECT = 16
 KEY_PARTS = 2
-VMEM = 58 * 1024 * 1024
+VMEM = 60 * 1024 * 1024
+SHORT = pl.CostEstimate(flops=0, bytes_accessed=0, transcendentals=0)
+MARK = (8, 128)
 MASKED = -1e30
 OPEN = 3e38
 NT = (((1,), (1,)), ((), ()))
@@ -24,13 +26,14 @@
     return jnp.dot(left, right, preferred_element_type=jnp.float32)
 
 
-def build_table(me, count, routes_ref, table_ref, capacity):
+def build_table(me, count, routes_ref, table_ref, capacity, cores):
     slots = routes_ref.shape[1]
     rows = table_ref.shape[0]
     place = lax.broadcasted_iota(jnp.int32, (rows, slots), 0)
     token = lax.broadcasted_iota(jnp.int32, (rows, slots), 1)
     block = place // capacity
-    expert = block ^ me
+    chips = rows // (capacity * cores)
+    expert = ((block % chips) * cores + block // chips) ^ me
     hit = ((routes_ref[0:1, :] == expert) | (routes_ref[1:2, :] == expert)) & (
         token < count * SPAN
     )
@@ -47,6 +50,8 @@
     capacity,
     group,
     first,
+    cores,
+    after,
     me_ref,
     count_ref,
     size_ref,
@@ -58,7 +63,8 @@
     fresh_hbm,
     *rest,
 ):
-    *out_refs, queries_ref, key_weight_ref, value_weight_ref, keys_ref = rest[:-4]
+    *out_refs, mark_ref, queries_ref, key_weight_ref, value_weight_ref, keys_ref = rest[after:-4]
+    mark_ref[...] = jnp.zeros_like(mark_ref)
     cap_ref, table_ref, attended_ref, sem = rest[-4:]
     slots = queries_ref.shape[0]
     past = prefix_hbm.shape[0]
@@ -108,7 +114,7 @@
     cap_ref[:, past:] = jnp.where(
         (col <= row) & (col < count * SPAN), jnp.float32(OPEN), jnp.float32(MASKED)
     )
-    build_table(me_ref[0], count, routes_ref, table_ref, capacity)
+    build_table(me_ref[0], count, routes_ref, table_ref, capacity, cores)
 
     scale = math.log2(math.e) / math.sqrt(dim)
     for copy in for_keys:
@@ -145,9 +151,10 @@
 
     lax.fori_loop(0, steps, body, 0)
     grouped = dot(table_ref[...], attended_ref[...]).astype(jnp.bfloat16)
-    rows = out_refs[0].shape[0]
-    for k, out_ref in enumerate(out_refs):
-        out_ref[...] = grouped[k * rows : (k + 1) * rows]
+    row = 0
+    for out_ref in out_refs:
+        out_ref[...] = grouped[row : row + out_ref.shape[0]]
+        row += out_ref.shape[0]
 
 
 def attend(
@@ -164,7 +171,9 @@
     size,
     routes,
     experts,
-    pieces,
+    parts,
+    cores,
+    after,
 ):
     slots = queries.shape[0]
     _, dim, latent = key_weight.shape
@@ -173,12 +182,12 @@
     smem = pl.BlockSpec(memory_space=pltpu.SMEM)
     vmem = pl.BlockSpec(memory_space=pltpu.VMEM)
     hbm = pl.BlockSpec(memory_space=pltpu.HBM)
-    piece = (places // pieces, heads * dim)
+    pieces = [jax.ShapeDtypeStruct((rows, heads * dim), jnp.bfloat16) for rows in parts]
     return pl.pallas_call(
-        functools.partial(attend_kernel, places // experts, group, first),
-        in_specs=[smem, smem, smem, vmem, hbm, hbm, hbm, hbm, hbm],
-        out_specs=[vmem] * pieces,
-        out_shape=[jax.ShapeDtypeStruct(piece, jnp.bfloat16)] * pieces,
+        functools.partial(attend_kernel, places // experts, group, first, cores, len(after)),
+        in_specs=[smem, smem, smem, vmem] + [hbm] * 5 + [vmem] * len(after),
+        out_specs=[vmem] * (len(pieces) + 1),
+        out_shape=pieces + [jax.ShapeDtypeStruct(MARK, jnp.float32)],
         scratch_shapes=[
             pltpu.VMEM((slots, heads * dim), jnp.bfloat16),
             pltpu.VMEM((heads, dim, latent), jnp.bfloat16),
@@ -195,7 +204,7 @@
             bytes_accessed=4 * heads * dim * latent,
             transcendentals=heads * slots * keys,
         ),
-    )(me, count, size, routes.T, queries, key_weight, value_weight, prefix, fresh)
+    )(me, count, size, routes.T, queries, key_weight, value_weight, prefix, fresh, *after)
 
 
 def run_copies(copies):
@@ -205,75 +214,69 @@
         copy.wait()
 
 
-def pass_on_kernel(cores, *refs):
-    *piece_refs, out_ref, sem = refs
-    capacity = piece_refs[0].shape[0] // cores
-    run_copies(
-        [
-            pltpu.make_async_copy(
-                piece_ref.at[pl.ds(capacity, capacity)],
-                out_ref.at[pl.ds(j * capacity, capacity)],
-                sem.at[j],
-            )
-            for j, piece_ref in enumerate(piece_refs)
+def join_kernel(*refs):
+    *refs, sem = refs
+    count = (len(refs) - 1) // 2
+    copies = []
+    for i, (kept_ref, out_ref) in enumerate(zip(refs[:count], refs[count + 1 :])):
+        rows = kept_ref.shape[0]
+        swapped = refs[count].at[pl.ds((i + 1) * rows, rows)]
+        copies += [
+            pltpu.make_async_copy(kept_ref, out_ref.at[pl.ds(0, rows)], sem.at[2 * i]),
+            pltpu.make_async_copy(swapped, out_ref.at[pl.ds(rows, rows)], sem.at[2 * i + 1]),
         ]
-    )
-
-
-def pass_on(pieces, cores):
-    rows, width = pieces[0].shape
+    run_copies(copies)
+
+
+def join(kept, swapped):
+    rows, width = kept[0].shape
     return pl.pallas_call(
-        functools.partial(pass_on_kernel, cores),
-        in_specs=[pl.BlockSpec(memory_space=pl.ANY)] * len(pieces),
-        out_specs=pl.BlockSpec(memory_space=pltpu.VMEM),
-        out_shape=jax.ShapeDtypeStruct((len(pieces) * rows // cores, width), jnp.bfloat16),
-        scratch_shapes=[pltpu.SemaphoreType.DMA((len(pieces),))],
+        join_kernel,
+        in_specs=[pl.BlockSpec(memory_space=pl.ANY)] * (len(kept) + 1),
+        out_specs=[pl.BlockSpec(memory_space=pltpu.VMEM)] * len(kept),
+        out_shape=[jax.ShapeDtypeStruct((2 * rows, width), jnp.bfloat16)] * len(kept),
+        scratch_shapes=[pltpu.SemaphoreType.DMA((2 * len(kept),))],
         compiler_params=pltpu.CompilerParams(vmem_limit_bytes=VMEM),
-    )(*pieces)
-
-
-def place_kernel(plan, cores, me_ref, *rest):
-    *refs, out_ref, whole_ref, sem = rest
-    _, capacity, features = whole_ref.shape
+        cost_estimate=SHORT,
+    )(*kept, swapped)
+
+
+def place_kernel(plan, cores, me_ref, *refs):
+    out_ref, sem = refs[-2:]
+    _, _, capacity, features = out_ref.shape
     features //= cores
     me = me_ref[0]
     copies = []
-    for i, (ref, (first, start, source)) in enumerate(plan):
+    for ref, row, start, bits in plan:
         ref = refs[ref]
-        width = ref.shape[1]
-        who = me ^ source
-        left = pl.multiple_of(who % cores * features + first, math.gcd(features, first))
+        who = me ^ bits
+        left = pl.multiple_of(who % cores * features + start, math.gcd(features, start))
+        target = out_ref.at[0, who // cores, :, pl.ds(left, ref.shape[1])]
         copies.append(
-            pltpu.make_async_copy(
-                ref.at[pl.ds(start, capacity)],
-                whole_ref.at[who // cores, :, pl.ds(left, width)],
-                sem.at[i],
-            )
+            pltpu.make_async_copy(ref.at[pl.ds(row, capacity)], target, sem.at[len(copies)])
         )
     run_copies(copies)
-    run_copies([pltpu.make_async_copy(whole_ref, out_ref.at[0], sem.at[0])])
-
-
-def assemble(me, arrays, plan, shape, cores):
+
+
+def place(me, arrays, plan, cores, shape, placed):
+    anywhere = pl.BlockSpec(memory_space=pl.ANY)
+    operands = [me, *arrays, *placed]
     return pl.pallas_call(
         functools.partial(place_kernel, plan, cores),
         in_specs=[pl.BlockSpec(memory_space=pltpu.SMEM)]
-        + [pl.BlockSpec(memory_space=pl.ANY)] * len(arrays),
-        out_specs=pl.BlockSpec(memory_space=pl.ANY),
+        + [pl.BlockSpec(memory_space=pltpu.VMEM)] * len(arrays)
+        + [anywhere] * len(placed),
+        out_specs=anywhere,
         out_shape=jax.ShapeDtypeStruct(shape, jnp.bfloat16),
-        scratch_shapes=[
-            pltpu.VMEM(shape[1:], jnp.bfloat16),
-            pltpu.SemaphoreType.DMA((len(plan),)),
-        ],
+        scratch_shapes=[pltpu.SemaphoreType.DMA((len(plan),))],
+        input_output_aliases={len(operands) - 1: 0} if placed else {},
         compiler_params=pltpu.CompilerParams(vmem_limit_bytes=VMEM),
-    )(me, *arrays)
+    )(*operands)
 
 
 def exchange_order(ranks):
     near, far = list(range(1, ranks // 2)), list(range(ranks // 2, ranks))
-    far = far[::2] + far[1::2]
-    half = len(far) // 2
-    return far[:half] + near[:1] + far[half:] + near[1:]
+    return far[::2] + far[1::2] + near
 
 
 def local(
@@ -292,17 +295,16 @@
     heads, dim, _ = key_weight.shape
     capacity = slots * routes.shape[1] // experts
     direct = ranks <= DIRECT and capacity % 16 == 0
-    index = lax.axis_index("dp") * cores + lax.axis_index("ep")
-    me = (index if direct else jnp.int32(0)).astype(jnp.int32).reshape(1)
+    me = (lax.axis_index("dp") * cores + lax.axis_index("ep")).astype(jnp.int32).reshape(1)
+    nobody = jnp.zeros((1,), jnp.int32)
     shares = [heads * share // sum(CHUNKS) for share in CHUNKS]
-    chunks, plan = [], []
-    first = 0
-    for group, share in zip(GROUPS, shares):
-        outgoing = attend(
-            group,
-            first,
-            share,
-            me,
+
+    def run(chunk, order, parts, cores, after):
+        return attend(
+            GROUPS[chunk],
+            sum(shares[:chunk]),
+            shares[chunk],
+            order,
             queries,
             key_weight,
             value_weight,
@@ -312,35 +314,43 @@
             prefix_lengths,
             routes,
             experts,
-            ranks if direct else 1,
-        )
-        if direct:
-            order = exchange_order(ranks)
-            pieces = [outgoing[0]]
-            for j in order:
-                pairs = [(i, i ^ j) for i in range(ranks)]
-                pieces.append(lax.ppermute(outgoing[j], "dp", pairs))
-            swapped = lax.ppermute(
-                pass_on(pieces, cores), "ep", [(i, i ^ 1) for i in range(cores)]
-            )
-            for at, j in enumerate([0] + order):
-                plan.append((len(chunks) + at, (first * dim, 0, j * cores)))
-                plan.append((len(chunks) + ranks, (first * dim, at * capacity, j * cores + 1)))
-            chunks += pieces + [swapped]
-        else:
-            arrived = lax.all_to_all(
-                outgoing[0].reshape(experts, capacity, share * dim),
-                ("dp", "ep"),
-                split_axis=0,
-                concat_axis=0,
-                tiled=True,
-            )
-            chunks.append(arrived.reshape(ranks, cores, capacity, share * dim))
-        first += share
-    if direct:
-        return assemble(me, chunks, plan, (1, ranks, capacity, cores * heads * dim), cores)
-    arrived = jnp.concatenate(chunks, axis=3).transpose(0, 2, 1, 3)
-    return arrived.reshape(1, ranks, capacity, cores * heads * dim)
+            parts,
+            cores,
+            after,
+        )
+
+    def to_all(outgoing):
+        return lax.all_to_all(
+            outgoing.reshape(experts, capacity, -1),
+            ("dp", "ep"),
+            split_axis=0,
+            concat_axis=0,
+            tiled=True,
+        )
+
+    if not direct:
+        outgoing = [run(chunk, nobody, [experts * capacity], 1, [])[0] for chunk in range(len(shares))]
+        arrived = jnp.concatenate([to_all(rows) for rows in outgoing], axis=2)
+        arrived = arrived.reshape(ranks, cores, capacity, -1).transpose(0, 2, 1, 3)
+        return arrived.reshape(1, ranks, capacity, cores * heads * dim)
+    opening, mark = run(0, nobody, [experts * capacity], 1, [])
+    first = to_all(opening).reshape(experts * capacity, -1)
+    parts = [capacity] * ranks + [(cores - 1) * ranks * capacity]
+    *kept, message, mark = run(1, me, parts, cores, [mark])
+    swapped = lax.ppermute(message, "ep", [(i, i ^ 1) for i in range(cores)])
+    order = exchange_order(ranks)
+    joined = dict(zip(range(1, ranks), join(kept[1:], swapped)))
+    arrays = [kept[0], swapped]
+    middle = shares[0] * dim
+    plan = [(0, 0, middle, 0), (1, 0, middle, 1)]
+    for j in order:
+        plan.append((len(arrays), 0, middle, j * cores))
+        plan.append((len(arrays), capacity, middle, j * cores + 1))
+        arrays.append(lax.ppermute(joined[j], "dp", [(i, i ^ j) for i in range(ranks)]))
+    shape = (1, ranks, capacity, cores * heads * dim)
+    first_plan = [(0, i * capacity, 0, i) for i in range(experts)]
+    placed = place(nobody, [first], first_plan, cores, shape, [])
+    return place(me, arrays, plan, cores, shape, [placed])
 
 
 def solution(mesh):

time: 75.5 us -> 77.3 us (1.024)
  waiting for transfers between devices: 11.3 us -> 19.3 us
  starting transfers between devices: 29.1 us -> 21.2 us
  local copies, waits for them, and re-layouts: 1.45 us -> 2.42 us
  Pallas kernels: 31.7 us -> 32.6 us
    ppermute x16 -> x8, starting transfers between devices: 29.1 us -> 13.8 us  [the longest x7 13.4 us: local(): lax.ppermute(joined[j], 'dp', [(i, i ^ j) for i in range(ranks)])]
    ppermute x16 -> x8, waiting for transfers between devices: 11.3 us -> 19.3 us  [the longest x7 17.5 us: local(): lax.ppermute(joined[j], 'dp', [(i, i ^ j) for i in range(ranks)])]
    all_to_all x0 -> x1, starting transfers between devices: none -> 7.4 us  [to_all(): lax.all_to_all(outgoing.reshape(experts, capacity, -1), ('dp', 'ep'), spl...]
    unnamed x36 -> x18, local copies, waits for them, and re-layouts: 1.45 us -> 2.42 us
    pallas_call x2, Pallas kernels: 24.7 us -> 25.6 us  [attend(): pl.pallas_call(functools.partial(attend_kernel, places // experts, group,...]
  transfers between devices with their start and end apart: 16 -> 9, of which waited for: 4 -> 4; matrix products, arithmetic and copies ran while one was open for 0% -> 0% of each run, Pallas kernels for 22% -> 23%
where the time goes in v10:
time: 77.3 us; the launch traced here: 76.9 us
  Pallas kernels  32.6 us (42%)
  starting transfers between devices  21.2 us (27%)
  waiting for transfers between devices  19.3 us (25%)
  local copies, waits for them, and re-layouts  2.42 us (3%)
  between operations  1.44 us (2%)
    pallas_call x2, Pallas kernels, attend(): pl.pallas_call(functools.partial(attend_kernel, places // experts, group,...  25.6 us
    ppermute x7, waiting for transfers between devices, local(): lax.ppermute(joined[j], 'dp', [(i, i ^ j) for i in range(ranks)])  17.5 us
    ppermute x7, starting transfers between devices, local(): lax.ppermute(joined[j], 'dp', [(i, i ^ j) for i in range(ranks)])  13.4 us
    all_to_all x1, starting transfers between devices, to_all(): lax.all_to_all(outgoing.reshape(experts, capacity, -1), ('dp', 'ep'), spl...  7.4 us
    pallas_call x2, Pallas kernels, place(): pl.pallas_call(functools.partial(place_kernel, plan, cores), in_specs=[pl...  4.72 us
    unnamed x18, local copies, waits for them, and re-layouts  2.42 us
    pallas_call x1, Pallas kernels, join(): pl.pallas_call(join_kernel, in_specs=[pl.BlockSpec(memory_space=pl.ANY)]...  2.24 us
    ppermute x1, waiting for transfers between devices, local(): swapped = lax.ppermute(message, 'ep', [(i, i ^ 1) for i in range(cores)])  1.75 us
  transfers between devices with their start and end apart: 9, of which 4 were waited for; matrix products, arithmetic and copies ran while one was open for 0% of the time, Pallas kernels for 23%

profile of v10, /device:TPU:0, one launch (start us, length us, event | category | flops | bytes accessed | tf_op | source)
XLA Modules:
  0.0 76.9 jit_solution(7313910940907508788)
XLA Ops:
  1.3 12.8 %shard_map.82 = (bf16[256,2048]{1,0:T(8,128)(2,1)}, f32[8,128]{1,0:T(8,128)}) custom-call(s32[1]{0:T(128)} %constant.11.clone.1.me_ref, s32[1]{0:T(128)S(6)} %copy.11.count_ref, s32[1]{0:T(128)S(6)} %copy.12.size_ref, s32[2,128]{1,0:T(2,128)} %bitcast.6, bf16[128,4096]{1,0:T(8,128)(2,1)} %queries_hbm.3, bf16[32,128,512]{2,1,0:T(8,128)(2,1)} %key_weight_hbm.3, ...), custom_call_target="tpu_custom_call" | custom-call | flops 4831838208 | bytes 4194304 | tf_op jit(solution)/shard_map/pallas_call | solution.py:186
  14.1 7.4 %all-to-all-start = ((bf16[16,16,2048]{2,1,0:T(8,128)(2,1)}), bf16[16,16,2048]{2,1,0:T(8,128)(2,1)S(1)}, u32[]{:S(2)}, u32[]{:S(2)}) async-start(bf16[16,16,2048]{2,1,0:T(8,128)(2,1)} %bitcast.5), calls=%async_computation | async-start | bytes 2097152 | tf_op jit(solution)/shard_map/all_to_all | solution.py:323
  21.5 12.8 %shard_map.83 = (bf16[16,2048]{1,0:T(8,128)(2,1)}, bf16[16,2048]{1,0:T(8,128)(2,1)}, bf16[16,2048]{1,0:T(8,128)(2,1)}, bf16[16,2048]{1,0:T(8,128)(2,1)}, bf16[16...) custom-call(s32[1]{0:T(128)} %bitcast.me_ref, ...), custom_call_target="tpu_custom_call" | custom-call | flops 4831838208 | bytes 4194304 | tf_op jit(solution)/shard_map/pallas_call | solution.py:186
  34.3 0.4 collective-permute-start
  34.8 1.7 %collective-permute-done.refs_7_.refs_1_ = bf16[128,2048]{1,0:T(8,128)(2,1)S(1)} collective-permute-done((bf16[128,2048]{1,0:T(8,128)(2,1)}, bf16[128,2048]{1,0:T(8,128)(2,1)S(1)}, u32[]{:S(2)}, u32[]{:S(2)}) %collective-permute-start) | collective-permute-done | bytes 524320 | tf_op jit(solution)/shard_map/ppermute | solution.py:340
  36.5 0.8 %copy-done.1 = bf16[128,2048]{1,0:T(8,128)(2,1)} copy-done((bf16[128,2048]{1,0:T(8,128)(2,1)}, bf16[128,2048]{1,0:T(8,128)(2,1)S(1)}, u32[]{:S(2)}) %copy-start.1) | copy-done | bytes 524312
  37.3 2.2 %shard_map.84 = (bf16[32,2048]{1,0:T(8,128)(2,1)}, bf16[32,2048]{1,0:T(8,128)(2,1)}, bf16[32,2048]{1,0:T(8,128)(2,1)}, bf16[32,2048]{1,0:T(8,128)(2,1)}, bf16[32...) custom-call(bf16[16,2048]{1,0:T(8,128)(2,1)} %get-tuple-element.26.refs_0_, ...), custom_call_target="tpu_custom_call" | custom-call | tf_op jit(solution)/shard_map/pallas_call | solution.py:233
  39.6 2.9 %collective-permute-start.1 = (bf16[32,2048]{1,0:T(8,128)(2,1)}, bf16[32,2048]{1,0:T(8,128)(2,1)S(1)}, u32[]{:S(2)}, u32[]{:S(2)}) collective-permute-start(bf16[32,2048]{1,0:T(8,128)(2,1)} %get-tuple-element.33), channel_id=1, source_target_pairs={{0,8},{2,10},{4,12},{6,14},{8,0},{10,2},{12,4},{14,6},{1,9},{3,11}... | collective-permute-start | bytes 393224 | tf_op jit(solution)/shard_map/ppermute | solution.py:349
  42.5 1.5 %collective-permute-start.2 = (bf16[32,2048]{1,0:T(8,128)(2,1)}, bf16[32,2048]{1,0:T(8,128)(2,1)S(1)}, u32[]{:S(2)}, u32[]{:S(2)}) collective-permute-start(bf16[32,2048]{1,0:T(8,128)(2,1)} %get-tuple-element.34), channel_id=1, source_target_pairs={{0,12},{2,14},{4,8},{6,10},{8,4},{10,6},{12,0},{14,2},{1,13},{3,15... | collective-permute-start | bytes 393224 | tf_op jit(solution)/shard_map/ppermute | solution.py:349
  43.9 2.4 %collective-permute-start.3 = (bf16[32,2048]{1,0:T(8,128)(2,1)}, bf16[32,2048]{1,0:T(8,128)(2,1)S(1)}, u32[]{:S(2)}, u32[]{:S(2)}) collective-permute-start(bf16[32,2048]{1,0:T(8,128)(2,1)} %get-tuple-element.35), channel_id=1, source_target_pairs={{0,10},{2,8},{4,14},{6,12},{8,2},{10,0},{12,6},{14,4},{1,11},{3,9}... | collective-permute-start | bytes 393224 | tf_op jit(solution)/shard_map/ppermute | solution.py:349
  46.3 0.9 %collective-permute-start.4 = (bf16[32,2048]{1,0:T(8,128)(2,1)}, bf16[32,2048]{1,0:T(8,128)(2,1)S(1)}, u32[]{:S(2)}, u32[]{:S(2)}) collective-permute-start(bf16[32,2048]{1,0:T(8,128)(2,1)} %get-tuple-element.36), channel_id=1, source_target_pairs={{0,14},{2,12},{4,10},{6,8},{8,6},{10,4},{12,2},{14,0},{1,15},{3,13... | collective-permute-start | bytes 393224 | tf_op jit(solution)/shard_map/ppermute | solution.py:349
  47.2 1.5 %collective-permute-start.5 = (bf16[32,2048]{1,0:T(8,128)(2,1)}, bf16[32,2048]{1,0:T(8,128)(2,1)S(1)}, u32[]{:S(2)}, u32[]{:S(2)}) collective-permute-start(bf16[32,2048]{1,0:T(8,128)(2,1)} %get-tuple-element.37), channel_id=1, source_target_pairs={{0,2},{2,0},{4,6},{6,4},{8,10},{10,8},{12,14},{14,12},{1,3},{3,1},... | collective-permute-start | bytes 393224 | tf_op jit(solution)/shard_map/ppermute | solution.py:349
  48.7 13.9 %collective-permute-done.1.refs_2_ = bf16[32,2048]{1,0:T(8,128)(2,1)S(1)} collective-permute-done((bf16[32,2048]{1,0:T(8,128)(2,1)}, bf16[32,2048]{1,0:T(8,128)(2,1)S(1)}, u32[]{:S(2)}, u32[]{:S(2)}) %collective-permute-start.1) | collective-permute-done | bytes 131104 | tf_op jit(solution)/shard_map/ppermute | solution.py:349
  62.6 0.0 collective-permute-start.6
  62.6 0.0 collective-permute-done.2.refs_3_
  62.6 0.0 copy-start.3
  62.6 4.3 %collective-permute-start.7 = (bf16[32,2048]{1,0:T(8,128)(2,1)}, bf16[32,2048]{1,0:T(8,128)(2,1)S(1)}, u32[]{:S(2)}, u32[]{:S(2)}) collective-permute-start(bf16[32,2048]{1,0:T(8,128)(2,1)} %get-tuple-element.39), channel_id=1, source_target_pairs={{0,6},{2,4},{4,2},{6,0},{8,14},{10,12},{12,10},{14,8},{1,7},{3,5},... | collective-permute-start | bytes 393224 | tf_op jit(solution)/shard_map/ppermute | solution.py:349
  66.9 0.0 all-to-all-done
  66.9 1.0 %copy-done = bf16[16,16,2048]{2,1,0:T(8,128)(2,1)} copy-done((bf16[16,16,2048]{2,1,0:T(8,128)(2,1)}, bf16[16,16,2048]{2,1,0:T(8,128)(2,1)S(1)}, u32[]{:S(2)}) %copy-start) | copy-done | bytes 1048600
  67.9 2.3 %shard_map.85.refs_9_ = bf16[1,8,16,8192]{3,2,1,0:T(8,128)(2,1)} custom-call(s32[1]{0:T(128)} %constant.11.clone.1.me_ref, bf16[256,2048]{1,0:T(8,128)(2,1)} %bitcast.4), custom_call_target="tpu_custom_call" | custom-call | tf_op jit(solution)/shard_map/pallas_call | solution.py:264
  70.2 0.0 collective-permute-done.3.refs_4_
  70.2 0.0 copy-start.4
  70.2 0.0 collective-permute-done.4.refs_5_
  70.3 0.0 copy-start.5
  70.3 0.0 collective-permute-done.5.refs_6_
  70.3 0.0 copy-start.6
  70.3 0.4 collective-permute-done.6.refs_7_
  70.7 3.2 %collective-permute-done.7.refs_8_ = bf16[32,2048]{1,0:T(8,128)(2,1)S(1)} collective-permute-done((bf16[32,2048]{1,0:T(8,128)(2,1)}, bf16[32,2048]{1,0:T(8,128)(2,1)S(1)}, u32[]{:S(2)}, u32[]{:S(2)}) %collective-permute-start.7) | collective-permute-done | bytes 131104 | tf_op jit(solution)/shard_map/ppermute | solution.py:349
  73.9 0.0 copy-done.2
  73.9 0.0 copy-done.3
  73.9 0.6 copy-done.8
  74.5 2.4 %shard_map.86 = bf16[1,8,16,8192]{3,2,1,0:T(8,128)(2,1)} custom-call(s32[1]{0:T(128)} %bitcast.me_ref, bf16[16,2048]{1,0:T(8,128)(2,1)} %get-tuple-element.24.refs_0_, bf16[128,2048]{1,0:T(8,128)(2,1)} %copy-done.1, bf16[32,2048]{1,0:T(8,128)(2,1)} %copy-done.2, bf16[32,2048]{1,0:T(8,128)(2,1)} %copy-done.3, ...), custom_call_target="tpu_custom_call", output_to_operand_aliasing={{}: (10, {})} | custom-call | tf_op jit(solution)/shard_map/pallas_call | solution.py:264
  (9 shorter events, 0.0 us)
Async XLA Ops:
  14.1 52.8 %all-to-all-start = ((bf16[16,16,2048]{2,1,0:T(8,128)(2,1)}), bf16[16,16,2048]{2,1,0:T(8,128)(2,1)S(1)}, u32[]{:S(2)}, u32[]{:S(2)}) async-start(bf16[16,16,2048]{2,1,0:T(8,128)(2,1)} %bitcast.5), calls=%async_computation | async-start | bytes 2097152 | tf_op jit(solution)/shard_map/all_to_all | solution.py:323
  34.3 2.2 %collective-permute-start = (bf16[128,2048]{1,0:T(8,128)(2,1)}, bf16[128,2048]{1,0:T(8,128)(2,1)S(1)}, u32[]{:S(2)}, u32[]{:S(2)}) collective-permute-start(bf16[128,2048]{1,0:T(8,128)(2,1)} %get-tuple-element.25), channel_id=1, source_target_pairs={{0,1},{1,0},{2,3},{3,2},{4,5},{5,4},{6,7},{7,6},{8,9},{9,8},{10,11... | collective-permute-start | bytes 1572872 | tf_op jit(solution)/shard_map/ppermute | solution.py:340
  36.5 0.8 %copy-start.1 = (bf16[128,2048]{1,0:T(8,128)(2,1)}, bf16[128,2048]{1,0:T(8,128)(2,1)S(1)}, u32[]{:S(2)}) copy-start(bf16[128,2048]{1,0:T(8,128)(2,1)S(1)} %collective-permute-done.refs_7_.refs_1_) | copy-start | bytes 1572868
  39.6 23.0 %collective-permute-start.1 = (bf16[32,2048]{1,0:T(8,128)(2,1)}, bf16[32,2048]{1,0:T(8,128)(2,1)S(1)}, u32[]{:S(2)}, u32[]{:S(2)}) collective-permute-start(bf16[32,2048]{1,0:T(8,128)(2,1)} %get-tuple-element.33), channel_id=1, source_target_pairs={{0,8},{2,10},{4,12},{6,14},{8,0},{10,2},{12,4},{14,6},{1,9},{3,11}... | collective-permute-start | bytes 393224 | tf_op jit(solution)/shard_map/ppermute | solution.py:349
  42.5 20.1 %collective-permute-start.2 = (bf16[32,2048]{1,0:T(8,128)(2,1)}, bf16[32,2048]{1,0:T(8,128)(2,1)S(1)}, u32[]{:S(2)}, u32[]{:S(2)}) collective-permute-start(bf16[32,2048]{1,0:T(8,128)(2,1)} %get-tuple-element.34), channel_id=1, source_target_pairs={{0,12},{2,14},{4,8},{6,10},{8,4},{10,6},{12,0},{14,2},{1,13},{3,15... | collective-permute-start | bytes 393224 | tf_op jit(solution)/shard_map/ppermute | solution.py:349
  43.9 26.3 %collective-permute-start.3 = (bf16[32,2048]{1,0:T(8,128)(2,1)}, bf16[32,2048]{1,0:T(8,128)(2,1)S(1)}, u32[]{:S(2)}, u32[]{:S(2)}) collective-permute-start(bf16[32,2048]{1,0:T(8,128)(2,1)} %get-tuple-element.35), channel_id=1, source_target_pairs={{0,10},{2,8},{4,14},{6,12},{8,2},{10,0},{12,6},{14,4},{1,11},{3,9}... | collective-permute-start | bytes 393224 | tf_op jit(solution)/shard_map/ppermute | solution.py:349
  46.3 24.0 %collective-permute-start.4 = (bf16[32,2048]{1,0:T(8,128)(2,1)}, bf16[32,2048]{1,0:T(8,128)(2,1)S(1)}, u32[]{:S(2)}, u32[]{:S(2)}) collective-permute-start(bf16[32,2048]{1,0:T(8,128)(2,1)} %get-tuple-element.36), channel_id=1, source_target_pairs={{0,14},{2,12},{4,10},{6,8},{8,6},{10,4},{12,2},{14,0},{1,15},{3,13... | collective-permute-start | bytes 393224 | tf_op jit(solution)/shard_map/ppermute | solution.py:349
  47.2 23.1 %collective-permute-start.5 = (bf16[32,2048]{1,0:T(8,128)(2,1)}, bf16[32,2048]{1,0:T(8,128)(2,1)S(1)}, u32[]{:S(2)}, u32[]{:S(2)}) collective-permute-start(bf16[32,2048]{1,0:T(8,128)(2,1)} %get-tuple-element.37), channel_id=1, source_target_pairs={{0,2},{2,0},{4,6},{6,4},{8,10},{10,8},{12,14},{14,12},{1,3},{3,1},... | collective-permute-start | bytes 393224 | tf_op jit(solution)/shard_map/ppermute | solution.py:349
  62.6 11.3 %copy-start.2 = (bf16[32,2048]{1,0:T(8,128)(2,1)}, bf16[32,2048]{1,0:T(8,128)(2,1)S(1)}, u32[]{:S(2)}) copy-start(bf16[32,2048]{1,0:T(8,128)(2,1)S(1)} %collective-permute-done.1.refs_2_) | copy-start | bytes 393220
  62.6 8.1 %collective-permute-start.6 = (bf16[32,2048]{1,0:T(8,128)(2,1)}, bf16[32,2048]{1,0:T(8,128)(2,1)S(1)}, u32[]{:S(2)}, u32[]{:S(2)}) collective-permute-start(bf16[32,2048]{1,0:T(8,128)(2,1)} %get-tuple-element.38), channel_id=1, source_target_pairs={{0,4},{2,6},{4,0},{6,2},{8,12},{10,14},{12,8},{14,10},{1,5},{3,7},... | collective-permute-start | bytes 393224 | tf_op jit(solution)/shard_map/ppermute | solution.py:349
  62.6 11.3 %copy-start.3 = (bf16[32,2048]{1,0:T(8,128)(2,1)}, bf16[32,2048]{1,0:T(8,128)(2,1)S(1)}, u32[]{:S(2)}) copy-start(bf16[32,2048]{1,0:T(8,128)(2,1)S(1)} %collective-permute-done.2.refs_3_) | copy-start | bytes 393220
  62.6 11.3 %collective-permute-start.7 = (bf16[32,2048]{1,0:T(8,128)(2,1)}, bf16[32,2048]{1,0:T(8,128)(2,1)S(1)}, u32[]{:S(2)}, u32[]{:S(2)}) collective-permute-start(bf16[32,2048]{1,0:T(8,128)(2,1)} %get-tuple-element.39), channel_id=1, source_target_pairs={{0,6},{2,4},{4,2},{6,0},{8,14},{10,12},{12,10},{14,8},{1,7},{3,5},... | collective-permute-start | bytes 393224 | tf_op jit(solution)/shard_map/ppermute | solution.py:349
  66.9 1.0 %copy-start = (bf16[16,16,2048]{2,1,0:T(8,128)(2,1)}, bf16[16,16,2048]{2,1,0:T(8,128)(2,1)S(1)}, u32[]{:S(2)}) copy-start(bf16[16,16,2048]{2,1,0:T(8,128)(2,1)S(1)} %all-to-all-done) | copy-start | bytes 3145732
  70.2 3.7 %copy-start.4 = (bf16[32,2048]{1,0:T(8,128)(2,1)}, bf16[32,2048]{1,0:T(8,128)(2,1)S(1)}, u32[]{:S(2)}) copy-start(bf16[32,2048]{1,0:T(8,128)(2,1)S(1)} %collective-permute-done.3.refs_4_) | copy-start | bytes 393220
  70.3 3.6 %copy-start.5 = (bf16[32,2048]{1,0:T(8,128)(2,1)}, bf16[32,2048]{1,0:T(8,128)(2,1)S(1)}, u32[]{:S(2)}) copy-start(bf16[32,2048]{1,0:T(8,128)(2,1)S(1)} %collective-permute-done.4.refs_5_) | copy-start | bytes 393220
  70.3 3.6 %copy-start.6 = (bf16[32,2048]{1,0:T(8,128)(2,1)}, bf16[32,2048]{1,0:T(8,128)(2,1)S(1)}, u32[]{:S(2)}) copy-start(bf16[32,2048]{1,0:T(8,128)(2,1)S(1)} %collective-permute-done.5.refs_6_) | copy-start | bytes 393220
  70.7 3.2 %copy-start.7 = (bf16[32,2048]{1,0:T(8,128)(2,1)}, bf16[32,2048]{1,0:T(8,128)(2,1)S(1)}, u32[]{:S(2)}) copy-start(bf16[32,2048]{1,0:T(8,128)(2,1)S(1)} %collective-permute-done.6.refs_7_) | copy-start | bytes 393220
  73.9 0.7 copy-start.8

commit v11 on v10

--- a/solution.py
+++ b/solution.py
@@ -276,7 +276,8 @@
 
 def exchange_order(ranks):
     near, far = list(range(1, ranks // 2)), list(range(ranks // 2, ranks))
-    return far[::2] + far[1::2] + near
+    far = far[::2] + far[1::2]
+    return far[:1] + near[:-1] + far[1:] + near[-1:]
 
 
 def local(

time: 77.3 us -> 74.9 us (0.969)
  starting transfers between devices: 21.2 us -> 18 us
    ppermute x7, starting transfers between devices: 13.4 us -> 10.2 us  [local(): lax.ppermute(joined[j], 'dp', [(i, i ^ j) for i in range(ranks)])]
where the time goes in v11:
time: 74.9 us; the launch traced here: 74.5 us
  Pallas kernels  32.6 us (44%)
  waiting for transfers between devices  20 us (27%)
  starting transfers between devices  18 us (24%)
  local copies, waits for them, and re-layouts  2.45 us (3%)
  between operations  1.43 us (2%)
    pallas_call x2, Pallas kernels, attend(): pl.pallas_call(functools.partial(attend_kernel, places // experts, group,...  25.6 us
    ppermute x7, waiting for transfers between devices, local(): lax.ppermute(joined[j], 'dp', [(i, i ^ j) for i in range(ranks)])  18.3 us
    ppermute x7, starting transfers between devices, local(): lax.ppermute(joined[j], 'dp', [(i, i ^ j) for i in range(ranks)])  10.2 us
    all_to_all x1, starting transfers between devices, to_all(): lax.all_to_all(outgoing.reshape(experts, capacity, -1), ('dp', 'ep'), spl...  7.4 us
    pallas_call x2, Pallas kernels, place(): pl.pallas_call(functools.partial(place_kernel, plan, cores), in_specs=[pl...  4.72 us
    unnamed x18, local copies, waits for them, and re-layouts  2.45 us
    pallas_call x1, Pallas kernels, join(): pl.pallas_call(join_kernel, in_specs=[pl.BlockSpec(memory_space=pl.ANY)]...  2.26 us
    ppermute x1, waiting for transfers between devices, local(): swapped = lax.ppermute(message, 'ep', [(i, i ^ 1) for i in range(cores)])  1.75 us
  transfers between devices with their start and end apart: 9, of which 4 were waited for; matrix products, arithmetic and copies ran while one was open for 0% of the time, Pallas kernels for 23%

profile of v11, /device:TPU:0, one launch (start us, length us, event | category | flops | bytes accessed | tf_op | source)
XLA Modules:
  0.0 74.5 jit_solution(3633989071079397373)
XLA Ops:
  1.3 12.8 %shard_map.82 = (bf16[256,2048]{1,0:T(8,128)(2,1)}, f32[8,128]{1,0:T(8,128)}) custom-call(s32[1]{0:T(128)} %constant.11.clone.1.me_ref, s32[1]{0:T(128)S(6)} %copy.11.count_ref, s32[1]{0:T(128)S(6)} %copy.12.size_ref, s32[2,128]{1,0:T(2,128)} %bitcast.6, bf16[128,4096]{1,0:T(8,128)(2,1)} %queries_hbm.3, bf16[32,128,512]{2,1,0:T(8,128)(2,1)} %key_weight_hbm.3, ...), custom_call_target="tpu_custom_call" | custom-call | flops 4831838208 | bytes 4194304 | tf_op jit(solution)/shard_map/pallas_call | solution.py:186
  14.1 7.4 %all-to-all-start = ((bf16[16,16,2048]{2,1,0:T(8,128)(2,1)}), bf16[16,16,2048]{2,1,0:T(8,128)(2,1)S(1)}, u32[]{:S(2)}, u32[]{:S(2)}) async-start(bf16[16,16,2048]{2,1,0:T(8,128)(2,1)} %bitcast.5), calls=%async_computation | async-start | bytes 2097152 | tf_op jit(solution)/shard_map/all_to_all | solution.py:324
  21.5 12.8 %shard_map.83 = (bf16[16,2048]{1,0:T(8,128)(2,1)}, bf16[16,2048]{1,0:T(8,128)(2,1)}, bf16[16,2048]{1,0:T(8,128)(2,1)}, bf16[16,2048]{1,0:T(8,128)(2,1)}, bf16[16...) custom-call(s32[1]{0:T(128)} %bitcast.me_ref, ...), custom_call_target="tpu_custom_call" | custom-call | flops 4831838208 | bytes 4194304 | tf_op jit(solution)/shard_map/pallas_call | solution.py:186
  34.3 0.4 collective-permute-start
  34.8 1.7 %collective-permute-done.refs_7_.refs_1_ = bf16[128,2048]{1,0:T(8,128)(2,1)S(1)} collective-permute-done((bf16[128,2048]{1,0:T(8,128)(2,1)}, bf16[128,2048]{1,0:T(8,128)(2,1)S(1)}, u32[]{:S(2)}, u32[]{:S(2)}) %collective-permute-start) | collective-permute-done | bytes 524320 | tf_op jit(solution)/shard_map/ppermute | solution.py:341
  36.5 0.8 %copy-done.1 = bf16[128,2048]{1,0:T(8,128)(2,1)} copy-done((bf16[128,2048]{1,0:T(8,128)(2,1)}, bf16[128,2048]{1,0:T(8,128)(2,1)S(1)}, u32[]{:S(2)}) %copy-start.1) | copy-done | bytes 524312
  37.3 2.3 %shard_map.84 = (bf16[32,2048]{1,0:T(8,128)(2,1)}, bf16[32,2048]{1,0:T(8,128)(2,1)}, bf16[32,2048]{1,0:T(8,128)(2,1)}, bf16[32,2048]{1,0:T(8,128)(2,1)}, bf16[32...) custom-call(bf16[16,2048]{1,0:T(8,128)(2,1)} %get-tuple-element.26.refs_0_, ...), custom_call_target="tpu_custom_call" | custom-call | tf_op jit(solution)/shard_map/pallas_call | solution.py:233
  39.6 2.9 %collective-permute-start.1 = (bf16[32,2048]{1,0:T(8,128)(2,1)}, bf16[32,2048]{1,0:T(8,128)(2,1)S(1)}, u32[]{:S(2)}, u32[]{:S(2)}) collective-permute-start(bf16[32,2048]{1,0:T(8,128)(2,1)} %get-tuple-element.33), channel_id=1, source_target_pairs={{0,8},{2,10},{4,12},{6,14},{8,0},{10,2},{12,4},{14,6},{1,9},{3,11}... | collective-permute-start | bytes 393224 | tf_op jit(solution)/shard_map/ppermute | solution.py:350
  42.5 1.5 %collective-permute-start.2 = (bf16[32,2048]{1,0:T(8,128)(2,1)}, bf16[32,2048]{1,0:T(8,128)(2,1)S(1)}, u32[]{:S(2)}, u32[]{:S(2)}) collective-permute-start(bf16[32,2048]{1,0:T(8,128)(2,1)} %get-tuple-element.34), channel_id=1, source_target_pairs={{0,2},{2,0},{4,6},{6,4},{8,10},{10,8},{12,14},{14,12},{1,3},{3,1},... | collective-permute-start | bytes 393224 | tf_op jit(solution)/shard_map/ppermute | solution.py:350
  43.9 1.5 %collective-permute-start.3 = (bf16[32,2048]{1,0:T(8,128)(2,1)}, bf16[32,2048]{1,0:T(8,128)(2,1)S(1)}, u32[]{:S(2)}, u32[]{:S(2)}) collective-permute-start(bf16[32,2048]{1,0:T(8,128)(2,1)} %get-tuple-element.35), channel_id=1, source_target_pairs={{0,4},{2,6},{4,0},{6,2},{8,12},{10,14},{12,8},{14,10},{1,5},{3,7},... | collective-permute-start | bytes 393224 | tf_op jit(solution)/shard_map/ppermute | solution.py:350
  45.4 0.6 collective-permute-start.4
  46.0 1.5 %collective-permute-start.5 = (bf16[32,2048]{1,0:T(8,128)(2,1)}, bf16[32,2048]{1,0:T(8,128)(2,1)S(1)}, u32[]{:S(2)}, u32[]{:S(2)}) collective-permute-start(bf16[32,2048]{1,0:T(8,128)(2,1)} %get-tuple-element.37), channel_id=1, source_target_pairs={{0,10},{2,8},{4,14},{6,12},{8,2},{10,0},{12,6},{14,4},{1,11},{3,9}... | collective-permute-start | bytes 393224 | tf_op jit(solution)/shard_map/ppermute | solution.py:350
  47.4 12.3 %collective-permute-done.1.refs_2_ = bf16[32,2048]{1,0:T(8,128)(2,1)S(1)} collective-permute-done((bf16[32,2048]{1,0:T(8,128)(2,1)}, bf16[32,2048]{1,0:T(8,128)(2,1)S(1)}, u32[]{:S(2)}, u32[]{:S(2)}) %collective-permute-start.1) | collective-permute-done | bytes 131104 | tf_op jit(solution)/shard_map/ppermute | solution.py:350
  59.8 2.4 %collective-permute-start.6 = (bf16[32,2048]{1,0:T(8,128)(2,1)}, bf16[32,2048]{1,0:T(8,128)(2,1)S(1)}, u32[]{:S(2)}, u32[]{:S(2)}) collective-permute-start(bf16[32,2048]{1,0:T(8,128)(2,1)} %get-tuple-element.38), channel_id=1, source_target_pairs={{0,14},{2,12},{4,10},{6,8},{8,6},{10,4},{12,2},{14,0},{1,15},{3,13... | collective-permute-start | bytes 393224 | tf_op jit(solution)/shard_map/ppermute | solution.py:350
  62.1 0.0 collective-permute-done.2.refs_3_
  62.1 0.0 collective-permute-start.7
  62.1 0.0 all-to-all-done
  62.2 0.0 copy-start
  62.2 1.0 %copy-done = bf16[16,16,2048]{2,1,0:T(8,128)(2,1)} copy-done((bf16[16,16,2048]{2,1,0:T(8,128)(2,1)}, bf16[16,16,2048]{2,1,0:T(8,128)(2,1)S(1)}, u32[]{:S(2)}) %copy-start) | copy-done | bytes 1048600
  63.2 2.3 %shard_map.85.refs_9_ = bf16[1,8,16,8192]{3,2,1,0:T(8,128)(2,1)} custom-call(s32[1]{0:T(128)} %constant.11.clone.1.me_ref, bf16[256,2048]{1,0:T(8,128)(2,1)} %bitcast.4), custom_call_target="tpu_custom_call" | custom-call | tf_op jit(solution)/shard_map/pallas_call | solution.py:264
  65.5 0.0 collective-permute-done.3.refs_4_
  65.5 0.0 copy-start.4
  65.5 0.0 collective-permute-done.4.refs_5_
  65.5 0.0 copy-start.5
  65.5 3.6 %collective-permute-done.5.refs_6_ = bf16[32,2048]{1,0:T(8,128)(2,1)S(1)} collective-permute-done((bf16[32,2048]{1,0:T(8,128)(2,1)}, bf16[32,2048]{1,0:T(8,128)(2,1)S(1)}, u32[]{:S(2)}, u32[]{:S(2)}) %collective-permute-start.5) | collective-permute-done | bytes 131104 | tf_op jit(solution)/shard_map/ppermute | solution.py:350
  69.2 0.0 collective-permute-done.6.refs_7_
  69.2 2.3 %collective-permute-done.7.refs_8_ = bf16[32,2048]{1,0:T(8,128)(2,1)S(1)} collective-permute-done((bf16[32,2048]{1,0:T(8,128)(2,1)}, bf16[32,2048]{1,0:T(8,128)(2,1)S(1)}, u32[]{:S(2)}, u32[]{:S(2)}) %collective-permute-start.7) | collective-permute-done | bytes 131104 | tf_op jit(solution)/shard_map/ppermute | solution.py:350
  71.5 0.0 copy-done.2
  71.5 0.0 copy-done.3
  71.5 0.0 copy-done.4
  71.5 0.6 copy-done.8
  72.1 2.4 %shard_map.86 = bf16[1,8,16,8192]{3,2,1,0:T(8,128)(2,1)} custom-call(s32[1]{0:T(128)} %bitcast.me_ref, bf16[16,2048]{1,0:T(8,128)(2,1)} %get-tuple-element.24.refs_0_, bf16[128,2048]{1,0:T(8,128)(2,1)} %copy-done.1, bf16[32,2048]{1,0:T(8,128)(2,1)} %copy-done.2, bf16[32,2048]{1,0:T(8,128)(2,1)} %copy-done.3, ...), custom_call_target="tpu_custom_call", output_to_operand_aliasing={{}: (10, {})} | custom-call | tf_op jit(solution)/shard_map/pallas_call | solution.py:264
  (9 shorter events, 0.0 us)
Async XLA Ops:
  14.1 48.0 %all-to-all-start = ((bf16[16,16,2048]{2,1,0:T(8,128)(2,1)}), bf16[16,16,2048]{2,1,0:T(8,128)(2,1)S(1)}, u32[]{:S(2)}, u32[]{:S(2)}) async-start(bf16[16,16,2048]{2,1,0:T(8,128)(2,1)} %bitcast.5), calls=%async_computation | async-start | bytes 2097152 | tf_op jit(solution)/shard_map/all_to_all | solution.py:324
  34.3 2.2 %collective-permute-start = (bf16[128,2048]{1,0:T(8,128)(2,1)}, bf16[128,2048]{1,0:T(8,128)(2,1)S(1)}, u32[]{:S(2)}, u32[]{:S(2)}) collective-permute-start(bf16[128,2048]{1,0:T(8,128)(2,1)} %get-tuple-element.25), channel_id=1, source_target_pairs={{0,1},{1,0},{2,3},{3,2},{4,5},{5,4},{6,7},{7,6},{8,9},{9,8},{10,11... | collective-permute-start | bytes 1572872 | tf_op jit(solution)/shard_map/ppermute | solution.py:341
  36.5 0.8 %copy-start.1 = (bf16[128,2048]{1,0:T(8,128)(2,1)}, bf16[128,2048]{1,0:T(8,128)(2,1)S(1)}, u32[]{:S(2)}) copy-start(bf16[128,2048]{1,0:T(8,128)(2,1)S(1)} %collective-permute-done.refs_7_.refs_1_) | copy-start | bytes 1572868
  39.6 20.2 %collective-permute-start.1 = (bf16[32,2048]{1,0:T(8,128)(2,1)}, bf16[32,2048]{1,0:T(8,128)(2,1)S(1)}, u32[]{:S(2)}, u32[]{:S(2)}) collective-permute-start(bf16[32,2048]{1,0:T(8,128)(2,1)} %get-tuple-element.33), channel_id=1, source_target_pairs={{0,8},{2,10},{4,12},{6,14},{8,0},{10,2},{12,4},{14,6},{1,9},{3,11}... | collective-permute-start | bytes 393224 | tf_op jit(solution)/shard_map/ppermute | solution.py:350
  42.5 19.7 %collective-permute-start.2 = (bf16[32,2048]{1,0:T(8,128)(2,1)}, bf16[32,2048]{1,0:T(8,128)(2,1)S(1)}, u32[]{:S(2)}, u32[]{:S(2)}) collective-permute-start(bf16[32,2048]{1,0:T(8,128)(2,1)} %get-tuple-element.34), channel_id=1, source_target_pairs={{0,2},{2,0},{4,6},{6,4},{8,10},{10,8},{12,14},{14,12},{1,3},{3,1},... | collective-permute-start | bytes 393224 | tf_op jit(solution)/shard_map/ppermute | solution.py:350
  43.9 21.6 %collective-permute-start.3 = (bf16[32,2048]{1,0:T(8,128)(2,1)}, bf16[32,2048]{1,0:T(8,128)(2,1)S(1)}, u32[]{:S(2)}, u32[]{:S(2)}) collective-permute-start(bf16[32,2048]{1,0:T(8,128)(2,1)} %get-tuple-element.35), channel_id=1, source_target_pairs={{0,4},{2,6},{4,0},{6,2},{8,12},{10,14},{12,8},{14,10},{1,5},{3,7},... | collective-permute-start | bytes 393224 | tf_op jit(solution)/shard_map/ppermute | solution.py:350
  45.4 20.1 %collective-permute-start.4 = (bf16[32,2048]{1,0:T(8,128)(2,1)}, bf16[32,2048]{1,0:T(8,128)(2,1)S(1)}, u32[]{:S(2)}, u32[]{:S(2)}) collective-permute-start(bf16[32,2048]{1,0:T(8,128)(2,1)} %get-tuple-element.36), channel_id=1, source_target_pairs={{0,12},{2,14},{4,8},{6,10},{8,4},{10,6},{12,0},{14,2},{1,13},{3,15... | collective-permute-start | bytes 393224 | tf_op jit(solution)/shard_map/ppermute | solution.py:350
  46.0 23.2 %collective-permute-start.5 = (bf16[32,2048]{1,0:T(8,128)(2,1)}, bf16[32,2048]{1,0:T(8,128)(2,1)S(1)}, u32[]{:S(2)}, u32[]{:S(2)}) collective-permute-start(bf16[32,2048]{1,0:T(8,128)(2,1)} %get-tuple-element.37), channel_id=1, source_target_pairs={{0,10},{2,8},{4,14},{6,12},{8,2},{10,0},{12,6},{14,4},{1,11},{3,9}... | collective-permute-start | bytes 393224 | tf_op jit(solution)/shard_map/ppermute | solution.py:350
  59.8 11.7 %copy-start.2 = (bf16[32,2048]{1,0:T(8,128)(2,1)}, bf16[32,2048]{1,0:T(8,128)(2,1)S(1)}, u32[]{:S(2)}) copy-start(bf16[32,2048]{1,0:T(8,128)(2,1)S(1)} %collective-permute-done.1.refs_2_) | copy-start | bytes 393220
  59.8 9.4 %collective-permute-start.6 = (bf16[32,2048]{1,0:T(8,128)(2,1)}, bf16[32,2048]{1,0:T(8,128)(2,1)S(1)}, u32[]{:S(2)}, u32[]{:S(2)}) collective-permute-start(bf16[32,2048]{1,0:T(8,128)(2,1)} %get-tuple-element.38), channel_id=1, source_target_pairs={{0,14},{2,12},{4,10},{6,8},{8,6},{10,4},{12,2},{14,0},{1,15},{3,13... | collective-permute-start | bytes 393224 | tf_op jit(solution)/shard_map/ppermute | solution.py:350
  62.1 9.3 %copy-start.3 = (bf16[32,2048]{1,0:T(8,128)(2,1)}, bf16[32,2048]{1,0:T(8,128)(2,1)S(1)}, u32[]{:S(2)}) copy-start(bf16[32,2048]{1,0:T(8,128)(2,1)S(1)} %collective-permute-done.2.refs_3_) | copy-start | bytes 393220
  62.1 9.3 %collective-permute-start.7 = (bf16[32,2048]{1,0:T(8,128)(2,1)}, bf16[32,2048]{1,0:T(8,128)(2,1)S(1)}, u32[]{:S(2)}, u32[]{:S(2)}) collective-permute-start(bf16[32,2048]{1,0:T(8,128)(2,1)} %get-tuple-element.39), channel_id=1, source_target_pairs={{0,6},{2,4},{4,2},{6,0},{8,14},{10,12},{12,10},{14,8},{1,7},{3,5},... | collective-permute-start | bytes 393224 | tf_op jit(solution)/shard_map/ppermute | solution.py:350
  62.2 1.0 %copy-start = (bf16[16,16,2048]{2,1,0:T(8,128)(2,1)}, bf16[16,16,2048]{2,1,0:T(8,128)(2,1)S(1)}, u32[]{:S(2)}) copy-start(bf16[16,16,2048]{2,1,0:T(8,128)(2,1)S(1)} %all-to-all-done) | copy-start | bytes 3145732
  65.5 6.0 %copy-start.4 = (bf16[32,2048]{1,0:T(8,128)(2,1)}, bf16[32,2048]{1,0:T(8,128)(2,1)S(1)}, u32[]{:S(2)}) copy-start(bf16[32,2048]{1,0:T(8,128)(2,1)S(1)} %collective-permute-done.3.refs_4_) | copy-start | bytes 393220
  65.5 5.9 %copy-start.5 = (bf16[32,2048]{1,0:T(8,128)(2,1)}, bf16[32,2048]{1,0:T(8,128)(2,1)S(1)}, u32[]{:S(2)}) copy-start(bf16[32,2048]{1,0:T(8,128)(2,1)S(1)} %collective-permute-done.4.refs_5_) | copy-start | bytes 393220
  69.2 2.3 %copy-start.6 = (bf16[32,2048]{1,0:T(8,128)(2,1)}, bf16[32,2048]{1,0:T(8,128)(2,1)S(1)}, u32[]{:S(2)}) copy-start(bf16[32,2048]{1,0:T(8,128)(2,1)S(1)} %collective-permute-done.5.refs_6_) | copy-start | bytes 393220
  69.2 2.3 %copy-start.7 = (bf16[32,2048]{1,0:T(8,128)(2,1)}, bf16[32,2048]{1,0:T(8,128)(2,1)S(1)}, u32[]{:S(2)}) copy-start(bf16[32,2048]{1,0:T(8,128)(2,1)S(1)} %collective-permute-done.6.refs_7_) | copy-start | bytes 393220
  71.5 0.7 copy-start.8

commit v12 on v9

--- a/solution.py
+++ b/solution.py
@@ -10,8 +10,8 @@
 
 SPAN = 64
 STACK = 4
-CHUNKS = (2, 3, 3)
-VMEM = 60 * 1024 * 1024
+CHUNKS = (3, 5)
+VMEM = 63_400_000
 SHORT = pl.CostEstimate(flops=0, bytes_accessed=0, transcendentals=0)
 MASKED = -1e30
 OPEN = 3e38
@@ -53,8 +53,8 @@
     fresh_hbm,
     *rest,
 ):
-    out_ref, mark_ref, queries_ref, key_weight_ref, value_weight_ref, keys_ref = rest[-10:-4]
-    cap_ref, table_ref, attended_ref, sem = rest[-4:]
+    out_hbm, mark_ref, queries_ref, key_weight_ref, value_weight_ref, keys_ref = rest[-10:-4]
+    cap_ref, table_ref, rows_ref, sem = rest[-4:]
     slots = queries_ref.shape[0]
     past = prefix_hbm.shape[0]
     heads, dim, _ = key_weight_ref.shape
@@ -68,7 +68,8 @@
         pltpu.make_async_copy(fresh_hbm, keys_ref.at[pl.ds(past, slots)], sem.at[3]),
         pltpu.make_async_copy(value_weight_hbm.at[here], value_weight_ref, sem.at[4]),
     ]
-    for copy in copies:
+    *needed, for_values = copies
+    for copy in needed:
         copy.start()
     mark_ref[...] = jnp.zeros_like(mark_ref)
     count, size = count_ref[0], size_ref[0]
@@ -80,8 +81,9 @@
         (col <= row) & (col < count * SPAN), jnp.float32(OPEN), jnp.float32(MASKED)
     )
     build_table(count, routes_ref, table_ref, capacity)
-    for copy in copies:
+    for copy in needed:
         copy.wait()
+    for_values.start()
 
     scale = math.log2(math.e) / math.sqrt(dim)
     keys = keys_ref[...]
@@ -94,6 +96,9 @@
             lifted.append(one.astype(jnp.bfloat16))
         lifted = jnp.concatenate(lifted, axis=0)
         scores.append(lax.dot_general(lifted, keys, NT, preferred_element_type=jnp.float32))
+    for_values.wait()
+    width = STACK * dim
+    sends = []
     for stack in range(stacks):
         score = scores[stack].reshape(STACK, slots, keys.shape[0])
         score = jnp.minimum(score, cap_ref[...][None])
@@ -102,11 +107,17 @@
         total = jnp.sum(weights, axis=-1, keepdims=True)
         weights = weights.astype(jnp.bfloat16).reshape(STACK * slots, keys.shape[0])
         mixed = dot(weights, keys).astype(jnp.bfloat16)
+        attended = []
         for g in range(STACK):
-            h = stack * STACK + g
-            projected = dot(mixed[g * slots : (g + 1) * slots], value_weight_ref[h])
-            attended_ref[:, h * dim : (h + 1) * dim] = (projected / total[g]).astype(jnp.bfloat16)
-    out_ref[...] = dot(table_ref[...], attended_ref[...]).astype(jnp.bfloat16)
+            projected = dot(mixed[g * slots : (g + 1) * slots], value_weight_ref[stack * STACK + g])
+            attended.append((projected / total[g]).astype(jnp.bfloat16))
+        attended = jnp.concatenate(attended, axis=1)
+        rows_ref[stack] = dot(table_ref[...], attended).astype(jnp.bfloat16)
+        there = out_hbm.at[:, pl.ds(stack * width, width)]
+        sends.append(pltpu.make_async_copy(rows_ref.at[stack], there, sem.at[5 + stack]))
+        sends[-1].start()
+    for send in sends:
+        send.wait()
 
 
 def attend(first, heads, operands, experts, after):
@@ -121,7 +132,7 @@
     return pl.pallas_call(
         functools.partial(attend_kernel, places // experts, first),
         in_specs=[smem, smem, vmem] + [hbm] * 5 + [vmem] * len(after),
-        out_specs=[vmem, vmem],
+        out_specs=[hbm, vmem],
         out_shape=[
             jax.ShapeDtypeStruct((places, heads * dim), jnp.bfloat16),
             jax.ShapeDtypeStruct((8, 128), jnp.float32),
@@ -133,39 +144,47 @@
             pltpu.VMEM((keys, latent), jnp.bfloat16),
             pltpu.VMEM((slots, keys), jnp.float32),
             pltpu.VMEM((places, slots), jnp.bfloat16),
-            pltpu.VMEM((slots, heads * dim), jnp.bfloat16),
-            pltpu.SemaphoreType.DMA((5,)),
+            pltpu.VMEM((heads // STACK, places, STACK * dim), jnp.bfloat16),
+            pltpu.SemaphoreType.DMA((5 + heads // STACK,)),
         ],
         compiler_params=pltpu.CompilerParams(vmem_limit_bytes=VMEM),
     )(*operands, *after)
 
 
 def place_kernel(starts, cores, *refs):
-    out_ref, sem = refs[-2:]
+    chunk_refs, out_ref = refs[: len(starts)], refs[-3 - len(starts)]
+    held_refs, arrive, leave = refs[-2 - len(starts) : -2], refs[-2], refs[-1]
     _, ranks, capacity, features = out_ref.shape
     features //= cores
-    copies = []
-    for ref, start in zip(refs, starts):
+    arrivals, leaves = [], []
+    for ref, held_ref, start in zip(chunk_refs, held_refs, starts):
         width = ref.shape[1]
         for source in range(ranks * cores):
-            left = source % cores * features + start
-            target = out_ref.at[0, source // cores, :, pl.ds(left, width)]
-            rows = ref.at[pl.ds(source * capacity, capacity)]
-            copies.append(pltpu.make_async_copy(rows, target, sem.at[len(copies)]))
-    for copy in copies:
+            rows = pl.ds(source * capacity, capacity)
+            columns = pl.ds(source % cores * features + start, width)
+            target = out_ref.at[0, source // cores, :, columns]
+            i = len(arrivals)
+            arrivals.append(pltpu.make_async_copy(ref.at[rows], held_ref.at[rows], arrive.at[i]))
+            leaves.append(pltpu.make_async_copy(held_ref.at[rows], target, leave.at[i]))
+    for copy in arrivals:
         copy.start()
-    for copy in copies:
+    for arrival, leaving in zip(arrivals, leaves):
+        arrival.wait()
+        leaving.start()
+    for copy in leaves:
         copy.wait()
 
 
 def place(chunks, starts, cores, shape, placed):
     anywhere = pl.BlockSpec(memory_space=pl.ANY)
+    pieces = len(chunks) * shape[1] * cores
     return pl.pallas_call(
         functools.partial(place_kernel, starts, cores),
-        in_specs=[pl.BlockSpec(memory_space=pltpu.VMEM)] * len(chunks) + [anywhere] * len(placed),
+        in_specs=[anywhere] * (len(chunks) + len(placed)),
         out_specs=anywhere,
         out_shape=jax.ShapeDtypeStruct(shape, jnp.bfloat16),
-        scratch_shapes=[pltpu.SemaphoreType.DMA((len(chunks) * shape[1] * cores,))],
+        scratch_shapes=[pltpu.VMEM(chunk.shape, chunk.dtype) for chunk in chunks]
+        + [pltpu.SemaphoreType.DMA((pieces,))] * 2,
         input_output_aliases={len(chunks): 0} if placed else {},
         compiler_params=pltpu.CompilerParams(vmem_limit_bytes=VMEM),
         cost_estimate=SHORT,

time: 81.7 us -> 77.8 us (0.952)
  the two profiles are of different devices: /device:TPU:0 before, /device:TPU:15 now
where the time goes in v12:
time: 77.8 us; the launch traced here: 77.3 us
  Pallas kernels  31.7 us (41%)
  waiting for transfers between devices  31.5 us (40%)
  starting transfers between devices  11.5 us (15%)
  between operations  1.49 us (2%)
  local copies, waits for them, and re-layouts  1.08 us (1%)
    all_to_all x2, waiting for transfers between devices, local(): lax.all_to_all(outgoing.reshape(experts, capacity, size * dim), ('dp', 'e...  31.5 us
    pallas_call x2, Pallas kernels, attend(): pl.pallas_call(functools.partial(attend_kernel, places // experts, first)...  27.4 us
    all_to_all x2, starting transfers between devices, local(): lax.all_to_all(outgoing.reshape(experts, capacity, size * dim), ('dp', 'e...  11.5 us
    pallas_call x2, Pallas kernels, place(): pl.pallas_call(functools.partial(place_kernel, starts, cores), in_specs=[...  4.32 us
  transfers between devices with their start and end apart: 2, of which 2 were waited for; matrix products, arithmetic and copies ran while one was open for 0% of the time, Pallas kernels for 24%

profile of v12, /device:TPU:15, one launch (start us, length us, event | category | flops | bytes accessed | tf_op | source)
XLA Modules:
  0.0 77.3 jit_solution(13882178049968698742)
XLA Ops:
  1.3 11.2 %shard_map.82 = (bf16[256,1536]{1,0:T(8,128)(2,1)}, f32[8,128]{1,0:T(8,128)}) custom-call(s32[1]{0:T(128)S(6)} %copy.11.count_ref, s32[1]{0:T(128)S(6)} %copy.12.size_ref, s32[2,128]{1,0:T(2,128)} %bitcast.9, bf16[128,4096]{1,0:T(8,128)(2,1)} %queries_hbm.3, bf16[32,128,512]{2,1,0:T(8,128)(2,1)} %key_weight_hbm.3, bf16[32,512,128]{2,1,0:T(8,128)(2,1)} %value_weight_hbm.3, ...), custom_call_target="tpu_custom_call" | custom-call | tf_op jit(solution)/shard_map/pallas_call | solution.py:132
  12.5 6.6 %all-to-all-start.1 = ((bf16[16,16,1536]{2,1,0:T(8,128)(2,1)}), bf16[16,16,1536]{2,1,0:T(8,128)(2,1)S(1)}, u32[]{:S(2)}, u32[]{:S(2)}) async-start(bf16[16,16,1536]{2,1,0:T(8,128)(2,1)} %bitcast.8), calls=%async_computation.1 | async-start | bytes 1572864 | tf_op jit(solution)/shard_map/all_to_all | solution.py:223
  19.1 16.2 %shard_map.83 = (bf16[256,2560]{1,0:T(8,128)(2,1)}, f32[8,128]{1,0:T(8,128)}) custom-call(s32[1]{0:T(128)S(6)} %copy.11.count_ref, s32[1]{0:T(128)S(6)} %copy.12.size_ref, s32[2,128]{1,0:T(2,128)} %bitcast.10, bf16[128,4096]{1,0:T(8,128)(2,1)} %queries_hbm.3, bf16[32,128,512]{2,1,0:T(8,128)(2,1)} %key_weight_hbm.3, bf16[32,512,128]{2,1,0:T(8,128)(2,1)} %value_weight_hbm.3, ...), custom_call_target="tpu_custom_call" | custom-call | tf_op jit(solution)/shard_map/pallas_call | solution.py:132
  35.3 3.0 %all-to-all-done.1 = bf16[16,16,1536]{2,1,0:T(8,128)(2,1)S(1)} async-done(((bf16[16,16,1536]{2,1,0:T(8,128)(2,1)}), bf16[16,16,1536]{2,1,0:T(8,128)(2,1)S(1)}, u32[]{:S(2)}, u32[]{:S(2)}) %all-to-all-start.1) | async-done | bytes 786464 | tf_op jit(solution)/shard_map/all_to_all | solution.py:223
  38.3 0.0 copy-start.1
  38.3 5.0 %all-to-all-start = ((bf16[16,16,2560]{2,1,0:T(8,128)(2,1)}), bf16[16,16,2560]{2,1,0:T(8,128)(2,1)S(1)}, u32[]{:S(2)}, u32[]{:S(2)}) async-start(bf16[16,16,2560]{2,1,0:T(8,128)(2,1)} %bitcast.7), calls=%async_computation | async-start | bytes 2621440 | tf_op jit(solution)/shard_map/all_to_all | solution.py:223
  43.2 0.0 copy-done.1
  43.3 2.0 %shard_map.84.refs_1_ = bf16[1,8,16,8192]{3,2,1,0:T(8,128)(2,1)} custom-call(bf16[256,1536]{1,0:T(8,128)(2,1)} %bitcast.6), custom_call_target="tpu_custom_call" | custom-call | tf_op jit(solution)/shard_map/pallas_call | solution.py:181
  45.3 28.5 %all-to-all-done = bf16[16,16,2560]{2,1,0:T(8,128)(2,1)S(1)} async-done(((bf16[16,16,2560]{2,1,0:T(8,128)(2,1)}), bf16[16,16,2560]{2,1,0:T(8,128)(2,1)S(1)}, u32[]{:S(2)}, u32[]{:S(2)}) %all-to-all-start) | async-done | bytes 1310752 | tf_op jit(solution)/shard_map/all_to_all | solution.py:223
  73.8 0.0 copy-start
  73.8 1.1 %copy-done = bf16[16,16,2560]{2,1,0:T(8,128)(2,1)} copy-done((bf16[16,16,2560]{2,1,0:T(8,128)(2,1)}, bf16[16,16,2560]{2,1,0:T(8,128)(2,1)S(1)}, u32[]{:S(2)}) %copy-start) | copy-done | bytes 1310744
  74.9 2.3 %shard_map.85 = bf16[1,8,16,8192]{3,2,1,0:T(8,128)(2,1)} custom-call(bf16[256,2560]{1,0:T(8,128)(2,1)} %bitcast.5, bf16[1,8,16,8192]{3,2,1,0:T(8,128)(2,1)} %shard_map.84.refs_1_), custom_call_target="tpu_custom_call", output_to_operand_aliasing={{}: (1, {})} | custom-call | tf_op jit(solution)/shard_map/pallas_call | solution.py:181
Async XLA Ops:
  12.5 25.8 %all-to-all-start.1 = ((bf16[16,16,1536]{2,1,0:T(8,128)(2,1)}), bf16[16,16,1536]{2,1,0:T(8,128)(2,1)S(1)}, u32[]{:S(2)}, u32[]{:S(2)}) async-start(bf16[16,16,1536]{2,1,0:T(8,128)(2,1)} %bitcast.8), calls=%async_computation.1 | async-start | bytes 1572864 | tf_op jit(solution)/shard_map/all_to_all | solution.py:223
  38.3 5.0 %copy-start.1 = (bf16[16,16,1536]{2,1,0:T(8,128)(2,1)}, bf16[16,16,1536]{2,1,0:T(8,128)(2,1)S(1)}, u32[]{:S(2)}) copy-start(bf16[16,16,1536]{2,1,0:T(8,128)(2,1)S(1)} %all-to-all-done.1) | copy-start | bytes 2359300
  38.3 35.5 %all-to-all-start = ((bf16[16,16,2560]{2,1,0:T(8,128)(2,1)}), bf16[16,16,2560]{2,1,0:T(8,128)(2,1)S(1)}, u32[]{:S(2)}, u32[]{:S(2)}) async-start(bf16[16,16,2560]{2,1,0:T(8,128)(2,1)} %bitcast.7), calls=%async_computation | async-start | bytes 2621440 | tf_op jit(solution)/shard_map/all_to_all | solution.py:223
  73.8 1.1 %copy-start = (bf16[16,16,2560]{2,1,0:T(8,128)(2,1)}, bf16[16,16,2560]{2,1,0:T(8,128)(2,1)S(1)}, u32[]{:S(2)}) copy-start(bf16[16,16,2560]{2,1,0:T(8,128)(2,1)S(1)} %all-to-all-done) | copy-start | bytes 3932164

commit v13 on v10

--- a/solution.py
+++ b/solution.py
@@ -9,11 +9,9 @@
 from jax.sharding import PartitionSpec as P
 
 SPAN = 64
-GROUPS = (2, 2)
-UNROLL = 2
+STACK = 4
 CHUNKS = (1, 1)
 DIRECT = 16
-KEY_PARTS = 2
 VMEM = 60 * 1024 * 1024
 SHORT = pl.CostEstimate(flops=0, bytes_accessed=0, transcendentals=0)
 MARK = (8, 128)
@@ -48,7 +46,6 @@
 
 def attend_kernel(
     capacity,
-    group,
     first,
     cores,
     after,
@@ -70,42 +67,18 @@
     past = prefix_hbm.shape[0]
     heads, dim, _ = key_weight_ref.shape
     here = pl.ds(first, heads)
-    step = group * UNROLL
-    steps = heads // step
-    part = past // KEY_PARTS
-
-    def copy_step(i):
-        def of(source, target, index):
-            here, there = pl.ds(i * step, step), pl.ds(first + i * step, step)
-            return pltpu.make_async_copy(source.at[there], target.at[here], sem.at[3 * i + index])
-
-        here, there = pl.ds(i * step * dim, step * dim), pl.ds((first + i * step) * dim, step * dim)
-        return [
-            pltpu.make_async_copy(queries_hbm.at[:, there], queries_ref.at[:, here], sem.at[3 * i]),
-            of(key_weight_hbm, key_weight_ref, 1),
-            of(value_weight_hbm, value_weight_ref, 2),
-        ]
-
-    for_keys = [
+    here = pl.ds(first, heads)
+    copies = [
         pltpu.make_async_copy(
-            prefix_hbm.at[pl.ds(i * part, part)],
-            keys_ref.at[pl.ds(i * part, part)],
-            sem.at[3 * steps + i],
-        )
-        for i in range(KEY_PARTS)
+            queries_hbm.at[:, pl.ds(first * dim, heads * dim)], queries_ref, sem.at[0]
+        ),
+        pltpu.make_async_copy(key_weight_hbm.at[here], key_weight_ref, sem.at[1]),
+        pltpu.make_async_copy(prefix_hbm, keys_ref.at[pl.ds(0, past)], sem.at[2]),
+        pltpu.make_async_copy(fresh_hbm, keys_ref.at[pl.ds(past, slots)], sem.at[3]),
+        pltpu.make_async_copy(value_weight_hbm.at[here], value_weight_ref, sem.at[4]),
     ]
-    for_keys.append(
-        pltpu.make_async_copy(
-            fresh_hbm, keys_ref.at[pl.ds(past, slots)], sem.at[3 * steps + KEY_PARTS]
-        )
-    )
-    opening = copy_step(0)
-    for copy in opening[:2] + for_keys + opening[2:]:
+    for copy in copies:
         copy.start()
-    for i in range(1, steps):
-        for copy in copy_step(i):
-            copy.start()
-
     count, size = count_ref[0], size_ref[0]
     lane = lax.broadcasted_iota(jnp.int32, (slots, past), 1)
     cap_ref[:, :past] = jnp.where(lane < size, jnp.float32(OPEN), jnp.float32(MASKED))
@@ -115,41 +88,32 @@
         (col <= row) & (col < count * SPAN), jnp.float32(OPEN), jnp.float32(MASKED)
     )
     build_table(me_ref[0], count, routes_ref, table_ref, capacity, cores)
+    for copy in copies:
+        copy.wait()
 
     scale = math.log2(math.e) / math.sqrt(dim)
-    for copy in for_keys:
-        copy.wait()
-
-    def body(i, carry):
-        for copy in copy_step(i):
-            copy.wait()
-        keys = keys_ref[...]
-        scores = []
-        for stack in range(UNROLL):
-            lifted = []
-            for g in range(group):
-                h = i * step + stack * group + g
-                query = queries_ref[:, pl.ds(pl.multiple_of(h * dim, dim), dim)]
-                lifted.append(dot(query, key_weight_ref[h]).astype(jnp.bfloat16))
-            lifted = jnp.concatenate(lifted, axis=0)
-            scores.append(lax.dot_general(lifted, keys, NT, preferred_element_type=jnp.float32))
-        for stack in range(UNROLL):
-            score = scores[stack].reshape(group, slots, keys.shape[0])
-            score = jnp.minimum(score, cap_ref[...][None])
-            highest = jnp.max(score, axis=-1, keepdims=True) * scale
-            weights = jnp.exp2(score * scale - highest)
-            total = jnp.sum(weights, axis=-1, keepdims=True)
-            weights = weights.astype(jnp.bfloat16).reshape(group * slots, keys.shape[0])
-            mixed = dot(weights, keys).astype(jnp.bfloat16)
-            for g in range(group):
-                h = i * step + stack * group + g
-                projected = dot(mixed[g * slots : (g + 1) * slots], value_weight_ref[h])
-                attended_ref[:, pl.ds(pl.multiple_of(h * dim, dim), dim)] = (
-                    projected / total[g]
-                ).astype(jnp.bfloat16)
-        return carry
-
-    lax.fori_loop(0, steps, body, 0)
+    keys = keys_ref[...]
+    stacks = heads // STACK
+    scores = []
+    for stack in range(stacks):
+        lifted = []
+        for h in range(stack * STACK, (stack + 1) * STACK):
+            one = dot(queries_ref[:, h * dim : (h + 1) * dim], key_weight_ref[h])
+            lifted.append(one.astype(jnp.bfloat16))
+        lifted = jnp.concatenate(lifted, axis=0)
+        scores.append(lax.dot_general(lifted, keys, NT, preferred_element_type=jnp.float32))
+    for stack in range(stacks):
+        score = scores[stack].reshape(STACK, slots, keys.shape[0])
+        score = jnp.minimum(score, cap_ref[...][None])
+        highest = jnp.max(score, axis=-1, keepdims=True) * scale
+        weights = jnp.exp2(score * scale - highest)
+        total = jnp.sum(weights, axis=-1, keepdims=True)
+        weights = weights.astype(jnp.bfloat16).reshape(STACK * slots, keys.shape[0])
+        mixed = dot(weights, keys).astype(jnp.bfloat16)
+        for g in range(STACK):
+            h = stack * STACK + g
+            projected = dot(mixed[g * slots : (g + 1) * slots], value_weight_ref[h])
+            attended_ref[:, h * dim : (h + 1) * dim] = (projected / total[g]).astype(jnp.bfloat16)
     grouped = dot(table_ref[...], attended_ref[...]).astype(jnp.bfloat16)
     row = 0
     for out_ref in out_refs:
@@ -158,7 +122,6 @@
 
 
 def attend(
-    group,
     first,
     heads,
     me,
@@ -184,7 +147,7 @@
     hbm = pl.BlockSpec(memory_space=pltpu.HBM)
     pieces = [jax.ShapeDtypeStruct((rows, heads * dim), jnp.bfloat16) for rows in parts]
     return pl.pallas_call(
-        functools.partial(attend_kernel, places // experts, group, first, cores, len(after)),
+        functools.partial(attend_kernel, places // experts, first, cores, len(after)),
         in_specs=[smem, smem, smem, vmem] + [hbm] * 5 + [vmem] * len(after),
         out_specs=[vmem] * (len(pieces) + 1),
         out_shape=pieces + [jax.ShapeDtypeStruct(MARK, jnp.float32)],
@@ -196,7 +159,7 @@
             pltpu.VMEM((slots, keys), jnp.float32),
             pltpu.VMEM((places, slots), jnp.bfloat16),
             pltpu.VMEM((slots, heads * dim), jnp.bfloat16),
-            pltpu.SemaphoreType.DMA((3 * heads // (group * UNROLL) + KEY_PARTS + 1,)),
+            pltpu.SemaphoreType.DMA((5,)),
         ],
         compiler_params=pltpu.CompilerParams(vmem_limit_bytes=VMEM),
         cost_estimate=pl.CostEstimate(
@@ -247,9 +210,9 @@
     features //= cores
     me = me_ref[0]
     copies = []
-    for ref, row, start, bits in plan:
+    for ref, row, start, bits, apart in plan:
         ref = refs[ref]
-        who = me ^ bits
+        who = me ^ bits if apart else jnp.int32(bits)
         left = pl.multiple_of(who % cores * features + start, math.gcd(features, start))
         target = out_ref.at[0, who // cores, :, pl.ds(left, ref.shape[1])]
         copies.append(
@@ -276,7 +239,7 @@
 
 def exchange_order(ranks):
     near, far = list(range(1, ranks // 2)), list(range(ranks // 2, ranks))
-    return far[::2] + far[1::2] + near
+    return near[:-1] + far[::2] + far[1::2] + near[-1:]
 
 
 def local(
@@ -301,7 +264,6 @@
 
     def run(chunk, order, parts, cores, after):
         return attend(
-            GROUPS[chunk],
             sum(shares[:chunk]),
             shares[chunk],
             order,
@@ -340,17 +302,20 @@
     swapped = lax.ppermute(message, "ep", [(i, i ^ 1) for i in range(cores)])
     order = exchange_order(ranks)
     joined = dict(zip(range(1, ranks), join(kept[1:], swapped)))
-    arrays = [kept[0], swapped]
     middle = shares[0] * dim
-    plan = [(0, 0, middle, 0), (1, 0, middle, 1)]
+    soon, late = [first, kept[0], swapped], []
+    soon_plan = [(0, i * capacity, 0, i, False) for i in range(experts)]
+    soon_plan += [(1, 0, middle, 0, True), (2, 0, middle, 1, True)]
+    late_plan = []
     for j in order:
-        plan.append((len(arrays), 0, middle, j * cores))
-        plan.append((len(arrays), capacity, middle, j * cores + 1))
-        arrays.append(lax.ppermute(joined[j], "dp", [(i, i ^ j) for i in range(ranks)]))
+        piece = lax.ppermute(joined[j], "dp", [(i, i ^ j) for i in range(ranks)])
+        arrays, plan = (soon, soon_plan) if j < ranks // 2 else (late, late_plan)
+        plan.append((len(arrays), 0, middle, j * cores, True))
+        plan.append((len(arrays), capacity, middle, j * cores + 1, True))
+        arrays.append(piece)
     shape = (1, ranks, capacity, cores * heads * dim)
-    first_plan = [(0, i * capacity, 0, i) for i in range(experts)]
-    placed = place(nobody, [first], first_plan, cores, shape, [])
-    return place(me, arrays, plan, cores, shape, [placed])
+    placed = place(me, soon, soon_plan, cores, shape, [])
+    return place(me, late, late_plan, cores, shape, [placed])
 
 
 def solution(mesh):

time: 77.3 us -> 72.5 us (0.938)
  waiting for transfers between devices: 19.3 us -> 15.7 us
  starting transfers between devices: 21.2 us -> 20.1 us
  Pallas kernels: 32.6 us -> 31.7 us
    ppermute x7, waiting for transfers between devices: 17.5 us -> 14 us  [local(): piece = lax.ppermute(joined[j], 'dp', [(i, i ^ j) for i in range(ranks)])]
    ppermute x7, starting transfers between devices: 13.4 us -> 12.2 us  [local(): piece = lax.ppermute(joined[j], 'dp', [(i, i ^ j) for i in range(ranks)])]
    pallas_call x2, Pallas kernels: 25.6 us -> 24.6 us  [attend(): pl.pallas_call(functools.partial(attend_kernel, places // experts, first,...]
  transfers between devices with their start and end apart: 9 -> 9, of which waited for: 4 -> 5; matrix products, arithmetic and copies ran while one was open for 0% -> 0% of each run, Pallas kernels for 23% -> 24%
where the time goes in v13:
time: 72.5 us; the launch traced here: 72.1 us
  Pallas kernels  31.7 us (44%)
  starting transfers between devices  20.1 us (28%)
  waiting for transfers between devices  15.7 us (22%)
  local copies, waits for them, and re-layouts  3.11 us (4%)
  between operations  1.54 us (2%)
    pallas_call x2, Pallas kernels, attend(): pl.pallas_call(functools.partial(attend_kernel, places // experts, first,...  24.6 us
    ppermute x7, waiting for transfers between devices, local(): piece = lax.ppermute(joined[j], 'dp', [(i, i ^ j) for i in range(ranks)])  14 us
    ppermute x7, starting transfers between devices, local(): piece = lax.ppermute(joined[j], 'dp', [(i, i ^ j) for i in range(ranks)])  12.2 us
    all_to_all x1, starting transfers between devices, to_all(): lax.all_to_all(outgoing.reshape(experts, capacity, -1), ('dp', 'ep'), spl...  7.41 us
    pallas_call x2, Pallas kernels, place(): pl.pallas_call(functools.partial(place_kernel, plan, cores), in_specs=[pl...  4.79 us
    unnamed x18, local copies, waits for them, and re-layouts  3.11 us
    pallas_call x1, Pallas kernels, join(): pl.pallas_call(join_kernel, in_specs=[pl.BlockSpec(memory_space=pl.ANY)]...  2.24 us
    ppermute x1, waiting for transfers between devices, local(): swapped = lax.ppermute(message, 'ep', [(i, i ^ 1) for i in range(cores)])  1.75 us
  transfers between devices with their start and end apart: 9, of which 5 were waited for; matrix products, arithmetic and copies ran while one was open for 0% of the time, Pallas kernels for 24%

profile of v13, /device:TPU:0, one launch (start us, length us, event | category | flops | bytes accessed | tf_op | source)
XLA Modules:
  0.0 72.1 jit_solution(12592147329476837719)
XLA Ops:
  1.3 12.3 %shard_map.82 = (bf16[256,2048]{1,0:T(8,128)(2,1)}, f32[8,128]{1,0:T(8,128)}) custom-call(s32[1]{0:T(128)} %constant.11.clone.1.me_ref, s32[1]{0:T(128)S(6)} %copy.11.count_ref, s32[1]{0:T(128)S(6)} %copy.12.size_ref, s32[2,128]{1,0:T(2,128)} %bitcast.6, bf16[128,4096]{1,0:T(8,128)(2,1)} %queries_hbm.3, bf16[32,128,512]{2,1,0:T(8,128)(2,1)} %key_weight_hbm.3, ...), custom_call_target="tpu_custom_call" | custom-call | flops 4831838208 | bytes 4194304 | tf_op jit(solution)/shard_map/pallas_call | solution.py:149
  13.6 7.4 %all-to-all-start = ((bf16[16,16,2048]{2,1,0:T(8,128)(2,1)}), bf16[16,16,2048]{2,1,0:T(8,128)(2,1)S(1)}, u32[]{:S(2)}, u32[]{:S(2)}) async-start(bf16[16,16,2048]{2,1,0:T(8,128)(2,1)} %bitcast.5), calls=%async_computation | async-start | bytes 2097152 | tf_op jit(solution)/shard_map/all_to_all | solution.py:285
  21.1 12.3 %shard_map.83 = (bf16[16,2048]{1,0:T(8,128)(2,1)}, bf16[16,2048]{1,0:T(8,128)(2,1)}, bf16[16,2048]{1,0:T(8,128)(2,1)}, bf16[16,2048]{1,0:T(8,128)(2,1)}, bf16[16...) custom-call(s32[1]{0:T(128)} %bitcast.me_ref, ...), custom_call_target="tpu_custom_call" | custom-call | flops 4831838208 | bytes 4194304 | tf_op jit(solution)/shard_map/pallas_call | solution.py:149
  33.4 0.5 collective-permute-start
  33.8 1.7 %collective-permute-done.refs_7_.refs_2_ = bf16[128,2048]{1,0:T(8,128)(2,1)S(1)} collective-permute-done((bf16[128,2048]{1,0:T(8,128)(2,1)}, bf16[128,2048]{1,0:T(8,128)(2,1)S(1)}, u32[]{:S(2)}, u32[]{:S(2)}) %collective-permute-start) | collective-permute-done | bytes 524320 | tf_op jit(solution)/shard_map/ppermute | solution.py:302
  35.6 0.8 %copy-done.1 = bf16[128,2048]{1,0:T(8,128)(2,1)} copy-done((bf16[128,2048]{1,0:T(8,128)(2,1)}, bf16[128,2048]{1,0:T(8,128)(2,1)S(1)}, u32[]{:S(2)}) %copy-start.1) | copy-done | bytes 524312
  36.4 2.2 %shard_map.84 = (bf16[32,2048]{1,0:T(8,128)(2,1)}, bf16[32,2048]{1,0:T(8,128)(2,1)}, bf16[32,2048]{1,0:T(8,128)(2,1)}, bf16[32,2048]{1,0:T(8,128)(2,1)}, bf16[32...) custom-call(bf16[16,2048]{1,0:T(8,128)(2,1)} %get-tuple-element.24.refs_0_, ...), custom_call_target="tpu_custom_call" | custom-call | tf_op jit(solution)/shard_map/pallas_call | solution.py:196
  38.6 2.0 %collective-permute-start.5 = (bf16[32,2048]{1,0:T(8,128)(2,1)}, bf16[32,2048]{1,0:T(8,128)(2,1)S(1)}, u32[]{:S(2)}, u32[]{:S(2)}) collective-permute-start(bf16[32,2048]{1,0:T(8,128)(2,1)} %get-tuple-element.38), channel_id=1, source_target_pairs={{0,2},{2,0},{4,6},{6,4},{8,10},{10,8},{12,14},{14,12},{1,3},{3,1},... | collective-permute-start | bytes 393224 | tf_op jit(solution)/shard_map/ppermute | solution.py:311
  40.6 1.5 %collective-permute-start.6 = (bf16[32,2048]{1,0:T(8,128)(2,1)}, bf16[32,2048]{1,0:T(8,128)(2,1)S(1)}, u32[]{:S(2)}, u32[]{:S(2)}) collective-permute-start(bf16[32,2048]{1,0:T(8,128)(2,1)} %get-tuple-element.39), channel_id=1, source_target_pairs={{0,4},{2,6},{4,0},{6,2},{8,12},{10,14},{12,8},{14,10},{1,5},{3,7},... | collective-permute-start | bytes 393224 | tf_op jit(solution)/shard_map/ppermute | solution.py:311
  42.0 2.4 %collective-permute-start.1 = (bf16[32,2048]{1,0:T(8,128)(2,1)}, bf16[32,2048]{1,0:T(8,128)(2,1)S(1)}, u32[]{:S(2)}, u32[]{:S(2)}) collective-permute-start(bf16[32,2048]{1,0:T(8,128)(2,1)} %get-tuple-element.32), channel_id=1, source_target_pairs={{0,8},{2,10},{4,12},{6,14},{8,0},{10,2},{12,4},{14,6},{1,9},{3,11}... | collective-permute-start | bytes 393224 | tf_op jit(solution)/shard_map/ppermute | solution.py:311
  44.4 0.6 collective-permute-start.7
  45.0 1.5 %collective-permute-start.2 = (bf16[32,2048]{1,0:T(8,128)(2,1)}, bf16[32,2048]{1,0:T(8,128)(2,1)S(1)}, u32[]{:S(2)}, u32[]{:S(2)}) collective-permute-start(bf16[32,2048]{1,0:T(8,128)(2,1)} %get-tuple-element.33), channel_id=1, source_target_pairs={{0,12},{2,14},{4,8},{6,10},{8,4},{10,6},{12,0},{14,2},{1,13},{3,15... | collective-permute-start | bytes 393224 | tf_op jit(solution)/shard_map/ppermute | solution.py:311
  46.4 0.6 collective-permute-done.5.refs_3_
  47.1 2.0 %collective-permute-start.3 = (bf16[32,2048]{1,0:T(8,128)(2,1)}, bf16[32,2048]{1,0:T(8,128)(2,1)S(1)}, u32[]{:S(2)}, u32[]{:S(2)}) collective-permute-start(bf16[32,2048]{1,0:T(8,128)(2,1)} %get-tuple-element.34), channel_id=1, source_target_pairs={{0,10},{2,8},{4,14},{6,12},{8,2},{10,0},{12,6},{14,4},{1,11},{3,9}... | collective-permute-start | bytes 393224 | tf_op jit(solution)/shard_map/ppermute | solution.py:311
  49.0 0.0 collective-permute-done.6.refs_4_
  49.1 2.4 %collective-permute-start.4 = (bf16[32,2048]{1,0:T(8,128)(2,1)}, bf16[32,2048]{1,0:T(8,128)(2,1)S(1)}, u32[]{:S(2)}, u32[]{:S(2)}) collective-permute-start(bf16[32,2048]{1,0:T(8,128)(2,1)} %get-tuple-element.35), channel_id=1, source_target_pairs={{0,14},{2,12},{4,10},{6,8},{8,6},{10,4},{12,2},{14,0},{1,15},{3,13... | collective-permute-start | bytes 393224 | tf_op jit(solution)/shard_map/ppermute | solution.py:311
  51.4 0.3 collective-permute-done.7.refs_5_
  51.8 0.0 all-to-all-done
  51.8 0.0 copy-done.4
  51.8 0.0 copy-done.6
  51.8 0.6 copy-done.8
  52.4 0.4 copy-done
  52.8 2.8 %shard_map.85.refs_4_ = bf16[1,8,16,8192]{3,2,1,0:T(8,128)(2,1)} custom-call(s32[1]{0:T(128)} %bitcast.me_ref, bf16[256,2048]{1,0:T(8,128)(2,1)} %bitcast.4, bf16[16,2048]{1,0:T(8,128)(2,1)} %get-tuple-element.37.refs_1_, bf16[128,2048]{1,0:T(8,128)(2,1)} %copy-done.1, bf16[32,2048]{1,0:T(8,128)(2,1)} %copy-done.4, bf16[32,2048]{1,0:T(8,128)(2,1)} %copy-done.6, ...), custom_call_target="tpu_custom_call" | custom-call | tf_op jit(solution)/shard_map/pallas_call | solution.py:227
  55.7 6.4 %collective-permute-done.1.refs_0_ = bf16[32,2048]{1,0:T(8,128)(2,1)S(1)} collective-permute-done((bf16[32,2048]{1,0:T(8,128)(2,1)}, bf16[32,2048]{1,0:T(8,128)(2,1)S(1)}, u32[]{:S(2)}, u32[]{:S(2)}) %collective-permute-start.1) | collective-permute-done | bytes 131104 | tf_op jit(solution)/shard_map/ppermute | solution.py:311
  62.1 0.0 collective-permute-done.2.refs_1_
  62.1 6.6 %collective-permute-done.3.refs_2_ = bf16[32,2048]{1,0:T(8,128)(2,1)S(1)} collective-permute-done((bf16[32,2048]{1,0:T(8,128)(2,1)}, bf16[32,2048]{1,0:T(8,128)(2,1)S(1)}, u32[]{:S(2)}, u32[]{:S(2)}) %collective-permute-start.3) | collective-permute-done | bytes 131104 | tf_op jit(solution)/shard_map/ppermute | solution.py:311
  68.7 0.0 collective-permute-done.4.refs_3_
  68.7 0.0 copy-done.2
  68.7 0.0 copy-done.3
  68.7 0.6 copy-done.5
  69.3 0.6 copy-done.7
  70.0 1.9 %shard_map.86 = bf16[1,8,16,8192]{3,2,1,0:T(8,128)(2,1)} custom-call(s32[1]{0:T(128)} %bitcast.me_ref, bf16[32,2048]{1,0:T(8,128)(2,1)} %copy-done.2, bf16[32,2048]{1,0:T(8,128)(2,1)} %copy-done.3, bf16[32,2048]{1,0:T(8,128)(2,1)} %copy-done.5, bf16[32,2048]{1,0:T(8,128)(2,1)} %copy-done.7, ...), custom_call_target="tpu_custom_call", output_to_operand_aliasing={{}: (5, {})} | custom-call | tf_op jit(solution)/shard_map/pallas_call | solution.py:227
  (9 shorter events, 0.0 us)
Async XLA Ops:
  13.6 38.1 %all-to-all-start = ((bf16[16,16,2048]{2,1,0:T(8,128)(2,1)}), bf16[16,16,2048]{2,1,0:T(8,128)(2,1)S(1)}, u32[]{:S(2)}, u32[]{:S(2)}) async-start(bf16[16,16,2048]{2,1,0:T(8,128)(2,1)} %bitcast.5), calls=%async_computation | async-start | bytes 2097152 | tf_op jit(solution)/shard_map/all_to_all | solution.py:285
  33.4 2.2 %collective-permute-start = (bf16[128,2048]{1,0:T(8,128)(2,1)}, bf16[128,2048]{1,0:T(8,128)(2,1)S(1)}, u32[]{:S(2)}, u32[]{:S(2)}) collective-permute-start(bf16[128,2048]{1,0:T(8,128)(2,1)} %get-tuple-element.31), channel_id=1, source_target_pairs={{0,1},{1,0},{2,3},{3,2},{4,5},{5,4},{6,7},{7,6},{8,9},{9,8},{10,11... | collective-permute-start | bytes 1572872 | tf_op jit(solution)/shard_map/ppermute | solution.py:302
  35.6 0.8 %copy-start.1 = (bf16[128,2048]{1,0:T(8,128)(2,1)}, bf16[128,2048]{1,0:T(8,128)(2,1)S(1)}, u32[]{:S(2)}) copy-start(bf16[128,2048]{1,0:T(8,128)(2,1)S(1)} %collective-permute-done.refs_7_.refs_2_) | copy-start | bytes 1572868
  38.6 8.4 %collective-permute-start.5 = (bf16[32,2048]{1,0:T(8,128)(2,1)}, bf16[32,2048]{1,0:T(8,128)(2,1)S(1)}, u32[]{:S(2)}, u32[]{:S(2)}) collective-permute-start(bf16[32,2048]{1,0:T(8,128)(2,1)} %get-tuple-element.38), channel_id=1, source_target_pairs={{0,2},{2,0},{4,6},{6,4},{8,10},{10,8},{12,14},{14,12},{1,3},{3,1},... | collective-permute-start | bytes 393224 | tf_op jit(solution)/shard_map/ppermute | solution.py:311
  40.6 8.5 %collective-permute-start.6 = (bf16[32,2048]{1,0:T(8,128)(2,1)}, bf16[32,2048]{1,0:T(8,128)(2,1)S(1)}, u32[]{:S(2)}, u32[]{:S(2)}) collective-permute-start(bf16[32,2048]{1,0:T(8,128)(2,1)} %get-tuple-element.39), channel_id=1, source_target_pairs={{0,4},{2,6},{4,0},{6,2},{8,12},{10,14},{12,8},{14,10},{1,5},{3,7},... | collective-permute-start | bytes 393224 | tf_op jit(solution)/shard_map/ppermute | solution.py:311
  42.0 20.1 %collective-permute-start.1 = (bf16[32,2048]{1,0:T(8,128)(2,1)}, bf16[32,2048]{1,0:T(8,128)(2,1)S(1)}, u32[]{:S(2)}, u32[]{:S(2)}) collective-permute-start(bf16[32,2048]{1,0:T(8,128)(2,1)} %get-tuple-element.32), channel_id=1, source_target_pairs={{0,8},{2,10},{4,12},{6,14},{8,0},{10,2},{12,4},{14,6},{1,9},{3,11}... | collective-permute-start | bytes 393224 | tf_op jit(solution)/shard_map/ppermute | solution.py:311
  44.4 7.4 %collective-permute-start.7 = (bf16[32,2048]{1,0:T(8,128)(2,1)}, bf16[32,2048]{1,0:T(8,128)(2,1)S(1)}, u32[]{:S(2)}, u32[]{:S(2)}) collective-permute-start(bf16[32,2048]{1,0:T(8,128)(2,1)} %get-tuple-element.40), channel_id=1, source_target_pairs={{0,6},{2,4},{4,2},{6,0},{8,14},{10,12},{12,10},{14,8},{1,7},{3,5},... | collective-permute-start | bytes 393224 | tf_op jit(solution)/shard_map/ppermute | solution.py:311
  45.0 17.1 %collective-permute-start.2 = (bf16[32,2048]{1,0:T(8,128)(2,1)}, bf16[32,2048]{1,0:T(8,128)(2,1)S(1)}, u32[]{:S(2)}, u32[]{:S(2)}) collective-permute-start(bf16[32,2048]{1,0:T(8,128)(2,1)} %get-tuple-element.33), channel_id=1, source_target_pairs={{0,12},{2,14},{4,8},{6,10},{8,4},{10,6},{12,0},{14,2},{1,13},{3,15... | collective-permute-start | bytes 393224 | tf_op jit(solution)/shard_map/ppermute | solution.py:311
  47.1 4.7 %copy-start.4 = (bf16[32,2048]{1,0:T(8,128)(2,1)}, bf16[32,2048]{1,0:T(8,128)(2,1)S(1)}, u32[]{:S(2)}) copy-start(bf16[32,2048]{1,0:T(8,128)(2,1)S(1)} %collective-permute-done.5.refs_3_) | copy-start | bytes 393220
  47.1 21.6 %collective-permute-start.3 = (bf16[32,2048]{1,0:T(8,128)(2,1)}, bf16[32,2048]{1,0:T(8,128)(2,1)S(1)}, u32[]{:S(2)}, u32[]{:S(2)}) collective-permute-start(bf16[32,2048]{1,0:T(8,128)(2,1)} %get-tuple-element.34), channel_id=1, source_target_pairs={{0,10},{2,8},{4,14},{6,12},{8,2},{10,0},{12,6},{14,4},{1,11},{3,9}... | collective-permute-start | bytes 393224 | tf_op jit(solution)/shard_map/ppermute | solution.py:311
  49.0 2.7 %copy-start.6 = (bf16[32,2048]{1,0:T(8,128)(2,1)}, bf16[32,2048]{1,0:T(8,128)(2,1)S(1)}, u32[]{:S(2)}) copy-start(bf16[32,2048]{1,0:T(8,128)(2,1)S(1)} %collective-permute-done.6.refs_4_) | copy-start | bytes 393220
  49.1 19.6 %collective-permute-start.4 = (bf16[32,2048]{1,0:T(8,128)(2,1)}, bf16[32,2048]{1,0:T(8,128)(2,1)S(1)}, u32[]{:S(2)}, u32[]{:S(2)}) collective-permute-start(bf16[32,2048]{1,0:T(8,128)(2,1)} %get-tuple-element.35), channel_id=1, source_target_pairs={{0,14},{2,12},{4,10},{6,8},{8,6},{10,4},{12,2},{14,0},{1,15},{3,13... | collective-permute-start | bytes 393224 | tf_op jit(solution)/shard_map/ppermute | solution.py:311
  51.8 0.6 copy-start.8
  51.8 1.0 %copy-start = (bf16[16,16,2048]{2,1,0:T(8,128)(2,1)}, bf16[16,16,2048]{2,1,0:T(8,128)(2,1)S(1)}, u32[]{:S(2)}) copy-start(bf16[16,16,2048]{2,1,0:T(8,128)(2,1)S(1)} %all-to-all-done) | copy-start | bytes 3145732
  62.1 6.6 %copy-start.2 = (bf16[32,2048]{1,0:T(8,128)(2,1)}, bf16[32,2048]{1,0:T(8,128)(2,1)S(1)}, u32[]{:S(2)}) copy-start(bf16[32,2048]{1,0:T(8,128)(2,1)S(1)} %collective-permute-done.1.refs_0_) | copy-start | bytes 393220
  62.1 6.6 %copy-start.3 = (bf16[32,2048]{1,0:T(8,128)(2,1)}, bf16[32,2048]{1,0:T(8,128)(2,1)S(1)}, u32[]{:S(2)}) copy-start(bf16[32,2048]{1,0:T(8,128)(2,1)S(1)} %collective-permute-done.2.refs_1_) | copy-start | bytes 393220
  68.7 0.6 copy-start.5
  69.3 0.6 copy-start.7

commit v14 on v13

--- a/solution.py
+++ b/solution.py
@@ -12,7 +12,8 @@
 STACK = 4
 CHUNKS = (1, 1)
 DIRECT = 16
-VMEM = 60 * 1024 * 1024
+ALL_VMEM = 60 * 1024 * 1024
+VMEM = 52 * 1024 * 1024
 SHORT = pl.CostEstimate(flops=0, bytes_accessed=0, transcendentals=0)
 MARK = (8, 128)
 MASKED = -1e30
@@ -148,7 +149,7 @@
     pieces = [jax.ShapeDtypeStruct((rows, heads * dim), jnp.bfloat16) for rows in parts]
     return pl.pallas_call(
         functools.partial(attend_kernel, places // experts, first, cores, len(after)),
-        in_specs=[smem, smem, smem, vmem] + [hbm] * 5 + [vmem] * len(after),
+        in_specs=[smem, smem, smem, vmem] + [hbm] * (5 + len(after)),
         out_specs=[vmem] * (len(pieces) + 1),
         out_shape=pieces + [jax.ShapeDtypeStruct(MARK, jnp.float32)],
         scratch_shapes=[
@@ -161,7 +162,7 @@
             pltpu.VMEM((slots, heads * dim), jnp.bfloat16),
             pltpu.SemaphoreType.DMA((5,)),
         ],
-        compiler_params=pltpu.CompilerParams(vmem_limit_bytes=VMEM),
+        compiler_params=pltpu.CompilerParams(vmem_limit_bytes=VMEM if first else ALL_VMEM),
         cost_estimate=pl.CostEstimate(
             flops=4 * slots * heads * keys * latent,
             bytes_accessed=4 * heads * dim * latent,

time: 72.5 us -> 70.1 us (0.967)
  Pallas kernels: 31.7 us -> 27.7 us
  waiting for transfers between devices: 15.7 us -> 17.8 us
  local copies, waits for them, and re-layouts: 3.11 us -> 1.66 us
  starting transfers between devices: 20.1 us -> 21 us
    ppermute x7, waiting for transfers between devices: 14 us -> 16.3 us  [local(): piece = lax.ppermute(joined[j], 'dp', [(i, i ^ j) for i in range(ranks)])]
    pallas_call x2, Pallas kernels: 24.6 us -> 23 us  [attend(): pl.pallas_call(functools.partial(attend_kernel, places // experts, first,...]
    unnamed x18 -> x8, local copies, waits for them, and re-layouts: 3.11 us -> 1.66 us
    pallas_call x2, Pallas kernels: 4.79 us -> 3.4 us  [place(): pl.pallas_call(functools.partial(place_kernel, plan, cores), in_specs=[pl...]
    pallas_call x1, Pallas kernels: 2.24 us -> 1.29 us  [join(): pl.pallas_call(join_kernel, in_specs=[pl.BlockSpec(memory_space=pl.ANY)]...]
    ppermute x7, starting transfers between devices: 12.2 us -> 13.1 us  [local(): piece = lax.ppermute(joined[j], 'dp', [(i, i ^ j) for i in range(ranks)])]
  transfers between devices with their start and end apart: 9 -> 9, of which waited for: 5 -> 4; matrix products, arithmetic and copies ran while one was open for 0% -> 0% of each run, Pallas kernels for 24% -> 21%
where the time goes in v14:
time: 70.1 us; the launch traced here: 69.8 us
  Pallas kernels  27.7 us (40%)
  starting transfers between devices  21 us (30%)
  waiting for transfers between devices  17.8 us (25%)
  local copies, waits for them, and re-layouts  1.66 us (2%)
  between operations  1.55 us (2%)
    pallas_call x2, Pallas kernels, attend(): pl.pallas_call(functools.partial(attend_kernel, places // experts, first,...  23 us
    ppermute x7, waiting for transfers between devices, local(): piece = lax.ppermute(joined[j], 'dp', [(i, i ^ j) for i in range(ranks)])  16.3 us
    ppermute x7, starting transfers between devices, local(): piece = lax.ppermute(joined[j], 'dp', [(i, i ^ j) for i in range(ranks)])  13.1 us
    all_to_all x1, starting transfers between devices, to_all(): lax.all_to_all(outgoing.reshape(experts, capacity, -1), ('dp', 'ep'), spl...  7.4 us
    pallas_call x2, Pallas kernels, place(): pl.pallas_call(functools.partial(place_kernel, plan, cores), in_specs=[pl...  3.4 us
    unnamed x8, local copies, waits for them, and re-layouts  1.66 us
    ppermute x1, waiting for transfers between devices, local(): swapped = lax.ppermute(message, 'ep', [(i, i ^ 1) for i in range(cores)])  1.54 us
  transfers between devices with their start and end apart: 9, of which 4 were waited for; matrix products, arithmetic and copies ran while one was open for 0% of the time, Pallas kernels for 21%

profile of v14, /device:TPU:0, one launch (start us, length us, event | category | flops | bytes accessed | tf_op | source)
XLA Modules:
  0.0 69.8 jit_solution(10911527399742184419)
XLA Ops:
  1.3 0.0 copy-start
  1.3 0.0 copy-start.1
  1.3 12.4 %shard_map.82 = (bf16[256,2048]{1,0:T(8,128)(2,1)}, f32[8,128]{1,0:T(8,128)}) custom-call(s32[1]{0:T(128)} %constant.11.clone.1.me_ref, s32[1]{0:T(128)S(6)} %copy.11.count_ref, s32[1]{0:T(128)S(6)} %copy.12.size_ref, s32[2,128]{1,0:T(2,128)} %bitcast.4, bf16[128,4096]{1,0:T(8,128)(2,1)} %queries_hbm.3, bf16[32,128,512]{2,1,0:T(8,128)(2,1)} %key_weight_hbm.3, ...), custom_call_target="tpu_custom_call" | custom-call | flops 4831838208 | bytes 4194304 | tf_op jit(solution)/shard_map/pallas_call | solution.py:150
  13.7 7.4 %all-to-all-start = ((bf16[16,16,2048]{2,1,0:T(8,128)(2,1)}), bf16[16,16,2048]{2,1,0:T(8,128)(2,1)S(1)}, u32[]{:S(2)}, u32[]{:S(2)}) async-start(bf16[16,16,2048]{2,1,0:T(8,128)(2,1)} %bitcast.7), calls=%async_computation | async-start | bytes 2097152 | tf_op jit(solution)/shard_map/all_to_all | solution.py:286
  21.1 0.0 copy-done
  21.1 0.0 copy-done.1
  21.1 0.0 copy-start.2
  21.2 0.7 copy-done.2
  21.8 10.7 %shard_map.83 = (bf16[16,2048]{1,0:T(8,128)(2,1)S(1)}, bf16[16,2048]{1,0:T(8,128)(2,1)S(1)}, bf16[16,2048]{1,0:T(8,128)(2,1)S(1)}, bf16[16,2048]{1,0:T(8,128)(2,...) custom-call(s32[1]{0:T(128)} %bitcast.me_ref, ...), custom_call_target="tpu_custom_call" | custom-call | flops 4831838208 | bytes 4194304 | tf_op jit(solution)/shard_map/pallas_call | solution.py:150
  32.5 0.5 collective-permute-start
  32.9 1.5 %collective-permute-done.refs_7_.refs_2_ = bf16[128,2048]{1,0:T(8,128)(2,1)S(1)} collective-permute-done((bf16[128,2048]{1,0:T(8,128)(2,1)S(1)}, bf16[128,2048]{1,0:T(8,128)(2,1)S(1)}, u32[]{:S(2)}, u32[]{:S(2)}) %collective-permute-start) | collective-permute-done | bytes 524320 | tf_op jit(solution)/shard_map/ppermute | solution.py:303
  34.5 1.3 %shard_map.84 = (bf16[32,2048]{1,0:T(8,128)(2,1)S(1)}, bf16[32,2048]{1,0:T(8,128)(2,1)S(1)}, bf16[32,2048]{1,0:T(8,128)(2,1)S(1)}, bf16[32,2048]{1,0:T(8,128)(2,...) custom-call(bf16[16,2048]{1,0:T(8,128)(2,1)S(1)} %get-tuple-element.24.refs_0_, ...), custom_call_target="tpu_custom_call" | custom-call | tf_op jit(solution)/shard_map/pallas_call | solution.py:197
  35.8 1.9 %collective-permute-start.5 = (bf16[32,2048]{1,0:T(8,128)(2,1)S(1)}, bf16[32,2048]{1,0:T(8,128)(2,1)S(1)}, u32[]{:S(2)}, u32[]{:S(2)}) collective-permute-start(bf16[32,2048]{1,0:T(8,128)(2,1)S(1)} %get-tuple-element.38), channel_id=1, source_target_pairs={{0,2},{2,0},{4,6},{6,4},{8,10},{10,8},{12,14},{14,12},{1,3},{3,1},... | collective-permute-start | bytes 393224 | tf_op jit(solution)/shard_map/ppermute | solution.py:312
  37.7 1.5 %collective-permute-start.6 = (bf16[32,2048]{1,0:T(8,128)(2,1)S(1)}, bf16[32,2048]{1,0:T(8,128)(2,1)S(1)}, u32[]{:S(2)}, u32[]{:S(2)}) collective-permute-start(bf16[32,2048]{1,0:T(8,128)(2,1)S(1)} %get-tuple-element.39), channel_id=1, source_target_pairs={{0,4},{2,6},{4,0},{6,2},{8,12},{10,14},{12,8},{14,10},{1,5},{3,7},... | collective-permute-start | bytes 393224 | tf_op jit(solution)/shard_map/ppermute | solution.py:312
  39.2 2.4 %collective-permute-start.1 = (bf16[32,2048]{1,0:T(8,128)(2,1)S(1)}, bf16[32,2048]{1,0:T(8,128)(2,1)S(1)}, u32[]{:S(2)}, u32[]{:S(2)}) collective-permute-start(bf16[32,2048]{1,0:T(8,128)(2,1)S(1)} %get-tuple-element.32), channel_id=1, source_target_pairs={{0,8},{2,10},{4,12},{6,14},{8,0},{10,2},{12,4},{14,6},{1,9},{3,11}... | collective-permute-start | bytes 393224 | tf_op jit(solution)/shard_map/ppermute | solution.py:312
  41.6 0.6 collective-permute-start.7
  42.1 1.4 %collective-permute-start.2 = (bf16[32,2048]{1,0:T(8,128)(2,1)S(1)}, bf16[32,2048]{1,0:T(8,128)(2,1)S(1)}, u32[]{:S(2)}, u32[]{:S(2)}) collective-permute-start(bf16[32,2048]{1,0:T(8,128)(2,1)S(1)} %get-tuple-element.33), channel_id=1, source_target_pairs={{0,12},{2,14},{4,8},{6,10},{8,4},{10,6},{12,0},{14,2},{1,13},{3,15... | collective-permute-start | bytes 393224 | tf_op jit(solution)/shard_map/ppermute | solution.py:312
  43.6 0.0 collective-permute-done.5.refs_3_
  43.6 4.1 %collective-permute-start.3 = (bf16[32,2048]{1,0:T(8,128)(2,1)S(1)}, bf16[32,2048]{1,0:T(8,128)(2,1)S(1)}, u32[]{:S(2)}, u32[]{:S(2)}) collective-permute-start(bf16[32,2048]{1,0:T(8,128)(2,1)S(1)} %get-tuple-element.34), channel_id=1, source_target_pairs={{0,10},{2,8},{4,14},{6,12},{8,2},{10,0},{12,6},{14,4},{1,11},{3,9}... | collective-permute-start | bytes 393224 | tf_op jit(solution)/shard_map/ppermute | solution.py:312
  47.6 0.0 collective-permute-done.6.refs_4_
  47.6 1.3 %collective-permute-start.4 = (bf16[32,2048]{1,0:T(8,128)(2,1)S(1)}, bf16[32,2048]{1,0:T(8,128)(2,1)S(1)}, u32[]{:S(2)}, u32[]{:S(2)}) collective-permute-start(bf16[32,2048]{1,0:T(8,128)(2,1)S(1)} %get-tuple-element.35), channel_id=1, source_target_pairs={{0,14},{2,12},{4,10},{6,8},{8,6},{10,4},{12,2},{14,0},{1,15},{3,13... | collective-permute-start | bytes 393224 | tf_op jit(solution)/shard_map/ppermute | solution.py:312
  48.9 0.9 %collective-permute-done.7.refs_5_ = bf16[32,2048]{1,0:T(8,128)(2,1)S(1)} collective-permute-done((bf16[32,2048]{1,0:T(8,128)(2,1)S(1)}, bf16[32,2048]{1,0:T(8,128)(2,1)S(1)}, u32[]{:S(2)}, u32[]{:S(2)}) %collective-permute-start.7) | collective-permute-done | bytes 131104 | tf_op jit(solution)/shard_map/ppermute | solution.py:312
  49.8 0.0 all-to-all-done
  49.8 0.0 copy-start.3
  49.8 1.0 %copy-done.3 = bf16[16,16,2048]{2,1,0:T(8,128)(2,1)} copy-done((bf16[16,16,2048]{2,1,0:T(8,128)(2,1)}, bf16[16,16,2048]{2,1,0:T(8,128)(2,1)S(1)}, u32[]{:S(2)}) %copy-start.3) | copy-done | bytes 1048600
  50.8 2.6 %shard_map.85.refs_4_ = bf16[1,8,16,8192]{3,2,1,0:T(8,128)(2,1)} custom-call(s32[1]{0:T(128)} %bitcast.me_ref, bf16[256,2048]{1,0:T(8,128)(2,1)} %bitcast.6, bf16[16,2048]{1,0:T(8,128)(2,1)S(1)} %get-tuple-element.37.refs_1_, bf16[128,2048]{1,0:T(8,128)(2,1)S(1)} %collective-permute-done.refs_7_.refs_2_, ...), custom_call_target="tpu_custom_call" | custom-call | tf_op jit(solution)/shard_map/pallas_call | solution.py:228
  53.4 8.8 %collective-permute-done.1.refs_0_ = bf16[32,2048]{1,0:T(8,128)(2,1)S(1)} collective-permute-done((bf16[32,2048]{1,0:T(8,128)(2,1)S(1)}, bf16[32,2048]{1,0:T(8,128)(2,1)S(1)}, u32[]{:S(2)}, u32[]{:S(2)}) %collective-permute-start.1) | collective-permute-done | bytes 131104 | tf_op jit(solution)/shard_map/ppermute | solution.py:312
  62.2 0.0 collective-permute-done.2.refs_1_
  62.2 6.5 %collective-permute-done.3.refs_2_ = bf16[32,2048]{1,0:T(8,128)(2,1)S(1)} collective-permute-done((bf16[32,2048]{1,0:T(8,128)(2,1)S(1)}, bf16[32,2048]{1,0:T(8,128)(2,1)S(1)}, u32[]{:S(2)}, u32[]{:S(2)}) %collective-permute-start.3) | collective-permute-done | bytes 131104 | tf_op jit(solution)/shard_map/ppermute | solution.py:312
  68.8 0.0 collective-permute-done.4.refs_3_
  68.8 0.8 %shard_map.86 = bf16[1,8,16,8192]{3,2,1,0:T(8,128)(2,1)} custom-call(s32[1]{0:T(128)} %bitcast.me_ref, bf16[32,2048]{1,0:T(8,128)(2,1)S(1)} %collective-permute-done.1.refs_0_, bf16[32,2048]{1,0:T(8,128)(2,1)S(1)} %collective-permute-done.2.refs_1_, bf16[32,2048]{1,0:T(8,128)(2,1)S(1)} %collective-permute-done.3.refs_2_, ...), custom_call_target="tpu_custom_call", output_to_operand_aliasing={{}: (5, {})} | custom-call | tf_op jit(solution)/shard_map/pallas_call | solution.py:228
Async XLA Ops:
  1.3 19.8 %copy-start = (bf16[128,512]{1,0:T(8,128)(2,1)S(1)}, bf16[128,512]{1,0:T(8,128)(2,1)}, u32[]{:S(2)}) copy-start(bf16[128,512]{1,0:T(8,128)(2,1)} %fresh_hbm.3) | copy-start | bytes 393220
  1.3 19.8 %copy-start.1 = (s32[128,2]{0,1:T(2,128)S(1)}, s32[128,2]{0,1:T(2,128)}, u32[]{:S(2)}) copy-start(s32[128,2]{0,1:T(2,128)} %param.15) | copy-start | bytes 3076
  13.7 36.1 %all-to-all-start = ((bf16[16,16,2048]{2,1,0:T(8,128)(2,1)}), bf16[16,16,2048]{2,1,0:T(8,128)(2,1)S(1)}, u32[]{:S(2)}, u32[]{:S(2)}) async-start(bf16[16,16,2048]{2,1,0:T(8,128)(2,1)} %bitcast.7), calls=%async_computation | async-start | bytes 2097152 | tf_op jit(solution)/shard_map/all_to_all | solution.py:286
  21.1 0.7 copy-start.2
  32.5 2.0 %collective-permute-start = (bf16[128,2048]{1,0:T(8,128)(2,1)S(1)}, bf16[128,2048]{1,0:T(8,128)(2,1)S(1)}, u32[]{:S(2)}, u32[]{:S(2)}) collective-permute-start(bf16[128,2048]{1,0:T(8,128)(2,1)S(1)} %get-tuple-element.31), channel_id=1, source_target_pairs={{0,1},{1,0},{2,3},{3,2},{4,5},{5,4},{6,7},{7,6},{8,9},{9,8},{10,11... | collective-permute-start | bytes 1572872 | tf_op jit(solution)/shard_map/ppermute | solution.py:303
  35.8 7.8 %collective-permute-start.5 = (bf16[32,2048]{1,0:T(8,128)(2,1)S(1)}, bf16[32,2048]{1,0:T(8,128)(2,1)S(1)}, u32[]{:S(2)}, u32[]{:S(2)}) collective-permute-start(bf16[32,2048]{1,0:T(8,128)(2,1)S(1)} %get-tuple-element.38), channel_id=1, source_target_pairs={{0,2},{2,0},{4,6},{6,4},{8,10},{10,8},{12,14},{14,12},{1,3},{3,1},... | collective-permute-start | bytes 393224 | tf_op jit(solution)/shard_map/ppermute | solution.py:312
  37.7 9.9 %collective-permute-start.6 = (bf16[32,2048]{1,0:T(8,128)(2,1)S(1)}, bf16[32,2048]{1,0:T(8,128)(2,1)S(1)}, u32[]{:S(2)}, u32[]{:S(2)}) collective-permute-start(bf16[32,2048]{1,0:T(8,128)(2,1)S(1)} %get-tuple-element.39), channel_id=1, source_target_pairs={{0,4},{2,6},{4,0},{6,2},{8,12},{10,14},{12,8},{14,10},{1,5},{3,7},... | collective-permute-start | bytes 393224 | tf_op jit(solution)/shard_map/ppermute | solution.py:312
  39.2 23.0 %collective-permute-start.1 = (bf16[32,2048]{1,0:T(8,128)(2,1)S(1)}, bf16[32,2048]{1,0:T(8,128)(2,1)S(1)}, u32[]{:S(2)}, u32[]{:S(2)}) collective-permute-start(bf16[32,2048]{1,0:T(8,128)(2,1)S(1)} %get-tuple-element.32), channel_id=1, source_target_pairs={{0,8},{2,10},{4,12},{6,14},{8,0},{10,2},{12,4},{14,6},{1,9},{3,11}... | collective-permute-start | bytes 393224 | tf_op jit(solution)/shard_map/ppermute | solution.py:312
  41.6 8.3 %collective-permute-start.7 = (bf16[32,2048]{1,0:T(8,128)(2,1)S(1)}, bf16[32,2048]{1,0:T(8,128)(2,1)S(1)}, u32[]{:S(2)}, u32[]{:S(2)}) collective-permute-start(bf16[32,2048]{1,0:T(8,128)(2,1)S(1)} %get-tuple-element.40), channel_id=1, source_target_pairs={{0,6},{2,4},{4,2},{6,0},{8,14},{10,12},{12,10},{14,8},{1,7},{3,5},... | collective-permute-start | bytes 393224 | tf_op jit(solution)/shard_map/ppermute | solution.py:312
  42.1 20.1 %collective-permute-start.2 = (bf16[32,2048]{1,0:T(8,128)(2,1)S(1)}, bf16[32,2048]{1,0:T(8,128)(2,1)S(1)}, u32[]{:S(2)}, u32[]{:S(2)}) collective-permute-start(bf16[32,2048]{1,0:T(8,128)(2,1)S(1)} %get-tuple-element.33), channel_id=1, source_target_pairs={{0,12},{2,14},{4,8},{6,10},{8,4},{10,6},{12,0},{14,2},{1,13},{3,15... | collective-permute-start | bytes 393224 | tf_op jit(solution)/shard_map/ppermute | solution.py:312
  43.6 25.2 %collective-permute-start.3 = (bf16[32,2048]{1,0:T(8,128)(2,1)S(1)}, bf16[32,2048]{1,0:T(8,128)(2,1)S(1)}, u32[]{:S(2)}, u32[]{:S(2)}) collective-permute-start(bf16[32,2048]{1,0:T(8,128)(2,1)S(1)} %get-tuple-element.34), channel_id=1, source_target_pairs={{0,10},{2,8},{4,14},{6,12},{8,2},{10,0},{12,6},{14,4},{1,11},{3,9}... | collective-permute-start | bytes 393224 | tf_op jit(solution)/shard_map/ppermute | solution.py:312
  47.6 21.1 %collective-permute-start.4 = (bf16[32,2048]{1,0:T(8,128)(2,1)S(1)}, bf16[32,2048]{1,0:T(8,128)(2,1)S(1)}, u32[]{:S(2)}, u32[]{:S(2)}) collective-permute-start(bf16[32,2048]{1,0:T(8,128)(2,1)S(1)} %get-tuple-element.35), channel_id=1, source_target_pairs={{0,14},{2,12},{4,10},{6,8},{8,6},{10,4},{12,2},{14,0},{1,15},{3,13... | collective-permute-start | bytes 393224 | tf_op jit(solution)/shard_map/ppermute | solution.py:312
  49.8 1.0 %copy-start.3 = (bf16[16,16,2048]{2,1,0:T(8,128)(2,1)}, bf16[16,16,2048]{2,1,0:T(8,128)(2,1)S(1)}, u32[]{:S(2)}) copy-start(bf16[16,16,2048]{2,1,0:T(8,128)(2,1)S(1)} %all-to-all-done) | copy-start | bytes 3145732

commit v15 on v14

--- a/solution.py
+++ b/solution.py
@@ -61,25 +61,28 @@
     fresh_hbm,
     *rest,
 ):
-    *out_refs, mark_ref, queries_ref, key_weight_ref, value_weight_ref, keys_ref = rest[after:-4]
+    *out_refs, mark_ref, queries_ref, key_weight_ref, value_weight_ref, keys_ref = rest[after:-5]
     mark_ref[...] = jnp.zeros_like(mark_ref)
-    cap_ref, table_ref, attended_ref, sem = rest[-4:]
+    cap_ref, table_ref, attended_ref, rows_ref, sem = rest[-5:]
+    staged = len(out_refs) == 1
     slots = queries_ref.shape[0]
     past = prefix_hbm.shape[0]
     heads, dim, _ = key_weight_ref.shape
-    here = pl.ds(first, heads)
-    here = pl.ds(first, heads)
-    copies = [
-        pltpu.make_async_copy(
-            queries_hbm.at[:, pl.ds(first * dim, heads * dim)], queries_ref, sem.at[0]
-        ),
-        pltpu.make_async_copy(key_weight_hbm.at[here], key_weight_ref, sem.at[1]),
-        pltpu.make_async_copy(prefix_hbm, keys_ref.at[pl.ds(0, past)], sem.at[2]),
-        pltpu.make_async_copy(fresh_hbm, keys_ref.at[pl.ds(past, slots)], sem.at[3]),
-        pltpu.make_async_copy(value_weight_hbm.at[here], value_weight_ref, sem.at[4]),
-    ]
-    for copy in copies:
-        copy.start()
+    copies = []
+
+    def start_copy(source, target, queue):
+        copies.append(pltpu.make_async_copy(source, target, sem.at[len(copies)]))
+        copies[-1].start(priority=queue)
+
+    half = heads // 2
+    halves = [(pl.ds(first + i * half, half), pl.ds(i * half, half), i) for i in range(2)]
+    for there, here, queue in halves:
+        start_copy(key_weight_hbm.at[there], key_weight_ref.at[here], queue)
+    start_copy(queries_hbm.at[:, pl.ds(first * dim, heads * dim)], queries_ref, 1)
+    start_copy(prefix_hbm, keys_ref.at[pl.ds(0, past)], 0)
+    start_copy(fresh_hbm, keys_ref.at[pl.ds(past, slots)], 1)
+    for there, here, queue in halves:
+        start_copy(value_weight_hbm.at[there], value_weight_ref.at[here], queue)
     count, size = count_ref[0], size_ref[0]
     lane = lax.broadcasted_iota(jnp.int32, (slots, past), 1)
     cap_ref[:, :past] = jnp.where(lane < size, jnp.float32(OPEN), jnp.float32(MASKED))
@@ -92,6 +95,7 @@
     for copy in copies:
         copy.wait()
 
+    sends = []
     scale = math.log2(math.e) / math.sqrt(dim)
     keys = keys_ref[...]
     stacks = heads // STACK
@@ -115,6 +119,18 @@
             h = stack * STACK + g
             projected = dot(mixed[g * slots : (g + 1) * slots], value_weight_ref[h])
             attended_ref[:, h * dim : (h + 1) * dim] = (projected / total[g]).astype(jnp.bfloat16)
+        if staged and 2 * (stack + 1) % stacks == 0:
+            i = 2 * (stack + 1) // stacks - 1
+            columns = pl.ds(i * half * dim, half * dim)
+            rows_ref[i] = dot(table_ref[...], attended_ref[:, columns]).astype(jnp.bfloat16)
+            sends.append(
+                pltpu.make_async_copy(rows_ref.at[i], out_refs[0].at[:, columns], sem.at[7 + i])
+            )
+            sends[-1].start()
+    for send in sends:
+        send.wait()
+    if staged:
+        return
     grouped = dot(table_ref[...], attended_ref[...]).astype(jnp.bfloat16)
     row = 0
     for out_ref in out_refs:
@@ -150,7 +166,7 @@
     return pl.pallas_call(
         functools.partial(attend_kernel, places // experts, first, cores, len(after)),
         in_specs=[smem, smem, smem, vmem] + [hbm] * (5 + len(after)),
-        out_specs=[vmem] * (len(pieces) + 1),
+        out_specs=[vmem if len(pieces) > 1 else hbm] * len(pieces) + [vmem],
         out_shape=pieces + [jax.ShapeDtypeStruct(MARK, jnp.float32)],
         scratch_shapes=[
             pltpu.VMEM((slots, heads * dim), jnp.bfloat16),
@@ -160,7 +176,8 @@
             pltpu.VMEM((slots, keys), jnp.float32),
             pltpu.VMEM((places, slots), jnp.bfloat16),
             pltpu.VMEM((slots, heads * dim), jnp.bfloat16),
-            pltpu.SemaphoreType.DMA((5,)),
+            pltpu.VMEM((2, places, heads // 2 * dim), jnp.bfloat16),
+            pltpu.SemaphoreType.DMA((7 + 2,)),
         ],
         compiler_params=pltpu.CompilerParams(vmem_limit_bytes=VMEM if first else ALL_VMEM),
         cost_estimate=pl.CostEstimate(

time: 70.1 us -> 70.7 us (level)
  transfers between devices with their start and end apart: 9 -> 9, of which waited for: 4 -> 4; matrix products, arithmetic and copies ran while one was open for 0% -> 0% of each run, Pallas kernels for 21% -> 20%
where the time goes in v15:
time: 70.7 us; the launch traced here: 70.4 us
  Pallas kernels  28.2 us (40%)
  starting transfers between devices  21 us (30%)
  waiting for transfers between devices  17.9 us (25%)
  local copies, waits for them, and re-layouts  1.66 us (2%)
  between operations  1.55 us (2%)
    pallas_call x2, Pallas kernels, attend(): pl.pallas_call(functools.partial(attend_kernel, places // experts, first,...  23.5 us
    ppermute x7, waiting for transfers between devices, local(): piece = lax.ppermute(joined[j], 'dp', [(i, i ^ j) for i in range(ranks)])  16.4 us
    ppermute x7, starting transfers between devices, local(): piece = lax.ppermute(joined[j], 'dp', [(i, i ^ j) for i in range(ranks)])  13.1 us
    all_to_all x1, starting transfers between devices, to_all(): lax.all_to_all(outgoing.reshape(experts, capacity, -1), ('dp', 'ep'), spl...  7.41 us
    pallas_call x2, Pallas kernels, place(): pl.pallas_call(functools.partial(place_kernel, plan, cores), in_specs=[pl...  3.4 us
    unnamed x8, local copies, waits for them, and re-layouts  1.66 us
    ppermute x1, waiting for transfers between devices, local(): swapped = lax.ppermute(message, 'ep', [(i, i ^ 1) for i in range(cores)])  1.54 us
  transfers between devices with their start and end apart: 9, of which 4 were waited for; matrix products, arithmetic and copies ran while one was open for 0% of the time, Pallas kernels for 20%

profile of v15, /device:TPU:0, one launch (start us, length us, event | category | flops | bytes accessed | tf_op | source)
XLA Modules:
  0.0 70.4 jit_solution(817445768035998925)
XLA Ops:
  1.3 0.0 copy-start
  1.3 0.0 copy-start.1
  1.3 13.0 %shard_map.82 = (bf16[256,2048]{1,0:T(8,128)(2,1)}, f32[8,128]{1,0:T(8,128)}) custom-call(s32[1]{0:T(128)} %constant.11.clone.1.me_ref, s32[1]{0:T(128)S(6)} %copy.11.count_ref, s32[1]{0:T(128)S(6)} %copy.12.size_ref, s32[2,128]{1,0:T(2,128)} %bitcast.4, bf16[128,4096]{1,0:T(8,128)(2,1)} %queries_hbm.3, bf16[32,128,512]{2,1,0:T(8,128)(2,1)} %key_weight_hbm.3, ...), custom_call_target="tpu_custom_call" | custom-call | flops 4831838208 | bytes 4194304 | tf_op jit(solution)/shard_map/pallas_call | solution.py:166
  14.3 7.4 %all-to-all-start = ((bf16[16,16,2048]{2,1,0:T(8,128)(2,1)}), bf16[16,16,2048]{2,1,0:T(8,128)(2,1)S(1)}, u32[]{:S(2)}, u32[]{:S(2)}) async-start(bf16[16,16,2048]{2,1,0:T(8,128)(2,1)} %bitcast.7), calls=%async_computation | async-start | bytes 2097152 | tf_op jit(solution)/shard_map/all_to_all | solution.py:303
  21.7 0.0 copy-done
  21.7 0.0 copy-done.1
  21.7 0.0 copy-start.2
  21.7 0.7 copy-done.2
  22.4 10.6 %shard_map.83 = (bf16[16,2048]{1,0:T(8,128)(2,1)S(1)}, bf16[16,2048]{1,0:T(8,128)(2,1)S(1)}, bf16[16,2048]{1,0:T(8,128)(2,1)S(1)}, bf16[16,2048]{1,0:T(8,128)(2,...) custom-call(s32[1]{0:T(128)} %bitcast.me_ref, ...), custom_call_target="tpu_custom_call" | custom-call | flops 4831838208 | bytes 4194304 | tf_op jit(solution)/shard_map/pallas_call | solution.py:166
  33.0 0.5 collective-permute-start
  33.5 1.5 %collective-permute-done.refs_7_.refs_2_ = bf16[128,2048]{1,0:T(8,128)(2,1)S(1)} collective-permute-done((bf16[128,2048]{1,0:T(8,128)(2,1)S(1)}, bf16[128,2048]{1,0:T(8,128)(2,1)S(1)}, u32[]{:S(2)}, u32[]{:S(2)}) %collective-permute-start) | collective-permute-done | bytes 524320 | tf_op jit(solution)/shard_map/ppermute | solution.py:320
  35.0 1.3 %shard_map.84 = (bf16[32,2048]{1,0:T(8,128)(2,1)S(1)}, bf16[32,2048]{1,0:T(8,128)(2,1)S(1)}, bf16[32,2048]{1,0:T(8,128)(2,1)S(1)}, bf16[32,2048]{1,0:T(8,128)(2,...) custom-call(bf16[16,2048]{1,0:T(8,128)(2,1)S(1)} %get-tuple-element.24.refs_0_, ...), custom_call_target="tpu_custom_call" | custom-call | tf_op jit(solution)/shard_map/pallas_call | solution.py:214
  36.3 2.0 %collective-permute-start.5 = (bf16[32,2048]{1,0:T(8,128)(2,1)S(1)}, bf16[32,2048]{1,0:T(8,128)(2,1)S(1)}, u32[]{:S(2)}, u32[]{:S(2)}) collective-permute-start(bf16[32,2048]{1,0:T(8,128)(2,1)S(1)} %get-tuple-element.38), channel_id=1, source_target_pairs={{0,2},{2,0},{4,6},{6,4},{8,10},{10,8},{12,14},{14,12},{1,3},{3,1},... | collective-permute-start | bytes 393224 | tf_op jit(solution)/shard_map/ppermute | solution.py:329
  38.3 1.5 %collective-permute-start.6 = (bf16[32,2048]{1,0:T(8,128)(2,1)S(1)}, bf16[32,2048]{1,0:T(8,128)(2,1)S(1)}, u32[]{:S(2)}, u32[]{:S(2)}) collective-permute-start(bf16[32,2048]{1,0:T(8,128)(2,1)S(1)} %get-tuple-element.39), channel_id=1, source_target_pairs={{0,4},{2,6},{4,0},{6,2},{8,12},{10,14},{12,8},{14,10},{1,5},{3,7},... | collective-permute-start | bytes 393224 | tf_op jit(solution)/shard_map/ppermute | solution.py:329
  39.7 2.4 %collective-permute-start.1 = (bf16[32,2048]{1,0:T(8,128)(2,1)S(1)}, bf16[32,2048]{1,0:T(8,128)(2,1)S(1)}, u32[]{:S(2)}, u32[]{:S(2)}) collective-permute-start(bf16[32,2048]{1,0:T(8,128)(2,1)S(1)} %get-tuple-element.32), channel_id=1, source_target_pairs={{0,8},{2,10},{4,12},{6,14},{8,0},{10,2},{12,4},{14,6},{1,9},{3,11}... | collective-permute-start | bytes 393224 | tf_op jit(solution)/shard_map/ppermute | solution.py:329
  42.1 0.6 collective-permute-start.7
  42.7 1.5 %collective-permute-start.2 = (bf16[32,2048]{1,0:T(8,128)(2,1)S(1)}, bf16[32,2048]{1,0:T(8,128)(2,1)S(1)}, u32[]{:S(2)}, u32[]{:S(2)}) collective-permute-start(bf16[32,2048]{1,0:T(8,128)(2,1)S(1)} %get-tuple-element.33), channel_id=1, source_target_pairs={{0,12},{2,14},{4,8},{6,10},{8,4},{10,6},{12,0},{14,2},{1,13},{3,15... | collective-permute-start | bytes 393224 | tf_op jit(solution)/shard_map/ppermute | solution.py:329
  44.1 0.0 collective-permute-done.5.refs_3_
  44.1 4.0 %collective-permute-start.3 = (bf16[32,2048]{1,0:T(8,128)(2,1)S(1)}, bf16[32,2048]{1,0:T(8,128)(2,1)S(1)}, u32[]{:S(2)}, u32[]{:S(2)}) collective-permute-start(bf16[32,2048]{1,0:T(8,128)(2,1)S(1)} %get-tuple-element.34), channel_id=1, source_target_pairs={{0,10},{2,8},{4,14},{6,12},{8,2},{10,0},{12,6},{14,4},{1,11},{3,9}... | collective-permute-start | bytes 393224 | tf_op jit(solution)/shard_map/ppermute | solution.py:329
  48.2 0.0 collective-permute-done.6.refs_4_
  48.2 1.3 %collective-permute-start.4 = (bf16[32,2048]{1,0:T(8,128)(2,1)S(1)}, bf16[32,2048]{1,0:T(8,128)(2,1)S(1)}, u32[]{:S(2)}, u32[]{:S(2)}) collective-permute-start(bf16[32,2048]{1,0:T(8,128)(2,1)S(1)} %get-tuple-element.35), channel_id=1, source_target_pairs={{0,14},{2,12},{4,10},{6,8},{8,6},{10,4},{12,2},{14,0},{1,15},{3,13... | collective-permute-start | bytes 393224 | tf_op jit(solution)/shard_map/ppermute | solution.py:329
  49.5 0.9 %collective-permute-done.7.refs_5_ = bf16[32,2048]{1,0:T(8,128)(2,1)S(1)} collective-permute-done((bf16[32,2048]{1,0:T(8,128)(2,1)S(1)}, bf16[32,2048]{1,0:T(8,128)(2,1)S(1)}, u32[]{:S(2)}, u32[]{:S(2)}) %collective-permute-start.7) | collective-permute-done | bytes 131104 | tf_op jit(solution)/shard_map/ppermute | solution.py:329
  50.4 0.0 all-to-all-done
  50.4 0.0 copy-start.3
  50.4 1.0 %copy-done.3 = bf16[16,16,2048]{2,1,0:T(8,128)(2,1)} copy-done((bf16[16,16,2048]{2,1,0:T(8,128)(2,1)}, bf16[16,16,2048]{2,1,0:T(8,128)(2,1)S(1)}, u32[]{:S(2)}) %copy-start.3) | copy-done | bytes 1048600
  51.3 2.6 %shard_map.85.refs_4_ = bf16[1,8,16,8192]{3,2,1,0:T(8,128)(2,1)} custom-call(s32[1]{0:T(128)} %bitcast.me_ref, bf16[256,2048]{1,0:T(8,128)(2,1)} %bitcast.6, bf16[16,2048]{1,0:T(8,128)(2,1)S(1)} %get-tuple-element.37.refs_1_, bf16[128,2048]{1,0:T(8,128)(2,1)S(1)} %collective-permute-done.refs_7_.refs_2_, ...), custom_call_target="tpu_custom_call" | custom-call | tf_op jit(solution)/shard_map/pallas_call | solution.py:245
  53.9 8.9 %collective-permute-done.1.refs_0_ = bf16[32,2048]{1,0:T(8,128)(2,1)S(1)} collective-permute-done((bf16[32,2048]{1,0:T(8,128)(2,1)S(1)}, bf16[32,2048]{1,0:T(8,128)(2,1)S(1)}, u32[]{:S(2)}, u32[]{:S(2)}) %collective-permute-start.1) | collective-permute-done | bytes 131104 | tf_op jit(solution)/shard_map/ppermute | solution.py:329
  62.8 0.0 collective-permute-done.2.refs_1_
  62.8 6.5 %collective-permute-done.3.refs_2_ = bf16[32,2048]{1,0:T(8,128)(2,1)S(1)} collective-permute-done((bf16[32,2048]{1,0:T(8,128)(2,1)S(1)}, bf16[32,2048]{1,0:T(8,128)(2,1)S(1)}, u32[]{:S(2)}, u32[]{:S(2)}) %collective-permute-start.3) | collective-permute-done | bytes 131104 | tf_op jit(solution)/shard_map/ppermute | solution.py:329
  69.3 0.0 collective-permute-done.4.refs_3_
  69.3 0.8 %shard_map.86 = bf16[1,8,16,8192]{3,2,1,0:T(8,128)(2,1)} custom-call(s32[1]{0:T(128)} %bitcast.me_ref, bf16[32,2048]{1,0:T(8,128)(2,1)S(1)} %collective-permute-done.1.refs_0_, bf16[32,2048]{1,0:T(8,128)(2,1)S(1)} %collective-permute-done.2.refs_1_, bf16[32,2048]{1,0:T(8,128)(2,1)S(1)} %collective-permute-done.3.refs_2_, ...), custom_call_target="tpu_custom_call", output_to_operand_aliasing={{}: (5, {})} | custom-call | tf_op jit(solution)/shard_map/pallas_call | solution.py:245
Async XLA Ops:
  1.3 20.4 %copy-start = (bf16[128,512]{1,0:T(8,128)(2,1)S(1)}, bf16[128,512]{1,0:T(8,128)(2,1)}, u32[]{:S(2)}) copy-start(bf16[128,512]{1,0:T(8,128)(2,1)} %fresh_hbm.3) | copy-start | bytes 393220
  1.3 20.4 %copy-start.1 = (s32[128,2]{0,1:T(2,128)S(1)}, s32[128,2]{0,1:T(2,128)}, u32[]{:S(2)}) copy-start(s32[128,2]{0,1:T(2,128)} %param.15) | copy-start | bytes 3076
  14.3 36.1 %all-to-all-start = ((bf16[16,16,2048]{2,1,0:T(8,128)(2,1)}), bf16[16,16,2048]{2,1,0:T(8,128)(2,1)S(1)}, u32[]{:S(2)}, u32[]{:S(2)}) async-start(bf16[16,16,2048]{2,1,0:T(8,128)(2,1)} %bitcast.7), calls=%async_computation | async-start | bytes 2097152 | tf_op jit(solution)/shard_map/all_to_all | solution.py:303
  21.7 0.7 copy-start.2
  33.0 2.0 %collective-permute-start = (bf16[128,2048]{1,0:T(8,128)(2,1)S(1)}, bf16[128,2048]{1,0:T(8,128)(2,1)S(1)}, u32[]{:S(2)}, u32[]{:S(2)}) collective-permute-start(bf16[128,2048]{1,0:T(8,128)(2,1)S(1)} %get-tuple-element.31), channel_id=1, source_target_pairs={{0,1},{1,0},{2,3},{3,2},{4,5},{5,4},{6,7},{7,6},{8,9},{9,8},{10,11... | collective-permute-start | bytes 1572872 | tf_op jit(solution)/shard_map/ppermute | solution.py:320
  36.3 7.8 %collective-permute-start.5 = (bf16[32,2048]{1,0:T(8,128)(2,1)S(1)}, bf16[32,2048]{1,0:T(8,128)(2,1)S(1)}, u32[]{:S(2)}, u32[]{:S(2)}) collective-permute-start(bf16[32,2048]{1,0:T(8,128)(2,1)S(1)} %get-tuple-element.38), channel_id=1, source_target_pairs={{0,2},{2,0},{4,6},{6,4},{8,10},{10,8},{12,14},{14,12},{1,3},{3,1},... | collective-permute-start | bytes 393224 | tf_op jit(solution)/shard_map/ppermute | solution.py:329
  38.3 9.9 %collective-permute-start.6 = (bf16[32,2048]{1,0:T(8,128)(2,1)S(1)}, bf16[32,2048]{1,0:T(8,128)(2,1)S(1)}, u32[]{:S(2)}, u32[]{:S(2)}) collective-permute-start(bf16[32,2048]{1,0:T(8,128)(2,1)S(1)} %get-tuple-element.39), channel_id=1, source_target_pairs={{0,4},{2,6},{4,0},{6,2},{8,12},{10,14},{12,8},{14,10},{1,5},{3,7},... | collective-permute-start | bytes 393224 | tf_op jit(solution)/shard_map/ppermute | solution.py:329
  39.7 23.1 %collective-permute-start.1 = (bf16[32,2048]{1,0:T(8,128)(2,1)S(1)}, bf16[32,2048]{1,0:T(8,128)(2,1)S(1)}, u32[]{:S(2)}, u32[]{:S(2)}) collective-permute-start(bf16[32,2048]{1,0:T(8,128)(2,1)S(1)} %get-tuple-element.32), channel_id=1, source_target_pairs={{0,8},{2,10},{4,12},{6,14},{8,0},{10,2},{12,4},{14,6},{1,9},{3,11}... | collective-permute-start | bytes 393224 | tf_op jit(solution)/shard_map/ppermute | solution.py:329
  42.1 8.3 %collective-permute-start.7 = (bf16[32,2048]{1,0:T(8,128)(2,1)S(1)}, bf16[32,2048]{1,0:T(8,128)(2,1)S(1)}, u32[]{:S(2)}, u32[]{:S(2)}) collective-permute-start(bf16[32,2048]{1,0:T(8,128)(2,1)S(1)} %get-tuple-element.40), channel_id=1, source_target_pairs={{0,6},{2,4},{4,2},{6,0},{8,14},{10,12},{12,10},{14,8},{1,7},{3,5},... | collective-permute-start | bytes 393224 | tf_op jit(solution)/shard_map/ppermute | solution.py:329
  42.7 20.2 %collective-permute-start.2 = (bf16[32,2048]{1,0:T(8,128)(2,1)S(1)}, bf16[32,2048]{1,0:T(8,128)(2,1)S(1)}, u32[]{:S(2)}, u32[]{:S(2)}) collective-permute-start(bf16[32,2048]{1,0:T(8,128)(2,1)S(1)} %get-tuple-element.33), channel_id=1, source_target_pairs={{0,12},{2,14},{4,8},{6,10},{8,4},{10,6},{12,0},{14,2},{1,13},{3,15... | collective-permute-start | bytes 393224 | tf_op jit(solution)/shard_map/ppermute | solution.py:329
  44.1 25.2 %collective-permute-start.3 = (bf16[32,2048]{1,0:T(8,128)(2,1)S(1)}, bf16[32,2048]{1,0:T(8,128)(2,1)S(1)}, u32[]{:S(2)}, u32[]{:S(2)}) collective-permute-start(bf16[32,2048]{1,0:T(8,128)(2,1)S(1)} %get-tuple-element.34), channel_id=1, source_target_pairs={{0,10},{2,8},{4,14},{6,12},{8,2},{10,0},{12,6},{14,4},{1,11},{3,9}... | collective-permute-start | bytes 393224 | tf_op jit(solution)/shard_map/ppermute | solution.py:329
  48.2 21.2 %collective-permute-start.4 = (bf16[32,2048]{1,0:T(8,128)(2,1)S(1)}, bf16[32,2048]{1,0:T(8,128)(2,1)S(1)}, u32[]{:S(2)}, u32[]{:S(2)}) collective-permute-start(bf16[32,2048]{1,0:T(8,128)(2,1)S(1)} %get-tuple-element.35), channel_id=1, source_target_pairs={{0,14},{2,12},{4,10},{6,8},{8,6},{10,4},{12,2},{14,0},{1,15},{3,13... | collective-permute-start | bytes 393224 | tf_op jit(solution)/shard_map/ppermute | solution.py:329
  50.4 1.0 %copy-start.3 = (bf16[16,16,2048]{2,1,0:T(8,128)(2,1)}, bf16[16,16,2048]{2,1,0:T(8,128)(2,1)S(1)}, u32[]{:S(2)}) copy-start(bf16[16,16,2048]{2,1,0:T(8,128)(2,1)S(1)} %all-to-all-done) | copy-start | bytes 3145732

commit v16 on v14

--- a/solution.py
+++ b/solution.py
@@ -10,10 +10,10 @@
 
 SPAN = 64
 STACK = 4
-CHUNKS = (1, 1)
+CHUNKS = (7, 9)
 DIRECT = 16
-ALL_VMEM = 60 * 1024 * 1024
-VMEM = 52 * 1024 * 1024
+ALL_VMEM = 63_400_000
+VMEM = 51 * 1024 * 1024
 SHORT = pl.CostEstimate(flops=0, bytes_accessed=0, transcendentals=0)
 MARK = (8, 128)
 MASKED = -1e30
@@ -94,25 +94,24 @@
 
     scale = math.log2(math.e) / math.sqrt(dim)
     keys = keys_ref[...]
-    stacks = heads // STACK
+    stacks = [range(h, min(h + STACK, heads)) for h in range(0, heads, STACK)]
     scores = []
-    for stack in range(stacks):
+    for stack in stacks:
         lifted = []
-        for h in range(stack * STACK, (stack + 1) * STACK):
+        for h in stack:
             one = dot(queries_ref[:, h * dim : (h + 1) * dim], key_weight_ref[h])
             lifted.append(one.astype(jnp.bfloat16))
         lifted = jnp.concatenate(lifted, axis=0)
         scores.append(lax.dot_general(lifted, keys, NT, preferred_element_type=jnp.float32))
-    for stack in range(stacks):
-        score = scores[stack].reshape(STACK, slots, keys.shape[0])
+    for stack, score in zip(stacks, scores):
+        score = score.reshape(len(stack), slots, keys.shape[0])
         score = jnp.minimum(score, cap_ref[...][None])
         highest = jnp.max(score, axis=-1, keepdims=True) * scale
         weights = jnp.exp2(score * scale - highest)
         total = jnp.sum(weights, axis=-1, keepdims=True)
-        weights = weights.astype(jnp.bfloat16).reshape(STACK * slots, keys.shape[0])
+        weights = weights.astype(jnp.bfloat16).reshape(len(stack) * slots, keys.shape[0])
         mixed = dot(weights, keys).astype(jnp.bfloat16)
-        for g in range(STACK):
-            h = stack * STACK + g
+        for g, h in enumerate(stack):
             projected = dot(mixed[g * slots : (g + 1) * slots], value_weight_ref[h])
             attended_ref[:, h * dim : (h + 1) * dim] = (projected / total[g]).astype(jnp.bfloat16)
     grouped = dot(table_ref[...], attended_ref[...]).astype(jnp.bfloat16)
@@ -240,7 +239,7 @@
 
 def exchange_order(ranks):
     near, far = list(range(1, ranks // 2)), list(range(ranks // 2, ranks))
-    return near[:-1] + far[::2] + far[1::2] + near[-1:]
+    return far[:1] + near + far[2::2] + far[1::2]
 
 
 def local(
@@ -310,10 +309,9 @@
     late_plan = []
     for j in order:
         piece = lax.ppermute(joined[j], "dp", [(i, i ^ j) for i in range(ranks)])
-        arrays, plan = (soon, soon_plan) if j < ranks // 2 else (late, late_plan)
-        plan.append((len(arrays), 0, middle, j * cores, True))
-        plan.append((len(arrays), capacity, middle, j * cores + 1, True))
-        arrays.append(piece)
+        late_plan.append((len(late), 0, middle, j * cores, True))
+        late_plan.append((len(late), capacity, middle, j * cores + 1, True))
+        late.append(piece)
     shape = (1, ranks, capacity, cores * heads * dim)
     placed = place(me, soon, soon_plan, cores, shape, [])
     return place(me, late, late_plan, cores, shape, [placed])

time: 70.1 us -> 69.9 us (level)
  waiting for transfers between devices: 17.8 us -> 25.1 us
  starting transfers between devices: 21 us -> 15.7 us
  Pallas kernels: 27.7 us -> 26.5 us
  local copies, waits for them, and re-layouts: 1.66 us -> 0.69 us
    ppermute x7, waiting for transfers between devices: 16.3 us -> 23.5 us  [local(): piece = lax.ppermute(joined[j], 'dp', [(i, i ^ j) for i in range(ranks)])]
    ppermute x7, starting transfers between devices: 13.1 us -> 7.83 us  [local(): piece = lax.ppermute(joined[j], 'dp', [(i, i ^ j) for i in range(ranks)])]
    pallas_call x2, Pallas kernels: 3.4 us -> 2.19 us  [place(): pl.pallas_call(functools.partial(place_kernel, plan, cores), in_specs=[pl...]
    unnamed x8, local copies, waits for them, and re-layouts: 1.66 us -> 0.69 us
  transfers between devices with their start and end apart: 9 -> 9, of which waited for: 4 -> 3; matrix products, arithmetic and copies ran while one was open for 0% -> 0% of each run, Pallas kernels for 21% -> 20%
where the time goes in v16:
time: 69.9 us; the launch traced here: 69.6 us
  Pallas kernels  26.5 us (38%)
  waiting for transfers between devices  25.1 us (36%)
  starting transfers between devices  15.7 us (22%)
  between operations  1.6 us (2%)
    ppermute x7, waiting for transfers between devices, local(): piece = lax.ppermute(joined[j], 'dp', [(i, i ^ j) for i in range(ranks)])  23.5 us
    pallas_call x2, Pallas kernels, attend(): pl.pallas_call(functools.partial(attend_kernel, places // experts, first,...  22.8 us
    ppermute x7, starting transfers between devices, local(): piece = lax.ppermute(joined[j], 'dp', [(i, i ^ j) for i in range(ranks)])  7.83 us
    all_to_all x1, starting transfers between devices, to_all(): lax.all_to_all(outgoing.reshape(experts, capacity, -1), ('dp', 'ep'), spl...  7.41 us
    pallas_call x2, Pallas kernels, place(): pl.pallas_call(functools.partial(place_kernel, plan, cores), in_specs=[pl...  2.19 us
    ppermute x1, waiting for transfers between devices, local(): swapped = lax.ppermute(message, 'ep', [(i, i ^ 1) for i in range(cores)])  1.63 us
    pallas_call x1, Pallas kernels, join(): pl.pallas_call(join_kernel, in_specs=[pl.BlockSpec(memory_space=pl.ANY)]...  1.44 us
  transfers between devices with their start and end apart: 9, of which 3 were waited for; matrix products, arithmetic and copies ran while one was open for 0% of the time, Pallas kernels for 20%

profile of v16, /device:TPU:0, one launch (start us, length us, event | category | flops | bytes accessed | tf_op | source)
XLA Modules:
  0.0 69.6 jit_solution(13395447365910802622)
XLA Ops:
  1.3 0.0 copy-start
  1.3 0.0 copy-start.1
  1.3 0.0 copy-start.2
  1.3 11.2 %shard_map.82 = (bf16[256,1792]{1,0:T(8,128)(2,1)}, f32[8,128]{1,0:T(8,128)}) custom-call(s32[1]{0:T(128)} %constant.11.clone.1.me_ref, s32[1]{0:T(128)S(6)} %copy.11.count_ref, s32[1]{0:T(128)S(6)} %copy.12.size_ref, s32[2,128]{1,0:T(2,128)} %bitcast.5, bf16[128,4096]{1,0:T(8,128)(2,1)} %queries_hbm.3, bf16[32,128,512]{2,1,0:T(8,128)(2,1)} %key_weight_hbm.3, ...), custom_call_target="tpu_custom_call" | custom-call | flops 4227858432 | bytes 3670016 | tf_op jit(solution)/shard_map/pallas_call | solution.py:149
  12.6 7.4 %all-to-all-start = ((bf16[16,16,1792]{2,1,0:T(8,128)(2,1)}), bf16[16,16,1792]{2,1,0:T(8,128)(2,1)S(1)}, u32[]{:S(2)}, u32[]{:S(2)}) async-start(bf16[16,16,1792]{2,1,0:T(8,128)(2,1)} %bitcast.7), calls=%async_computation | async-start | bytes 1835008 | tf_op jit(solution)/shard_map/all_to_all | solution.py:285
  20.0 0.0 copy-done
  20.0 0.0 copy-done.1
  20.0 0.0 copy-done.2
  20.0 0.0 copy-start.3
  20.0 0.7 copy-done.3
  20.7 11.6 %shard_map.83 = (bf16[16,2304]{1,0:T(8,128)(2,1)S(1)}, bf16[16,2304]{1,0:T(8,128)(2,1)S(1)}, bf16[16,2304]{1,0:T(8,128)(2,1)S(1)}, bf16[16,2304]{1,0:T(8,128)(2,...) custom-call(s32[1]{0:T(128)} %bitcast.me_ref, ...), custom_call_target="tpu_custom_call" | custom-call | flops 5435817984 | bytes 4718592 | tf_op jit(solution)/shard_map/pallas_call | solution.py:149
  32.3 0.4 collective-permute-start
  32.8 1.6 %collective-permute-done.refs_7_.refs_2_ = bf16[128,2304]{1,0:T(8,128)(2,1)S(1)} collective-permute-done((bf16[128,2304]{1,0:T(8,128)(2,1)S(1)}, bf16[128,2304]{1,0:T(8,128)(2,1)S(1)}, u32[]{:S(2)}, u32[]{:S(2)}) %collective-permute-start) | collective-permute-done | bytes 589856 | tf_op jit(solution)/shard_map/ppermute | solution.py:302
  34.4 1.4 %shard_map.84 = (bf16[32,2304]{1,0:T(8,128)(2,1)S(1)}, bf16[32,2304]{1,0:T(8,128)(2,1)S(1)}, bf16[32,2304]{1,0:T(8,128)(2,1)S(1)}, bf16[32,2304]{1,0:T(8,128)(2,...) custom-call(bf16[16,2304]{1,0:T(8,128)(2,1)S(1)} %get-tuple-element.24.refs_0_, ...), custom_call_target="tpu_custom_call" | custom-call | tf_op jit(solution)/shard_map/pallas_call | solution.py:196
  35.8 2.9 %collective-permute-start.1 = (bf16[32,2304]{1,0:T(8,128)(2,1)S(1)}, bf16[32,2304]{1,0:T(8,128)(2,1)S(1)}, u32[]{:S(2)}, u32[]{:S(2)}) collective-permute-start(bf16[32,2304]{1,0:T(8,128)(2,1)S(1)} %get-tuple-element.32), channel_id=1, source_target_pairs={{0,8},{2,10},{4,12},{6,14},{8,0},{10,2},{12,4},{14,6},{1,9},{3,11}... | collective-permute-start | bytes 442376 | tf_op jit(solution)/shard_map/ppermute | solution.py:311
  38.7 1.5 %collective-permute-start.2 = (bf16[32,2304]{1,0:T(8,128)(2,1)S(1)}, bf16[32,2304]{1,0:T(8,128)(2,1)S(1)}, u32[]{:S(2)}, u32[]{:S(2)}) collective-permute-start(bf16[32,2304]{1,0:T(8,128)(2,1)S(1)} %get-tuple-element.33), channel_id=1, source_target_pairs={{0,2},{2,0},{4,6},{6,4},{8,10},{10,8},{12,14},{14,12},{1,3},{3,1},... | collective-permute-start | bytes 442376 | tf_op jit(solution)/shard_map/ppermute | solution.py:311
  40.2 1.5 %collective-permute-start.3 = (bf16[32,2304]{1,0:T(8,128)(2,1)S(1)}, bf16[32,2304]{1,0:T(8,128)(2,1)S(1)}, u32[]{:S(2)}, u32[]{:S(2)}) collective-permute-start(bf16[32,2304]{1,0:T(8,128)(2,1)S(1)} %get-tuple-element.34), channel_id=1, source_target_pairs={{0,4},{2,6},{4,0},{6,2},{8,12},{10,14},{12,8},{14,10},{1,5},{3,7},... | collective-permute-start | bytes 442376 | tf_op jit(solution)/shard_map/ppermute | solution.py:311
  41.6 0.6 collective-permute-start.4
  42.2 1.5 %collective-permute-start.5 = (bf16[32,2304]{1,0:T(8,128)(2,1)S(1)}, bf16[32,2304]{1,0:T(8,128)(2,1)S(1)}, u32[]{:S(2)}, u32[]{:S(2)}) collective-permute-start(bf16[32,2304]{1,0:T(8,128)(2,1)S(1)} %get-tuple-element.36), channel_id=1, source_target_pairs={{0,12},{2,14},{4,8},{6,10},{8,4},{10,6},{12,0},{14,2},{1,13},{3,15... | collective-permute-start | bytes 442376 | tf_op jit(solution)/shard_map/ppermute | solution.py:311
  43.7 14.8 %collective-permute-done.1.refs_0_ = bf16[32,2304]{1,0:T(8,128)(2,1)S(1)} collective-permute-done((bf16[32,2304]{1,0:T(8,128)(2,1)S(1)}, bf16[32,2304]{1,0:T(8,128)(2,1)S(1)}, u32[]{:S(2)}, u32[]{:S(2)}) %collective-permute-start.1) | collective-permute-done | bytes 147488 | tf_op jit(solution)/shard_map/ppermute | solution.py:311
  58.4 0.0 collective-permute-start.6
  58.5 0.0 collective-permute-done.2.refs_1_
  58.5 0.0 collective-permute-start.7
  58.5 0.0 all-to-all-done
  58.5 1.1 %shard_map.85.refs_7_ = bf16[1,8,16,8192]{3,2,1,0:T(8,128)(2,1)} custom-call(s32[1]{0:T(128)} %bitcast.me_ref, bf16[256,1792]{1,0:T(8,128)(2,1)S(1)} %bitcast.4, bf16[16,2304]{1,0:T(8,128)(2,1)S(1)} %get-tuple-element.40.refs_1_, bf16[128,2304]{1,0:T(8,128)(2,1)S(1)} %collective-permute-done.refs_7_.refs_2_), custom_call_target="tpu_custom_call" | custom-call | tf_op jit(solution)/shard_map/pallas_call | solution.py:227
  59.6 0.0 collective-permute-done.3.refs_2_
  59.6 0.0 collective-permute-done.4.refs_3_
  59.6 0.0 collective-permute-done.5.refs_4_
  59.6 8.7 %collective-permute-done.6.refs_5_ = bf16[32,2304]{1,0:T(8,128)(2,1)S(1)} collective-permute-done((bf16[32,2304]{1,0:T(8,128)(2,1)S(1)}, bf16[32,2304]{1,0:T(8,128)(2,1)S(1)}, u32[]{:S(2)}, u32[]{:S(2)}) %collective-permute-start.6) | collective-permute-done | bytes 147488 | tf_op jit(solution)/shard_map/ppermute | solution.py:311
  68.4 0.0 collective-permute-done.7.refs_6_
  68.4 1.1 %shard_map.86 = bf16[1,8,16,8192]{3,2,1,0:T(8,128)(2,1)} custom-call(s32[1]{0:T(128)} %bitcast.me_ref, bf16[32,2304]{1,0:T(8,128)(2,1)S(1)} %collective-permute-done.1.refs_0_, bf16[32,2304]{1,0:T(8,128)(2,1)S(1)} %collective-permute-done.2.refs_1_, bf16[32,2304]{1,0:T(8,128)(2,1)S(1)} %collective-permute-done.3.refs_2_, ...), custom_call_target="tpu_custom_call", output_to_operand_aliasing={{}: (8, {})} | custom-call | tf_op jit(solution)/shard_map/pallas_call | solution.py:227
Async XLA Ops:
  1.3 18.7 %copy-start = (bf16[128,4096]{1,0:T(8,128)(2,1)S(1)}, bf16[128,4096]{1,0:T(8,128)(2,1)}, u32[]{:S(2)}) copy-start(bf16[128,4096]{1,0:T(8,128)(2,1)} %queries_hbm.3) | copy-start | bytes 3145732
  1.3 18.7 %copy-start.1 = (bf16[128,512]{1,0:T(8,128)(2,1)S(1)}, bf16[128,512]{1,0:T(8,128)(2,1)}, u32[]{:S(2)}) copy-start(bf16[128,512]{1,0:T(8,128)(2,1)} %fresh_hbm.3) | copy-start | bytes 393220
  1.3 18.7 %copy-start.2 = (s32[128,2]{0,1:T(2,128)S(1)}, s32[128,2]{0,1:T(2,128)}, u32[]{:S(2)}) copy-start(s32[128,2]{0,1:T(2,128)} %param.15) | copy-start | bytes 3076
  12.6 45.9 %all-to-all-start = ((bf16[16,16,1792]{2,1,0:T(8,128)(2,1)}), bf16[16,16,1792]{2,1,0:T(8,128)(2,1)S(1)}, u32[]{:S(2)}, u32[]{:S(2)}) async-start(bf16[16,16,1792]{2,1,0:T(8,128)(2,1)} %bitcast.7), calls=%async_computation | async-start | bytes 1835008 | tf_op jit(solution)/shard_map/all_to_all | solution.py:285
  20.0 0.7 copy-start.3
  32.3 2.1 %collective-permute-start = (bf16[128,2304]{1,0:T(8,128)(2,1)S(1)}, bf16[128,2304]{1,0:T(8,128)(2,1)S(1)}, u32[]{:S(2)}, u32[]{:S(2)}) collective-permute-start(bf16[128,2304]{1,0:T(8,128)(2,1)S(1)} %get-tuple-element.31), channel_id=1, source_target_pairs={{0,1},{1,0},{2,3},{3,2},{4,5},{5,4},{6,7},{7,6},{8,9},{9,8},{10,11... | collective-permute-start | bytes 1769480 | tf_op jit(solution)/shard_map/ppermute | solution.py:302
  35.8 22.6 %collective-permute-start.1 = (bf16[32,2304]{1,0:T(8,128)(2,1)S(1)}, bf16[32,2304]{1,0:T(8,128)(2,1)S(1)}, u32[]{:S(2)}, u32[]{:S(2)}) collective-permute-start(bf16[32,2304]{1,0:T(8,128)(2,1)S(1)} %get-tuple-element.32), channel_id=1, source_target_pairs={{0,8},{2,10},{4,12},{6,14},{8,0},{10,2},{12,4},{14,6},{1,9},{3,11}... | collective-permute-start | bytes 442376 | tf_op jit(solution)/shard_map/ppermute | solution.py:311
  38.7 19.7 %collective-permute-start.2 = (bf16[32,2304]{1,0:T(8,128)(2,1)S(1)}, bf16[32,2304]{1,0:T(8,128)(2,1)S(1)}, u32[]{:S(2)}, u32[]{:S(2)}) collective-permute-start(bf16[32,2304]{1,0:T(8,128)(2,1)S(1)} %get-tuple-element.33), channel_id=1, source_target_pairs={{0,2},{2,0},{4,6},{6,4},{8,10},{10,8},{12,14},{14,12},{1,3},{3,1},... | collective-permute-start | bytes 442376 | tf_op jit(solution)/shard_map/ppermute | solution.py:311
  40.2 19.4 %collective-permute-start.3 = (bf16[32,2304]{1,0:T(8,128)(2,1)S(1)}, bf16[32,2304]{1,0:T(8,128)(2,1)S(1)}, u32[]{:S(2)}, u32[]{:S(2)}) collective-permute-start(bf16[32,2304]{1,0:T(8,128)(2,1)S(1)} %get-tuple-element.34), channel_id=1, source_target_pairs={{0,4},{2,6},{4,0},{6,2},{8,12},{10,14},{12,8},{14,10},{1,5},{3,7},... | collective-permute-start | bytes 442376 | tf_op jit(solution)/shard_map/ppermute | solution.py:311
  41.6 18.0 %collective-permute-start.4 = (bf16[32,2304]{1,0:T(8,128)(2,1)S(1)}, bf16[32,2304]{1,0:T(8,128)(2,1)S(1)}, u32[]{:S(2)}, u32[]{:S(2)}) collective-permute-start(bf16[32,2304]{1,0:T(8,128)(2,1)S(1)} %get-tuple-element.35), channel_id=1, source_target_pairs={{0,6},{2,4},{4,2},{6,0},{8,14},{10,12},{12,10},{14,8},{1,7},{3,5},... | collective-permute-start | bytes 442376 | tf_op jit(solution)/shard_map/ppermute | solution.py:311
  42.2 17.4 %collective-permute-start.5 = (bf16[32,2304]{1,0:T(8,128)(2,1)S(1)}, bf16[32,2304]{1,0:T(8,128)(2,1)S(1)}, u32[]{:S(2)}, u32[]{:S(2)}) collective-permute-start(bf16[32,2304]{1,0:T(8,128)(2,1)S(1)} %get-tuple-element.36), channel_id=1, source_target_pairs={{0,12},{2,14},{4,8},{6,10},{8,4},{10,6},{12,0},{14,2},{1,13},{3,15... | collective-permute-start | bytes 442376 | tf_op jit(solution)/shard_map/ppermute | solution.py:311
  58.4 9.9 %collective-permute-start.6 = (bf16[32,2304]{1,0:T(8,128)(2,1)S(1)}, bf16[32,2304]{1,0:T(8,128)(2,1)S(1)}, u32[]{:S(2)}, u32[]{:S(2)}) collective-permute-start(bf16[32,2304]{1,0:T(8,128)(2,1)S(1)} %get-tuple-element.37), channel_id=1, source_target_pairs={{0,10},{2,8},{4,14},{6,12},{8,2},{10,0},{12,6},{14,4},{1,11},{3,9}... | collective-permute-start | bytes 442376 | tf_op jit(solution)/shard_map/ppermute | solution.py:311
  58.5 9.9 %collective-permute-start.7 = (bf16[32,2304]{1,0:T(8,128)(2,1)S(1)}, bf16[32,2304]{1,0:T(8,128)(2,1)S(1)}, u32[]{:S(2)}, u32[]{:S(2)}) collective-permute-start(bf16[32,2304]{1,0:T(8,128)(2,1)S(1)} %get-tuple-element.38), channel_id=1, source_target_pairs={{0,14},{2,12},{4,10},{6,8},{8,6},{10,4},{12,2},{14,0},{1,15},{3,13... | collective-permute-start | bytes 442376 | tf_op jit(solution)/shard_map/ppermute | solution.py:311

commit v17 on v16

--- a/solution.py
+++ b/solution.py
@@ -239,7 +239,7 @@
 
 def exchange_order(ranks):
     near, far = list(range(1, ranks // 2)), list(range(ranks // 2, ranks))
-    return far[:1] + near + far[2::2] + far[1::2]
+    return near[:-1] + far[::2] + far[1::2] + near[-1:]
 
 
 def local(

time: 69.9 us -> 68.9 us (0.986)
  waiting for transfers between devices: 25.1 us -> 20.5 us
  starting transfers between devices: 15.7 us -> 19.3 us
    ppermute x7, waiting for transfers between devices: 23.5 us -> 18.8 us  [local(): piece = lax.ppermute(joined[j], 'dp', [(i, i ^ j) for i in range(ranks)])]
    ppermute x7, starting transfers between devices: 7.83 us -> 11.4 us  [local(): piece = lax.ppermute(joined[j], 'dp', [(i, i ^ j) for i in range(ranks)])]
  transfers between devices with their start and end apart: 9 -> 9, of which waited for: 3 -> 4; matrix products, arithmetic and copies ran while one was open for 0% -> 0% of each run, Pallas kernels for 20% -> 21%
where the time goes in v17:
time: 68.9 us; the launch traced here: 68.5 us
  Pallas kernels  26.5 us (38%)
  waiting for transfers between devices  20.5 us (30%)
  starting transfers between devices  19.3 us (28%)
  between operations  1.57 us (2%)
  local copies, waits for them, and re-layouts  0.69 us (1%)
    pallas_call x2, Pallas kernels, attend(): pl.pallas_call(functools.partial(attend_kernel, places // experts, first,...  22.8 us
    ppermute x7, waiting for transfers between devices, local(): piece = lax.ppermute(joined[j], 'dp', [(i, i ^ j) for i in range(ranks)])  18.8 us
    ppermute x7, starting transfers between devices, local(): piece = lax.ppermute(joined[j], 'dp', [(i, i ^ j) for i in range(ranks)])  11.4 us
    all_to_all x1, starting transfers between devices, to_all(): lax.all_to_all(outgoing.reshape(experts, capacity, -1), ('dp', 'ep'), spl...  7.41 us
    pallas_call x2, Pallas kernels, place(): pl.pallas_call(functools.partial(place_kernel, plan, cores), in_specs=[pl...  2.19 us
    ppermute x1, waiting for transfers between devices, local(): swapped = lax.ppermute(message, 'ep', [(i, i ^ 1) for i in range(cores)])  1.63 us
    pallas_call x1, Pallas kernels, join(): pl.pallas_call(join_kernel, in_specs=[pl.BlockSpec(memory_space=pl.ANY)]...  1.44 us
  transfers between devices with their start and end apart: 9, of which 4 were waited for; matrix products, arithmetic and copies ran while one was open for 0% of the time, Pallas kernels for 21%

profile of v17, /device:TPU:0, one launch (start us, length us, event | category | flops | bytes accessed | tf_op | source)
XLA Modules:
  0.0 68.5 jit_solution(13201911327488403087)
XLA Ops:
  1.3 0.0 copy-start
  1.3 0.0 copy-start.1
  1.3 0.0 copy-start.2
  1.3 11.2 %shard_map.82 = (bf16[256,1792]{1,0:T(8,128)(2,1)}, f32[8,128]{1,0:T(8,128)}) custom-call(s32[1]{0:T(128)} %constant.11.clone.1.me_ref, s32[1]{0:T(128)S(6)} %copy.11.count_ref, s32[1]{0:T(128)S(6)} %copy.12.size_ref, s32[2,128]{1,0:T(2,128)} %bitcast.5, bf16[128,4096]{1,0:T(8,128)(2,1)} %queries_hbm.3, bf16[32,128,512]{2,1,0:T(8,128)(2,1)} %key_weight_hbm.3, ...), custom_call_target="tpu_custom_call" | custom-call | flops 4227858432 | bytes 3670016 | tf_op jit(solution)/shard_map/pallas_call | solution.py:149
  12.6 7.4 %all-to-all-start = ((bf16[16,16,1792]{2,1,0:T(8,128)(2,1)}), bf16[16,16,1792]{2,1,0:T(8,128)(2,1)S(1)}, u32[]{:S(2)}, u32[]{:S(2)}) async-start(bf16[16,16,1792]{2,1,0:T(8,128)(2,1)} %bitcast.7), calls=%async_computation | async-start | bytes 1835008 | tf_op jit(solution)/shard_map/all_to_all | solution.py:285
  20.0 0.0 copy-done
  20.0 0.0 copy-done.1
  20.0 0.0 copy-done.2
  20.0 0.0 copy-start.3
  20.0 0.7 copy-done.3
  20.7 11.6 %shard_map.83 = (bf16[16,2304]{1,0:T(8,128)(2,1)S(1)}, bf16[16,2304]{1,0:T(8,128)(2,1)S(1)}, bf16[16,2304]{1,0:T(8,128)(2,1)S(1)}, bf16[16,2304]{1,0:T(8,128)(2,...) custom-call(s32[1]{0:T(128)} %bitcast.me_ref, ...), custom_call_target="tpu_custom_call" | custom-call | flops 5435817984 | bytes 4718592 | tf_op jit(solution)/shard_map/pallas_call | solution.py:149
  32.3 0.4 collective-permute-start
  32.8 1.6 %collective-permute-done.refs_7_.refs_2_ = bf16[128,2304]{1,0:T(8,128)(2,1)S(1)} collective-permute-done((bf16[128,2304]{1,0:T(8,128)(2,1)S(1)}, bf16[128,2304]{1,0:T(8,128)(2,1)S(1)}, u32[]{:S(2)}, u32[]{:S(2)}) %collective-permute-start) | collective-permute-done | bytes 589856 | tf_op jit(solution)/shard_map/ppermute | solution.py:302
  34.4 1.4 %shard_map.84 = (bf16[32,2304]{1,0:T(8,128)(2,1)S(1)}, bf16[32,2304]{1,0:T(8,128)(2,1)S(1)}, bf16[32,2304]{1,0:T(8,128)(2,1)S(1)}, bf16[32,2304]{1,0:T(8,128)(2,...) custom-call(bf16[16,2304]{1,0:T(8,128)(2,1)S(1)} %get-tuple-element.24.refs_0_, ...), custom_call_target="tpu_custom_call" | custom-call | tf_op jit(solution)/shard_map/pallas_call | solution.py:196
  35.8 2.0 %collective-permute-start.1 = (bf16[32,2304]{1,0:T(8,128)(2,1)S(1)}, bf16[32,2304]{1,0:T(8,128)(2,1)S(1)}, u32[]{:S(2)}, u32[]{:S(2)}) collective-permute-start(bf16[32,2304]{1,0:T(8,128)(2,1)S(1)} %get-tuple-element.32), channel_id=1, source_target_pairs={{0,2},{2,0},{4,6},{6,4},{8,10},{10,8},{12,14},{14,12},{1,3},{3,1},... | collective-permute-start | bytes 442376 | tf_op jit(solution)/shard_map/ppermute | solution.py:311
  37.8 1.5 %collective-permute-start.2 = (bf16[32,2304]{1,0:T(8,128)(2,1)S(1)}, bf16[32,2304]{1,0:T(8,128)(2,1)S(1)}, u32[]{:S(2)}, u32[]{:S(2)}) collective-permute-start(bf16[32,2304]{1,0:T(8,128)(2,1)S(1)} %get-tuple-element.33), channel_id=1, source_target_pairs={{0,4},{2,6},{4,0},{6,2},{8,12},{10,14},{12,8},{14,10},{1,5},{3,7},... | collective-permute-start | bytes 442376 | tf_op jit(solution)/shard_map/ppermute | solution.py:311
  39.3 2.4 %collective-permute-start.3 = (bf16[32,2304]{1,0:T(8,128)(2,1)S(1)}, bf16[32,2304]{1,0:T(8,128)(2,1)S(1)}, u32[]{:S(2)}, u32[]{:S(2)}) collective-permute-start(bf16[32,2304]{1,0:T(8,128)(2,1)S(1)} %get-tuple-element.34), channel_id=1, source_target_pairs={{0,8},{2,10},{4,12},{6,14},{8,0},{10,2},{12,4},{14,6},{1,9},{3,11}... | collective-permute-start | bytes 442376 | tf_op jit(solution)/shard_map/ppermute | solution.py:311
  41.6 0.6 collective-permute-start.4
  42.2 1.5 %collective-permute-start.5 = (bf16[32,2304]{1,0:T(8,128)(2,1)S(1)}, bf16[32,2304]{1,0:T(8,128)(2,1)S(1)}, u32[]{:S(2)}, u32[]{:S(2)}) collective-permute-start(bf16[32,2304]{1,0:T(8,128)(2,1)S(1)} %get-tuple-element.36), channel_id=1, source_target_pairs={{0,10},{2,8},{4,14},{6,12},{8,2},{10,0},{12,6},{14,4},{1,11},{3,9}... | collective-permute-start | bytes 442376 | tf_op jit(solution)/shard_map/ppermute | solution.py:311
  43.7 0.4 collective-permute-done.1.refs_0_
  44.1 3.6 %collective-permute-start.6 = (bf16[32,2304]{1,0:T(8,128)(2,1)S(1)}, bf16[32,2304]{1,0:T(8,128)(2,1)S(1)}, u32[]{:S(2)}, u32[]{:S(2)}) collective-permute-start(bf16[32,2304]{1,0:T(8,128)(2,1)S(1)} %get-tuple-element.37), channel_id=1, source_target_pairs={{0,14},{2,12},{4,10},{6,8},{8,6},{10,4},{12,2},{14,0},{1,15},{3,13... | collective-permute-start | bytes 442376 | tf_op jit(solution)/shard_map/ppermute | solution.py:311
  47.6 0.0 collective-permute-done.2.refs_1_
  47.7 0.0 collective-permute-start.7
  47.7 0.0 all-to-all-done
  47.7 1.1 %shard_map.85.refs_7_ = bf16[1,8,16,8192]{3,2,1,0:T(8,128)(2,1)} custom-call(s32[1]{0:T(128)} %bitcast.me_ref, bf16[256,1792]{1,0:T(8,128)(2,1)S(1)} %bitcast.4, bf16[16,2304]{1,0:T(8,128)(2,1)S(1)} %get-tuple-element.40.refs_1_, bf16[128,2304]{1,0:T(8,128)(2,1)S(1)} %collective-permute-done.refs_7_.refs_2_), custom_call_target="tpu_custom_call" | custom-call | tf_op jit(solution)/shard_map/pallas_call | solution.py:227
  48.8 11.2 %collective-permute-done.3.refs_2_ = bf16[32,2304]{1,0:T(8,128)(2,1)S(1)} collective-permute-done((bf16[32,2304]{1,0:T(8,128)(2,1)S(1)}, bf16[32,2304]{1,0:T(8,128)(2,1)S(1)}, u32[]{:S(2)}, u32[]{:S(2)}) %collective-permute-start.3) | collective-permute-done | bytes 147488 | tf_op jit(solution)/shard_map/ppermute | solution.py:311
  60.0 0.0 collective-permute-done.4.refs_3_
  60.0 7.2 %collective-permute-done.5.refs_4_ = bf16[32,2304]{1,0:T(8,128)(2,1)S(1)} collective-permute-done((bf16[32,2304]{1,0:T(8,128)(2,1)S(1)}, bf16[32,2304]{1,0:T(8,128)(2,1)S(1)}, u32[]{:S(2)}, u32[]{:S(2)}) %collective-permute-start.5) | collective-permute-done | bytes 147488 | tf_op jit(solution)/shard_map/ppermute | solution.py:311
  67.2 0.0 collective-permute-done.6.refs_5_
  67.2 0.0 collective-permute-done.7.refs_6_
  67.2 1.1 %shard_map.86 = bf16[1,8,16,8192]{3,2,1,0:T(8,128)(2,1)} custom-call(s32[1]{0:T(128)} %bitcast.me_ref, bf16[32,2304]{1,0:T(8,128)(2,1)S(1)} %collective-permute-done.1.refs_0_, bf16[32,2304]{1,0:T(8,128)(2,1)S(1)} %collective-permute-done.2.refs_1_, bf16[32,2304]{1,0:T(8,128)(2,1)S(1)} %collective-permute-done.3.refs_2_, ...), custom_call_target="tpu_custom_call", output_to_operand_aliasing={{}: (8, {})} | custom-call | tf_op jit(solution)/shard_map/pallas_call | solution.py:227
Async XLA Ops:
  1.3 18.7 %copy-start = (bf16[128,4096]{1,0:T(8,128)(2,1)S(1)}, bf16[128,4096]{1,0:T(8,128)(2,1)}, u32[]{:S(2)}) copy-start(bf16[128,4096]{1,0:T(8,128)(2,1)} %queries_hbm.3) | copy-start | bytes 3145732
  1.3 18.7 %copy-start.1 = (bf16[128,512]{1,0:T(8,128)(2,1)S(1)}, bf16[128,512]{1,0:T(8,128)(2,1)}, u32[]{:S(2)}) copy-start(bf16[128,512]{1,0:T(8,128)(2,1)} %fresh_hbm.3) | copy-start | bytes 393220
  1.3 18.7 %copy-start.2 = (s32[128,2]{0,1:T(2,128)S(1)}, s32[128,2]{0,1:T(2,128)}, u32[]{:S(2)}) copy-start(s32[128,2]{0,1:T(2,128)} %param.15) | copy-start | bytes 3076
  12.6 35.1 %all-to-all-start = ((bf16[16,16,1792]{2,1,0:T(8,128)(2,1)}), bf16[16,16,1792]{2,1,0:T(8,128)(2,1)S(1)}, u32[]{:S(2)}, u32[]{:S(2)}) async-start(bf16[16,16,1792]{2,1,0:T(8,128)(2,1)} %bitcast.7), calls=%async_computation | async-start | bytes 1835008 | tf_op jit(solution)/shard_map/all_to_all | solution.py:285
  20.0 0.7 %copy-start.3 = (f32[8,128]{1,0:T(8,128)S(1)}, f32[8,128]{1,0:T(8,128)}, u32[]{:S(2)}) copy-start(f32[8,128]{1,0:T(8,128)} %get-tuple-element.23.rest_0_) | copy-start | bytes 12292
  32.3 2.1 %collective-permute-start = (bf16[128,2304]{1,0:T(8,128)(2,1)S(1)}, bf16[128,2304]{1,0:T(8,128)(2,1)S(1)}, u32[]{:S(2)}, u32[]{:S(2)}) collective-permute-start(bf16[128,2304]{1,0:T(8,128)(2,1)S(1)} %get-tuple-element.31), channel_id=1, source_target_pairs={{0,1},{1,0},{2,3},{3,2},{4,5},{5,4},{6,7},{7,6},{8,9},{9,8},{10,11... | collective-permute-start | bytes 1769480 | tf_op jit(solution)/shard_map/ppermute | solution.py:302
  35.8 8.2 %collective-permute-start.1 = (bf16[32,2304]{1,0:T(8,128)(2,1)S(1)}, bf16[32,2304]{1,0:T(8,128)(2,1)S(1)}, u32[]{:S(2)}, u32[]{:S(2)}) collective-permute-start(bf16[32,2304]{1,0:T(8,128)(2,1)S(1)} %get-tuple-element.32), channel_id=1, source_target_pairs={{0,2},{2,0},{4,6},{6,4},{8,10},{10,8},{12,14},{14,12},{1,3},{3,1},... | collective-permute-start | bytes 442376 | tf_op jit(solution)/shard_map/ppermute | solution.py:311
  37.8 9.8 %collective-permute-start.2 = (bf16[32,2304]{1,0:T(8,128)(2,1)S(1)}, bf16[32,2304]{1,0:T(8,128)(2,1)S(1)}, u32[]{:S(2)}, u32[]{:S(2)}) collective-permute-start(bf16[32,2304]{1,0:T(8,128)(2,1)S(1)} %get-tuple-element.33), channel_id=1, source_target_pairs={{0,4},{2,6},{4,0},{6,2},{8,12},{10,14},{12,8},{14,10},{1,5},{3,7},... | collective-permute-start | bytes 442376 | tf_op jit(solution)/shard_map/ppermute | solution.py:311
  39.3 20.7 %collective-permute-start.3 = (bf16[32,2304]{1,0:T(8,128)(2,1)S(1)}, bf16[32,2304]{1,0:T(8,128)(2,1)S(1)}, u32[]{:S(2)}, u32[]{:S(2)}) collective-permute-start(bf16[32,2304]{1,0:T(8,128)(2,1)S(1)} %get-tuple-element.34), channel_id=1, source_target_pairs={{0,8},{2,10},{4,12},{6,14},{8,0},{10,2},{12,4},{14,6},{1,9},{3,11}... | collective-permute-start | bytes 442376 | tf_op jit(solution)/shard_map/ppermute | solution.py:311
  41.6 18.4 %collective-permute-start.4 = (bf16[32,2304]{1,0:T(8,128)(2,1)S(1)}, bf16[32,2304]{1,0:T(8,128)(2,1)S(1)}, u32[]{:S(2)}, u32[]{:S(2)}) collective-permute-start(bf16[32,2304]{1,0:T(8,128)(2,1)S(1)} %get-tuple-element.35), channel_id=1, source_target_pairs={{0,12},{2,14},{4,8},{6,10},{8,4},{10,6},{12,0},{14,2},{1,13},{3,15... | collective-permute-start | bytes 442376 | tf_op jit(solution)/shard_map/ppermute | solution.py:311
  42.2 25.0 %collective-permute-start.5 = (bf16[32,2304]{1,0:T(8,128)(2,1)S(1)}, bf16[32,2304]{1,0:T(8,128)(2,1)S(1)}, u32[]{:S(2)}, u32[]{:S(2)}) collective-permute-start(bf16[32,2304]{1,0:T(8,128)(2,1)S(1)} %get-tuple-element.36), channel_id=1, source_target_pairs={{0,10},{2,8},{4,14},{6,12},{8,2},{10,0},{12,6},{14,4},{1,11},{3,9}... | collective-permute-start | bytes 442376 | tf_op jit(solution)/shard_map/ppermute | solution.py:311
  44.1 23.2 %collective-permute-start.6 = (bf16[32,2304]{1,0:T(8,128)(2,1)S(1)}, bf16[32,2304]{1,0:T(8,128)(2,1)S(1)}, u32[]{:S(2)}, u32[]{:S(2)}) collective-permute-start(bf16[32,2304]{1,0:T(8,128)(2,1)S(1)} %get-tuple-element.37), channel_id=1, source_target_pairs={{0,14},{2,12},{4,10},{6,8},{8,6},{10,4},{12,2},{14,0},{1,15},{3,13... | collective-permute-start | bytes 442376 | tf_op jit(solution)/shard_map/ppermute | solution.py:311
  47.7 19.6 %collective-permute-start.7 = (bf16[32,2304]{1,0:T(8,128)(2,1)S(1)}, bf16[32,2304]{1,0:T(8,128)(2,1)S(1)}, u32[]{:S(2)}, u32[]{:S(2)}) collective-permute-start(bf16[32,2304]{1,0:T(8,128)(2,1)S(1)} %get-tuple-element.38), channel_id=1, source_target_pairs={{0,6},{2,4},{4,2},{6,0},{8,14},{10,12},{12,10},{14,8},{1,7},{3,5},... | collective-permute-start | bytes 442376 | tf_op jit(solution)/shard_map/ppermute | solution.py:311

commit v18 on v17

--- a/solution.py
+++ b/solution.py
@@ -10,7 +10,7 @@
 
 SPAN = 64
 STACK = 4
-CHUNKS = (7, 9)
+CHUNKS = (15, 17)
 DIRECT = 16
 ALL_VMEM = 63_400_000
 VMEM = 51 * 1024 * 1024

time: 68.9 us -> 69.6 us (1.010)
  local copies, waits for them, and re-layouts: 0.69 us -> 1.91 us
    unnamed x8, local copies, waits for them, and re-layouts: 0.69 us -> 1.91 us
  transfers between devices with their start and end apart: 9 -> 9, of which waited for: 4 -> 4; matrix products, arithmetic and copies ran while one was open for 0% -> 0% of each run, Pallas kernels for 21% -> 20%
where the time goes in v18:
time: 69.6 us; the launch traced here: 69.3 us
  Pallas kernels  26.6 us (38%)
  waiting for transfers between devices  20.3 us (29%)
  starting transfers between devices  18.9 us (27%)
  local copies, waits for them, and re-layouts  1.91 us (3%)
  between operations  1.56 us (2%)
    pallas_call x2, Pallas kernels, attend(): pl.pallas_call(functools.partial(attend_kernel, places // experts, first,...  23.1 us
    ppermute x7, waiting for transfers between devices, local(): piece = lax.ppermute(joined[j], 'dp', [(i, i ^ j) for i in range(ranks)])  18.7 us
    ppermute x7, starting transfers between devices, local(): piece = lax.ppermute(joined[j], 'dp', [(i, i ^ j) for i in range(ranks)])  11 us
    all_to_all x1, starting transfers between devices, to_all(): lax.all_to_all(outgoing.reshape(experts, capacity, -1), ('dp', 'ep'), spl...  7.41 us
    pallas_call x2, Pallas kernels, place(): pl.pallas_call(functools.partial(place_kernel, plan, cores), in_specs=[pl...  2.19 us
    unnamed x8, local copies, waits for them, and re-layouts  1.91 us
    ppermute x1, waiting for transfers between devices, local(): swapped = lax.ppermute(message, 'ep', [(i, i ^ 1) for i in range(cores)])  1.58 us
  transfers between devices with their start and end apart: 9, of which 4 were waited for; matrix products, arithmetic and copies ran while one was open for 0% of the time, Pallas kernels for 20%

profile of v18, /device:TPU:0, one launch (start us, length us, event | category | flops | bytes accessed | tf_op | source)
XLA Modules:
  0.0 69.3 jit_solution(9987805041554146287)
XLA Ops:
  1.3 0.0 copy-start.1
  1.3 0.0 copy-start.2
  1.3 11.9 %shard_map.82 = (bf16[256,1920]{1,0:T(8,128)(2,1)}, f32[8,128]{1,0:T(8,128)}) custom-call(s32[1]{0:T(128)} %constant.11.clone.1.me_ref, s32[1]{0:T(128)S(6)} %copy.11.count_ref, s32[1]{0:T(128)S(6)} %copy.12.size_ref, s32[2,128]{1,0:T(2,128)} %bitcast.5, bf16[128,4096]{1,0:T(8,128)(2,1)} %queries_hbm.3, bf16[32,128,512]{2,1,0:T(8,128)(2,1)} %key_weight_hbm.3, ...), custom_call_target="tpu_custom_call" | custom-call | flops 4529848320 | bytes 3932160 | tf_op jit(solution)/shard_map/pallas_call | solution.py:149
  13.2 7.4 %all-to-all-start = ((bf16[16,16,1920]{2,1,0:T(8,128)(2,1)}), bf16[16,16,1920]{2,1,0:T(8,128)(2,1)S(1)}, u32[]{:S(2)}, u32[]{:S(2)}) async-start(bf16[16,16,1920]{2,1,0:T(8,128)(2,1)} %bitcast.7), calls=%async_computation | async-start | bytes 1966080 | tf_op jit(solution)/shard_map/all_to_all | solution.py:285
  20.6 0.0 copy-done.1
  20.6 0.0 copy-done.2
  20.6 0.0 copy-start
  20.7 1.2 %copy-done = bf16[128,4096]{1,0:T(8,128)(2,1)S(1)} copy-done((bf16[128,4096]{1,0:T(8,128)(2,1)S(1)}, bf16[128,4096]{1,0:T(8,128)(2,1)}, u32[]{:S(2)}) %copy-start) | copy-done | bytes 1048600
  21.9 0.0 copy-start.3
  21.9 0.7 copy-done.3
  22.6 11.2 %shard_map.83 = (bf16[16,2176]{1,0:T(8,128)(2,1)S(1)}, bf16[16,2176]{1,0:T(8,128)(2,1)S(1)}, bf16[16,2176]{1,0:T(8,128)(2,1)S(1)}, bf16[16,2176]{1,0:T(8,128)(2,...) custom-call(s32[1]{0:T(128)} %bitcast.me_ref, ...), custom_call_target="tpu_custom_call" | custom-call | flops 5133828096 | bytes 4456448 | tf_op jit(solution)/shard_map/pallas_call | solution.py:149
  33.8 0.5 collective-permute-start
  34.2 1.6 %collective-permute-done.refs_7_.refs_2_ = bf16[128,2176]{1,0:T(8,128)(2,1)S(1)} collective-permute-done((bf16[128,2176]{1,0:T(8,128)(2,1)S(1)}, bf16[128,2176]{1,0:T(8,128)(2,1)S(1)}, u32[]{:S(2)}, u32[]{:S(2)}) %collective-permute-start) | collective-permute-done | bytes 557088 | tf_op jit(solution)/shard_map/ppermute | solution.py:302
  35.8 1.4 %shard_map.84 = (bf16[32,2176]{1,0:T(8,128)(2,1)S(1)}, bf16[32,2176]{1,0:T(8,128)(2,1)S(1)}, bf16[32,2176]{1,0:T(8,128)(2,1)S(1)}, bf16[32,2176]{1,0:T(8,128)(2,...) custom-call(bf16[16,2176]{1,0:T(8,128)(2,1)S(1)} %get-tuple-element.24.refs_0_, ...), custom_call_target="tpu_custom_call" | custom-call | tf_op jit(solution)/shard_map/pallas_call | solution.py:196
  37.2 2.0 %collective-permute-start.1 = (bf16[32,2176]{1,0:T(8,128)(2,1)S(1)}, bf16[32,2176]{1,0:T(8,128)(2,1)S(1)}, u32[]{:S(2)}, u32[]{:S(2)}) collective-permute-start(bf16[32,2176]{1,0:T(8,128)(2,1)S(1)} %get-tuple-element.32), channel_id=1, source_target_pairs={{0,2},{2,0},{4,6},{6,4},{8,10},{10,8},{12,14},{14,12},{1,3},{3,1},... | collective-permute-start | bytes 417800 | tf_op jit(solution)/shard_map/ppermute | solution.py:311
  39.1 1.5 %collective-permute-start.2 = (bf16[32,2176]{1,0:T(8,128)(2,1)S(1)}, bf16[32,2176]{1,0:T(8,128)(2,1)S(1)}, u32[]{:S(2)}, u32[]{:S(2)}) collective-permute-start(bf16[32,2176]{1,0:T(8,128)(2,1)S(1)} %get-tuple-element.33), channel_id=1, source_target_pairs={{0,4},{2,6},{4,0},{6,2},{8,12},{10,14},{12,8},{14,10},{1,5},{3,7},... | collective-permute-start | bytes 417800 | tf_op jit(solution)/shard_map/ppermute | solution.py:311
  40.6 2.4 %collective-permute-start.3 = (bf16[32,2176]{1,0:T(8,128)(2,1)S(1)}, bf16[32,2176]{1,0:T(8,128)(2,1)S(1)}, u32[]{:S(2)}, u32[]{:S(2)}) collective-permute-start(bf16[32,2176]{1,0:T(8,128)(2,1)S(1)} %get-tuple-element.34), channel_id=1, source_target_pairs={{0,8},{2,10},{4,12},{6,14},{8,0},{10,2},{12,4},{14,6},{1,9},{3,11}... | collective-permute-start | bytes 417800 | tf_op jit(solution)/shard_map/ppermute | solution.py:311
  43.0 0.6 collective-permute-start.4
  43.5 1.5 %collective-permute-start.5 = (bf16[32,2176]{1,0:T(8,128)(2,1)S(1)}, bf16[32,2176]{1,0:T(8,128)(2,1)S(1)}, u32[]{:S(2)}, u32[]{:S(2)}) collective-permute-start(bf16[32,2176]{1,0:T(8,128)(2,1)S(1)} %get-tuple-element.36), channel_id=1, source_target_pairs={{0,10},{2,8},{4,14},{6,12},{8,2},{10,0},{12,6},{14,4},{1,11},{3,9}... | collective-permute-start | bytes 417800 | tf_op jit(solution)/shard_map/ppermute | solution.py:311
  45.0 0.5 collective-permute-done.1.refs_0_
  45.5 3.2 %collective-permute-start.6 = (bf16[32,2176]{1,0:T(8,128)(2,1)S(1)}, bf16[32,2176]{1,0:T(8,128)(2,1)S(1)}, u32[]{:S(2)}, u32[]{:S(2)}) collective-permute-start(bf16[32,2176]{1,0:T(8,128)(2,1)S(1)} %get-tuple-element.37), channel_id=1, source_target_pairs={{0,14},{2,12},{4,10},{6,8},{8,6},{10,4},{12,2},{14,0},{1,15},{3,13... | collective-permute-start | bytes 417800 | tf_op jit(solution)/shard_map/ppermute | solution.py:311
  48.7 0.0 collective-permute-done.2.refs_1_
  48.7 0.0 collective-permute-start.7
  48.7 0.0 all-to-all-done
  48.7 1.1 %shard_map.85.refs_7_ = bf16[1,8,16,8192]{3,2,1,0:T(8,128)(2,1)} custom-call(s32[1]{0:T(128)} %bitcast.me_ref, bf16[256,1920]{1,0:T(8,128)(2,1)S(1)} %bitcast.4, bf16[16,2176]{1,0:T(8,128)(2,1)S(1)} %get-tuple-element.40.refs_1_, bf16[128,2176]{1,0:T(8,128)(2,1)S(1)} %collective-permute-done.refs_7_.refs_2_), custom_call_target="tpu_custom_call" | custom-call | tf_op jit(solution)/shard_map/pallas_call | solution.py:227
  49.9 11.3 %collective-permute-done.3.refs_2_ = bf16[32,2176]{1,0:T(8,128)(2,1)S(1)} collective-permute-done((bf16[32,2176]{1,0:T(8,128)(2,1)S(1)}, bf16[32,2176]{1,0:T(8,128)(2,1)S(1)}, u32[]{:S(2)}, u32[]{:S(2)}) %collective-permute-start.3) | collective-permute-done | bytes 139296 | tf_op jit(solution)/shard_map/ppermute | solution.py:311
  61.1 0.0 collective-permute-done.4.refs_3_
  61.1 6.9 %collective-permute-done.5.refs_4_ = bf16[32,2176]{1,0:T(8,128)(2,1)S(1)} collective-permute-done((bf16[32,2176]{1,0:T(8,128)(2,1)S(1)}, bf16[32,2176]{1,0:T(8,128)(2,1)S(1)}, u32[]{:S(2)}, u32[]{:S(2)}) %collective-permute-start.5) | collective-permute-done | bytes 139296 | tf_op jit(solution)/shard_map/ppermute | solution.py:311
  68.1 0.0 collective-permute-done.6.refs_5_
  68.1 0.0 collective-permute-done.7.refs_6_
  68.1 1.1 %shard_map.86 = bf16[1,8,16,8192]{3,2,1,0:T(8,128)(2,1)} custom-call(s32[1]{0:T(128)} %bitcast.me_ref, bf16[32,2176]{1,0:T(8,128)(2,1)S(1)} %collective-permute-done.1.refs_0_, bf16[32,2176]{1,0:T(8,128)(2,1)S(1)} %collective-permute-done.2.refs_1_, bf16[32,2176]{1,0:T(8,128)(2,1)S(1)} %collective-permute-done.3.refs_2_, ...), custom_call_target="tpu_custom_call", output_to_operand_aliasing={{}: (8, {})} | custom-call | tf_op jit(solution)/shard_map/pallas_call | solution.py:227
Async XLA Ops:
  1.3 19.3 %copy-start.1 = (bf16[128,512]{1,0:T(8,128)(2,1)S(1)}, bf16[128,512]{1,0:T(8,128)(2,1)}, u32[]{:S(2)}) copy-start(bf16[128,512]{1,0:T(8,128)(2,1)} %fresh_hbm.3) | copy-start | bytes 393220
  1.3 19.3 %copy-start.2 = (s32[128,2]{0,1:T(2,128)S(1)}, s32[128,2]{0,1:T(2,128)}, u32[]{:S(2)}) copy-start(s32[128,2]{0,1:T(2,128)} %param.15) | copy-start | bytes 3076
  13.2 35.5 %all-to-all-start = ((bf16[16,16,1920]{2,1,0:T(8,128)(2,1)}), bf16[16,16,1920]{2,1,0:T(8,128)(2,1)S(1)}, u32[]{:S(2)}, u32[]{:S(2)}) async-start(bf16[16,16,1920]{2,1,0:T(8,128)(2,1)} %bitcast.7), calls=%async_computation | async-start | bytes 1966080 | tf_op jit(solution)/shard_map/all_to_all | solution.py:285
  20.6 1.2 %copy-start = (bf16[128,4096]{1,0:T(8,128)(2,1)S(1)}, bf16[128,4096]{1,0:T(8,128)(2,1)}, u32[]{:S(2)}) copy-start(bf16[128,4096]{1,0:T(8,128)(2,1)} %queries_hbm.3) | copy-start | bytes 3145732
  21.9 0.7 copy-start.3
  33.8 2.0 %collective-permute-start = (bf16[128,2176]{1,0:T(8,128)(2,1)S(1)}, bf16[128,2176]{1,0:T(8,128)(2,1)S(1)}, u32[]{:S(2)}, u32[]{:S(2)}) collective-permute-start(bf16[128,2176]{1,0:T(8,128)(2,1)S(1)} %get-tuple-element.31), channel_id=1, source_target_pairs={{0,1},{1,0},{2,3},{3,2},{4,5},{5,4},{6,7},{7,6},{8,9},{9,8},{10,11... | collective-permute-start | bytes 1671176 | tf_op jit(solution)/shard_map/ppermute | solution.py:302
  37.2 8.3 %collective-permute-start.1 = (bf16[32,2176]{1,0:T(8,128)(2,1)S(1)}, bf16[32,2176]{1,0:T(8,128)(2,1)S(1)}, u32[]{:S(2)}, u32[]{:S(2)}) collective-permute-start(bf16[32,2176]{1,0:T(8,128)(2,1)S(1)} %get-tuple-element.32), channel_id=1, source_target_pairs={{0,2},{2,0},{4,6},{6,4},{8,10},{10,8},{12,14},{14,12},{1,3},{3,1},... | collective-permute-start | bytes 417800 | tf_op jit(solution)/shard_map/ppermute | solution.py:311
  39.1 9.6 %collective-permute-start.2 = (bf16[32,2176]{1,0:T(8,128)(2,1)S(1)}, bf16[32,2176]{1,0:T(8,128)(2,1)S(1)}, u32[]{:S(2)}, u32[]{:S(2)}) collective-permute-start(bf16[32,2176]{1,0:T(8,128)(2,1)S(1)} %get-tuple-element.33), channel_id=1, source_target_pairs={{0,4},{2,6},{4,0},{6,2},{8,12},{10,14},{12,8},{14,10},{1,5},{3,7},... | collective-permute-start | bytes 417800 | tf_op jit(solution)/shard_map/ppermute | solution.py:311
  40.6 20.5 %collective-permute-start.3 = (bf16[32,2176]{1,0:T(8,128)(2,1)S(1)}, bf16[32,2176]{1,0:T(8,128)(2,1)S(1)}, u32[]{:S(2)}, u32[]{:S(2)}) collective-permute-start(bf16[32,2176]{1,0:T(8,128)(2,1)S(1)} %get-tuple-element.34), channel_id=1, source_target_pairs={{0,8},{2,10},{4,12},{6,14},{8,0},{10,2},{12,4},{14,6},{1,9},{3,11}... | collective-permute-start | bytes 417800 | tf_op jit(solution)/shard_map/ppermute | solution.py:311
  43.0 18.2 %collective-permute-start.4 = (bf16[32,2176]{1,0:T(8,128)(2,1)S(1)}, bf16[32,2176]{1,0:T(8,128)(2,1)S(1)}, u32[]{:S(2)}, u32[]{:S(2)}) collective-permute-start(bf16[32,2176]{1,0:T(8,128)(2,1)S(1)} %get-tuple-element.35), channel_id=1, source_target_pairs={{0,12},{2,14},{4,8},{6,10},{8,4},{10,6},{12,0},{14,2},{1,13},{3,15... | collective-permute-start | bytes 417800 | tf_op jit(solution)/shard_map/ppermute | solution.py:311
  43.5 24.5 %collective-permute-start.5 = (bf16[32,2176]{1,0:T(8,128)(2,1)S(1)}, bf16[32,2176]{1,0:T(8,128)(2,1)S(1)}, u32[]{:S(2)}, u32[]{:S(2)}) collective-permute-start(bf16[32,2176]{1,0:T(8,128)(2,1)S(1)} %get-tuple-element.36), channel_id=1, source_target_pairs={{0,10},{2,8},{4,14},{6,12},{8,2},{10,0},{12,6},{14,4},{1,11},{3,9}... | collective-permute-start | bytes 417800 | tf_op jit(solution)/shard_map/ppermute | solution.py:311
  45.5 22.5 %collective-permute-start.6 = (bf16[32,2176]{1,0:T(8,128)(2,1)S(1)}, bf16[32,2176]{1,0:T(8,128)(2,1)S(1)}, u32[]{:S(2)}, u32[]{:S(2)}) collective-permute-start(bf16[32,2176]{1,0:T(8,128)(2,1)S(1)} %get-tuple-element.37), channel_id=1, source_target_pairs={{0,14},{2,12},{4,10},{6,8},{8,6},{10,4},{12,2},{14,0},{1,15},{3,13... | collective-permute-start | bytes 417800 | tf_op jit(solution)/shard_map/ppermute | solution.py:311
  48.7 19.3 %collective-permute-start.7 = (bf16[32,2176]{1,0:T(8,128)(2,1)S(1)}, bf16[32,2176]{1,0:T(8,128)(2,1)S(1)}, u32[]{:S(2)}, u32[]{:S(2)}) collective-permute-start(bf16[32,2176]{1,0:T(8,128)(2,1)S(1)} %get-tuple-element.38), channel_id=1, source_target_pairs={{0,6},{2,4},{4,2},{6,0},{8,14},{10,12},{12,10},{14,8},{1,7},{3,5},... | collective-permute-start | bytes 417800 | tf_op jit(solution)/shard_map/ppermute | solution.py:311
